TPU v7x, 32 devices: a whole 2x2x4 slice. The times are simulated.
32 devices in a mesh: rows: 8 (over z, y), feat: 4 (over x, core).
Axes of the slice: x: 2, y: 2, z: 4, core: 2. Of those that a mesh axis runs over, the one named last changes fastest.
Arguments:
- features: bfloat16 [3072, 24576], P('rows', 'feat'), may hold values from -6 to 6
- targets: float32 [3072, 512], P('rows'), may hold values from -6 to 6
- block_index: int32 [3, 128], replicated, may hold values from 0 to 3071, as said below
- inverse: float32 [3, 128, 128], replicated, may hold values from -0.5 to 0.5
Outputs:
- residual: float32 [3072, 512], P('rows')
- coeffs: float32 [3072, 512], P('rows')
Inputs may be any that keep to these rules, and one draw needn't show every extreme that they name: `block_index`: entries 16 * d to 16 * (d + 1) - 1 of each row are distinct examples among 384 * d to 384 * (d + 1) - 1.
All inputs are finite; a program needn't handle non-finite values.
Results may differ from a plain program's by a relative error of at most 0.0003.
Values may be sent and summed in bfloat16 or wider, within the bound.
No kernel may reach another device: no remote copies, remote signals or barrier semaphores. Data moves between devices by JAX's collectives and lax.ppermute only.
A program may use at most 64 MiB of HBM per device.

v0:
```python
import jax
import jax.numpy as jnp
from jax import lax
from jax.sharding import PartitionSpec as P

F = 24576


def quadratic(gram):
    scaled = gram / F
    return scaled + scaled * scaled


def local(features, targets, block_index, inverse):
    row_rank = lax.axis_index("rows")
    row_count = lax.axis_size("rows")
    rows_here = features.shape[0]
    steps_total = block_index.shape[0]
    per_device = block_index.shape[1] // row_count
    residual = targets
    coeffs = jnp.zeros(targets.shape, jnp.float32)
    own_picks = (
        lax.dynamic_slice_in_dim(block_index, row_rank * per_device, per_device, 1)
        - row_rank * rows_here
    )
    kernels = []
    every_picked = jnp.take(features, own_picks.reshape(-1), axis=0)
    every_part = lax.dot_general(
        features,
        lax.all_gather(every_picked, "rows", axis=0, tiled=True),
        (((1,), (1,)), ((), ())),
        preferred_element_type=jnp.float32,
    )
    every_gram = lax.psum(every_part, "feat")
    every_kernel = quadratic(every_gram)
    arranged = every_kernel.reshape(rows_here, row_count, steps_total, per_device)
    for step in range(steps_total):
        kernels.append(arranged[:, :, step, :].reshape(rows_here, row_count * per_device))
    for step in range(steps_total):
        picks = own_picks[step]
        kernel = kernels[step]
        own_resid = jnp.take(residual, picks, axis=0)
        block_resid = lax.all_gather(own_resid, "rows", axis=0, tiled=True)
        precond = inverse[step]
        delta = jnp.dot(
            precond,
            block_resid,
            precision=lax.Precision.HIGHEST,
            preferred_element_type=jnp.float32,
        )
        update = jnp.dot(
            kernel, delta, precision=lax.Precision.HIGHEST, preferred_element_type=jnp.float32
        )
        own_delta = lax.dynamic_slice_in_dim(delta, row_rank * per_device, per_device, 0)
        residual = residual - update
        residual = residual.at[picks].add(-1.0 * own_delta)
        coeffs = coeffs.at[picks].add(own_delta)
    return (residual, coeffs)


def solution(mesh):
    return jax.shard_map(
        local,
        mesh=mesh,
        in_specs=(P("rows", "feat"), P("rows", None), P(), P()),
        out_specs=(P("rows", None), P("rows", None)),
        check_vma=False,
    )
```

profile of v0, /device:TPU:0, one launch (start us, length us, event | category | flops | bytes accessed | tf_op | source)
XLA Modules:
  0.0 217.2 jit_solution(6580847421701751144)
XLA Ops:
  7.2 0.0 copy-start
  7.2 0.0 copy-start.3
  7.2 0.0 all-gather.2.cloned.1.call-start
  7.2 0.8 dynamic-slice_subtract_fusion
  8.1 0.1 reshape.136
  8.2 0.1 reshape.135
  8.3 4.4 %gather_fusion = bf16[48,6144]{1,0:T(8,128)(2,1)S(1)} fusion(bf16[384,6144]{1,0:T(8,128)(2,1)} %param.6, s32[1024]{0:T(1024)S(1)} %pad_clamp_fusion.3), kind=kCustom, calls=%fused_computation.3 | custom fusion | bytes 1179840 | tf_op jit(solution)/shard_map/jit(_take)/gather | solution.py:27
  12.7 0.9 broadcast_select_fusion
  13.6 0.0 all-gather.2.cloned.1.call-update
  13.6 0.0 all-reduce.2.cloned.1.call-start
  13.7 0.0 copy-done
  13.7 0.6 gather_fusion.1
  14.3 0.1 broadcast_select_fusion.3
  14.4 33.5 %all_gather.13 = f32[128,512]{1,0:T(8,128)S(1)} all-gather(f32[16,512]{1,0:T(8,128)S(1)} %broadcast_select_fusion.3), channel_id=1, replica_groups=mesh['rows'=8,'feat'=4] {'rows'}, dimensions={0}, use_global_device_ids=true | all-gather | bytes 294912 | tf_op jit(solution)/shard_map/all_gather | solution.py:43
  47.9 0.0 copy-done.3
  47.9 0.4 fusion.6
  48.3 49.7 %all-gather.2.cloned.1.call-done = bf16[384,6144]{1,0:T(8,128)(2,1)} async-done(((bf16[48,6144]{1,0:T(8,128)(2,1)}), bf16[384,6144]{1,0:T(8,128)(2,1)}) %all-gather.2.cloned.1.call-update) | async-done | bytes 4718608 | tf_op jit(solution)/shard_map/all_gather | solution.py:30
  98.0 7.2 %convolution_bitcast_fusion = f32[384,384]{0,1:T(8,128)} fusion(bf16[384,6144]{1,0:T(8,128)(2,1)} %all-gather.2.cloned.1.call-done, bf16[384,6144]{1,0:T(8,128)(2,1)} %param.6), kind=kOutput, calls=%fused_computation.13 | convolution fusion | flops 1811939328 | bytes 10027008 | tf_op jit(solution)/shard_map/dot_general | solution.py:28
  105.2 0.0 all-reduce.2.cloned.1.call-update
  105.2 0.9 scatter_custom_fusion.3
  106.1 30.8 %all-reduce.2.cloned.1.call-done = f32[384,384]{0,1:T(8,128)} async-done(((f32[384,384]{0,1:T(8,128)}), f32[384,384]{0,1:T(8,128)}) %all-reduce.2.cloned.1.call-update) | async-done | bytes 589840 | tf_op jit(solution)/shard_map/psum | solution.py:34
  136.9 1.1 multiply_add_fusion
  138.1 0.8 convolution_subtract_fusion.2
  139.0 1.0 scatter_custom_fusion
  140.0 0.6 gather_fusion.2
  140.6 0.1 broadcast_select_fusion.2
  140.6 30.8 %all_gather.14 = f32[128,512]{1,0:T(8,128)S(1)} all-gather(f32[16,512]{1,0:T(8,128)S(1)} %broadcast_select_fusion.2), channel_id=1, replica_groups=mesh['rows'=8,'feat'=4] {'rows'}, dimensions={0}, use_global_device_ids=true | all-gather | bytes 294912 | tf_op jit(solution)/shard_map/all_gather | solution.py:43
  171.4 0.4 fusion.4
  171.8 0.9 convolution_subtract_fusion.1
  172.7 1.0 scatter_custom_fusion.1
  173.7 0.6 gather_fusion.3
  174.3 0.1 broadcast_select_fusion.1
  174.4 30.7 %all_gather.15 = f32[128,512]{1,0:T(8,128)S(1)} all-gather(f32[16,512]{1,0:T(8,128)S(1)} %broadcast_select_fusion.1), channel_id=1, replica_groups=mesh['rows'=8,'feat'=4] {'rows'}, dimensions={0}, use_global_device_ids=true | all-gather | bytes 294912 | tf_op jit(solution)/shard_map/all_gather | solution.py:43
  205.1 0.4 fusion.2
  205.5 1.0 scatter_custom_fusion.4
  206.5 0.9 convolution_subtract_fusion
  207.4 1.0 scatter_custom_fusion.2
  208.4 0.0 copy-start.2
  208.4 1.0 scatter_custom_fusion.5
  209.4 0.0 copy-done.2
  209.5 0.0 copy-start.1
  209.5 0.9 copy-done.1
  (9 shorter events, 0.1 us)
Async XLA Ops:
  7.2 6.6 %copy-start = (f32[384,512]{1,0:T(8,128)S(1)}, f32[384,512]{1,0:T(8,128)}, u32[]{:S(2)}) copy-start(f32[384,512]{1,0:T(8,128)} %param.7) | copy-start | bytes 2359300
  7.2 40.7 %copy-start.3 = (f32[3,128,128]{2,1,0:T(8,128)S(1)}, f32[3,128,128]{2,1,0:T(8,128)}, u32[]{:S(2)}) copy-start(f32[3,128,128]{2,1,0:T(8,128)} %param.9) | copy-start | bytes 589828
  7.2 90.8 %all-gather.2.cloned.1.call-start = ((), (), s32[]{:S(2)}) async-start(), calls=%async_computation | async-start | bytes 5308416 | tf_op jit(solution)/shard_map/all_gather | solution.py:30
  13.6 123.3 %all-reduce.2.cloned.1.call-start = ((), (), s32[]{:S(2)}) async-start(), calls=%async_computation.1 | async-start | bytes 1179648 | tf_op jit(solution)/shard_map/psum | solution.py:34
  208.4 1.0 copy-start.2
  209.5 0.9 copy-start.1
Sparse Core Ops, SparseCore 0:
  13.8 84.1 all-gather.1
  105.3 31.5 all-reduce.1
where the time goes:
time: 217 us
  blocking collectives  95 us (44%)
  waiting for transfers between devices  80.5 us (37%)
  between operations  14.3 us (7%)
  matrix products  10.9 us (5%)
  other arithmetic  9.12 us (4%)
  local copies, waits for them, and re-layouts  7.23 us (3%)
    all_gather x3, blocking collectives, local(): block_resid = lax.all_gather(own_resid, 'rows', axis=0, tiled=True)  95 us
    all_gather x1, waiting for transfers between devices, local(): lax.all_gather(every_picked, 'rows', axis=0, tiled=True)  49.7 us
    psum x1, waiting for transfers between devices, local(): every_gram = lax.psum(every_part, 'feat')  30.8 us
    dot_general x1, matrix products, local(): lax.dot_general(features, lax.all_gather(every_picked, 'rows', axis=0, ti...  7.2 us
    gather x1, local copies, waits for them, and re-layouts, local(): every_picked = jnp.take(features, own_picks.reshape(-1), axis=0)  4.41 us
  transfers between devices with their start and end apart: 2, of which 2 were waited for; matrix products, arithmetic and copies ran while one was open for 1% of the time, Pallas kernels for 0%

commit v1 on v0

v1 whole, which is shorter than its diff:
```python
import functools

import jax
import jax.numpy as jnp
from jax import lax
from jax.experimental import pallas as pl
from jax.experimental.pallas import tpu as pltpu
from jax.sharding import PartitionSpec as P

F = 24576
EXACT = lax.Precision.HIGHEST


def quadratic(gram):
    scaled = gram * (1.0 / F)
    return scaled + scaled * scaled


def dot_rows(left, right):
    return lax.dot_general(
        left, right, (((1,), (1,)), ((), ())), preferred_element_type=jnp.float32
    )


def exact_dot(left, right, contract=1):
    return lax.dot_general(
        left,
        right,
        (((contract,), (0,)), ((), ())),
        precision=EXACT,
        preferred_element_type=jnp.float32,
    )


def finish_kernel(steps, per, early_slots, *refs):
    if early_slots:
        early_ref, *refs = refs
    late_ref, cross_ref, same_ref, first_ref, inverse_ref, own_ref, targets_ref, resid_ref, coeff_ref = refs
    block = first_ref.shape[1]
    rows = targets_ref.shape[0]
    deltas = []
    for step in range(steps):
        delta = first_ref[step]
        if step:
            base = step * (step - 1) // 2 * block
            change = jnp.zeros_like(delta)
            for before in range(step):
                at = slice(base + before * block, base + (before + 1) * block)
                change += exact_dot(quadratic(cross_ref[:, at]) + same_ref[:, at], deltas[before])
            delta = delta - exact_dot(inverse_ref[step], change)
        deltas.append(delta)
    spread = (own_ref[...] == lax.broadcasted_iota(jnp.int32, (steps * per, rows), 1)).astype(jnp.float32)
    own = jnp.concatenate([delta[:per] for delta in deltas], axis=0)
    coeffs = exact_dot(spread, own, 0)
    coeff_ref[...] = coeffs
    resid = targets_ref[...] - coeffs
    late = quadratic(late_ref[...]).reshape(-1, steps, per, rows)
    if early_slots:
        late = jnp.concatenate(
            [quadratic(early_ref[...]).reshape(-1, steps, per, rows), late], axis=0
        )
    for step in range(steps):
        resid = resid - exact_dot(late[:, step].reshape(block, rows), deltas[step], 0)
    resid_ref[...] = resid


def by_step(array, steps, per):
    parts = array.reshape(-1, steps, per, array.shape[-1])
    return jnp.swapaxes(parts, 0, 1).reshape(steps, -1, array.shape[-1])


class Lines:
    def __init__(self):
        self.beside = [(r, r ^ 1) for r in range(8)]
        self.pair = [(r, r ^ 2) for r in range(8)]
        self.across = [(r, r ^ 4) for r in range(8)]
        self.inner = [(r, r ^ 6) for r in range(2, 6)]
        self.outer = [(2, 0), (3, 1), (4, 6), (5, 7)]
        rank = lax.axis_index("rows")
        self.feat = lax.axis_index("feat")
        z, y = rank // 2, rank % 2
        self.is_inner = (z == 1) | (z == 2)
        low = z < 2
        line = jnp.stack([z, z ^ 1, jnp.where(low, 2, 1), jnp.where(low, 3, 0)])
        self.order = (line[:, None] * 2 + jnp.stack([y, 1 - y])[None, :]).reshape(-1)

    def rows(self, array, pairs):
        return lax.ppermute(array, "rows", pairs)

    def blocks(self, own):
        near = self.rows(own, self.pair)
        mid = self.rows(own, self.inner)
        own_b = self.rows(own, self.beside)
        near, mid, own_b = lax.optimization_barrier((near, mid, own_b))
        far = self.rows(near, self.inner)
        mid_end = self.rows(mid, self.outer)
        near_b = self.rows(near, self.beside)
        far, mid_end, near_b = lax.optimization_barrier((far, mid_end, near_b))
        far_end = self.rows(far, self.outer)
        mid = jnp.where(self.is_inner, mid, mid_end)
        mid_b = self.rows(mid, self.beside)
        far_end, mid_b = lax.optimization_barrier((far_end, mid_b))
        far = jnp.where(self.is_inner, far, far_end)
        far_b = self.rows(far, self.beside)
        return [own, own_b, near, near_b, mid, mid_b], [far, far_b]

    def residuals(self, own):
        both = jnp.concatenate([own, self.rows(own, self.beside)], axis=0)
        both = jnp.concatenate([both, self.rows(both, self.pair)], axis=0)
        other = self.rows(both, self.across)
        half = other.shape[0] // 2
        other = jnp.where(self.is_inner, jnp.concatenate([other[half:], other[:half]], axis=0), other)
        both = jnp.concatenate([both, other], axis=0)
        for bit in (1, 2):
            other = lax.ppermute(both, "feat", [(f, f ^ bit) for f in range(4)])
            first = (self.feat & bit) == 0
            both = jnp.where(
                first,
                jnp.concatenate([both, other], axis=1),
                jnp.concatenate([other, both], axis=1),
            )
        return both

    def total(self, array):
        for bit in (1, 2):
            array = array + lax.ppermute(array, "feat", [(f, f ^ bit) for f in range(4)])
        return array


class Gathers:
    def __init__(self):
        size = lax.axis_size("rows")
        self.order = (lax.axis_index("rows") + jnp.arange(size)) % size

    def turn(self, own):
        every = lax.all_gather(own, "rows", axis=0, tiled=True)
        start = lax.axis_index("rows") * own.shape[0]
        return lax.dynamic_slice_in_dim(
            jnp.concatenate([every, every], axis=0), start, every.shape[0], 0
        )

    def blocks(self, own):
        return [], [self.turn(own)]

    def residuals(self, own):
        return lax.all_gather(self.turn(own), "feat", axis=1, tiled=True)

    def total(self, array):
        return lax.psum(array, "feat")


def local(features, targets, block_index, inverse):
    rank = lax.axis_index("rows")
    row_count = lax.axis_size("rows")
    feat_count = lax.axis_size("feat")
    rows_here, columns = targets.shape
    steps, block = block_index.shape
    per = block // row_count
    lined = row_count == 8 and feat_count == 4
    mover = Lines() if lined else Gathers()
    order = mover.order

    own_picks = lax.dynamic_slice_in_dim(block_index, rank * per, per, 1) - rank * rows_here
    own_picks = own_picks.reshape(-1)
    onehot = (own_picks[:, None] == jnp.arange(rows_here)[None, :]).astype(features.dtype)
    own = lax.dot_general(
        onehot, features, (((1,), (0,)), ((), ())), preferred_element_type=features.dtype
    )
    share = columns // feat_count
    own_share = jnp.take(
        lax.dynamic_slice_in_dim(targets, lax.axis_index("feat") * share, share, 1), own_picks, axis=0
    )
    first = by_step(mover.residuals(own_share), steps, per)

    place = jnp.arange(block)
    moved = jnp.repeat(order, per) * per + place % per
    swap = moved[:, None] == place[None, :]
    picks = jnp.sum(jnp.where(swap[None], block_index[:, None, :], 0), axis=2)
    swap = swap.astype(jnp.float32)
    turned = jnp.stack(
        [exact_dot(exact_dot(swap, inverse[step]), swap.T) for step in range(steps)]
    )
    first = lax.dot_general(
        turned, first, (((2,), (1,)), ((0,), (0,))), precision=EXACT, preferred_element_type=jnp.float32
    )
    same = jnp.concatenate(
        [
            (picks[step][:, None] == picks[before][None, :]).astype(jnp.float32)
            for step in range(steps)
            for before in range(step)
        ],
        axis=1,
    )

    early, late = mover.blocks(own)
    operands = []
    if early:
        operands.append(mover.total(dot_rows(jnp.concatenate(early, axis=0), features)))
    blocks = by_step(jnp.concatenate(early + late, axis=0), steps, per)
    cross = [
        dot_rows(blocks[step], blocks[:step].reshape(step * block, -1)) for step in range(1, steps)
    ]
    late = dot_rows(jnp.concatenate(late, axis=0), features)
    flat = jnp.concatenate([late.reshape(-1)] + [part.reshape(-1) for part in cross]).reshape(-1, 128)
    flat = mover.total(flat)
    late_total = flat[: late.size // 128].reshape(late.shape)
    at = late.size // 128
    cross_total = []
    for part in cross:
        cross_total.append(flat[at : at + part.size // 128].reshape(part.shape))
        at += part.size // 128
    operands += [
        late_total,
        jnp.concatenate(cross_total, axis=1),
        same,
        first,
        turned,
        own_picks[:, None],
        targets,
    ]
    out = jax.ShapeDtypeStruct(targets.shape, jnp.float32)
    vmem = pl.BlockSpec(memory_space=pltpu.VMEM)
    return pl.pallas_call(
        functools.partial(finish_kernel, steps, per, len(early)),
        out_shape=(out, out),
        in_specs=[vmem] * len(operands),
        out_specs=(vmem, vmem),
        compiler_params=pltpu.CompilerParams(vmem_limit_bytes=48 * 1024 * 1024),
    )(*operands)


def solution(mesh):
    return jax.shard_map(
        local,
        mesh=mesh,
        in_specs=(P("rows", "feat"), P("rows", None), P(), P()),
        out_specs=(P("rows", None), P("rows", None)),
        check_vma=False,
    )
```

time: 217 us -> 121 us (0.56)
  blocking collectives: 95 us -> 0 us
  starting transfers between devices: 0.08 us -> 21.8 us
  waiting for transfers between devices: 80.5 us -> 62.1 us
  between operations: 14.3 us -> 1.08 us
  Pallas kernels: 0 us -> 5.11 us
  matrix products: 10.9 us -> 14.9 us
  other arithmetic: 9.12 us -> 6.52 us
    all_gather x3 -> x0, blocking collectives: 95 us -> none  [local(): block_resid = lax.all_gather(own_resid, 'rows', axis=0, tiled=True)]
    ppermute x0 -> x18, waiting for transfers between devices: none -> 62.1 us  [the longest x12 39.5 us: rows(): return lax.ppermute(array, 'rows', pairs)]
    all_gather x1 -> x0, waiting for transfers between devices: 49.7 us -> none  [local(): lax.all_gather(every_picked, 'rows', axis=0, tiled=True)]
    psum x1 -> x0, waiting for transfers between devices: 30.8 us -> none  [local(): every_gram = lax.psum(every_part, 'feat')]
    ppermute x0 -> x18, starting transfers between devices: none -> 21.8 us  [the longest x12 17.7 us: rows(): return lax.ppermute(array, 'rows', pairs)]
    scatter-add x6 -> x0, other arithmetic: 5.96 us -> none  [the longest x3 3.05 us: local(): residual = residual.at[picks].add(-1.0 * own_delta)]
    unnamed x8 -> x20, local copies, waits for them, and re-layouts: 0.89 us -> 6.55 us
    gather x4 -> x1, local copies, waits for them, and re-layouts: 6.14 us -> 0.59 us  [local(): jnp.take(lax.dynamic_slice_in_dim(targets, lax.axis_index('feat') * share...]
  transfers between devices with their start and end apart: 2 -> 18, of which waited for: 2 -> 10; matrix products, arithmetic and copies ran while one was open for 1% -> 19% of each run, Pallas kernels for 0% -> 0%
where the time goes in v1:
time: 121 us; the launch traced here: 120 us
  waiting for transfers between devices  62.1 us (51%)
  starting transfers between devices  21.8 us (18%)
  matrix products  14.9 us (12%)
  local copies, waits for them, and re-layouts  8.94 us (7%)
  other arithmetic  6.52 us (5%)
  Pallas kernels  5.11 us (4%)
    ppermute x12, waiting for transfers between devices, rows(): return lax.ppermute(array, 'rows', pairs)  39.5 us
    ppermute x12, starting transfers between devices, rows(): return lax.ppermute(array, 'rows', pairs)  17.7 us
    ppermute x4, waiting for transfers between devices, total(): lax.ppermute(array, 'feat', [(f, f ^ bit) for f in range(4)])  15.5 us
    dot_general x4, matrix products, dot_rows(): lax.dot_general(left, right, (((1,), (1,)), ((), ())), preferred_element_...  8.21 us
    ppermute x2, waiting for transfers between devices, residuals(): other = lax.ppermute(both, 'feat', [(f, f ^ bit) for f in range(4)])  7.08 us
    unnamed x20, local copies, waits for them, and re-layouts  6.55 us
    pallas_call x1, Pallas kernels, local(): pl.pallas_call(functools.partial(finish_kernel, steps, per, len(early)),...  5.11 us
    dot_general x1, matrix products, local(): lax.dot_general(onehot, features, (((1,), (0,)), ((), ())), preferred_ele...  4.4 us
  transfers between devices with their start and end apart: 18, of which 10 were waited for; matrix products, arithmetic and copies ran while one was open for 19% of the time, Pallas kernels for 0%

profile of v1, /device:TPU:0, one launch (start us, length us, event | category | flops | bytes accessed | tf_op | source)
XLA Modules:
  0.0 120.5 jit_solution(15485431854948767726)
XLA Ops:
  0.6 0.8 dynamic-slice_subtract_fusion
  1.6 4.4 %constant_dynamic-update-slice_fusion.13 = (bf16[384,6144]{1,0:T(8,128)(2,1)}, bf16[288,6144]{1,0:T(8,128)(2,1)}, bf16[48,6144]{1,0:T(8,128)(2,1)S(1)}) fusion(bf16[384,6144]{1,0:T(8,128)(2,1)} %param.4, s32[48]{0:T(128)S(1)} %eq.89), kind=kOutput, calls=%fused_computation.61 | convolution fusion | flops 226510848 | bytes 6488256 | tf_op jit(solution)/shard_map/dot_general | solution.py:166
  6.0 3.0 %collective-permute-start = (bf16[48,6144]{1,0:T(8,128)(2,1)S(1)}, bf16[48,6144]{1,0:T(8,128)(2,1)S(1)}, u32[]{:S(2)}, u32[]{:S(2)}) collective-permute-start(bf16[48,6144]{1,0:T(8,128)(2,1)S(1)} %get-tuple-element.43), channel_id=1, source_target_pairs={{0,8},{4,12},{8,0},{12,4},{16,24},{20,28},{24,16},{28,20},{1,9},{5... | collective-permute-start | bytes 1769480 | tf_op jit(solution)/shard_map/ppermute | solution.py:88
  9.0 0.7 collective-permute-start.1
  9.7 1.6 %collective-permute-start.2 = (bf16[48,6144]{1,0:T(8,128)(2,1)S(1)}, bf16[48,6144]{1,0:T(8,128)(2,1)}, u32[]{:S(2)}, u32[]{:S(2)}) collective-permute-start(bf16[48,6144]{1,0:T(8,128)(2,1)S(1)} %get-tuple-element.43), channel_id=1, source_target_pairs={{0,4},{4,0},{8,12},{12,8},{16,20},{20,16},{24,28},{28,24},{1,5},{5... | collective-permute-start | bytes 1769480 | tf_op jit(solution)/shard_map/ppermute | solution.py:88
  11.4 0.6 gather_fusion
  12.1 0.5 collective-permute-start.13
  14.2 0.3 convolution_bitcast_fusion.2
  14.5 10.6 %collective-permute-done.13 = f32[48,128]{1,0:T(8,128)S(1)} collective-permute-done((f32[48,128]{1,0:T(8,128)S(1)}, f32[48,128]{1,0:T(8,128)S(1)}, u32[]{:S(2)}, u32[]{:S(2)}) %collective-permute-start.13) | collective-permute-done | bytes 24608 | tf_op jit(solution)/shard_map/ppermute | solution.py:88
  25.1 4.1 %collective-permute-start.14 = (f32[96,128]{1,0:T(8,128)S(1)}, f32[96,128]{1,0:T(8,128)S(1)}, u32[]{:S(2)}, u32[]{:S(2)}) collective-permute-start(f32[96,128]{1,0:T(8,128)S(1)} %pad_maximum_fusion.4), channel_id=1, source_target_pairs={{0,8},{4,12},{8,0},{12,4},{16,24},{20,28},{24,16},{28,20},{1,9},{5... | collective-permute-start | bytes 147464 | tf_op jit(solution)/shard_map/ppermute | solution.py:88
  29.4 1.8 %collective-permute-done.14 = f32[96,128]{1,0:T(8,128)S(1)} collective-permute-done((f32[96,128]{1,0:T(8,128)S(1)}, f32[96,128]{1,0:T(8,128)S(1)}, u32[]{:S(2)}, u32[]{:S(2)}) %collective-permute-start.14) | collective-permute-done | bytes 49184 | tf_op jit(solution)/shard_map/ppermute | solution.py:88
  31.2 1.8 %collective-permute-start.15 = (f32[192,128]{1,0:T(8,128)S(1)}, f32[192,128]{1,0:T(8,128)S(1)}, u32[]{:S(2)}, u32[]{:S(2)}) collective-permute-start(f32[192,128]{1,0:T(8,128)S(1)} %pad_maximum_fusion.3), channel_id=1, source_target_pairs={{0,16},{4,20},{8,24},{12,28},{16,0},{20,4},{24,8},{28,12},{1,17},{... | collective-permute-start | bytes 294920 | tf_op jit(solution)/shard_map/ppermute | solution.py:88
  33.3 3.5 %collective-permute-done.15 = f32[192,128]{1,0:T(8,128)S(1)} collective-permute-done((f32[192,128]{1,0:T(8,128)S(1)}, f32[192,128]{1,0:T(8,128)S(1)}, u32[]{:S(2)}, u32[]{:S(2)}) %collective-permute-start.15) | collective-permute-done | bytes 98336 | tf_op jit(solution)/shard_map/ppermute | solution.py:88
  36.9 0.7 collective-permute-start.3
  37.6 1.6 %collective-permute-start.5 = (bf16[48,6144]{1,0:T(8,128)(2,1)S(1)}, bf16[48,6144]{1,0:T(8,128)(2,1)S(1)}, u32[]{:S(2)}, u32[]{:S(2)}) collective-permute-start(bf16[48,6144]{1,0:T(8,128)(2,1)S(1)} %collective-permute-done), channel_id=1, source_target_pairs={{0,4},{4,0},{8,12},{12,8},{16,20},{20,16},{24,28},{28,24},{1,5},{5... | collective-permute-start | bytes 1769480 | tf_op jit(solution)/shard_map/ppermute | solution.py:88
  39.2 1.3 %collective-permute-start.4 = (bf16[48,6144]{1,0:T(8,128)(2,1)S(1)}, bf16[48,6144]{1,0:T(8,128)(2,1)S(1)}, u32[]{:S(2)}, u32[]{:S(2)}) collective-permute-start(bf16[48,6144]{1,0:T(8,128)(2,1)S(1)} %collective-permute-done.1), channel_id=1, source_target_pairs={{8,0},{12,4},{16,24},{20,28},{9,1},{13,5},{17,25},{21,29},{10,2},{... | collective-permute-start | bytes 1769480 | tf_op jit(solution)/shard_map/ppermute | solution.py:88
  40.5 2.2 %constant_dynamic-update-slice_fusion.12 = (bf16[384,6144]{1,0:T(8,128)(2,1)}, bf16[288,6144]{1,0:T(8,128)(2,1)}) fusion(bf16[384,6144]{1,0:T(8,128)(2,1)} %get-tuple-element.33, bf16[48,6144]{1,0:T(8,128)(2,1)} %collective-permute-done.2, bf16[288,6144]{1,0:T(8,128)(2,1)} %get-tuple-element.34), kind=kLoop, calls=%fused_computation.60 | loop fusion | bytes 1769472
  42.6 1.1 constant_dynamic-update-slice_fusion.11
  43.8 9.8 %collective-permute-done.4 = bf16[48,6144]{1,0:T(8,128)(2,1)S(1)} collective-permute-done((bf16[48,6144]{1,0:T(8,128)(2,1)S(1)}, bf16[48,6144]{1,0:T(8,128)(2,1)S(1)}, u32[]{:S(2)}, u32[]{:S(2)}) %collective-permute-start.4) | collective-permute-done | bytes 589856 | tf_op jit(solution)/shard_map/ppermute | solution.py:88
  53.5 1.5 %collective-permute-start.6 = (bf16[48,6144]{1,0:T(8,128)(2,1)S(1)}, bf16[48,6144]{1,0:T(8,128)(2,1)S(1)}, u32[]{:S(2)}, u32[]{:S(2)}) collective-permute-start(bf16[48,6144]{1,0:T(8,128)(2,1)S(1)} %collective-permute-done.3), channel_id=1, source_target_pairs={{8,0},{12,4},{16,24},{20,28},{9,1},{13,5},{17,25},{21,29},{10,2},{... | collective-permute-start | bytes 1769480 | tf_op jit(solution)/shard_map/ppermute | solution.py:88
  55.0 1.1 constant_dynamic-update-slice_fusion.10
  56.1 1.0 constant_dynamic-update-slice_fusion.9
  57.1 0.5 collective-permute-start.7
  57.6 0.9 constant_dynamic-update-slice_fusion.1
  58.5 7.5 %collective-permute-done.6 = bf16[48,6144]{1,0:T(8,128)(2,1)S(1)} collective-permute-done((bf16[48,6144]{1,0:T(8,128)(2,1)S(1)}, bf16[48,6144]{1,0:T(8,128)(2,1)S(1)}, u32[]{:S(2)}, u32[]{:S(2)}) %collective-permute-start.6) | collective-permute-done | bytes 589856 | tf_op jit(solution)/shard_map/ppermute | solution.py:88
  66.0 2.5 %collective-permute-done.7 = bf16[48,6144]{1,0:T(8,128)(2,1)S(1)} collective-permute-done((bf16[48,6144]{1,0:T(8,128)(2,1)S(1)}, bf16[48,6144]{1,0:T(8,128)(2,1)S(1)}, u32[]{:S(2)}, u32[]{:S(2)}) %collective-permute-start.7) | collective-permute-done | bytes 589856 | tf_op jit(solution)/shard_map/ppermute | solution.py:88
  68.5 1.2 constant_dynamic-update-slice_fusion.8
  69.7 1.0 constant_dynamic-update-slice_fusion.7
  70.6 0.5 collective-permute-start.10
  71.3 4.9 %fusion.29 = f32[288,384]{1,0:T(8,128)} fusion(bf16[288,6144]{1,0:T(8,128)(2,1)} %get-tuple-element.26, bf16[384,6144]{1,0:T(8,128)(2,1)S(1)} %bitcast.69), kind=kOutput, calls=%fused_computation.83 | convolution fusion | flops 1358954496 | bytes 8699904 | tf_op jit(solution)/shard_map/dot_general | solution.py:20
  76.2 0.4 collective-permute-start.8
  76.6 3.9 %collective-permute-done.10 = bf16[48,6144]{1,0:T(8,128)(2,1)S(1)} collective-permute-done((bf16[48,6144]{1,0:T(8,128)(2,1)S(1)}, bf16[48,6144]{1,0:T(8,128)(2,1)S(1)}, u32[]{:S(2)}, u32[]{:S(2)}) %collective-permute-start.10) | collective-permute-done | bytes 589856 | tf_op jit(solution)/shard_map/ppermute | solution.py:88
  80.6 0.5 copy.16
  81.1 0.3 fusion.27
  81.6 1.2 convolution_bitcast_fusion.1
  82.8 1.5 %fusion = f32[96,384]{1,0:T(8,128)S(1)} fusion(bf16[384,6144]{1,0:T(8,128)(2,1)S(1)} %bitcast.69, bf16[48,6144]{1,0:T(8,128)(2,1)S(1)} %collective-permute-done.10, bf16[48,6144]{1,0:T(8,128)(2,1)S(1)} %get-tuple-element.19), kind=kOutput, calls=%fused_computation.3 | convolution fusion | flops 455344128 | bytes 6045696 | tf_op jit(solution)/shard_map/dot_general | solution.py:20
  84.4 0.6 convolution_bitcast_fusion
  85.0 0.7 maximum_bitcast_fusion
  85.8 0.8 maximum_select_fusion.2
  86.6 1.5 %collective-permute-start.17 = (f32[384,256]{1,0:T(8,128)}, f32[384,256]{1,0:T(8,128)S(1)}, u32[]{:S(2)}, u32[]{:S(2)}) collective-permute-start(f32[384,256]{1,0:T(8,128)} %maximum_select_fusion.2), channel_id=1, source_target_pairs={{0,2},{1,3},{2,0},{3,1},{4,6},{5,7},{6,4},{7,5},{8,10},{9,11},{10,... | collective-permute-start | bytes 1179656 | tf_op jit(solution)/shard_map/ppermute | solution.py:115
  88.2 1.2 add.77
  89.4 0.6 collective-permute-start.9
  90.0 1.6 %collective-permute-start.12 = (f32[672,128]{1,0:T(8,128)S(1)}, f32[672,128]{1,0:T(8,128)S(1)}, u32[]{:S(2)}, u32[]{:S(2)}) collective-permute-start(f32[672,128]{1,0:T(8,128)S(1)} %fusion.26), channel_id=1, source_target_pairs={{0,2},{1,3},{2,0},{3,1},{4,6},{5,7},{6,4},{7,5},{8,10},{9,11},{10,... | collective-permute-start | bytes 1032200 | tf_op jit(solution)/shard_map/ppermute | solution.py:126
  91.6 7.1 %collective-permute-done.17 = f32[384,256]{1,0:T(8,128)S(1)} collective-permute-done((f32[384,256]{1,0:T(8,128)}, f32[384,256]{1,0:T(8,128)S(1)}, u32[]{:S(2)}, u32[]{:S(2)}) %collective-permute-start.17) | collective-permute-done | bytes 393248 | tf_op jit(solution)/shard_map/ppermute | solution.py:115
  98.8 0.8 fusion.25.refs_4_
  99.6 8.5 %collective-permute-done.9 = f32[288,384]{1,0:T(8,128)S(1)} collective-permute-done((f32[288,384]{1,0:T(8,128)S(1)}, f32[288,384]{1,0:T(8,128)S(1)}, u32[]{:S(2)}, u32[]{:S(2)}) %collective-permute-start.9) | collective-permute-done | bytes 442400 | tf_op jit(solution)/shard_map/ppermute | solution.py:126
  108.2 6.9 %collective-permute-done.12 = f32[672,128]{1,0:T(8,128)S(1)} collective-permute-done((f32[672,128]{1,0:T(8,128)S(1)}, f32[672,128]{1,0:T(8,128)S(1)}, u32[]{:S(2)}, u32[]{:S(2)}) %collective-permute-start.12) | collective-permute-done | bytes 344096 | tf_op jit(solution)/shard_map/ppermute | solution.py:126
  115.4 5.1 %shard_map.59 = (f32[384,512]{1,0:T(8,128)}, f32[384,512]{1,0:T(8,128)}) custom-call(f32[288,384]{1,0:T(8,128)S(1)} %add.78.refs_0_, f32[96,384]{1,0:T(8,128)S(1)} %reshape.178.refs_1_, f32[128,384]{1,0:T(8,128)S(1)} %pad_maximum_fusion.refs_2_, f32[128,384]{1,0:T(8,128)S(1)} %add_convert_fusion.refs_3_, f32[3,128,512]{2,1,0:T(8,128)S(1)} %fusion.25.refs_4_, ...), custom_call_target="tpu_custom_call" | custom-call | tf_op jit(solution)/shard_map/pallas_call | solution.py:223
  (73 shorter events, 3.4 us)
Async XLA Ops:
  0.6 10.7 %copy-start = (f32[384,512]{1,0:T(8,128)S(1)}, f32[384,512]{1,0:T(8,128)}, u32[]{:S(2)}) copy-start(f32[384,512]{1,0:T(8,128)} %refs_7_.1) | copy-start | bytes 2359300
  1.6 11.6 %copy-start.1 = (f32[3,128,128]{2,1,0:T(8,128)S(1)}, f32[3,128,128]{2,1,0:T(8,128)}, u32[]{:S(2)}) copy-start(f32[3,128,128]{2,1,0:T(8,128)} %param.7) | copy-start | bytes 589828
  1.6 12.3 %copy-start.2 = (s32[3,128]{1,0:T(4,128)S(1)}, s32[3,128]{1,0:T(4,128)}, u32[]{:S(2)}) copy-start(s32[3,128]{1,0:T(4,128)} %param.6) | copy-start | bytes 4612
  6.0 30.9 %collective-permute-start = (bf16[48,6144]{1,0:T(8,128)(2,1)S(1)}, bf16[48,6144]{1,0:T(8,128)(2,1)S(1)}, u32[]{:S(2)}, u32[]{:S(2)}) collective-permute-start(bf16[48,6144]{1,0:T(8,128)(2,1)S(1)} %get-tuple-element.43), channel_id=1, source_target_pairs={{0,8},{4,12},{8,0},{12,4},{16,24},{20,28},{24,16},{28,20},{1,9},{5... | collective-permute-start | bytes 1769480 | tf_op jit(solution)/shard_map/ppermute | solution.py:88
  9.0 27.9 %collective-permute-start.1 = (bf16[48,6144]{1,0:T(8,128)(2,1)S(1)}, bf16[48,6144]{1,0:T(8,128)(2,1)S(1)}, u32[]{:S(2)}, u32[]{:S(2)}) collective-permute-start(bf16[48,6144]{1,0:T(8,128)(2,1)S(1)} %get-tuple-element.43), channel_id=1, source_target_pairs={{8,16},{12,20},{16,8},{20,12},{9,17},{13,21},{17,9},{21,13},{10,18... | collective-permute-start | bytes 1769480 | tf_op jit(solution)/shard_map/ppermute | solution.py:88
  9.7 27.2 %collective-permute-start.2 = (bf16[48,6144]{1,0:T(8,128)(2,1)S(1)}, bf16[48,6144]{1,0:T(8,128)(2,1)}, u32[]{:S(2)}, u32[]{:S(2)}) collective-permute-start(bf16[48,6144]{1,0:T(8,128)(2,1)S(1)} %get-tuple-element.43), channel_id=1, source_target_pairs={{0,4},{4,0},{8,12},{12,8},{16,20},{20,16},{24,28},{28,24},{1,5},{5... | collective-permute-start | bytes 1769480 | tf_op jit(solution)/shard_map/ppermute | solution.py:88
  12.1 13.0 %collective-permute-start.13 = (f32[48,128]{1,0:T(8,128)S(1)}, f32[48,128]{1,0:T(8,128)S(1)}, u32[]{:S(2)}, u32[]{:S(2)}) collective-permute-start(f32[48,128]{1,0:T(8,128)S(1)} %broadcast_select_fusion.2), channel_id=1, source_target_pairs={{0,4},{4,0},{8,12},{12,8},{16,20},{20,16},{24,28},{28,24},{1,5},{5... | collective-permute-start | bytes 73736 | tf_op jit(solution)/shard_map/ppermute | solution.py:88
  25.1 6.1 %collective-permute-start.14 = (f32[96,128]{1,0:T(8,128)S(1)}, f32[96,128]{1,0:T(8,128)S(1)}, u32[]{:S(2)}, u32[]{:S(2)}) collective-permute-start(f32[96,128]{1,0:T(8,128)S(1)} %pad_maximum_fusion.4), channel_id=1, source_target_pairs={{0,8},{4,12},{8,0},{12,4},{16,24},{20,28},{24,16},{28,20},{1,9},{5... | collective-permute-start | bytes 147464 | tf_op jit(solution)/shard_map/ppermute | solution.py:88
  31.2 5.6 %collective-permute-start.15 = (f32[192,128]{1,0:T(8,128)S(1)}, f32[192,128]{1,0:T(8,128)S(1)}, u32[]{:S(2)}, u32[]{:S(2)}) collective-permute-start(f32[192,128]{1,0:T(8,128)S(1)} %pad_maximum_fusion.3), channel_id=1, source_target_pairs={{0,16},{4,20},{8,24},{12,28},{16,0},{20,4},{24,8},{28,12},{1,17},{... | collective-permute-start | bytes 294920 | tf_op jit(solution)/shard_map/ppermute | solution.py:88
  36.9 6.9 %collective-permute-start.3 = (bf16[48,6144]{1,0:T(8,128)(2,1)S(1)}, bf16[48,6144]{1,0:T(8,128)(2,1)S(1)}, u32[]{:S(2)}, u32[]{:S(2)}) collective-permute-start(bf16[48,6144]{1,0:T(8,128)(2,1)S(1)} %collective-permute-done), channel_id=1, source_target_pairs={{8,16},{12,20},{16,8},{20,12},{9,17},{13,21},{17,9},{21,13},{10,18... | collective-permute-start | bytes 1769480 | tf_op jit(solution)/shard_map/ppermute | solution.py:88
  37.6 16.0 %collective-permute-start.5 = (bf16[48,6144]{1,0:T(8,128)(2,1)S(1)}, bf16[48,6144]{1,0:T(8,128)(2,1)S(1)}, u32[]{:S(2)}, u32[]{:S(2)}) collective-permute-start(bf16[48,6144]{1,0:T(8,128)(2,1)S(1)} %collective-permute-done), channel_id=1, source_target_pairs={{0,4},{4,0},{8,12},{12,8},{16,20},{20,16},{24,28},{28,24},{1,5},{5... | collective-permute-start | bytes 1769480 | tf_op jit(solution)/shard_map/ppermute | solution.py:88
  39.2 14.4 %collective-permute-start.4 = (bf16[48,6144]{1,0:T(8,128)(2,1)S(1)}, bf16[48,6144]{1,0:T(8,128)(2,1)S(1)}, u32[]{:S(2)}, u32[]{:S(2)}) collective-permute-start(bf16[48,6144]{1,0:T(8,128)(2,1)S(1)} %collective-permute-done.1), channel_id=1, source_target_pairs={{8,0},{12,4},{16,24},{20,28},{9,1},{13,5},{17,25},{21,29},{10,2},{... | collective-permute-start | bytes 1769480 | tf_op jit(solution)/shard_map/ppermute | solution.py:88
  42.6 28.6 %slice-start = ((s8[4718592]{0:T(1024)(128)(4,1)}), s8[4194304]{0:T(1024)(128)(4,1)S(1)}, s32[]{:S(2)}) async-start(s8[4718592]{0:T(1024)(128)(4,1)} %bitcast.68), calls=%async_computation | async-start | bytes 8388608
  53.5 12.4 %collective-permute-start.6 = (bf16[48,6144]{1,0:T(8,128)(2,1)S(1)}, bf16[48,6144]{1,0:T(8,128)(2,1)S(1)}, u32[]{:S(2)}, u32[]{:S(2)}) collective-permute-start(bf16[48,6144]{1,0:T(8,128)(2,1)S(1)} %collective-permute-done.3), channel_id=1, source_target_pairs={{8,0},{12,4},{16,24},{20,28},{9,1},{13,5},{17,25},{21,29},{10,2},{... | collective-permute-start | bytes 1769480 | tf_op jit(solution)/shard_map/ppermute | solution.py:88
  56.1 15.1 %slice-start.1 = ((s8[4718592]{0:T(1024)(128)(4,1)}), s8[524288]{0:T(1024)(128)(4,1)S(1)}, s32[]{:S(2)}) async-start(s8[4718592]{0:T(1024)(128)(4,1)} %bitcast.68), calls=%async_computation.1 | async-start | bytes 1048576
  57.1 11.3 %collective-permute-start.7 = (bf16[48,6144]{1,0:T(8,128)(2,1)S(1)}, bf16[48,6144]{1,0:T(8,128)(2,1)S(1)}, u32[]{:S(2)}, u32[]{:S(2)}) collective-permute-start(bf16[48,6144]{1,0:T(8,128)(2,1)S(1)} %get-tuple-element.21), channel_id=1, source_target_pairs={{0,4},{4,0},{8,12},{12,8},{16,20},{20,16},{24,28},{28,24},{1,5},{5... | collective-permute-start | bytes 1769480 | tf_op jit(solution)/shard_map/ppermute | solution.py:88
  70.6 9.9 %collective-permute-start.10 = (bf16[48,6144]{1,0:T(8,128)(2,1)S(1)}, bf16[48,6144]{1,0:T(8,128)(2,1)S(1)}, u32[]{:S(2)}, u32[]{:S(2)}) collective-permute-start(bf16[48,6144]{1,0:T(8,128)(2,1)S(1)} %get-tuple-element.19), channel_id=1, source_target_pairs={{0,4},{4,0},{8,12},{12,8},{16,20},{20,16},{24,28},{28,24},{1,5},{5... | collective-permute-start | bytes 1769480 | tf_op jit(solution)/shard_map/ppermute | solution.py:88
  71.1 9.4 %slice-start.2 = ((s8[4718592]{0:T(1024)(128)(4,1)}), s8[4194304]{0:T(1024)(128)(4,1)S(1)}, s32[]{:S(2)}) async-start(s8[4718592]{0:T(1024)(128)(4,1)} %bitcast.74), calls=%async_computation.2 | async-start | bytes 8388608
  71.2 14.6 %collective-permute-start.16 = (f32[384,128]{1,0:T(8,128)S(1)}, f32[384,128]{1,0:T(8,128)S(1)}, u32[]{:S(2)}, u32[]{:S(2)}) collective-permute-start(f32[384,128]{1,0:T(8,128)S(1)} %pad_maximum_fusion.2), channel_id=1, source_target_pairs={{0,1},{1,0},{2,3},{3,2},{4,5},{5,4},{6,7},{7,6},{8,9},{9,8},{10,11... | collective-permute-start | bytes 589832 | tf_op jit(solution)/shard_map/ppermute | solution.py:115
  71.3 9.3 %slice-start.3 = ((s8[4718592]{0:T(1024)(128)(4,1)}), s8[524288]{0:T(1024)(128)(4,1)S(1)}, s32[]{:S(2)}) async-start(s8[4718592]{0:T(1024)(128)(4,1)} %bitcast.74), calls=%async_computation.3 | async-start | bytes 1048576
  76.2 12.0 %collective-permute-start.8 = (f32[288,384]{1,0:T(8,128)}, f32[288,384]{1,0:T(8,128)}, u32[]{:S(2)}, u32[]{:S(2)}) collective-permute-start(f32[288,384]{1,0:T(8,128)} %fusion.29), channel_id=1, source_target_pairs={{0,1},{1,0},{2,3},{3,2},{4,5},{5,4},{6,7},{7,6},{8,9},{9,8},{10,11... | collective-permute-start | bytes 1327112 | tf_op jit(solution)/shard_map/ppermute | solution.py:126
  85.8 4.2 %collective-permute-start.11 = (f32[672,128]{1,0:T(8,128)}, f32[672,128]{1,0:T(8,128)S(1)}, u32[]{:S(2)}, u32[]{:S(2)}) collective-permute-start(f32[672,128]{1,0:T(8,128)} %maximum_bitcast_fusion), channel_id=1, source_target_pairs={{0,1},{1,0},{2,3},{3,2},{4,5},{5,4},{6,7},{7,6},{8,9},{9,8},{10,11... | collective-permute-start | bytes 1032200 | tf_op jit(solution)/shard_map/ppermute | solution.py:126
  86.6 12.1 %collective-permute-start.17 = (f32[384,256]{1,0:T(8,128)}, f32[384,256]{1,0:T(8,128)S(1)}, u32[]{:S(2)}, u32[]{:S(2)}) collective-permute-start(f32[384,256]{1,0:T(8,128)} %maximum_select_fusion.2), channel_id=1, source_target_pairs={{0,2},{1,3},{2,0},{3,1},{4,6},{5,7},{6,4},{7,5},{8,10},{9,11},{10,... | collective-permute-start | bytes 1179656 | tf_op jit(solution)/shard_map/ppermute | solution.py:115
  89.4 18.8 %collective-permute-start.9 = (f32[288,384]{1,0:T(8,128)S(1)}, f32[288,384]{1,0:T(8,128)S(1)}, u32[]{:S(2)}, u32[]{:S(2)}) collective-permute-start(f32[288,384]{1,0:T(8,128)S(1)} %add.77), channel_id=1, source_target_pairs={{0,2},{1,3},{2,0},{3,1},{4,6},{5,7},{6,4},{7,5},{8,10},{9,11},{10,... | collective-permute-start | bytes 1327112 | tf_op jit(solution)/shard_map/ppermute | solution.py:126
  90.0 25.1 %collective-permute-start.12 = (f32[672,128]{1,0:T(8,128)S(1)}, f32[672,128]{1,0:T(8,128)S(1)}, u32[]{:S(2)}, u32[]{:S(2)}) collective-permute-start(f32[672,128]{1,0:T(8,128)S(1)} %fusion.26), channel_id=1, source_target_pairs={{0,2},{1,3},{2,0},{3,1},{4,6},{5,7},{6,4},{7,5},{8,10},{9,11},{10,... | collective-permute-start | bytes 1032200 | tf_op jit(solution)/shard_map/ppermute | solution.py:126

commit v2 on v1

v2 whole, which is shorter than its diff:
```python
import functools
import math

import jax
import jax.numpy as jnp
from jax import lax
from jax.experimental import pallas as pl
from jax.experimental.pallas import tpu as pltpu
from jax.sharding import PartitionSpec as P

F = 24576
EXACT = lax.Precision.HIGHEST


def quadratic(gram):
    scaled = gram * (1.0 / F)
    return scaled + scaled * scaled


def dot_rows(left, right):
    return lax.dot_general(
        left, right, (((1,), (1,)), ((), ())), preferred_element_type=jnp.float32
    )


def exact_dot(left, right, contract=1):
    return lax.dot_general(
        left,
        right,
        (((contract,), (0,)), ((), ())),
        precision=EXACT,
        preferred_element_type=jnp.float32,
    )


def pairs_of(steps):
    return [(step, before) for step in range(steps) for before in range(step)]


def finish_kernel(steps, per, grams, last, *refs):
    gram_refs, refs = refs[:grams], refs[grams:]
    if last:
        last_ref, *refs = refs
    cross_ref, same_ref, first_ref, inverse_ref, own_ref, targets_ref, resid_ref, coeff_ref = refs
    block = first_ref.shape[1]
    rows = targets_ref.shape[0]
    between = {}
    for at, (step, before) in enumerate(pairs_of(steps)):
        gram = cross_ref[:, at * block : (at + 1) * block]
        if last:
            def of(one, other):
                return jnp.concatenate(
                    [
                        jnp.zeros((block - per, block), jnp.float32),
                        last_ref[one * per : (one + 1) * per, other * block : (other + 1) * block],
                    ],
                    axis=0,
                )

            column = lax.broadcasted_iota(jnp.int32, (block, block), 0) < block - per
            gram = gram + of(step, before) + jnp.where(column, of(before, step).T, 0.0)
        between[step, before] = quadratic(gram) + same_ref[:, at * block : (at + 1) * block]
    deltas = []
    for step in range(steps):
        delta = first_ref[step]
        if step:
            change = jnp.zeros_like(delta)
            for before in range(step):
                change += exact_dot(between[step, before], deltas[before])
            delta = delta - exact_dot(inverse_ref[step], change)
        deltas.append(delta)
    spread = (own_ref[...] == lax.broadcasted_iota(jnp.int32, (steps * per, rows), 1)).astype(jnp.float32)
    own = jnp.concatenate([delta[:per] for delta in deltas], axis=0)
    coeffs = exact_dot(spread, own, 0)
    coeff_ref[...] = coeffs
    resid = targets_ref[...] - coeffs
    kernel = jnp.concatenate(
        [quadratic(ref[...]).reshape(-1, steps, per, rows) for ref in gram_refs], axis=0
    )
    for step in range(steps):
        resid = resid - exact_dot(kernel[:, step].reshape(block, rows), deltas[step], 0)
    resid_ref[...] = resid


def chunks_of(columns):
    width = math.gcd(columns, 1024)
    return [slice(at, at + width) for at in range(0, columns, width)]


def pick_kernel(picks_ref, features_ref, out_ref):
    rows = features_ref.shape[0]
    onehot = picks_ref[...] == lax.broadcasted_iota(jnp.int32, (picks_ref.shape[0], rows), 1)
    onehot = onehot.astype(jnp.float32).astype(features_ref.dtype)
    out_ref[...] = jnp.dot(onehot, features_ref[...], preferred_element_type=jnp.float32).astype(
        out_ref.dtype
    )


def pick(picks, features):
    rows, columns = features.shape
    width = math.gcd(columns, 1024)
    return pl.pallas_call(
        pick_kernel,
        grid=(columns // width,),
        out_shape=jax.ShapeDtypeStruct((picks.shape[0], columns), features.dtype),
        in_specs=[
            pl.BlockSpec((picks.shape[0], 1), lambda i: (0, 0)),
            pl.BlockSpec((rows, width), lambda i: (0, i)),
        ],
        out_specs=pl.BlockSpec((picks.shape[0], width), lambda i: (0, i)),
        cost_estimate=pl.CostEstimate(
            flops=2 * picks.shape[0] * rows * columns, bytes_accessed=rows * columns * 2, transcendentals=0
        ),
    )(picks[:, None], features)


def gram_kernel(chunks, flagged, *refs):
    if flagged:
        flag_ref, *refs = refs
    *slot_refs, features_ref, out_ref = refs
    total = jnp.zeros(out_ref.shape, jnp.float32)
    for at in chunks:
        new = [ref[:, at] for ref in slot_refs]
        total = total + dot_rows(jnp.concatenate(new, axis=0), features_ref[:, at])
    out_ref[...] = total


def cross_kernel(steps, per, chunks, count, flag_ref, *refs):
    *slot_refs, other_ref, features_ref, out_ref, pair_ref = refs
    inner = flag_ref[0] == 1
    total = jnp.zeros(out_ref.shape, jnp.float32)
    pairs = [jnp.zeros((pair_ref.shape[0], pair_ref.shape[0]), jnp.float32) for _ in pairs_of(steps)]
    for at in chunks:
        slots = [ref[:, at] for ref in slot_refs]
        slots[-1] = jnp.where(inner, slots[-1], other_ref[:, at])
        total = total + dot_rows(jnp.concatenate(slots[count:], axis=0), features_ref[:, at])
        slots.append(jnp.zeros_like(slots[0]))
        step_rows = [
            jnp.concatenate([slot[step * per : (step + 1) * per] for slot in slots], axis=0)
            for step in range(steps)
        ]
        for i, (step, before) in enumerate(pairs_of(steps)):
            pairs[i] = pairs[i] + dot_rows(step_rows[step], step_rows[before])
    out_ref[...] = total
    pair_ref[...] = jnp.concatenate(pairs, axis=1)


def last_kernel(steps, per, chunks, flag_ref, *refs):
    *slot_refs, mid_ref, end_ref, inner_ref, left_ref, right_ref, features_ref, out_ref = refs
    inner = flag_ref[0] == 1
    wide = features_ref.shape[0]
    half = left_ref.shape[1]
    total = jnp.zeros((left_ref.shape[0], wide), jnp.float32)
    cross = jnp.zeros(out_ref.shape[:1] + (out_ref.shape[1] - wide,), jnp.float32)
    for at in chunks:
        if at.start < half:
            last = left_ref[:, at]
        else:
            last = right_ref[:, at.start - half : at.stop - half]
        last = jnp.where(inner, inner_ref[:, at], last)
        slots = [ref[:, at] for ref in slot_refs] + [jnp.where(inner, mid_ref[:, at], end_ref[:, at]), last]
        every = jnp.concatenate(
            [slot[step * per : (step + 1) * per] for step in range(steps) for slot in slots], axis=0
        )
        total = total + dot_rows(last, features_ref[:, at])
        cross = cross + dot_rows(last, every)
    out_ref[:, :wide] = total
    out_ref[:, wide:] = cross


VMEM = pl.BlockSpec(memory_space=pltpu.VMEM)
SMEM = pl.BlockSpec(memory_space=pltpu.SMEM)
PARAMS = pltpu.CompilerParams(vmem_limit_bytes=48 * 1024 * 1024)


def cost(shapes, columns):
    rows = sum(m * n for m, n in shapes)
    return pl.CostEstimate(flops=2 * rows * columns, bytes_accessed=4 * rows, transcendentals=0)


def by_step(array, steps, per):
    parts = array.reshape(-1, steps, per, array.shape[-1])
    return jnp.swapaxes(parts, 0, 1).reshape(steps, -1, array.shape[-1])


class Lines:
    def __init__(self):
        self.beside = [(r, r ^ 1) for r in range(8)]
        self.pair = [(r, r ^ 2) for r in range(8)]
        self.across = [(r, r ^ 4) for r in range(8)]
        self.inner = [(r, r ^ 6) for r in range(2, 6)]
        self.outer = [(2, 0), (3, 1), (4, 6), (5, 7)]
        self.ends = [(r, r ^ 1) for r in (0, 1, 6, 7)]
        rank = lax.axis_index("rows")
        self.feat = lax.axis_index("feat")
        self.is_inner = (rank >= 2) & (rank < 6)
        self.order = rank ^ jnp.arange(8)

    def rows(self, array, pairs):
        return lax.ppermute(array, "rows", pairs)

    def near(self, array, bit):
        return lax.ppermute(array, "feat", [(f, f ^ bit) for f in range(4)])

    def joined(self, array, bit):
        other = self.near(array, bit)
        return jnp.where(
            (self.feat & bit) == 0,
            jnp.concatenate([array, other], axis=1),
            jnp.concatenate([other, array], axis=1),
        )

    def run(self, own, share, features, steps, per):
        rows = features.shape[0]
        columns = features.shape[1]
        count = own.shape[0]
        chunks = chunks_of(columns)
        half = columns // 2
        flag = self.is_inner.astype(jnp.int32)[None]
        hold = lax.optimization_barrier

        pair = self.rows(own, self.pair)
        mid = self.rows(own, self.inner)
        own_b = self.rows(own, self.beside)
        share = jnp.concatenate([share, self.rows(share, self.across)], axis=0)
        pair, mid, own_b, share = hold((pair, mid, own_b, share))

        far = self.rows(pair, self.inner)
        mid_end = self.rows(mid, self.outer)
        pair_b = self.rows(pair, self.beside)
        share = jnp.concatenate([share, self.rows(share, self.pair)], axis=0)
        far, mid_end, pair_b, share = hold((far, mid_end, pair_b, share))

        third = jnp.where(self.is_inner, far, mid_end)
        third_b = self.rows(third, self.beside)
        far_end = self.rows(far, self.outer)
        last_in = self.rows(own_b, self.inner)
        share = jnp.concatenate([share, self.rows(share, self.beside)], axis=0)
        slots = [own, own_b, pair, pair_b, third]
        first_gram = pl.pallas_call(
            functools.partial(gram_kernel, chunks, False),
            out_shape=jax.ShapeDtypeStruct((len(slots) * count, rows), jnp.float32),
            in_specs=[VMEM] * (len(slots) + 1),
            out_specs=VMEM,
            compiler_params=PARAMS,
            cost_estimate=cost([(len(slots) * count, rows)], columns),
        )(*slots, features)
        first_gram = first_gram + self.near(first_gram, 1)
        third_b, far_end, last_in, share, first_gram = hold((third_b, far_end, last_in, share, first_gram))

        last_left = self.rows(far_end[:, :half], self.ends)
        last_right = self.rows(third_b[:, half:], self.outer)
        share = self.joined(share, 1)
        first_gram = first_gram + self.near(first_gram, 2)
        slots = slots + [third_b]
        block = 8 * per
        pairs = len(pairs_of(steps))
        second_gram, cross = pl.pallas_call(
            functools.partial(cross_kernel, steps, per, chunks, 5),
            out_shape=(
                jax.ShapeDtypeStruct((2 * count, rows), jnp.float32),
                jax.ShapeDtypeStruct((block, pairs * block), jnp.float32),
            ),
            in_specs=[SMEM] + [VMEM] * (len(slots) + 3),
            out_specs=(VMEM, VMEM),
            compiler_params=PARAMS,
            cost_estimate=cost([(2 * count, rows), (block, pairs * block)], columns),
        )(flag, *slots, mid, far_end, features)
        second = jnp.concatenate([second_gram.reshape(-1, 128), cross.reshape(-1, 128)], axis=0)
        second = second + self.near(second, 1)
        last_left, last_right, share, second, first_gram = hold(
            (last_left, last_right, share, second, first_gram)
        )

        share = self.joined(share, 2)
        second = second + self.near(second, 2)
        last = pl.pallas_call(
            functools.partial(last_kernel, steps, per, chunks),
            out_shape=jax.ShapeDtypeStruct((count, rows + steps * block), jnp.float32),
            in_specs=[SMEM] + [VMEM] * (len(slots) + 6),
            out_specs=VMEM,
            compiler_params=PARAMS,
            cost_estimate=cost([(count, rows + steps * block)], columns),
        )(flag, *slots, mid, far_end, last_in, last_left, last_right, features)
        last = last + self.near(last, 1)
        last = last + self.near(last, 2)
        at = second_gram.size // 128
        second_gram = second[:at].reshape(second_gram.shape)
        cross = second[at:].reshape(cross.shape)
        share = share.reshape(2, 2, 2, count, -1).transpose(2, 1, 0, 3, 4)
        return [first_gram, second_gram, last[:, :rows]], [last[:, rows:]], cross, share.reshape(8 * count, -1)


class Gathers:
    def __init__(self):
        size = lax.axis_size("rows")
        self.order = (lax.axis_index("rows") + jnp.arange(size)) % size

    def turn(self, own):
        every = lax.all_gather(own, "rows", axis=0, tiled=True)
        start = lax.axis_index("rows") * own.shape[0]
        return lax.dynamic_slice_in_dim(
            jnp.concatenate([every, every], axis=0), start, every.shape[0], 0
        )

    def run(self, own, share, features, steps, per):
        every = self.turn(own)
        blocks = by_step(every, steps, per)
        cross = jnp.concatenate(
            [dot_rows(blocks[step], blocks[before]) for step, before in pairs_of(steps)], axis=1
        )
        gram = lax.psum(dot_rows(every, features), "feat")
        share = lax.all_gather(self.turn(share), "feat", axis=1, tiled=True)
        return [gram], [], lax.psum(cross, "feat"), share


def local(features, targets, block_index, inverse):
    rank = lax.axis_index("rows")
    row_count = lax.axis_size("rows")
    feat_count = lax.axis_size("feat")
    rows_here, columns = targets.shape
    steps, block = block_index.shape
    per = block // row_count
    mover = Lines() if (row_count, feat_count) == (8, 4) else Gathers()

    own_picks = lax.dynamic_slice_in_dim(block_index, rank * per, per, 1) - rank * rows_here
    own_picks = own_picks.reshape(-1)
    own = pick(own_picks, features)
    width = columns // feat_count
    share = jnp.take(
        lax.dynamic_slice_in_dim(targets, lax.axis_index("feat") * width, width, 1), own_picks, axis=0
    )

    place = jnp.arange(block)
    moved = jnp.repeat(mover.order, per) * per + place % per
    swap = moved[:, None] == place[None, :]
    picks = jnp.sum(jnp.where(swap[None], block_index[:, None, :], 0), axis=2)
    swap = swap.astype(jnp.float32)
    turned = jnp.stack(
        [exact_dot(exact_dot(swap, inverse[step]), swap.T) for step in range(steps)]
    )
    same = jnp.concatenate(
        [
            (picks[step][:, None] == picks[before][None, :]).astype(jnp.float32)
            for step, before in pairs_of(steps)
        ],
        axis=1,
    )

    grams, last, cross, first = mover.run(own, share, features, steps, per)
    first = lax.dot_general(
        turned,
        by_step(first, steps, per),
        (((2,), (1,)), ((0,), (0,))),
        precision=EXACT,
        preferred_element_type=jnp.float32,
    )
    operands = grams + last + [cross, same, first, turned, own_picks[:, None], targets]
    out = jax.ShapeDtypeStruct(targets.shape, jnp.float32)
    return pl.pallas_call(
        functools.partial(finish_kernel, steps, per, len(grams), bool(last)),
        out_shape=(out, out),
        in_specs=[VMEM] * len(operands),
        out_specs=(VMEM, VMEM),
        compiler_params=PARAMS,
    )(*operands)


def solution(mesh):
    return jax.shard_map(
        local,
        mesh=mesh,
        in_specs=(P("rows", "feat"), P("rows", None), P(), P()),
        out_specs=(P("rows", None), P("rows", None)),
        check_vma=False,
    )
```

time: 121 us -> 140 us (1.16)
  Pallas kernels: 5.11 us -> 26 us
  waiting for transfers between devices: 62.1 us -> 45.2 us
  matrix products: 14.9 us -> 4.79 us
  starting transfers between devices: 21.8 us -> 30.4 us
  other arithmetic: 6.52 us -> 14.8 us
  local copies, waits for them, and re-layouts: 8.94 us -> 16.4 us
    pallas_call x1 -> x5, Pallas kernels: 5.11 us -> 26 us  [the longest x1 5.74 us: run(): pl.pallas_call(functools.partial(last_kernel, steps, per, chunks), out_sh...]
    ppermute x12 -> x14, waiting for transfers between devices: 39.5 us -> 23.8 us  [rows(): return lax.ppermute(array, 'rows', pairs)]
    dot_general x6 -> x1, matrix products: 13.4 us -> 0.78 us  [local(): lax.dot_general(turned, by_step(first, steps, per), (((2,), (1,)), ((0,),...]
    ppermute x12 -> x14, starting transfers between devices: 17.7 us -> 24.8 us  [rows(): return lax.ppermute(array, 'rows', pairs)]
    add x5 -> x7, other arithmetic: 1.35 us -> 5.39 us  [the longest x1 1.8 us: run(): first_gram = first_gram + self.near(first_gram, 2)]
    reshape x4, local copies, waits for them, and re-layouts: 0.6 us -> 3.28 us  [the longest x1 1.62 us: run(): cross.reshape(-1, 128)]
    concatenate x4, other arithmetic: 0.04 us -> 2.7 us  [the longest x1 1.36 us: joined(): jnp.concatenate([array, other], axis=1)]
    select_n x5, other arithmetic: 0.9 us -> 3.39 us  [the longest x2 2.17 us: joined(): jnp.where(self.feat & bit == 0, jnp.concatenate([array, other], axis=1),...]
  transfers between devices with their start and end apart: 18 -> 22, of which waited for: 10 -> 6; matrix products, arithmetic and copies ran while one was open for 19% -> 19% of each run, Pallas kernels for 0% -> 7%
where the time goes in v2:
time: 140 us; the launch traced here: 139 us
  waiting for transfers between devices  45.2 us (32%)
  starting transfers between devices  30.4 us (22%)
  Pallas kernels  26 us (19%)
  local copies, waits for them, and re-layouts  16.4 us (12%)
  other arithmetic  14.8 us (11%)
  matrix products  4.79 us (3%)
    ppermute x14, starting transfers between devices, rows(): return lax.ppermute(array, 'rows', pairs)  24.8 us
    ppermute x14, waiting for transfers between devices, rows(): return lax.ppermute(array, 'rows', pairs)  23.8 us
    ppermute x8, waiting for transfers between devices, near(): return lax.ppermute(array, 'feat', [(f, f ^ bit) for f in range(4)])  21.4 us
    unnamed x43, local copies, waits for them, and re-layouts  5.93 us
    pallas_call x1, Pallas kernels, run(): pl.pallas_call(functools.partial(last_kernel, steps, per, chunks), out_sh...  5.74 us
    pallas_call x1, Pallas kernels, pick(): pl.pallas_call(pick_kernel, grid=(columns // width,), out_shape=jax.Shape...  5.73 us
    ppermute x8, starting transfers between devices, near(): return lax.ppermute(array, 'feat', [(f, f ^ bit) for f in range(4)])  5.62 us
    pallas_call x1, Pallas kernels, run(): pl.pallas_call(functools.partial(cross_kernel, steps, per, chunks, 5), ou...  5.19 us
  transfers between devices with their start and end apart: 22, of which 6 were waited for; matrix products, arithmetic and copies ran while one was open for 19% of the time, Pallas kernels for 7%

profile of v2, /device:TPU:0, one launch (start us, length us, event | category | flops | bytes accessed | tf_op | source)
XLA Modules:
  0.0 138.7 jit_solution(18309050647422476271)
XLA Ops:
  2.2 5.7 %shard_map.59.refs_0_ = bf16[48,6144]{1,0:T(8,128)(2,1)} custom-call(s32[48,1]{1,0:T(8,128)} %copy.21.picks_ref.refs_8_, bf16[384,6144]{1,0:T(8,128)(2,1)} %refs_11_.1), custom_call_target="tpu_custom_call" | custom-call | flops 226492416 | bytes 4718592 | tf_op jit(solution)/shard_map/pallas_call | solution.py:102
  8.0 3.0 %collective-permute-start = (bf16[48,6144]{1,0:T(8,128)(2,1)}, bf16[48,6144]{1,0:T(8,128)(2,1)S(1)}, u32[]{:S(2)}, u32[]{:S(2)}) collective-permute-start(bf16[48,6144]{1,0:T(8,128)(2,1)} %shard_map.59.refs_0_), channel_id=1, source_target_pairs={{0,8},{4,12},{8,0},{12,4},{16,24},{20,28},{24,16},{28,20},{1,9},{5... | collective-permute-start | bytes 1769480 | tf_op jit(solution)/shard_map/ppermute | solution.py:200
  11.7 1.6 %collective-permute-start.2 = (bf16[48,6144]{1,0:T(8,128)(2,1)}, bf16[48,6144]{1,0:T(8,128)(2,1)S(1)}, u32[]{:S(2)}, u32[]{:S(2)}) collective-permute-start(bf16[48,6144]{1,0:T(8,128)(2,1)} %shard_map.59.refs_0_), channel_id=1, source_target_pairs={{0,4},{4,0},{8,12},{12,8},{16,20},{20,16},{24,28},{28,24},{1,5},{5... | collective-permute-start | bytes 1769480 | tf_op jit(solution)/shard_map/ppermute | solution.py:200
  13.4 0.9 constant_dynamic-slice_fusion
  15.0 3.8 %collective-permute-start.3 = (f32[48,128]{1,0:T(8,128)S(1)}, f32[48,128]{1,0:T(8,128)S(1)}, u32[]{:S(2)}, u32[]{:S(2)}) collective-permute-start(f32[48,128]{1,0:T(8,128)S(1)} %broadcast_select_fusion.1), channel_id=1, source_target_pairs={{0,16},{4,20},{8,24},{12,28},{16,0},{20,4},{24,8},{28,12},{1,17},{... | collective-permute-start | bytes 73736 | tf_op jit(solution)/shard_map/ppermute | solution.py:200
  19.0 0.9 fusion
  19.8 9.9 %collective-permute-done.3 = f32[48,128]{1,0:T(8,128)S(1)} collective-permute-done((f32[48,128]{1,0:T(8,128)S(1)}, f32[48,128]{1,0:T(8,128)S(1)}, u32[]{:S(2)}, u32[]{:S(2)}) %collective-permute-start.3) | collective-permute-done | bytes 24608 | tf_op jit(solution)/shard_map/ppermute | solution.py:200
  29.8 1.5 %collective-permute-start.4 = (bf16[48,6144]{1,0:T(8,128)(2,1)S(1)}, bf16[48,6144]{1,0:T(8,128)(2,1)}, u32[]{:S(2)}, u32[]{:S(2)}) collective-permute-start(bf16[48,6144]{1,0:T(8,128)(2,1)S(1)} %collective-permute-done.refs_2_), channel_id=1, source_target_pairs={{8,16},{12,20},{16,8},{20,12},{9,17},{13,21},{17,9},{21,13},{10,18... | collective-permute-start | bytes 1769480 | tf_op jit(solution)/shard_map/ppermute | solution.py:200
  31.3 1.5 %collective-permute-start.6 = (bf16[48,6144]{1,0:T(8,128)(2,1)S(1)}, bf16[48,6144]{1,0:T(8,128)(2,1)S(1)}, u32[]{:S(2)}, u32[]{:S(2)}) collective-permute-start(bf16[48,6144]{1,0:T(8,128)(2,1)S(1)} %collective-permute-done.refs_2_), channel_id=1, source_target_pairs={{0,4},{4,0},{8,12},{12,8},{16,20},{20,16},{24,28},{28,24},{1,5},{5... | collective-permute-start | bytes 1769480 | tf_op jit(solution)/shard_map/ppermute | solution.py:200
  32.8 1.3 collective-permute-start.5
  34.1 0.8 fusion.2
  35.0 0.8 fusion.4
  35.8 2.7 %collective-permute-start.7 = (f32[96,128]{1,0:T(8,128)S(1)}, f32[96,128]{1,0:T(8,128)S(1)}, u32[]{:S(2)}, u32[]{:S(2)}) collective-permute-start(f32[96,128]{1,0:T(8,128)S(1)} %pad_maximum_fusion.5), channel_id=1, source_target_pairs={{0,8},{4,12},{8,0},{12,4},{16,24},{20,28},{24,16},{28,20},{1,9},{5... | collective-permute-start | bytes 147464 | tf_op jit(solution)/shard_map/ppermute | solution.py:200
  38.6 1.5 %collective-permute-start.10 = (bf16[48,6144]{1,0:T(8,128)(2,1)S(1)}, bf16[48,6144]{1,0:T(8,128)(2,1)}, u32[]{:S(2)}, u32[]{:S(2)}) collective-permute-start(bf16[48,6144]{1,0:T(8,128)(2,1)S(1)} %collective-permute-done.2.refs_1_), channel_id=1, source_target_pairs={{8,16},{12,20},{16,8},{20,12},{9,17},{13,21},{17,9},{21,13},{10,18... | collective-permute-start | bytes 1769480 | tf_op jit(solution)/shard_map/ppermute | solution.py:200
  40.1 9.3 %collective-permute-done.7 = f32[96,128]{1,0:T(8,128)S(1)} collective-permute-done((f32[96,128]{1,0:T(8,128)S(1)}, f32[96,128]{1,0:T(8,128)S(1)}, u32[]{:S(2)}, u32[]{:S(2)}) %collective-permute-start.7) | collective-permute-done | bytes 49184 | tf_op jit(solution)/shard_map/ppermute | solution.py:200
  50.0 0.8 copy-done.11
  50.9 1.3 collective-permute-start.9
  52.1 1.1 broadcast_select_fusion.refs_4_
  53.9 1.4 %select_reduce_fusion = s32[3,128]{1,0:T(4,128)} fusion(s32[3,128]{1,0:T(4,128)} %param.6, pred[128,128]{1,0:T(8,128)(4,1)S(1)} %iota_compare_fusion), kind=kLoop, calls=%fused_computation.11 | loop fusion | flops 97920 | bytes 19456 | tf_op jit(solution)/shard_map/reduce_sum | solution.py:337
  55.3 1.1 copy-done
  56.4 4.2 %shard_map.60 = f32[240,384]{1,0:T(8,128)S(1)} custom-call(bf16[48,6144]{1,0:T(8,128)(2,1)S(1)} %copy-done, bf16[48,6144]{1,0:T(8,128)(2,1)S(1)} %collective-permute-done.2.refs_1_, bf16[48,6144]{1,0:T(8,128)(2,1)S(1)} %collective-permute-done.refs_2_, bf16[48,6144]{1,0:T(8,128)(2,1)S(1)} %collective-permute-done.6.refs_3_, ...), custom_call_target="tpu_custom_call" | custom-call | flops 1132462080 | bytes 368640 | tf_op jit(solution)/shard_map/pallas_call | solution.py:240
  61.2 1.5 %collective-permute-start.11 = (f32[192,128]{1,0:T(8,128)S(1)}, f32[192,128]{1,0:T(8,128)S(1)}, u32[]{:S(2)}, u32[]{:S(2)}) collective-permute-start(f32[192,128]{1,0:T(8,128)S(1)} %copy-done.12), channel_id=1, source_target_pairs={{0,4},{4,0},{8,12},{12,8},{16,20},{20,16},{24,28},{28,24},{1,5},{5... | collective-permute-start | bytes 294920 | tf_op jit(solution)/shard_map/ppermute | solution.py:200
  62.7 0.9 convolution_bitcast_fusion
  63.6 4.6 %collective-permute-done.11 = f32[192,128]{1,0:T(8,128)S(1)} collective-permute-done((f32[192,128]{1,0:T(8,128)S(1)}, f32[192,128]{1,0:T(8,128)S(1)}, u32[]{:S(2)}, u32[]{:S(2)}) %collective-permute-start.11) | collective-permute-done | bytes 98336 | tf_op jit(solution)/shard_map/ppermute | solution.py:200
  70.4 2.4 %collective-permute-start.13 = (bf16[48,3072]{1,0:T(8,128)(2,1)}, bf16[48,3072]{1,0:T(8,128)(2,1)}, u32[]{:S(2)}, u32[]{:S(2)}) collective-permute-start(bf16[48,3072]{1,0:T(8,128)(2,1)} %slice.39), channel_id=1, source_target_pairs={{0,4},{4,0},{24,28},{28,24},{1,5},{5,1},{25,29},{29,25},{2,6},{6,2... | collective-permute-start | bytes 884744 | tf_op jit(solution)/shard_map/ppermute | solution.py:200
  72.8 1.7 %slice.40 = bf16[48,3072]{1,0:T(8,128)(2,1)} slice(bf16[48,6144]{1,0:T(8,128)(2,1)} %collective-permute-done.8.refs_5_), slice={[0:48], [3072:6144]} | slice | bytes 589824 | tf_op jit(solution)/shard_map/slice | solution.py:252
  74.5 1.5 %collective-permute-start.14 = (bf16[48,3072]{1,0:T(8,128)(2,1)}, bf16[48,3072]{1,0:T(8,128)(2,1)}, u32[]{:S(2)}, u32[]{:S(2)}) collective-permute-start(bf16[48,3072]{1,0:T(8,128)(2,1)} %slice.40), channel_id=1, source_target_pairs={{8,0},{12,4},{16,24},{20,28},{9,1},{13,5},{17,25},{21,29},{10,2},{... | collective-permute-start | bytes 884744 | tf_op jit(solution)/shard_map/ppermute | solution.py:200
  76.1 5.2 %shard_map.61 = (f32[96,384]{1,0:T(8,128)S(1)}, f32[128,384]{1,0:T(8,128)S(1)}) custom-call(s32[1]{0:T(128)} %bitcast.1.flag_ref, bf16[48,6144]{1,0:T(8,128)(2,1)S(1)} %copy-done.1, bf16[48,6144]{1,0:T(8,128)(2,1)S(1)} %collective-permute-done.2.refs_1_, bf16[48,6144]{1,0:T(8,128)(2,1)S(1)} %collective-permute-done.refs_2_, ...), custom_call_target="tpu_custom_call" | custom-call | flops 1056964608 | bytes 344064 | tf_op jit(solution)/shard_map/pallas_call | solution.py:258
  82.6 1.6 %reshape.102 = f32[288,128]{1,0:T(8,128)} reshape(f32[96,384]{1,0:T(8,128)} %copy-done.9) | data formatting | bytes 294912 | tf_op jit(solution)/shard_map/reshape | solution.py:269
  84.2 1.6 %constant_dynamic-update-slice_fusion.1 = f32[672,128]{1,0:T(8,128)} fusion(f32[288,128]{1,0:T(8,128)} %reshape.102), kind=kLoop, calls=%fused_computation.37 | loop fusion | bytes 294912
  85.8 1.6 %reshape.103 = f32[384,128]{1,0:T(8,128)} reshape(f32[128,384]{1,0:T(8,128)} %copy-done.8) | data formatting | bytes 393216 | tf_op jit(solution)/shard_map/reshape | solution.py:269
  87.4 1.5 %collective-permute-start.17 = (f32[240,384]{1,0:T(8,128)}, f32[240,384]{1,0:T(8,128)S(1)}, u32[]{:S(2)}, u32[]{:S(2)}) collective-permute-start(f32[240,384]{1,0:T(8,128)} %add.68), channel_id=1, source_target_pairs={{0,2},{1,3},{2,0},{3,1},{4,6},{5,7},{6,4},{7,5},{8,10},{9,11},{10,... | collective-permute-start | bytes 1105928 | tf_op jit(solution)/shard_map/ppermute | solution.py:203
  88.9 1.6 %constant_dynamic-update-slice_fusion = f32[672,128]{1,0:T(8,128)} fusion(f32[672,128]{1,0:T(8,128)} %constant_dynamic-update-slice_fusion.1, f32[384,128]{1,0:T(8,128)} %reshape.103), kind=kLoop, calls=%fused_computation.36 | loop fusion | bytes 393216 | tf_op jit(solution)/shard_map/concatenate | solution.py:269
  90.8 2.0 %maximum_select_fusion = f32[384,256]{1,0:T(8,128)} fusion(f32[384,128]{1,0:T(8,128)} %collective-permute-done.15, f32[384,128]{1,0:T(8,128)} %pad_maximum_fusion.2, pred[]{:T(512)S(6)} %eq.66), kind=kLoop, calls=%fused_computation.8 | loop fusion | flops 294912 | bytes 786433 | tf_op jit(solution)/shard_map/jit(_where)/select_n | solution.py:207
  92.8 1.7 %add.69 = f32[672,128]{1,0:T(8,128)} add(f32[672,128]{1,0:T(8,128)} %constant_dynamic-update-slice_fusion, f32[672,128]{1,0:T(8,128)S(1)} %collective-permute-done.16) | non-fusion elementwise | flops 86016 | bytes 1032192 | tf_op jit(solution)/shard_map/add | solution.py:270
  94.6 4.0 %collective-permute-done.17 = f32[240,384]{1,0:T(8,128)S(1)} collective-permute-done((f32[240,384]{1,0:T(8,128)}, f32[240,384]{1,0:T(8,128)S(1)}, u32[]{:S(2)}, u32[]{:S(2)}) %collective-permute-start.17) | collective-permute-done | bytes 368672 | tf_op jit(solution)/shard_map/ppermute | solution.py:203
  98.6 1.8 %add.70.refs_0_ = f32[240,384]{1,0:T(8,128)} add(f32[240,384]{1,0:T(8,128)} %add.68, f32[240,384]{1,0:T(8,128)S(1)} %collective-permute-done.17) | non-fusion elementwise | flops 92160 | bytes 1105920 | tf_op jit(solution)/shard_map/add | solution.py:254
  100.4 1.1 copy-done.4
  101.4 5.7 %shard_map.62 = f32[48,768]{1,0:T(8,128)S(1)} custom-call(s32[1]{0:T(128)} %bitcast.1.flag_ref, bf16[48,6144]{1,0:T(8,128)(2,1)S(1)} %copy-done.1, bf16[48,6144]{1,0:T(8,128)(2,1)S(1)} %collective-permute-done.2.refs_1_, bf16[48,6144]{1,0:T(8,128)(2,1)S(1)} %collective-permute-done.refs_2_, bf16[48,6144]{1,0:T(8,128)(2,1)S(1)} %collective-permute-done.6.refs_3_, ...), custom_call_target="tpu_custom_call" | custom-call | flops 452984832 | bytes 147456 | tf_op jit(solution)/shard_map/pallas_call | solution.py:277
  107.6 1.6 %collective-permute-start.21 = (f32[384,256]{1,0:T(8,128)}, f32[384,256]{1,0:T(8,128)S(1)}, u32[]{:S(2)}, u32[]{:S(2)}) collective-permute-start(f32[384,256]{1,0:T(8,128)} %maximum_select_fusion), channel_id=1, source_target_pairs={{0,2},{1,3},{2,0},{3,1},{4,6},{5,7},{6,4},{7,5},{8,10},{9,11},{10,... | collective-permute-start | bytes 1179656 | tf_op jit(solution)/shard_map/ppermute | solution.py:203
  109.2 1.0 collective-permute-start.20
  110.5 1.1 collective-permute-start.18
  111.6 0.9 pad_maximum_fusion.3.refs_7_
  112.5 10.4 %collective-permute-done.20 = f32[48,768]{1,0:T(8,128)S(1)} collective-permute-done((f32[48,768]{1,0:T(8,128)S(1)}, f32[48,768]{1,0:T(8,128)S(1)}, u32[]{:S(2)}, u32[]{:S(2)}) %collective-permute-start.20) | collective-permute-done | bytes 147488 | tf_op jit(solution)/shard_map/ppermute | solution.py:203
  123.0 6.9 %collective-permute-done.18 = f32[672,128]{1,0:T(8,128)S(1)} collective-permute-done((f32[672,128]{1,0:T(8,128)}, f32[672,128]{1,0:T(8,128)S(1)}, u32[]{:S(2)}, u32[]{:S(2)}) %collective-permute-start.18) | collective-permute-done | bytes 344096 | tf_op jit(solution)/shard_map/ppermute | solution.py:203
  129.9 1.0 add.71
  131.1 1.4 pad_maximum_fusion
  133.6 5.1 %shard_map.63 = (f32[384,512]{1,0:T(8,128)}, f32[384,512]{1,0:T(8,128)}) custom-call(f32[240,384]{1,0:T(8,128)S(1)} %copy-done.5, f32[96,384]{1,0:T(8,128)S(1)} %reshape.104.refs_1_, f32[48,384]{1,0:T(8,128)S(1)} %get-tuple-element.45.refs_2_, f32[48,384]{1,0:T(8,128)S(1)} %get-tuple-element.44.refs_3_, f32[128,384]{1,0:T(8,128)S(1)} %reshape.105.refs_4_, ...), custom_call_target="tpu_custom_call" | custom-call | tf_op jit(solution)/shard_map/pallas_call | solution.py:360
  (95 shorter events, 10.9 us)
Async XLA Ops:
  0.6 18.3 %copy-start.16 = (f32[3,128,128]{2,1,0:T(8,128)S(1)}, f32[3,128,128]{2,1,0:T(8,128)}, u32[]{:S(2)}) copy-start(f32[3,128,128]{2,1,0:T(8,128)} %param.7) | copy-start | bytes 589828
  8.0 21.8 %collective-permute-start = (bf16[48,6144]{1,0:T(8,128)(2,1)}, bf16[48,6144]{1,0:T(8,128)(2,1)S(1)}, u32[]{:S(2)}, u32[]{:S(2)}) collective-permute-start(bf16[48,6144]{1,0:T(8,128)(2,1)} %shard_map.59.refs_0_), channel_id=1, source_target_pairs={{0,8},{4,12},{8,0},{12,4},{16,24},{20,28},{24,16},{28,20},{1,9},{5... | collective-permute-start | bytes 1769480 | tf_op jit(solution)/shard_map/ppermute | solution.py:200
  11.0 18.8 %collective-permute-start.1 = (bf16[48,6144]{1,0:T(8,128)(2,1)}, bf16[48,6144]{1,0:T(8,128)(2,1)S(1)}, u32[]{:S(2)}, u32[]{:S(2)}) collective-permute-start(bf16[48,6144]{1,0:T(8,128)(2,1)} %shard_map.59.refs_0_), channel_id=1, source_target_pairs={{8,16},{12,20},{16,8},{20,12},{9,17},{13,21},{17,9},{21,13},{10,18... | collective-permute-start | bytes 1769480 | tf_op jit(solution)/shard_map/ppermute | solution.py:200
  11.7 18.1 %collective-permute-start.2 = (bf16[48,6144]{1,0:T(8,128)(2,1)}, bf16[48,6144]{1,0:T(8,128)(2,1)S(1)}, u32[]{:S(2)}, u32[]{:S(2)}) collective-permute-start(bf16[48,6144]{1,0:T(8,128)(2,1)} %shard_map.59.refs_0_), channel_id=1, source_target_pairs={{0,4},{4,0},{8,12},{12,8},{16,20},{20,16},{24,28},{28,24},{1,5},{5... | collective-permute-start | bytes 1769480 | tf_op jit(solution)/shard_map/ppermute | solution.py:200
  15.0 14.8 %collective-permute-start.3 = (f32[48,128]{1,0:T(8,128)S(1)}, f32[48,128]{1,0:T(8,128)S(1)}, u32[]{:S(2)}, u32[]{:S(2)}) collective-permute-start(f32[48,128]{1,0:T(8,128)S(1)} %broadcast_select_fusion.1), channel_id=1, source_target_pairs={{0,16},{4,20},{8,24},{12,28},{16,0},{20,4},{24,8},{28,12},{1,17},{... | collective-permute-start | bytes 73736 | tf_op jit(solution)/shard_map/ppermute | solution.py:200
  19.0 31.9 %copy-start.17 = (s32[128]{0:T(128)}, s32[128]{0:T(128)S(1)}, u32[]{:S(2)}) copy-start(s32[128]{0:T(128)S(1)} %fusion.15) | copy-start | bytes 1540
  29.8 25.5 %copy-start.2 = (bf16[48,6144]{1,0:T(8,128)(2,1)}, bf16[48,6144]{1,0:T(8,128)(2,1)S(1)}, u32[]{:S(2)}) copy-start(bf16[48,6144]{1,0:T(8,128)(2,1)S(1)} %collective-permute-done.1.refs_6_) | copy-start | bytes 1769476
  29.8 20.2 %collective-permute-start.4 = (bf16[48,6144]{1,0:T(8,128)(2,1)S(1)}, bf16[48,6144]{1,0:T(8,128)(2,1)}, u32[]{:S(2)}, u32[]{:S(2)}) collective-permute-start(bf16[48,6144]{1,0:T(8,128)(2,1)S(1)} %collective-permute-done.refs_2_), channel_id=1, source_target_pairs={{8,16},{12,20},{16,8},{20,12},{9,17},{13,21},{17,9},{21,13},{10,18... | collective-permute-start | bytes 1769480 | tf_op jit(solution)/shard_map/ppermute | solution.py:200
  31.3 19.5 %collective-permute-start.6 = (bf16[48,6144]{1,0:T(8,128)(2,1)S(1)}, bf16[48,6144]{1,0:T(8,128)(2,1)S(1)}, u32[]{:S(2)}, u32[]{:S(2)}) collective-permute-start(bf16[48,6144]{1,0:T(8,128)(2,1)S(1)} %collective-permute-done.refs_2_), channel_id=1, source_target_pairs={{0,4},{4,0},{8,12},{12,8},{16,20},{20,16},{24,28},{28,24},{1,5},{5... | collective-permute-start | bytes 1769480 | tf_op jit(solution)/shard_map/ppermute | solution.py:200
  32.8 17.2 %collective-permute-start.5 = (bf16[48,6144]{1,0:T(8,128)(2,1)S(1)}, bf16[48,6144]{1,0:T(8,128)(2,1)S(1)}, u32[]{:S(2)}, u32[]{:S(2)}) collective-permute-start(bf16[48,6144]{1,0:T(8,128)(2,1)S(1)} %collective-permute-done.1.refs_6_), channel_id=1, source_target_pairs={{8,0},{12,4},{16,24},{20,28},{9,1},{13,5},{17,25},{21,29},{10,2},{... | collective-permute-start | bytes 1769480 | tf_op jit(solution)/shard_map/ppermute | solution.py:200
  35.8 13.6 %collective-permute-start.7 = (f32[96,128]{1,0:T(8,128)S(1)}, f32[96,128]{1,0:T(8,128)S(1)}, u32[]{:S(2)}, u32[]{:S(2)}) collective-permute-start(f32[96,128]{1,0:T(8,128)S(1)} %pad_maximum_fusion.5), channel_id=1, source_target_pairs={{0,8},{4,12},{8,0},{12,4},{16,24},{20,28},{24,16},{28,20},{1,9},{5... | collective-permute-start | bytes 147464 | tf_op jit(solution)/shard_map/ppermute | solution.py:200
  38.6 31.1 %collective-permute-start.10 = (bf16[48,6144]{1,0:T(8,128)(2,1)S(1)}, bf16[48,6144]{1,0:T(8,128)(2,1)}, u32[]{:S(2)}, u32[]{:S(2)}) collective-permute-start(bf16[48,6144]{1,0:T(8,128)(2,1)S(1)} %collective-permute-done.2.refs_1_), channel_id=1, source_target_pairs={{8,16},{12,20},{16,8},{20,12},{9,17},{13,21},{17,9},{21,13},{10,18... | collective-permute-start | bytes 1769480 | tf_op jit(solution)/shard_map/ppermute | solution.py:200
  50.0 0.8 copy-start.11
  50.9 18.8 %collective-permute-start.9 = (bf16[48,6144]{1,0:T(8,128)(2,1)}, bf16[48,6144]{1,0:T(8,128)(2,1)S(1)}, u32[]{:S(2)}, u32[]{:S(2)}) collective-permute-start(bf16[48,6144]{1,0:T(8,128)(2,1)} %collective-permute-done.4), channel_id=1, source_target_pairs={{8,0},{12,4},{16,24},{20,28},{9,1},{13,5},{17,25},{21,29},{10,2},{... | collective-permute-start | bytes 1769480 | tf_op jit(solution)/shard_map/ppermute | solution.py:200
  53.3 16.4 %collective-permute-start.8 = (bf16[48,6144]{1,0:T(8,128)(2,1)S(1)}, bf16[48,6144]{1,0:T(8,128)(2,1)}, u32[]{:S(2)}, u32[]{:S(2)}) collective-permute-start(bf16[48,6144]{1,0:T(8,128)(2,1)S(1)} %broadcast_select_fusion.refs_4_), channel_id=1, source_target_pairs={{0,4},{4,0},{8,12},{12,8},{16,20},{20,16},{24,28},{28,24},{1,5},{5... | collective-permute-start | bytes 1769480 | tf_op jit(solution)/shard_map/ppermute | solution.py:200
  55.3 5.4 %copy-start.19 = (s32[3,128]{1,0:T(4,128)S(1)}, s32[3,128]{1,0:T(4,128)}, u32[]{:S(2)}) copy-start(s32[3,128]{1,0:T(4,128)} %select_reduce_fusion) | copy-start | bytes 4612
  55.3 7.4 %copy-start.18 = (s32[128]{0:T(128)S(1)}, s32[128]{0:T(128)}, u32[]{:S(2)}) copy-start(s32[128]{0:T(128)} %copy-done.17) | copy-start | bytes 1540
  55.3 1.1 copy-start
  56.4 4.8 %copy-start.12 = (f32[192,128]{1,0:T(8,128)S(1)}, f32[192,128]{1,0:T(8,128)}, u32[]{:S(2)}) copy-start(f32[192,128]{1,0:T(8,128)} %pad_maximum_fusion.4) | copy-start | bytes 294916
  56.4 6.4 %copy-start.15 = (f32[128,128]{1,0:T(8,128)S(1)}, f32[128,128]{1,0:T(8,128)}, u32[]{:S(2)}) copy-start(f32[128,128]{1,0:T(8,128)} %fusion) | copy-start | bytes 196612
  56.4 19.7 %copy-start.1 = (bf16[48,6144]{1,0:T(8,128)(2,1)S(1)}, bf16[48,6144]{1,0:T(8,128)(2,1)}, u32[]{:S(2)}) copy-start(bf16[48,6144]{1,0:T(8,128)(2,1)} %shard_map.59.refs_0_) | copy-start | bytes 1769476
  56.4 19.7 %copy-start.3 = (bf16[48,6144]{1,0:T(8,128)(2,1)S(1)}, bf16[48,6144]{1,0:T(8,128)(2,1)}, u32[]{:S(2)}) copy-start(bf16[48,6144]{1,0:T(8,128)(2,1)} %copy-done.2) | copy-start | bytes 1769476
  60.6 8.3 %collective-permute-start.12 = (f32[240,384]{1,0:T(8,128)S(1)}, f32[240,384]{1,0:T(8,128)S(1)}, u32[]{:S(2)}, u32[]{:S(2)}) collective-permute-start(f32[240,384]{1,0:T(8,128)S(1)} %shard_map.60), channel_id=1, source_target_pairs={{0,1},{1,0},{2,3},{3,2},{4,5},{5,4},{6,7},{7,6},{8,9},{9,8},{10,11... | collective-permute-start | bytes 1105928 | tf_op jit(solution)/shard_map/ppermute | solution.py:203
  61.2 7.0 %collective-permute-start.11 = (f32[192,128]{1,0:T(8,128)S(1)}, f32[192,128]{1,0:T(8,128)S(1)}, u32[]{:S(2)}, u32[]{:S(2)}) collective-permute-start(f32[192,128]{1,0:T(8,128)S(1)} %copy-done.12), channel_id=1, source_target_pairs={{0,4},{4,0},{8,12},{12,8},{16,20},{20,16},{24,28},{28,24},{1,5},{5... | collective-permute-start | bytes 294920 | tf_op jit(solution)/shard_map/ppermute | solution.py:200
  70.4 30.0 %collective-permute-start.13 = (bf16[48,3072]{1,0:T(8,128)(2,1)}, bf16[48,3072]{1,0:T(8,128)(2,1)}, u32[]{:S(2)}, u32[]{:S(2)}) collective-permute-start(bf16[48,3072]{1,0:T(8,128)(2,1)} %slice.39), channel_id=1, source_target_pairs={{0,4},{4,0},{24,28},{28,24},{1,5},{5,1},{25,29},{29,25},{2,6},{6,2... | collective-permute-start | bytes 884744 | tf_op jit(solution)/shard_map/ppermute | solution.py:200
  74.5 25.9 %collective-permute-start.14 = (bf16[48,3072]{1,0:T(8,128)(2,1)}, bf16[48,3072]{1,0:T(8,128)(2,1)}, u32[]{:S(2)}, u32[]{:S(2)}) collective-permute-start(bf16[48,3072]{1,0:T(8,128)(2,1)} %slice.40), channel_id=1, source_target_pairs={{8,0},{12,4},{16,24},{20,28},{9,1},{13,5},{17,25},{21,29},{10,2},{... | collective-permute-start | bytes 884744 | tf_op jit(solution)/shard_map/ppermute | solution.py:200
  76.0 14.9 %collective-permute-start.15 = (f32[384,128]{1,0:T(8,128)}, f32[384,128]{1,0:T(8,128)}, u32[]{:S(2)}, u32[]{:S(2)}) collective-permute-start(f32[384,128]{1,0:T(8,128)} %pad_maximum_fusion.2), channel_id=1, source_target_pairs={{0,1},{1,0},{2,3},{3,2},{4,5},{5,4},{6,7},{7,6},{8,9},{9,8},{10,11... | collective-permute-start | bytes 589832 | tf_op jit(solution)/shard_map/ppermute | solution.py:203
  76.1 14.6 %copy-start.20 = (s32[128]{0:T(128)S(1)}, s32[128]{0:T(128)}, u32[]{:S(2)}) copy-start(s32[128]{0:T(128)} %get-tuple-element.47) | copy-start | bytes 1540
  81.3 0.7 copy-start.8
  82.0 0.7 copy-start.9
  87.4 11.2 %collective-permute-start.17 = (f32[240,384]{1,0:T(8,128)}, f32[240,384]{1,0:T(8,128)S(1)}, u32[]{:S(2)}, u32[]{:S(2)}) collective-permute-start(f32[240,384]{1,0:T(8,128)} %add.68), channel_id=1, source_target_pairs={{0,2},{1,3},{2,0},{3,1},{4,6},{5,7},{6,4},{7,5},{8,10},{9,11},{10,... | collective-permute-start | bytes 1105928 | tf_op jit(solution)/shard_map/ppermute | solution.py:203
  90.5 2.3 %collective-permute-start.16 = (f32[672,128]{1,0:T(8,128)}, f32[672,128]{1,0:T(8,128)S(1)}, u32[]{:S(2)}, u32[]{:S(2)}) collective-permute-start(f32[672,128]{1,0:T(8,128)} %constant_dynamic-update-slice_fusion), channel_id=1, source_target_pairs={{0,1},{1,0},{2,3},{3,2},{4,5},{5,4},{6,7},{7,6},{8,9},{9,8},{10,11... | collective-permute-start | bytes 1032200 | tf_op jit(solution)/shard_map/ppermute | solution.py:203
  98.6 8.7 %copy-start.14 = (f32[128,128]{1,0:T(8,128)S(1)}, f32[128,128]{1,0:T(8,128)}, u32[]{:S(2)}) copy-start(f32[128,128]{1,0:T(8,128)} %fusion.2) | copy-start | bytes 196612
  98.6 11.6 %copy-start.13 = (f32[128,128]{1,0:T(8,128)S(1)}, f32[128,128]{1,0:T(8,128)}, u32[]{:S(2)}) copy-start(f32[128,128]{1,0:T(8,128)} %fusion.4) | copy-start | bytes 196612
  100.4 1.1 copy-start.4
  107.2 2.0 %collective-permute-start.19 = (f32[48,768]{1,0:T(8,128)S(1)}, f32[48,768]{1,0:T(8,128)S(1)}, u32[]{:S(2)}, u32[]{:S(2)}) collective-permute-start(f32[48,768]{1,0:T(8,128)S(1)} %shard_map.62), channel_id=1, source_target_pairs={{0,1},{1,0},{2,3},{3,2},{4,5},{5,4},{6,7},{7,6},{8,9},{9,8},{10,11... | collective-permute-start | bytes 442376 | tf_op jit(solution)/shard_map/ppermute | solution.py:203
  107.6 23.5 %collective-permute-start.21 = (f32[384,256]{1,0:T(8,128)}, f32[384,256]{1,0:T(8,128)S(1)}, u32[]{:S(2)}, u32[]{:S(2)}) collective-permute-start(f32[384,256]{1,0:T(8,128)} %maximum_select_fusion), channel_id=1, source_target_pairs={{0,2},{1,3},{2,0},{3,1},{4,6},{5,7},{6,4},{7,5},{8,10},{9,11},{10,... | collective-permute-start | bytes 1179656 | tf_op jit(solution)/shard_map/ppermute | solution.py:203
  109.2 13.8 %collective-permute-start.20 = (f32[48,768]{1,0:T(8,128)S(1)}, f32[48,768]{1,0:T(8,128)S(1)}, u32[]{:S(2)}, u32[]{:S(2)}) collective-permute-start(f32[48,768]{1,0:T(8,128)S(1)} %add.72), channel_id=1, source_target_pairs={{0,2},{1,3},{2,0},{3,1},{4,6},{5,7},{6,4},{7,5},{8,10},{9,11},{10,... | collective-permute-start | bytes 442376 | tf_op jit(solution)/shard_map/ppermute | solution.py:203
  110.5 19.4 %collective-permute-start.18 = (f32[672,128]{1,0:T(8,128)}, f32[672,128]{1,0:T(8,128)S(1)}, u32[]{:S(2)}, u32[]{:S(2)}) collective-permute-start(f32[672,128]{1,0:T(8,128)} %add.69), channel_id=1, source_target_pairs={{0,2},{1,3},{2,0},{3,1},{4,6},{5,7},{6,4},{7,5},{8,10},{9,11},{10,... | collective-permute-start | bytes 1032200 | tf_op jit(solution)/shard_map/ppermute | solution.py:203
  112.5 20.2 %copy-start.10 = (f32[1,128,128]{2,1,0:T(8,128)S(1)}, f32[1,128,128]{2,1,0:T(8,128)}, u32[]{:S(2)}) copy-start(f32[1,128,128]{2,1,0:T(8,128)} %convolution_bitcast_fusion) | copy-start | bytes 196612
  130.9 2.6 %copy-start.5 = (f32[240,384]{1,0:T(8,128)S(1)}, f32[240,384]{1,0:T(8,128)}, u32[]{:S(2)}) copy-start(f32[240,384]{1,0:T(8,128)} %add.70.refs_0_) | copy-start | bytes 1105924
  130.9 2.6 %copy-start.6 = (f32[384,512]{1,0:T(8,128)S(1)}, f32[384,512]{1,0:T(8,128)}, u32[]{:S(2)}) copy-start(f32[384,512]{1,0:T(8,128)} %refs_9_.1) | copy-start | bytes 2359300
  131.0 2.6 %copy-start.7 = (s32[48,1]{1,0:T(8,128)S(1)}, s32[48,1]{1,0:T(8,128)}, u32[]{:S(2)}) copy-start(s32[48,1]{1,0:T(8,128)} %copy.21.picks_ref.refs_8_) | copy-start | bytes 580

commit v3 on v0

v3 whole, which is shorter than its diff:
```python
import functools

import jax
import jax.numpy as jnp
from jax import lax
from jax.experimental import pallas as pl
from jax.experimental.pallas import tpu as pltpu
from jax.sharding import PartitionSpec as P

F = 24576
VMEM = pl.BlockSpec(memory_space=pltpu.VMEM)
SMEM = pl.BlockSpec(memory_space=pltpu.SMEM)
PARAMS = pltpu.CompilerParams(vmem_limit_bytes=24 * 1024 * 1024)


def quadratic(gram):
    scaled = gram * (1.0 / F)
    return scaled + scaled * scaled


def dot_rows(left, right):
    return lax.dot_general(
        left, right, (((1,), (1,)), ((), ())), preferred_element_type=jnp.float32
    )


def exact_dot(left, right):
    return jnp.dot(
        left, right, precision=lax.Precision.HIGHEST, preferred_element_type=jnp.float32
    )


def split(array):
    high = array.astype(jnp.bfloat16)
    return high, (array - high.astype(jnp.float32)).astype(jnp.bfloat16)


def fine_dot(left, right, contract=1):
    sides = (((contract,), (0,)), ((), ()))
    left_high, left_low = left if isinstance(left, tuple) else split(left)
    right_high, right_low = right if isinstance(right, tuple) else split(right)

    def part(one, other):
        return lax.dot_general(one, other, sides, preferred_element_type=jnp.float32)

    return part(left_high, right_high) + (part(left_high, right_low) + part(left_low, right_high))


def pairs_of(steps):
    return [(step, before) for step in range(steps) for before in range(step)]


def of_step(slots, step, per):
    return jnp.concatenate([slot[step * per : (step + 1) * per] for slot in slots], axis=0)


def by_step(array, steps, per):
    parts = array.reshape(-1, steps, per, array.shape[-1])
    return jnp.swapaxes(parts, 0, 1).reshape(steps, -1, array.shape[-1])


def cost(rows, columns):
    return pl.CostEstimate(flops=2 * rows * columns, bytes_accessed=4 * rows, transcendentals=0)


def finish_kernel(steps, per, grams, last, *refs):
    refs = list(refs)
    gram = [refs.pop(0)[...] + refs.pop(0)[...] for _ in range(grams)]
    if last:
        end = refs.pop(0)[...] + refs.pop(0)[...]
    else:
        cross = refs.pop(0)
    same_ref, first_ref, inverse_ref, own_ref, targets_ref, resid_ref, coeff_ref = refs
    block = first_ref.shape[1]
    rows = targets_ref.shape[0]
    if last:
        cross = gram[1][-block:]
        gram[1] = gram[1][:-block]
        gram.append(end[:, :rows])
        end = end[:, rows:]
        column = lax.broadcasted_iota(jnp.int32, (block, block), 0) < block - per

        def of(one, other):
            part = end[one * per : (one + 1) * per, other * block : (other + 1) * block]
            return jnp.concatenate([jnp.zeros((block - per, block), jnp.float32), part], axis=0)

    between = {}
    for at, (step, before) in enumerate(pairs_of(steps)):
        part = cross[:, at * block : (at + 1) * block]
        if last:
            part = part + of(step, before) + jnp.where(column, of(before, step).T, 0.0)
        between[step, before] = split(quadratic(part) + same_ref[:, at * block : (at + 1) * block])
    deltas = []
    for step in range(steps):
        delta = first_ref[step]
        if step:
            change = fine_dot(between[step, 0], deltas[0])
            for before in range(1, step):
                change += fine_dot(between[step, before], deltas[before])
            delta = delta - fine_dot(inverse_ref[step], change)
        deltas.append(delta if step + 1 == steps else split(delta))
    deltas[-1] = split(deltas[-1])
    kernel = jnp.concatenate([quadratic(part) for part in gram], axis=0)
    kernel = kernel.reshape(-1, steps, per, rows)
    spread = own_ref[...] == lax.broadcasted_iota(jnp.int32, (steps * per, rows), 1)
    spread = spread.astype(jnp.float32).astype(jnp.bfloat16)
    sides = (((0,), (0,)), ((), ()))
    coeffs = jnp.zeros(targets_ref.shape, jnp.float32)
    resid = targets_ref[...]
    for high_or_low in (0, 1):
        own = jnp.concatenate([delta[high_or_low][:per] for delta in deltas], axis=0)
        coeffs += lax.dot_general(spread, own, sides, preferred_element_type=jnp.float32)
    coeff_ref[...] = coeffs
    for step in range(steps):
        resid = resid - fine_dot(kernel[:, step].reshape(block, rows), deltas[step], 0)
    resid_ref[...] = resid - coeffs


def first_kernel(steps, flag_ref, mine_ref, other_ref, inverse_ref, out_ref):
    core = flag_ref[0]
    block = inverse_ref.shape[1]
    half = mine_ref.shape[1]
    for step in range(steps):
        rows = slice(step * block, (step + 1) * block)
        inverse = split(inverse_ref[step])
        mine, other = mine_ref[rows], other_ref[rows]
        left = jnp.where(core == 0, mine, other)
        right = jnp.where(core == 0, other, mine)
        out_ref[step, :, :half] = fine_dot(inverse, left)
        out_ref[step, :, half:] = fine_dot(inverse, right)


def pick_kernel(per, low, index_ref, place_ref, features_ref, targets_ref, out_ref):
    rank, core = place_ref[0], place_ref[1]
    rows, half = features_ref.shape
    steps = index_ref.shape[0]
    line = lax.broadcasted_iota(jnp.int32, (steps * per, rows), 0)
    wanted = jnp.zeros((steps * per, rows), jnp.int32)
    for step in range(steps):
        for i in range(per):
            wanted = jnp.where(line == step * per + i, index_ref[step, rank * per + i], wanted)
    chosen = wanted - rank * rows == lax.broadcasted_iota(jnp.int32, wanted.shape, 1)
    chosen = chosen.astype(jnp.float32).astype(jnp.bfloat16)

    def take(array):
        return jnp.dot(chosen, array, preferred_element_type=jnp.float32).astype(jnp.bfloat16)

    out_ref[:, :half] = take(features_ref[...])
    width = targets_ref.shape[1] // 2
    values = jnp.where(core == 0, targets_ref[:, :width], targets_ref[:, width:])
    out_ref[:, half:] = take(split(values)[low])


def pick(block_index, place, features, targets, per, side):
    rows, columns = features.shape
    half = columns // 2
    count = block_index.shape[0] * per
    wide = half + targets.shape[1] // 2
    return pl.pallas_call(
        functools.partial(pick_kernel, per, side),
        grid=(1,),
        out_shape=jax.ShapeDtypeStruct((count, wide), features.dtype),
        in_specs=[
            SMEM,
            SMEM,
            pl.BlockSpec((rows, half), lambda i: (0, side)),
            pl.BlockSpec(targets.shape, lambda i: (0, 0)),
        ],
        out_specs=pl.BlockSpec((count, wide), lambda i: (0, 0)),
        compiler_params=PARAMS,
        cost_estimate=cost(count * rows, wide),
    )(block_index, place, features, targets)


def halves(features_ref):
    half = features_ref.shape[1] // 2
    return [(0, slice(0, half), slice(0, half)), (1, slice(0, half), slice(half, 2 * half))]


def gram_kernel(*refs):
    *slot_refs, features_ref, out_ref = refs
    total = None
    for side, at, there in halves(features_ref):
        slots = jnp.concatenate([ref[:, at] for ref in slot_refs[side::2]], axis=0)
        part = dot_rows(slots, features_ref[:, there])
        total = part if total is None else total + part
    out_ref[...] = total


def cross_kernel(steps, per, count, place_ref, *refs):
    *slot_refs, features_ref, out_ref = refs
    inner = place_ref[2] == 1
    total = [None] * (1 + len(pairs_of(steps)))
    for side, at, there in halves(features_ref):
        slots = [ref[:, at] for ref in slot_refs[side::2]]
        other = slots.pop()
        slots[-1] = jnp.where(inner, slots[-1], other)
        parts = [dot_rows(jnp.concatenate(slots[count:], axis=0), features_ref[:, there])]
        slots.append(jnp.zeros_like(other))
        rows = [of_step(slots, step, per) for step in range(steps)]
        parts += [dot_rows(rows[step], rows[before]) for step, before in pairs_of(steps)]
        total = [part if sum_ is None else sum_ + part for sum_, part in zip(total, parts)]
    new = total[0].shape[0]
    out_ref[:new] = total[0]
    out_ref[new:] = jnp.concatenate(total[1:], axis=1)


def last_kernel(steps, per, place_ref, *refs):
    *slot_refs, features_ref, out_ref, first_ref = refs
    inner = place_ref[2] == 1
    total, cross, first = None, None, 0.0
    for side, at, there in halves(features_ref):
        refs = slot_refs[side::2]
        for at in (at, slice(at.stop, refs[0].shape[1])):
            slots = [ref[:, at] for ref in refs]
            last, last_inner = slots.pop(), slots.pop()
            other = slots.pop()
            slots[-1] = jnp.where(inner, slots[-1], other)
            last = jnp.where(inner, last_inner, last)
            every = [of_step(slots + [last], step, per) for step in range(steps)]
            every = jnp.concatenate(every, axis=0)
            if at.start:
                first = first + every.astype(jnp.float32)
            else:
                part, near = dot_rows(features_ref[:, there], last), dot_rows(every, last)
                total = part if total is None else total + part
                cross = near if cross is None else cross + near
    wide = features_ref.shape[0]
    out_ref[:, :wide] = total.T
    out_ref[:, wide:] = cross.T
    first_ref[...] = first


class Lines:
    def __init__(self):
        self.beside = [(r, r ^ 1) for r in range(8)]
        self.pair = [(r, r ^ 2) for r in range(8)]
        self.inner = [(r, r ^ 6) for r in range(2, 6)]
        self.outer = [(2, 0), (3, 1), (4, 6), (5, 7)]
        self.ends = [(r, r ^ 1) for r in (0, 1, 6, 7)]
        rank = lax.axis_index("rows")
        core = lax.axis_index("feat") % 2
        self.is_inner = (rank >= 2) & (rank < 6)
        self.order = rank ^ jnp.arange(8)
        self.place = jnp.stack([rank, core, self.is_inner.astype(jnp.int32)])

    def near(self, array, bit):
        return lax.ppermute(array, "feat", [(f, f ^ bit) for f in range(4)])

    def send(self, arrays, pairs):
        return [lax.ppermute(array, "rows", pairs) for array in arrays]

    def run(self, features, targets, block_index, turned, per):
        rows, columns = features.shape
        steps, block = block_index.shape
        count = steps * per
        hold = lax.optimization_barrier
        own = [pick(block_index, self.place, features, targets, per, side) for side in range(2)]

        pair = self.send(own, self.pair)
        mid = self.send(own, self.inner)
        own_b = self.send(own, self.beside)
        for side in range(2):
            pair[side], mid[side], own_b[side] = hold((pair[side], mid[side], own_b[side]))

        far = self.send(pair, self.inner)
        mid_end = self.send(mid, self.outer)
        pair_b = self.send(pair, self.beside)
        for side in range(2):
            far[side], mid_end[side], pair_b[side] = hold((far[side], mid_end[side], pair_b[side]))

        third = [jnp.where(self.is_inner, far[side], mid_end[side]) for side in range(2)]
        third_b = self.send(third, self.beside)
        far_end = self.send(far, self.outer)
        last_in = self.send(own_b, self.inner)
        slots = own + own_b + pair + pair_b + third
        gram = pl.pallas_call(
            gram_kernel,
            out_shape=jax.ShapeDtypeStruct((5 * count, rows), jnp.float32),
            in_specs=[VMEM] * (len(slots) + 1),
            out_specs=VMEM,
            compiler_params=PARAMS,
            cost_estimate=cost(5 * count * rows, columns),
        )(*slots, features)
        gram = gram + self.near(gram, 1)
        third_b[0], far_end[0], last_in[0] = hold((third_b[0], far_end[0], last_in[0]))
        third_b[1], far_end[1], last_in[1], gram = hold((third_b[1], far_end[1], last_in[1], gram))

        ends = self.send(far_end[:1], self.ends) + self.send(third_b[1:], self.outer)
        gram_near = self.near(gram, 2)
        slots = slots + third_b + mid + far_end
        second = pl.pallas_call(
            functools.partial(cross_kernel, steps, per, 5),
            out_shape=jax.ShapeDtypeStruct((2 * count + block, rows), jnp.float32),
            in_specs=[SMEM] + [VMEM] * (len(slots) + 1),
            out_specs=VMEM,
            compiler_params=PARAMS,
            cost_estimate=cost((2 * count + block) * rows, columns),
        )(self.place, *slots, features)
        second = second + self.near(second, 1)
        ends[0], ends[1], gram_near, second = hold((ends[0], ends[1], gram_near, second))

        second_near = self.near(second, 2)
        slots = slots + last_in + ends
        last, first = pl.pallas_call(
            functools.partial(last_kernel, steps, per),
            out_shape=(
                jax.ShapeDtypeStruct((count, rows + steps * block), jnp.float32),
                jax.ShapeDtypeStruct((steps * block, targets.shape[1] // 2), jnp.float32),
            ),
            in_specs=[SMEM] + [VMEM] * (len(slots) + 1),
            out_specs=(VMEM, VMEM),
            compiler_params=PARAMS,
            cost_estimate=cost(count * (rows + steps * block), columns),
        )(self.place, *slots, features)
        last, second_near = hold((last, second_near))
        last = last + self.near(last, 1)
        last_near = self.near(last, 2)
        first = pl.pallas_call(
            functools.partial(first_kernel, steps),
            out_shape=jax.ShapeDtypeStruct((steps, block, targets.shape[1]), jnp.float32),
            in_specs=[SMEM] + [VMEM] * 3,
            out_specs=VMEM,
            compiler_params=PARAMS,
            cost_estimate=cost(3 * steps * block * block, targets.shape[1]),
        )(self.place[1:2], first, self.near(first, 1), turned)
        return 2, [gram, gram_near, second, second_near, last, last_near], first


class Gathers:
    def __init__(self):
        size = lax.axis_size("rows")
        self.order = (lax.axis_index("rows") + jnp.arange(size)) % size

    def turn(self, own):
        every = lax.all_gather(own, "rows", axis=0, tiled=True)
        start = lax.axis_index("rows") * own.shape[0]
        return lax.dynamic_slice_in_dim(
            jnp.concatenate([every, every], axis=0), start, every.shape[0], 0
        )

    def run(self, features, targets, block_index, turned, per):
        steps = block_index.shape[0]
        rank = lax.axis_index("rows")
        picks = lax.dynamic_slice_in_dim(block_index, rank * per, per, 1).reshape(-1)
        picks = picks - rank * features.shape[0]
        every = self.turn(jnp.take(features, picks, axis=0))
        width = targets.shape[1] // lax.axis_size("feat")
        start = lax.axis_index("feat") * width
        share = jnp.take(lax.dynamic_slice_in_dim(targets, start, width, 1), picks, axis=0)
        share = lax.all_gather(self.turn(share), "feat", axis=1, tiled=True)
        blocks = by_step(every, steps, per)
        cross = jnp.concatenate(
            [dot_rows(blocks[step], blocks[before]) for step, before in pairs_of(steps)], axis=1
        )
        gram, cross = lax.psum((dot_rows(every, features), cross), "feat")
        first = lax.dot_general(
            turned,
            by_step(share, steps, per),
            (((2,), (1,)), ((0,), (0,))),
            precision=lax.Precision.HIGHEST,
            preferred_element_type=jnp.float32,
        )
        return 1, [gram, jnp.zeros_like(gram), cross], first


def local(features, targets, block_index, inverse):
    rank = lax.axis_index("rows")
    row_count = lax.axis_size("rows")
    rows = features.shape[0]
    steps, block = block_index.shape
    per = block // row_count
    mover = Lines() if (row_count, lax.axis_size("feat")) == (8, 4) else Gathers()

    place = jnp.arange(block)
    moved = jnp.repeat(mover.order, per) * per + place % per
    swap = moved[:, None] == place[None, :]
    picks = jnp.sum(jnp.where(swap[None], block_index[:, None, :], 0), axis=2)
    swap = swap.astype(jnp.float32)
    turned = jnp.stack([exact_dot(exact_dot(swap, inverse[step]), swap.T) for step in range(steps)])
    same = jnp.concatenate(
        [
            (picks[step][:, None] == picks[before][None, :]).astype(jnp.float32)
            for step, before in pairs_of(steps)
        ],
        axis=1,
    )
    own = picks[:, :per].reshape(-1, 1) - rank * rows

    grams, sums, first = mover.run(features, targets, block_index, turned, per)
    operands = sums + [same, first, turned, own, targets]
    out = jax.ShapeDtypeStruct(targets.shape, jnp.float32)
    return pl.pallas_call(
        functools.partial(finish_kernel, steps, per, grams, len(sums) == 6),
        out_shape=(out, out),
        in_specs=[VMEM] * len(operands),
        out_specs=(VMEM, VMEM),
        compiler_params=PARAMS,
        cost_estimate=cost(3 * rows * steps * block, targets.shape[1]),
    )(*operands)


def solution(mesh):
    return jax.shard_map(
        local,
        mesh=mesh,
        in_specs=(P("rows", "feat"), P("rows", None), P(), P()),
        out_specs=(P("rows", None), P("rows", None)),
        check_vma=False,
    )
```

time: 217 us -> 111 us (0.51)
  blocking collectives: 95 us -> 0 us
  waiting for transfers between devices: 80.5 us -> 31.8 us
  starting transfers between devices: 0.08 us -> 33.6 us
  Pallas kernels: 0 us -> 17.9 us
  local copies, waits for them, and re-layouts: 7.23 us -> 20.8 us
  between operations: 14.3 us -> 1.12 us
  matrix products: 10.9 us -> 2.36 us
  other arithmetic: 9.12 us -> 2.43 us
    all_gather x3 -> x0, blocking collectives: 95 us -> none  [local(): block_resid = lax.all_gather(own_resid, 'rows', axis=0, tiled=True)]
    all_gather x1 -> x0, waiting for transfers between devices: 49.7 us -> none  [local(): lax.all_gather(every_picked, 'rows', axis=0, tiled=True)]
    ppermute x0 -> x27, starting transfers between devices: none -> 33.6 us  [the longest x20 30.7 us: send(): return [lax.ppermute(array, 'rows', pairs) for array in arrays]]
    ppermute x0 -> x27, waiting for transfers between devices: none -> 31.8 us  [the longest x20 24.5 us: send(): return [lax.ppermute(array, 'rows', pairs) for array in arrays]]
    psum x1 -> x0, waiting for transfers between devices: 30.8 us -> none  [local(): every_gram = lax.psum(every_part, 'feat')]
    unnamed x8 -> x64, local copies, waits for them, and re-layouts: 0.89 us -> 20.5 us
    pallas_call x0 -> x7, Pallas kernels: none -> 17.9 us  [the longest x1 4.75 us: run(): pl.pallas_call(functools.partial(last_kernel, steps, per), out_shape=(jax...]
    dot_general x7 -> x6, matrix products: 10.9 us -> 2.36 us  [exact_dot(): jnp.dot(left, right, precision=lax.Precision.HIGHEST, preferred_element_t...]
  transfers between devices with their start and end apart: 2 -> 27, of which waited for: 2 -> 9; matrix products, arithmetic and copies ran while one was open for 1% -> 5% of each run, Pallas kernels for 0% -> 12%
where the time goes in v3:
time: 111 us; the launch traced here: 110 us
  starting transfers between devices  33.6 us (30%)
  waiting for transfers between devices  31.8 us (29%)
  local copies, waits for them, and re-layouts  20.8 us (19%)
  Pallas kernels  17.9 us (16%)
  other arithmetic  2.43 us (2%)
  matrix products  2.36 us (2%)
  between operations  1.12 us (1%)
    ppermute x20, starting transfers between devices, send(): return [lax.ppermute(array, 'rows', pairs) for array in arrays]  30.7 us
    ppermute x20, waiting for transfers between devices, send(): return [lax.ppermute(array, 'rows', pairs) for array in arrays]  24.5 us
    unnamed x64, local copies, waits for them, and re-layouts  20.5 us
    ppermute x7, waiting for transfers between devices, near(): return lax.ppermute(array, 'feat', [(f, f ^ bit) for f in range(4)])  7.33 us
    pallas_call x1, Pallas kernels, run(): pl.pallas_call(functools.partial(last_kernel, steps, per), out_shape=(jax...  4.75 us
    pallas_call x1, Pallas kernels, run(): pl.pallas_call(functools.partial(cross_kernel, steps, per, 5), out_shape=...  3.86 us
    pallas_call x1, Pallas kernels, local(): pl.pallas_call(functools.partial(finish_kernel, steps, per, grams, len(su...  3.13 us
    ppermute x7, starting transfers between devices, near(): return lax.ppermute(array, 'feat', [(f, f ^ bit) for f in range(4)])  2.88 us
  transfers between devices with their start and end apart: 27, of which 9 were waited for; matrix products, arithmetic and copies ran while one was open for 5% of the time, Pallas kernels for 12%

profile of v3, /device:TPU:0, one launch (start us, length us, event | category | flops | bytes accessed | tf_op | source)
XLA Modules:
  0.0 110.0 jit_solution(2150446499366560622)
XLA Ops:
  0.7 2.3 %copy-done = bf16[384,6144]{1,0:T(8,128)(2,1)S(1)} copy-done((bf16[384,6144]{1,0:T(8,128)(2,1)S(1)}, bf16[384,6144]{1,0:T(8,128)(2,1)}, u32[]{:S(2)}) %copy-start) | copy-done | bytes 4718616
  3.1 1.1 %copy-done.3 = f32[384,512]{1,0:T(8,128)S(1)} copy-done((f32[384,512]{1,0:T(8,128)S(1)}, f32[384,512]{1,0:T(8,128)}, u32[]{:S(2)}) %copy-start.3) | copy-done | bytes 786456
  4.9 1.1 %shard_map.59.refs_1_ = bf16[48,3328]{1,0:T(8,128)(2,1)S(1)} custom-call(s32[3,128]{1,0:T(4,128)S(1)} %copy-done.26, s32[3]{0:T(128)S(1)} %pad_add_fusion.place_ref, bf16[384,6144]{1,0:T(8,128)(2,1)S(1)} %copy-done, f32[384,512]{1,0:T(8,128)S(1)} %copy-done.3), custom_call_target="tpu_custom_call" | custom-call | flops 122683392 | bytes 73728 | tf_op jit(solution)/shard_map/pallas_call | solution.py:159
  6.0 3.1 %collective-permute-start = (bf16[48,3328]{1,0:T(8,128)(2,1)S(1)}, bf16[48,3328]{1,0:T(8,128)(2,1)S(1)}, u32[]{:S(2)}, u32[]{:S(2)}) collective-permute-start(bf16[48,3328]{1,0:T(8,128)(2,1)S(1)} %shard_map.59.refs_1_), channel_id=1, source_target_pairs={{0,8},{4,12},{8,0},{12,4},{16,24},{20,28},{24,16},{28,20},{1,9},{5... | collective-permute-start | bytes 958472 | tf_op jit(solution)/shard_map/ppermute | solution.py:251
  9.8 1.6 %collective-permute-start.2 = (bf16[48,3328]{1,0:T(8,128)(2,1)S(1)}, bf16[48,3328]{1,0:T(8,128)(2,1)S(1)}, u32[]{:S(2)}, u32[]{:S(2)}) collective-permute-start(bf16[48,3328]{1,0:T(8,128)(2,1)S(1)} %shard_map.59.refs_1_), channel_id=1, source_target_pairs={{0,4},{4,0},{8,12},{12,8},{16,20},{20,16},{24,28},{28,24},{1,5},{5... | collective-permute-start | bytes 958472 | tf_op jit(solution)/shard_map/ppermute | solution.py:251
  11.4 1.1 %shard_map.60.refs_0_ = bf16[48,3328]{1,0:T(8,128)(2,1)S(1)} custom-call(s32[3,128]{1,0:T(4,128)S(1)} %copy-done.26, s32[3]{0:T(128)S(1)} %pad_add_fusion.place_ref, bf16[384,6144]{1,0:T(8,128)(2,1)S(1)} %copy-done, f32[384,512]{1,0:T(8,128)S(1)} %copy-done.3), custom_call_target="tpu_custom_call" | custom-call | flops 122683392 | bytes 73728 | tf_op jit(solution)/shard_map/pallas_call | solution.py:159
  12.5 4.4 %collective-permute-start.9 = (bf16[48,3328]{1,0:T(8,128)(2,1)S(1)}, bf16[48,3328]{1,0:T(8,128)(2,1)S(1)}, u32[]{:S(2)}, u32[]{:S(2)}) collective-permute-start(bf16[48,3328]{1,0:T(8,128)(2,1)S(1)} %shard_map.60.refs_0_), channel_id=1, source_target_pairs={{0,8},{4,12},{8,0},{12,4},{16,24},{20,28},{24,16},{28,20},{1,9},{5... | collective-permute-start | bytes 958472 | tf_op jit(solution)/shard_map/ppermute | solution.py:251
  17.8 1.5 %collective-permute-start.11 = (bf16[48,3328]{1,0:T(8,128)(2,1)S(1)}, bf16[48,3328]{1,0:T(8,128)(2,1)S(1)}, u32[]{:S(2)}, u32[]{:S(2)}) collective-permute-start(bf16[48,3328]{1,0:T(8,128)(2,1)S(1)} %shard_map.60.refs_0_), channel_id=1, source_target_pairs={{0,4},{4,0},{8,12},{12,8},{16,20},{20,16},{24,28},{28,24},{1,5},{5... | collective-permute-start | bytes 958472 | tf_op jit(solution)/shard_map/ppermute | solution.py:251
  19.3 1.4 %collective-permute-start.3 = (bf16[48,3328]{1,0:T(8,128)(2,1)S(1)}, bf16[48,3328]{1,0:T(8,128)(2,1)}, u32[]{:S(2)}, u32[]{:S(2)}) collective-permute-start(bf16[48,3328]{1,0:T(8,128)(2,1)S(1)} %collective-permute-done.refs_5_), channel_id=1, source_target_pairs={{8,16},{12,20},{16,8},{20,12},{9,17},{13,21},{17,9},{21,13},{10,18... | collective-permute-start | bytes 958472 | tf_op jit(solution)/shard_map/ppermute | solution.py:251
  20.8 1.6 %collective-permute-start.5 = (bf16[48,3328]{1,0:T(8,128)(2,1)S(1)}, bf16[48,3328]{1,0:T(8,128)(2,1)S(1)}, u32[]{:S(2)}, u32[]{:S(2)}) collective-permute-start(bf16[48,3328]{1,0:T(8,128)(2,1)S(1)} %collective-permute-done.refs_5_), channel_id=1, source_target_pairs={{0,4},{4,0},{8,12},{12,8},{16,20},{20,16},{24,28},{28,24},{1,5},{5... | collective-permute-start | bytes 958472 | tf_op jit(solution)/shard_map/ppermute | solution.py:251
  22.3 1.3 %collective-permute-done.9.refs_4_ = bf16[48,3328]{1,0:T(8,128)(2,1)S(1)} collective-permute-done((bf16[48,3328]{1,0:T(8,128)(2,1)S(1)}, bf16[48,3328]{1,0:T(8,128)(2,1)S(1)}, u32[]{:S(2)}, u32[]{:S(2)}) %collective-permute-start.9) | collective-permute-done | bytes 319520 | tf_op jit(solution)/shard_map/ppermute | solution.py:251
  23.6 4.7 %collective-permute-done.11.refs_2_ = bf16[48,3328]{1,0:T(8,128)(2,1)S(1)} collective-permute-done((bf16[48,3328]{1,0:T(8,128)(2,1)S(1)}, bf16[48,3328]{1,0:T(8,128)(2,1)S(1)}, u32[]{:S(2)}, u32[]{:S(2)}) %collective-permute-start.11) | collective-permute-done | bytes 319520 | tf_op jit(solution)/shard_map/ppermute | solution.py:251
  28.3 1.4 %collective-permute-start.12 = (bf16[48,3328]{1,0:T(8,128)(2,1)S(1)}, bf16[48,3328]{1,0:T(8,128)(2,1)}, u32[]{:S(2)}, u32[]{:S(2)}) collective-permute-start(bf16[48,3328]{1,0:T(8,128)(2,1)S(1)} %collective-permute-done.9.refs_4_), channel_id=1, source_target_pairs={{8,16},{12,20},{16,8},{20,12},{9,17},{13,21},{17,9},{21,13},{10,18... | collective-permute-start | bytes 958472 | tf_op jit(solution)/shard_map/ppermute | solution.py:251
  29.7 1.4 %collective-permute-start.14 = (bf16[48,3328]{1,0:T(8,128)(2,1)S(1)}, bf16[48,3328]{1,0:T(8,128)(2,1)S(1)}, u32[]{:S(2)}, u32[]{:S(2)}) collective-permute-start(bf16[48,3328]{1,0:T(8,128)(2,1)S(1)} %collective-permute-done.9.refs_4_), channel_id=1, source_target_pairs={{0,4},{4,0},{8,12},{12,8},{16,20},{20,16},{24,28},{28,24},{1,5},{5... | collective-permute-start | bytes 958472 | tf_op jit(solution)/shard_map/ppermute | solution.py:251
  31.1 1.3 %collective-permute-start.4 = (bf16[48,3328]{1,0:T(8,128)(2,1)S(1)}, bf16[48,3328]{1,0:T(8,128)(2,1)S(1)}, u32[]{:S(2)}, u32[]{:S(2)}) collective-permute-start(bf16[48,3328]{1,0:T(8,128)(2,1)S(1)} %collective-permute-done.1.refs_13_), channel_id=1, source_target_pairs={{8,0},{12,4},{16,24},{20,28},{9,1},{13,5},{17,25},{21,29},{10,2},{... | collective-permute-start | bytes 958472 | tf_op jit(solution)/shard_map/ppermute | solution.py:251
  33.1 1.3 %collective-permute-start.13 = (bf16[48,3328]{1,0:T(8,128)(2,1)S(1)}, bf16[48,3328]{1,0:T(8,128)(2,1)S(1)}, u32[]{:S(2)}, u32[]{:S(2)}) collective-permute-start(bf16[48,3328]{1,0:T(8,128)(2,1)S(1)} %collective-permute-done.10.refs_12_), channel_id=1, source_target_pairs={{8,0},{12,4},{16,24},{20,28},{9,1},{13,5},{17,25},{21,29},{10,2},{... | collective-permute-start | bytes 958472 | tf_op jit(solution)/shard_map/ppermute | solution.py:251
  35.3 8.7 %collective-permute-done.4 = bf16[48,3328]{1,0:T(8,128)(2,1)S(1)} collective-permute-done((bf16[48,3328]{1,0:T(8,128)(2,1)S(1)}, bf16[48,3328]{1,0:T(8,128)(2,1)S(1)}, u32[]{:S(2)}, u32[]{:S(2)}) %collective-permute-start.4) | collective-permute-done | bytes 319520 | tf_op jit(solution)/shard_map/ppermute | solution.py:251
  44.0 1.4 %collective-permute-start.8 = (bf16[48,3328]{1,0:T(8,128)(2,1)S(1)}, bf16[48,3328]{1,0:T(8,128)(2,1)}, u32[]{:S(2)}, u32[]{:S(2)}) collective-permute-start(bf16[48,3328]{1,0:T(8,128)(2,1)S(1)} %collective-permute-done.2.refs_3_), channel_id=1, source_target_pairs={{8,16},{12,20},{16,8},{20,12},{9,17},{13,21},{17,9},{21,13},{10,18... | collective-permute-start | bytes 958472 | tf_op jit(solution)/shard_map/ppermute | solution.py:251
  46.1 1.3 %collective-permute-start.7 = (bf16[48,3328]{1,0:T(8,128)(2,1)}, bf16[48,3328]{1,0:T(8,128)(2,1)}, u32[]{:S(2)}, u32[]{:S(2)}) collective-permute-start(bf16[48,3328]{1,0:T(8,128)(2,1)} %collective-permute-done.3), channel_id=1, source_target_pairs={{8,0},{12,4},{16,24},{20,28},{9,1},{13,5},{17,25},{21,29},{10,2},{... | collective-permute-start | bytes 958472 | tf_op jit(solution)/shard_map/ppermute | solution.py:251
  47.4 2.9 %collective-permute-done.13 = bf16[48,3328]{1,0:T(8,128)(2,1)S(1)} collective-permute-done((bf16[48,3328]{1,0:T(8,128)(2,1)S(1)}, bf16[48,3328]{1,0:T(8,128)(2,1)S(1)}, u32[]{:S(2)}, u32[]{:S(2)}) %collective-permute-start.13) | collective-permute-done | bytes 319520 | tf_op jit(solution)/shard_map/ppermute | solution.py:251
  50.7 1.9 %collective-permute-start.6 = (bf16[48,3328]{1,0:T(8,128)(2,1)S(1)}, bf16[48,3328]{1,0:T(8,128)(2,1)}, u32[]{:S(2)}, u32[]{:S(2)}) collective-permute-start(bf16[48,3328]{1,0:T(8,128)(2,1)S(1)} %broadcast_select_fusion.1.refs_9_), channel_id=1, source_target_pairs={{0,4},{4,0},{8,12},{12,8},{16,20},{20,16},{24,28},{28,24},{1,5},{5... | collective-permute-start | bytes 958472 | tf_op jit(solution)/shard_map/ppermute | solution.py:251
  52.6 2.3 %copy-done.1 = bf16[384,6144]{1,0:T(8,128)(2,1)S(1)} copy-done((bf16[384,6144]{1,0:T(8,128)(2,1)S(1)}, bf16[384,6144]{1,0:T(8,128)(2,1)}, u32[]{:S(2)}) %copy-start.1) | copy-done | bytes 4718616
  54.9 2.5 %shard_map.61 = f32[240,384]{1,0:T(8,128)} custom-call(bf16[48,3328]{1,0:T(8,128)(2,1)S(1)} %shard_map.60.refs_0_, bf16[48,3328]{1,0:T(8,128)(2,1)S(1)} %shard_map.59.refs_1_, bf16[48,3328]{1,0:T(8,128)(2,1)S(1)} %collective-permute-done.11.refs_2_, bf16[48,3328]{1,0:T(8,128)(2,1)S(1)} %collective-permute-done.2.refs_3_, ...), custom_call_target="tpu_custom_call" | custom-call | flops 1132462080 | bytes 368640 | tf_op jit(solution)/shard_map/pallas_call | solution.py:277
  58.2 1.3 %collective-permute-start.17 = (bf16[48,3328]{1,0:T(8,128)(2,1)}, bf16[48,3328]{1,0:T(8,128)(2,1)}, u32[]{:S(2)}, u32[]{:S(2)}) collective-permute-start(bf16[48,3328]{1,0:T(8,128)(2,1)} %collective-permute-done.12), channel_id=1, source_target_pairs={{8,0},{12,4},{16,24},{20,28},{9,1},{13,5},{17,25},{21,29},{10,2},{... | collective-permute-start | bytes 958472 | tf_op jit(solution)/shard_map/ppermute | solution.py:251
  61.1 6.8 %collective-permute-done.17.refs_14_ = bf16[48,3328]{1,0:T(8,128)(2,1)} collective-permute-done((bf16[48,3328]{1,0:T(8,128)(2,1)}, bf16[48,3328]{1,0:T(8,128)(2,1)}, u32[]{:S(2)}, u32[]{:S(2)}) %collective-permute-start.17) | collective-permute-done | bytes 319520 | tf_op jit(solution)/shard_map/ppermute | solution.py:251
  67.9 2.4 %collective-permute-start.19 = (bf16[48,3328]{1,0:T(8,128)(2,1)}, bf16[48,3328]{1,0:T(8,128)(2,1)S(1)}, u32[]{:S(2)}, u32[]{:S(2)}) collective-permute-start(bf16[48,3328]{1,0:T(8,128)(2,1)} %collective-permute-done.17.refs_14_), channel_id=1, source_target_pairs={{0,4},{4,0},{24,28},{28,24},{1,5},{5,1},{25,29},{29,25},{2,6},{6,2... | collective-permute-start | bytes 958472 | tf_op jit(solution)/shard_map/ppermute | solution.py:251
  70.3 1.2 %add.31.refs_0_ = f32[240,384]{1,0:T(8,128)S(1)} add(f32[240,384]{1,0:T(8,128)} %shard_map.61, f32[240,384]{1,0:T(8,128)} %collective-permute-done.15) | non-fusion elementwise | flops 92160 | bytes 1105920 | tf_op jit(solution)/shard_map/add | solution.py:285
  71.6 1.3 %collective-permute-start.20 = (bf16[48,3328]{1,0:T(8,128)(2,1)}, bf16[48,3328]{1,0:T(8,128)(2,1)S(1)}, u32[]{:S(2)}, u32[]{:S(2)}) collective-permute-start(bf16[48,3328]{1,0:T(8,128)(2,1)} %collective-permute-done.6.refs_11_), channel_id=1, source_target_pairs={{8,0},{12,4},{16,24},{20,28},{9,1},{13,5},{17,25},{21,29},{10,2},{... | collective-permute-start | bytes 958472 | tf_op jit(solution)/shard_map/ppermute | solution.py:251
  72.9 1.6 %collective-permute-start.21 = (f32[240,384]{1,0:T(8,128)S(1)}, f32[240,384]{1,0:T(8,128)S(1)}, u32[]{:S(2)}, u32[]{:S(2)}) collective-permute-start(f32[240,384]{1,0:T(8,128)S(1)} %add.31.refs_0_), channel_id=1, source_target_pairs={{0,2},{1,3},{2,0},{3,1},{4,6},{5,7},{6,4},{7,5},{8,10},{9,11},{10,... | collective-permute-start | bytes 1105928 | tf_op jit(solution)/shard_map/ppermute | solution.py:248
  74.4 2.3 %copy-done.2 = bf16[384,6144]{1,0:T(8,128)(2,1)S(1)} copy-done((bf16[384,6144]{1,0:T(8,128)(2,1)S(1)}, bf16[384,6144]{1,0:T(8,128)(2,1)}, u32[]{:S(2)}) %copy-start.2) | copy-done | bytes 4718616
  76.8 1.0 copy-done.14
  77.7 1.0 copy-done.16
  78.7 1.0 copy-done.18
  79.7 3.9 %shard_map.62 = f32[224,384]{1,0:T(8,128)S(1)} custom-call(s32[3]{0:T(128)S(1)} %pad_add_fusion.place_ref, bf16[48,3328]{1,0:T(8,128)(2,1)S(1)} %shard_map.60.refs_0_, bf16[48,3328]{1,0:T(8,128)(2,1)S(1)} %shard_map.59.refs_1_, bf16[48,3328]{1,0:T(8,128)(2,1)S(1)} %collective-permute-done.11.refs_2_, bf16[48,3328]{1,0:T(8,128)(2,1)S(1)} %collective-permute-done.2.refs_3_, ...), custom_call_target="tpu_custom_call" | custom-call | flops 1056964608 | bytes 344064 | tf_op jit(solution)/shard_map/pallas_call | solution.py:292
  83.9 1.4 %collective-permute-done.22 = f32[224,384]{1,0:T(8,128)S(1)} collective-permute-done((f32[224,384]{1,0:T(8,128)S(1)}, f32[224,384]{1,0:T(8,128)S(1)}, u32[]{:S(2)}, u32[]{:S(2)}) %collective-permute-start.22) | collective-permute-done | bytes 344096 | tf_op jit(solution)/shard_map/ppermute | solution.py:248
  86.2 1.1 fusion.4
  87.4 1.0 copy-done.6
  88.3 1.0 copy-done.8
  89.3 4.8 %shard_map.63 = (f32[48,768]{1,0:T(8,128)S(1)}, f32[384,256]{1,0:T(8,128)}) custom-call(s32[3]{0:T(128)S(1)} %pad_add_fusion.place_ref, bf16[48,3328]{1,0:T(8,128)(2,1)S(1)} %shard_map.60.refs_0_, bf16[48,3328]{1,0:T(8,128)(2,1)S(1)} %shard_map.59.refs_1_, bf16[48,3328]{1,0:T(8,128)(2,1)S(1)} %collective-permute-done.11.refs_2_, ...), custom_call_target="tpu_custom_call" | custom-call | flops 452984832 | bytes 147456 | tf_op jit(solution)/shard_map/pallas_call | solution.py:305
  94.1 1.5 %collective-permute-done.23.refs_3_ = f32[224,384]{1,0:T(8,128)S(1)} collective-permute-done((f32[224,384]{1,0:T(8,128)S(1)}, f32[224,384]{1,0:T(8,128)S(1)}, u32[]{:S(2)}, u32[]{:S(2)}) %collective-permute-start.23) | collective-permute-done | bytes 344096 | tf_op jit(solution)/shard_map/ppermute | solution.py:248
  95.9 1.0 collective-permute-done.24
  98.0 1.5 %shard_map.64.refs_7_ = f32[3,128,512]{2,1,0:T(8,128)S(1)} custom-call(s32[1]{0:T(128)} %bitcast.1.flag_ref, f32[384,256]{1,0:T(8,128)} %get-tuple-element.55.mine_ref, f32[384,256]{1,0:T(8,128)S(1)} %collective-permute-done.26.other_ref, f32[3,128,128]{2,1,0:T(8,128)S(1)} %pad_maximum_fusion.inverse_ref.refs_8_), custom_call_target="tpu_custom_call" | custom-call | flops 150994944 | bytes 589824 | tf_op jit(solution)/shard_map/pallas_call | solution.py:319
  99.4 3.4 %collective-permute-done.25.refs_5_ = f32[48,768]{1,0:T(8,128)S(1)} collective-permute-done((f32[48,768]{1,0:T(8,128)S(1)}, f32[48,768]{1,0:T(8,128)S(1)}, u32[]{:S(2)}, u32[]{:S(2)}) %collective-permute-start.25) | collective-permute-done | bytes 147488 | tf_op jit(solution)/shard_map/ppermute | solution.py:248
  102.9 1.0 copy-done.10
  103.9 1.0 copy-done.12
  104.9 1.0 copy-done.21
  105.9 1.0 copy-done.23
  106.8 3.1 %shard_map.65 = (f32[384,512]{1,0:T(8,128)}, f32[384,512]{1,0:T(8,128)}) custom-call(f32[240,384]{1,0:T(8,128)S(1)} %copy-done.10, f32[240,384]{1,0:T(8,128)S(1)} %copy-done.21, f32[224,384]{1,0:T(8,128)S(1)} %copy-done.12, f32[224,384]{1,0:T(8,128)S(1)} %copy-done.23, f32[48,768]{1,0:T(8,128)S(1)} %add.33.refs_4_, ...), custom_call_target="tpu_custom_call" | custom-call | flops 452984832 | bytes 1769472 | tf_op jit(solution)/shard_map/pallas_call | solution.py:393
  (101 shorter events, 10.0 us)
Async XLA Ops:
  0.7 2.3 %copy-start = (bf16[384,6144]{1,0:T(8,128)(2,1)S(1)}, bf16[384,6144]{1,0:T(8,128)(2,1)}, u32[]{:S(2)}) copy-start(bf16[384,6144]{1,0:T(8,128)(2,1)} %refs_20_.1) | copy-start | bytes 14155780
  3.1 1.1 %copy-start.3 = (f32[384,512]{1,0:T(8,128)S(1)}, f32[384,512]{1,0:T(8,128)}, u32[]{:S(2)}) copy-start(f32[384,512]{1,0:T(8,128)} %refs_10_.3) | copy-start | bytes 2359300
  4.9 30.3 %copy-start.27 = (s32[3,128]{1,0:T(4,128)S(1)}, s32[3,128]{1,0:T(4,128)}, u32[]{:S(2)}) copy-start(s32[3,128]{1,0:T(4,128)} %index_ref.3) | copy-start | bytes 4612
  6.0 11.8 %collective-permute-start = (bf16[48,3328]{1,0:T(8,128)(2,1)S(1)}, bf16[48,3328]{1,0:T(8,128)(2,1)S(1)}, u32[]{:S(2)}, u32[]{:S(2)}) collective-permute-start(bf16[48,3328]{1,0:T(8,128)(2,1)S(1)} %shard_map.59.refs_1_), channel_id=1, source_target_pairs={{0,8},{4,12},{8,0},{12,4},{16,24},{20,28},{24,16},{28,20},{1,9},{5... | collective-permute-start | bytes 958472 | tf_op jit(solution)/shard_map/ppermute | solution.py:251
  9.1 10.2 %collective-permute-start.1 = (bf16[48,3328]{1,0:T(8,128)(2,1)S(1)}, bf16[48,3328]{1,0:T(8,128)(2,1)S(1)}, u32[]{:S(2)}, u32[]{:S(2)}) collective-permute-start(bf16[48,3328]{1,0:T(8,128)(2,1)S(1)} %shard_map.59.refs_1_), channel_id=1, source_target_pairs={{8,16},{12,20},{16,8},{20,12},{9,17},{13,21},{17,9},{21,13},{10,18... | collective-permute-start | bytes 958472 | tf_op jit(solution)/shard_map/ppermute | solution.py:251
  9.8 9.5 %collective-permute-start.2 = (bf16[48,3328]{1,0:T(8,128)(2,1)S(1)}, bf16[48,3328]{1,0:T(8,128)(2,1)S(1)}, u32[]{:S(2)}, u32[]{:S(2)}) collective-permute-start(bf16[48,3328]{1,0:T(8,128)(2,1)S(1)} %shard_map.59.refs_1_), channel_id=1, source_target_pairs={{0,4},{4,0},{8,12},{12,8},{16,20},{20,16},{24,28},{28,24},{1,5},{5... | collective-permute-start | bytes 958472 | tf_op jit(solution)/shard_map/ppermute | solution.py:251
  12.5 11.1 %collective-permute-start.9 = (bf16[48,3328]{1,0:T(8,128)(2,1)S(1)}, bf16[48,3328]{1,0:T(8,128)(2,1)S(1)}, u32[]{:S(2)}, u32[]{:S(2)}) collective-permute-start(bf16[48,3328]{1,0:T(8,128)(2,1)S(1)} %shard_map.60.refs_0_), channel_id=1, source_target_pairs={{0,8},{4,12},{8,0},{12,4},{16,24},{20,28},{24,16},{28,20},{1,9},{5... | collective-permute-start | bytes 958472 | tf_op jit(solution)/shard_map/ppermute | solution.py:251
  16.9 6.7 %collective-permute-start.10 = (bf16[48,3328]{1,0:T(8,128)(2,1)S(1)}, bf16[48,3328]{1,0:T(8,128)(2,1)S(1)}, u32[]{:S(2)}, u32[]{:S(2)}) collective-permute-start(bf16[48,3328]{1,0:T(8,128)(2,1)S(1)} %shard_map.60.refs_0_), channel_id=1, source_target_pairs={{8,16},{12,20},{16,8},{20,12},{9,17},{13,21},{17,9},{21,13},{10,18... | collective-permute-start | bytes 958472 | tf_op jit(solution)/shard_map/ppermute | solution.py:251
  17.8 10.5 %collective-permute-start.11 = (bf16[48,3328]{1,0:T(8,128)(2,1)S(1)}, bf16[48,3328]{1,0:T(8,128)(2,1)S(1)}, u32[]{:S(2)}, u32[]{:S(2)}) collective-permute-start(bf16[48,3328]{1,0:T(8,128)(2,1)S(1)} %shard_map.60.refs_0_), channel_id=1, source_target_pairs={{0,4},{4,0},{8,12},{12,8},{16,20},{20,16},{24,28},{28,24},{1,5},{5... | collective-permute-start | bytes 958472 | tf_op jit(solution)/shard_map/ppermute | solution.py:251
  19.3 13.9 %collective-permute-start.3 = (bf16[48,3328]{1,0:T(8,128)(2,1)S(1)}, bf16[48,3328]{1,0:T(8,128)(2,1)}, u32[]{:S(2)}, u32[]{:S(2)}) collective-permute-start(bf16[48,3328]{1,0:T(8,128)(2,1)S(1)} %collective-permute-done.refs_5_), channel_id=1, source_target_pairs={{8,16},{12,20},{16,8},{20,12},{9,17},{13,21},{17,9},{21,13},{10,18... | collective-permute-start | bytes 958472 | tf_op jit(solution)/shard_map/ppermute | solution.py:251
  20.8 24.7 %collective-permute-start.5 = (bf16[48,3328]{1,0:T(8,128)(2,1)S(1)}, bf16[48,3328]{1,0:T(8,128)(2,1)S(1)}, u32[]{:S(2)}, u32[]{:S(2)}) collective-permute-start(bf16[48,3328]{1,0:T(8,128)(2,1)S(1)} %collective-permute-done.refs_5_), channel_id=1, source_target_pairs={{0,4},{4,0},{8,12},{12,8},{16,20},{20,16},{24,28},{28,24},{1,5},{5... | collective-permute-start | bytes 958472 | tf_op jit(solution)/shard_map/ppermute | solution.py:251
  28.3 17.8 %collective-permute-start.12 = (bf16[48,3328]{1,0:T(8,128)(2,1)S(1)}, bf16[48,3328]{1,0:T(8,128)(2,1)}, u32[]{:S(2)}, u32[]{:S(2)}) collective-permute-start(bf16[48,3328]{1,0:T(8,128)(2,1)S(1)} %collective-permute-done.9.refs_4_), channel_id=1, source_target_pairs={{8,16},{12,20},{16,8},{20,12},{9,17},{13,21},{17,9},{21,13},{10,18... | collective-permute-start | bytes 958472 | tf_op jit(solution)/shard_map/ppermute | solution.py:251
  29.7 20.6 %collective-permute-start.14 = (bf16[48,3328]{1,0:T(8,128)(2,1)S(1)}, bf16[48,3328]{1,0:T(8,128)(2,1)S(1)}, u32[]{:S(2)}, u32[]{:S(2)}) collective-permute-start(bf16[48,3328]{1,0:T(8,128)(2,1)S(1)} %collective-permute-done.9.refs_4_), channel_id=1, source_target_pairs={{0,4},{4,0},{8,12},{12,8},{16,20},{20,16},{24,28},{28,24},{1,5},{5... | collective-permute-start | bytes 958472 | tf_op jit(solution)/shard_map/ppermute | solution.py:251
  31.1 12.9 %collective-permute-start.4 = (bf16[48,3328]{1,0:T(8,128)(2,1)S(1)}, bf16[48,3328]{1,0:T(8,128)(2,1)S(1)}, u32[]{:S(2)}, u32[]{:S(2)}) collective-permute-start(bf16[48,3328]{1,0:T(8,128)(2,1)S(1)} %collective-permute-done.1.refs_13_), channel_id=1, source_target_pairs={{8,0},{12,4},{16,24},{20,28},{9,1},{13,5},{17,25},{21,29},{10,2},{... | collective-permute-start | bytes 958472 | tf_op jit(solution)/shard_map/ppermute | solution.py:251
  33.1 17.2 %collective-permute-start.13 = (bf16[48,3328]{1,0:T(8,128)(2,1)S(1)}, bf16[48,3328]{1,0:T(8,128)(2,1)S(1)}, u32[]{:S(2)}, u32[]{:S(2)}) collective-permute-start(bf16[48,3328]{1,0:T(8,128)(2,1)S(1)} %collective-permute-done.10.refs_12_), channel_id=1, source_target_pairs={{8,0},{12,4},{16,24},{20,28},{9,1},{13,5},{17,25},{21,29},{10,2},{... | collective-permute-start | bytes 958472 | tf_op jit(solution)/shard_map/ppermute | solution.py:251
  44.0 27.5 %collective-permute-start.8 = (bf16[48,3328]{1,0:T(8,128)(2,1)S(1)}, bf16[48,3328]{1,0:T(8,128)(2,1)}, u32[]{:S(2)}, u32[]{:S(2)}) collective-permute-start(bf16[48,3328]{1,0:T(8,128)(2,1)S(1)} %collective-permute-done.2.refs_3_), channel_id=1, source_target_pairs={{8,16},{12,20},{16,8},{20,12},{9,17},{13,21},{17,9},{21,13},{10,18... | collective-permute-start | bytes 958472 | tf_op jit(solution)/shard_map/ppermute | solution.py:251
  45.4 29.0 %copy-start.5 = (bf16[48,3328]{1,0:T(8,128)(2,1)}, bf16[48,3328]{1,0:T(8,128)(2,1)S(1)}, u32[]{:S(2)}) copy-start(bf16[48,3328]{1,0:T(8,128)(2,1)S(1)} %collective-permute-done.5.refs_7_) | copy-start | bytes 958468
  45.4 12.0 %collective-permute-start.18 = (bf16[48,3328]{1,0:T(8,128)(2,1)S(1)}, bf16[48,3328]{1,0:T(8,128)(2,1)S(1)}, u32[]{:S(2)}, u32[]{:S(2)}) collective-permute-start(bf16[48,3328]{1,0:T(8,128)(2,1)S(1)} %collective-permute-done.11.refs_2_), channel_id=1, source_target_pairs={{8,16},{12,20},{16,8},{20,12},{9,17},{13,21},{17,9},{21,13},{10,18... | collective-permute-start | bytes 958472 | tf_op jit(solution)/shard_map/ppermute | solution.py:251
  46.1 25.4 %collective-permute-start.7 = (bf16[48,3328]{1,0:T(8,128)(2,1)}, bf16[48,3328]{1,0:T(8,128)(2,1)}, u32[]{:S(2)}, u32[]{:S(2)}) collective-permute-start(bf16[48,3328]{1,0:T(8,128)(2,1)} %collective-permute-done.3), channel_id=1, source_target_pairs={{8,0},{12,4},{16,24},{20,28},{9,1},{13,5},{17,25},{21,29},{10,2},{... | collective-permute-start | bytes 958472 | tf_op jit(solution)/shard_map/ppermute | solution.py:251
  50.3 24.1 %copy-start.7 = (bf16[48,3328]{1,0:T(8,128)(2,1)}, bf16[48,3328]{1,0:T(8,128)(2,1)S(1)}, u32[]{:S(2)}) copy-start(bf16[48,3328]{1,0:T(8,128)(2,1)S(1)} %collective-permute-done.14.refs_6_) | copy-start | bytes 958468
  50.4 10.5 %copy-start.28 = (f32[3,128,128]{2,1,0:T(8,128)S(1)}, f32[3,128,128]{2,1,0:T(8,128)}, u32[]{:S(2)}) copy-start(f32[3,128,128]{2,1,0:T(8,128)} %param.7) | copy-start | bytes 589828
  50.4 9.1 %collective-permute-start.16 = (bf16[48,3328]{1,0:T(8,128)(2,1)S(1)}, bf16[48,3328]{1,0:T(8,128)(2,1)S(1)}, u32[]{:S(2)}, u32[]{:S(2)}) collective-permute-start(bf16[48,3328]{1,0:T(8,128)(2,1)S(1)} %broadcast_select_fusion.refs_8_), channel_id=1, source_target_pairs={{0,4},{4,0},{8,12},{12,8},{16,20},{20,16},{24,28},{28,24},{1,5},{5... | collective-permute-start | bytes 958472 | tf_op jit(solution)/shard_map/ppermute | solution.py:251
  50.7 20.8 %collective-permute-start.6 = (bf16[48,3328]{1,0:T(8,128)(2,1)S(1)}, bf16[48,3328]{1,0:T(8,128)(2,1)}, u32[]{:S(2)}, u32[]{:S(2)}) collective-permute-start(bf16[48,3328]{1,0:T(8,128)(2,1)S(1)} %broadcast_select_fusion.1.refs_9_), channel_id=1, source_target_pairs={{0,4},{4,0},{8,12},{12,8},{16,20},{20,16},{24,28},{28,24},{1,5},{5... | collective-permute-start | bytes 958472 | tf_op jit(solution)/shard_map/ppermute | solution.py:251
  52.6 2.3 %copy-start.1 = (bf16[384,6144]{1,0:T(8,128)(2,1)S(1)}, bf16[384,6144]{1,0:T(8,128)(2,1)}, u32[]{:S(2)}) copy-start(bf16[384,6144]{1,0:T(8,128)(2,1)} %refs_20_.1) | copy-start | bytes 14155780
  58.2 9.8 %collective-permute-start.17 = (bf16[48,3328]{1,0:T(8,128)(2,1)}, bf16[48,3328]{1,0:T(8,128)(2,1)}, u32[]{:S(2)}, u32[]{:S(2)}) collective-permute-start(bf16[48,3328]{1,0:T(8,128)(2,1)} %collective-permute-done.12), channel_id=1, source_target_pairs={{8,0},{12,4},{16,24},{20,28},{9,1},{13,5},{17,25},{21,29},{10,2},{... | collective-permute-start | bytes 958472 | tf_op jit(solution)/shard_map/ppermute | solution.py:251
  60.2 10.1 %collective-permute-start.15 = (f32[240,384]{1,0:T(8,128)}, f32[240,384]{1,0:T(8,128)}, u32[]{:S(2)}, u32[]{:S(2)}) collective-permute-start(f32[240,384]{1,0:T(8,128)} %shard_map.61), channel_id=1, source_target_pairs={{0,1},{1,0},{2,3},{3,2},{4,5},{5,4},{6,7},{7,6},{8,9},{9,8},{10,11... | collective-permute-start | bytes 1105928 | tf_op jit(solution)/shard_map/ppermute | solution.py:248
  67.9 17.4 %collective-permute-start.19 = (bf16[48,3328]{1,0:T(8,128)(2,1)}, bf16[48,3328]{1,0:T(8,128)(2,1)S(1)}, u32[]{:S(2)}, u32[]{:S(2)}) collective-permute-start(bf16[48,3328]{1,0:T(8,128)(2,1)} %collective-permute-done.17.refs_14_), channel_id=1, source_target_pairs={{0,4},{4,0},{24,28},{28,24},{1,5},{5,1},{25,29},{29,25},{2,6},{6,2... | collective-permute-start | bytes 958472 | tf_op jit(solution)/shard_map/ppermute | solution.py:251
  70.3 17.0 %copy-start.19 = (bf16[48,3328]{1,0:T(8,128)(2,1)S(1)}, bf16[48,3328]{1,0:T(8,128)(2,1)}, u32[]{:S(2)}) copy-start(bf16[48,3328]{1,0:T(8,128)(2,1)} %copy-done.17) | copy-start | bytes 958468
  70.3 17.0 %copy-start.25 = (bf16[48,3328]{1,0:T(8,128)(2,1)S(1)}, bf16[48,3328]{1,0:T(8,128)(2,1)}, u32[]{:S(2)}) copy-start(bf16[48,3328]{1,0:T(8,128)(2,1)} %copy-done.24) | copy-start | bytes 958468
  71.5 12.0 %copy-start.9 = (f32[240,384]{1,0:T(8,128)}, f32[240,384]{1,0:T(8,128)S(1)}, u32[]{:S(2)}) copy-start(f32[240,384]{1,0:T(8,128)S(1)} %add.31.refs_0_) | copy-start | bytes 1105924
  71.6 13.8 %collective-permute-start.20 = (bf16[48,3328]{1,0:T(8,128)(2,1)}, bf16[48,3328]{1,0:T(8,128)(2,1)S(1)}, u32[]{:S(2)}, u32[]{:S(2)}) collective-permute-start(bf16[48,3328]{1,0:T(8,128)(2,1)} %collective-permute-done.6.refs_11_), channel_id=1, source_target_pairs={{8,0},{12,4},{16,24},{20,28},{9,1},{13,5},{17,25},{21,29},{10,2},{... | collective-permute-start | bytes 958472 | tf_op jit(solution)/shard_map/ppermute | solution.py:251
  72.9 12.5 %collective-permute-start.21 = (f32[240,384]{1,0:T(8,128)S(1)}, f32[240,384]{1,0:T(8,128)S(1)}, u32[]{:S(2)}, u32[]{:S(2)}) collective-permute-start(f32[240,384]{1,0:T(8,128)S(1)} %add.31.refs_0_), channel_id=1, source_target_pairs={{0,2},{1,3},{2,0},{3,1},{4,6},{5,7},{6,4},{7,5},{8,10},{9,11},{10,... | collective-permute-start | bytes 1105928 | tf_op jit(solution)/shard_map/ppermute | solution.py:248
  74.4 2.3 %copy-start.2 = (bf16[384,6144]{1,0:T(8,128)(2,1)S(1)}, bf16[384,6144]{1,0:T(8,128)(2,1)}, u32[]{:S(2)}) copy-start(bf16[384,6144]{1,0:T(8,128)(2,1)} %refs_20_.1) | copy-start | bytes 14155780
  83.5 1.7 %collective-permute-start.22 = (f32[224,384]{1,0:T(8,128)S(1)}, f32[224,384]{1,0:T(8,128)S(1)}, u32[]{:S(2)}, u32[]{:S(2)}) collective-permute-start(f32[224,384]{1,0:T(8,128)S(1)} %shard_map.62), channel_id=1, source_target_pairs={{0,1},{1,0},{2,3},{3,2},{4,5},{5,4},{6,7},{7,6},{8,9},{9,8},{10,11... | collective-permute-start | bytes 1032200 | tf_op jit(solution)/shard_map/ppermute | solution.py:248
  85.3 8.7 %copy-start.11 = (f32[224,384]{1,0:T(8,128)}, f32[224,384]{1,0:T(8,128)S(1)}, u32[]{:S(2)}) copy-start(f32[224,384]{1,0:T(8,128)S(1)} %add.32.refs_2_) | copy-start | bytes 1032196
  85.3 8.7 %copy-start.20 = (f32[240,384]{1,0:T(8,128)}, f32[240,384]{1,0:T(8,128)S(1)}, u32[]{:S(2)}) copy-start(f32[240,384]{1,0:T(8,128)S(1)} %collective-permute-done.21.refs_1_) | copy-start | bytes 1105924
  85.4 10.2 %collective-permute-start.23 = (f32[224,384]{1,0:T(8,128)S(1)}, f32[224,384]{1,0:T(8,128)S(1)}, u32[]{:S(2)}, u32[]{:S(2)}) collective-permute-start(f32[224,384]{1,0:T(8,128)S(1)} %add.32.refs_2_), channel_id=1, source_target_pairs={{0,2},{1,3},{2,0},{3,1},{4,6},{5,7},{6,4},{7,5},{8,10},{9,11},{10,... | collective-permute-start | bytes 1032200 | tf_op jit(solution)/shard_map/ppermute | solution.py:248
  89.3 6.5 %copy-start.29 = (pred[128,128]{1,0:T(8,128)(4,1)S(1)}, pred[128,128]{1,0:T(8,128)(4,1)}, u32[]{:S(2)}) copy-start(pred[128,128]{1,0:T(8,128)(4,1)} %get-tuple-element.59) | copy-start | bytes 49156
  89.3 6.5 %copy-start.30 = (pred[128,128]{1,0:T(8,128)(4,1)S(1)}, pred[128,128]{1,0:T(8,128)(4,1)}, u32[]{:S(2)}) copy-start(pred[128,128]{1,0:T(8,128)(4,1)} %get-tuple-element.60) | copy-start | bytes 49156
  89.3 6.6 %copy-start.31 = (pred[128,128]{1,0:T(8,128)(4,1)S(1)}, pred[128,128]{1,0:T(8,128)(4,1)}, u32[]{:S(2)}) copy-start(pred[128,128]{1,0:T(8,128)(4,1)} %get-tuple-element.61) | copy-start | bytes 49156
  89.3 13.6 %copy-start.4 = (f32[384,512]{1,0:T(8,128)S(1)}, f32[384,512]{1,0:T(8,128)}, u32[]{:S(2)}) copy-start(f32[384,512]{1,0:T(8,128)} %refs_10_.3) | copy-start | bytes 2359300
  94.1 3.9 %collective-permute-start.26 = (f32[384,256]{1,0:T(8,128)}, f32[384,256]{1,0:T(8,128)S(1)}, u32[]{:S(2)}, u32[]{:S(2)}) collective-permute-start(f32[384,256]{1,0:T(8,128)} %get-tuple-element.55.mine_ref), channel_id=1, source_target_pairs={{0,1},{1,0},{2,3},{3,2},{4,5},{5,4},{6,7},{7,6},{8,9},{9,8},{10,11... | collective-permute-start | bytes 1179656 | tf_op jit(solution)/shard_map/ppermute | solution.py:248
  95.5 1.4 %copy-start.22 = (f32[224,384]{1,0:T(8,128)}, f32[224,384]{1,0:T(8,128)S(1)}, u32[]{:S(2)}) copy-start(f32[224,384]{1,0:T(8,128)S(1)} %collective-permute-done.23.refs_3_) | copy-start | bytes 1032196
  95.5 1.4 %collective-permute-start.24 = (f32[48,768]{1,0:T(8,128)S(1)}, f32[48,768]{1,0:T(8,128)S(1)}, u32[]{:S(2)}, u32[]{:S(2)}) collective-permute-start(f32[48,768]{1,0:T(8,128)S(1)} %get-tuple-element.54), channel_id=1, source_target_pairs={{0,1},{1,0},{2,3},{3,2},{4,5},{5,4},{6,7},{7,6},{8,9},{9,8},{10,11... | collective-permute-start | bytes 442376 | tf_op jit(solution)/shard_map/ppermute | solution.py:248
  96.9 6.0 %collective-permute-start.25 = (f32[48,768]{1,0:T(8,128)S(1)}, f32[48,768]{1,0:T(8,128)S(1)}, u32[]{:S(2)}, u32[]{:S(2)}) collective-permute-start(f32[48,768]{1,0:T(8,128)S(1)} %add.33.refs_4_), channel_id=1, source_target_pairs={{0,2},{1,3},{2,0},{3,1},{4,6},{5,7},{6,4},{7,5},{8,10},{9,11},{10,... | collective-permute-start | bytes 442376 | tf_op jit(solution)/shard_map/ppermute | solution.py:248
  102.9 1.0 copy-start.10
  103.9 1.0 copy-start.12
  104.9 1.0 copy-start.21
  (11 other events, 9.4 us)

commit v4 on v3

v4 whole, which is shorter than its diff:
```python
import functools

import jax
import jax.numpy as jnp
from jax import lax
from jax.experimental import pallas as pl
from jax.experimental.pallas import tpu as pltpu
from jax.sharding import PartitionSpec as P

F = 24576
VMEM = pl.BlockSpec(memory_space=pltpu.VMEM)
SMEM = pl.BlockSpec(memory_space=pltpu.SMEM)
HBM = pl.BlockSpec(memory_space=pltpu.HBM)
PIECES = 4
PARAMS = pltpu.CompilerParams(vmem_limit_bytes=24 * 1024 * 1024)
PICK = pltpu.CompilerParams(vmem_limit_bytes=58 * 1024 * 1024)
GRAM = pltpu.CompilerParams(vmem_limit_bytes=46 * 1024 * 1024)


def quadratic(gram):
    scaled = gram * (1.0 / F)
    return scaled + scaled * scaled


def dot_rows(left, right):
    return lax.dot_general(
        left, right, (((1,), (1,)), ((), ())), preferred_element_type=jnp.float32
    )


def exact_dot(left, right):
    return jnp.dot(
        left, right, precision=lax.Precision.HIGHEST, preferred_element_type=jnp.float32
    )


def split(array):
    high = array.astype(jnp.bfloat16)
    return high, (array - high.astype(jnp.float32)).astype(jnp.bfloat16)


def fine_dot(left, right, contract=1):
    sides = (((contract,), (0,)), ((), ()))
    left_high, left_low = left if isinstance(left, tuple) else split(left)
    right_high, right_low = right if isinstance(right, tuple) else split(right)

    def part(one, other):
        return lax.dot_general(one, other, sides, preferred_element_type=jnp.float32)

    return part(left_high, right_high) + (part(left_high, right_low) + part(left_low, right_high))


def pairs_of(steps):
    return [(step, before) for step in range(steps) for before in range(step)]


def of_step(slots, step, per):
    return jnp.concatenate([slot[step * per : (step + 1) * per] for slot in slots], axis=0)


def by_step(array, steps, per):
    parts = array.reshape(-1, steps, per, array.shape[-1])
    return jnp.swapaxes(parts, 0, 1).reshape(steps, -1, array.shape[-1])


def cost(rows, columns):
    return pl.CostEstimate(flops=2 * rows * columns, bytes_accessed=4 * rows, transcendentals=0)


def finish_kernel(steps, per, last, *refs):
    refs = list(refs)
    if last:
        high_ref, low_ref, cross_ref = refs[:3]
        end = refs[3][...] + refs[4][...]
        refs = refs[5:]
    else:
        gram_ref, cross_ref = refs[:2]
        refs = refs[2:]
    same_ref, first_ref, inverse_ref, own_ref, targets_ref, resid_ref, coeff_ref = refs
    block = first_ref.shape[1]
    rows = targets_ref.shape[0]
    if last:
        column = lax.broadcasted_iota(jnp.int32, (block, block), 0) < block - per
        end_gram = quadratic(end[:, :rows])
        end = end[:, rows:]

        def of(one, other):
            part = end[one * per : (one + 1) * per, other * block : (other + 1) * block]
            return jnp.concatenate([jnp.zeros((block - per, block), jnp.float32), part], axis=0)

    between = {}
    for at, (step, before) in enumerate(pairs_of(steps)):
        part = cross_ref[:, at * block : (at + 1) * block]
        if last:
            part = part + of(step, before) + jnp.where(column, of(before, step).T, 0.0)
        between[step, before] = split(quadratic(part) + same_ref[:, at * block : (at + 1) * block])
    deltas = []
    for step in range(steps):
        delta = first_ref[step]
        if step:
            change = fine_dot(between[step, 0], deltas[0])
            for before in range(1, step):
                change += fine_dot(between[step, before], deltas[before])
            delta = delta - fine_dot(inverse_ref[step], change)
        deltas.append(split(delta))
    spread = own_ref[...] == lax.broadcasted_iota(jnp.int32, (steps * per, rows), 1)
    spread = spread.astype(jnp.float32).astype(jnp.bfloat16)
    sides = (((0,), (0,)), ((), ()))
    coeffs = jnp.zeros(targets_ref.shape, jnp.float32)
    resid = targets_ref[...]
    for high_or_low in (0, 1):
        own = jnp.concatenate([delta[high_or_low][:per] for delta in deltas], axis=0)
        coeffs += lax.dot_general(spread, own, sides, preferred_element_type=jnp.float32)
    coeff_ref[...] = coeffs
    for step in range(steps):
        if last:
            part = split(end_gram[step * per : (step + 1) * per])
            kernel = tuple(
                jnp.concatenate([ref[step], one], axis=0) for ref, one in zip((high_ref, low_ref), part)
            )
        else:
            kernel = quadratic(gram_ref[...].reshape(-1, steps, per, rows)[:, step].reshape(block, rows))
        resid = resid - fine_dot(kernel, deltas[step], 0)
    resid_ref[...] = resid - coeffs


def ready_kernel(steps, per, place_ref, *refs):
    mine_ref, other_ref, inverse_ref, *gram_refs, first_ref, high_ref, low_ref, cross_ref = refs
    core = place_ref[1]
    block = inverse_ref.shape[1]
    half = mine_ref.shape[1]
    for step in range(steps):
        rows = slice(step * block, (step + 1) * block)
        inverse = split(inverse_ref[step])
        mine, other = mine_ref[rows], other_ref[rows]
        first_ref[step, :, :half] = fine_dot(inverse, jnp.where(core == 0, mine, other))
        first_ref[step, :, half:] = fine_dot(inverse, jnp.where(core == 0, other, mine))
    gram = gram_refs[0][...] + gram_refs[1][...]
    second = gram_refs[2][...] + gram_refs[3][...]
    cross_ref[...] = second[-block:]
    kernel = quadratic(jnp.concatenate([gram, second[:-block]], axis=0))
    kernel = kernel.reshape(-1, steps, per, kernel.shape[-1])
    for step in range(steps):
        high_ref[step], low_ref[step] = split(kernel[:, step].reshape(block - per, -1))


def pieces_of(features_ref):
    width = features_ref.shape[1] // PIECES
    return [slice(i * width, (i + 1) * width) for i in range(PIECES)]


def fetch(features_ref, held_ref, sems):
    copies = []
    for i, at in enumerate(pieces_of(features_ref)):
        copies.append(pltpu.make_async_copy(features_ref.at[:, at], held_ref.at[:, at], sems.at[i]))
        copies[-1].start()
    return copies


def held(features):
    return [pltpu.VMEM(features.shape, features.dtype), pltpu.SemaphoreType.DMA((PIECES,))]


def add(total, part):
    return part if total is None else total + part


def pick_kernel(
    per, index_hbm, place_ref, features_ref, targets_ref, out_ref, index_ref, held_targets, side_sems, held_ref, sems
):
    index = pltpu.make_async_copy(index_hbm, index_ref, side_sems.at[0])
    index.start()
    copies = fetch(features_ref, held_ref, sems)
    side = pltpu.make_async_copy(targets_ref, held_targets, side_sems.at[1])
    side.start()
    index.wait()
    rank, core = place_ref[0], place_ref[1]
    rows, columns = features_ref.shape
    steps = index_ref.shape[0]
    line = lax.broadcasted_iota(jnp.int32, (steps * per, rows), 0)
    wanted = jnp.zeros((steps * per, rows), jnp.int32)
    for step in range(steps):
        for i in range(per):
            wanted = jnp.where(line == step * per + i, index_ref[step, rank * per + i], wanted)
    chosen = wanted - rank * rows == lax.broadcasted_iota(jnp.int32, wanted.shape, 1)
    chosen = chosen.astype(jnp.float32).astype(jnp.bfloat16)

    def take(array):
        return jnp.dot(chosen, array, preferred_element_type=jnp.float32).astype(jnp.bfloat16)

    for copy, at in zip(copies, pieces_of(features_ref)):
        copy.wait()
        out_ref[:, at] = take(held_ref[:, at])
    side.wait()
    width = targets_ref.shape[1] // 2
    values = jnp.where(core == 0, held_targets[:, :width], held_targets[:, width:])
    high, low = split(values)
    out_ref[:, columns : columns + width] = take(high)
    out_ref[:, columns + width :] = take(low)


def pick(block_index, place, features, targets, per):
    count = block_index.shape[0] * per
    wide = features.shape[1] + targets.shape[1]
    return pl.pallas_call(
        functools.partial(pick_kernel, per),
        out_shape=jax.ShapeDtypeStruct((count, wide), features.dtype),
        in_specs=[HBM, SMEM, HBM, HBM],
        out_specs=VMEM,
        scratch_shapes=[
            pltpu.SMEM(block_index.shape, jnp.int32),
            pltpu.VMEM(targets.shape, jnp.float32),
            pltpu.SemaphoreType.DMA((2,)),
        ]
        + held(features),
        compiler_params=PICK,
        cost_estimate=cost(count * features.shape[0], wide),
    )(block_index, place, features, targets)


def gram_kernel(*refs):
    *slot_refs, features_ref, out_ref, held_ref, sems = refs
    total = None
    for copy, at in zip(fetch(features_ref, held_ref, sems), pieces_of(features_ref)):
        slots = jnp.concatenate([ref[:, at] for ref in slot_refs], axis=0)
        copy.wait()
        total = add(total, dot_rows(slots, held_ref[:, at]))
    out_ref[...] = total


def cross_kernel(steps, per, count, place_ref, *refs):
    *slot_refs, features_ref, out_ref, held_ref, sems = refs
    inner = place_ref[2] == 1
    total = [None] * (1 + len(pairs_of(steps)))
    copies = fetch(features_ref, held_ref, sems)
    for copy, at in zip(copies, pieces_of(features_ref)):
        slots = [ref[:, at] for ref in slot_refs]
        other = slots.pop()
        slots[-1] = jnp.where(inner, slots[-1], other)
        rows = [of_step(slots + [jnp.zeros_like(other)], step, per) for step in range(steps)]
        for i, (step, before) in enumerate(pairs_of(steps)):
            total[1 + i] = add(total[1 + i], dot_rows(rows[step], rows[before]))
        copy.wait()
        total[0] = add(total[0], dot_rows(jnp.concatenate(slots[count:], axis=0), held_ref[:, at]))
    new = total[0].shape[0]
    out_ref[:new] = total[0]
    out_ref[new:] = jnp.concatenate(total[1:], axis=1)


def last_kernel(steps, per, place_ref, *refs):
    *slot_refs, inner_ref, left_ref, right_ref, features_ref, out_ref, first_ref, held_ref, sems = refs
    inner = place_ref[2] == 1
    columns = features_ref.shape[1]
    half = left_ref.shape[1]
    copies = fetch(features_ref, held_ref, sems)

    def every(at):
        slots = [ref[:, at] for ref in slot_refs]
        other = slots.pop()
        slots[-1] = jnp.where(inner, slots[-1], other)
        if at.start < half:
            last = left_ref[:, at]
        else:
            last = right_ref[:, at.start - half : at.stop - half]
        last = jnp.where(inner, inner_ref[:, at], last)
        rows = [of_step(slots + [last], step, per) for step in range(steps)]
        return last, jnp.concatenate(rows, axis=0)

    total, cross = None, None
    for copy, at in zip(copies, pieces_of(features_ref)):
        last, rows = every(at)
        cross = add(cross, dot_rows(rows, last))
        copy.wait()
        total = add(total, dot_rows(held_ref[:, at], last))
    wide = features_ref.shape[0]
    out_ref[:, :wide] = total.T
    out_ref[:, wide:] = cross.T
    width = (inner_ref.shape[1] - columns) // 2
    high = every(slice(columns, columns + width))[1]
    low = every(slice(columns + width, columns + 2 * width))[1]
    first_ref[...] = high.astype(jnp.float32) + low.astype(jnp.float32)


class Lines:
    def __init__(self):
        self.beside = [(r, r ^ 1) for r in range(8)]
        self.pair = [(r, r ^ 2) for r in range(8)]
        self.inner = [(r, r ^ 6) for r in range(2, 6)]
        self.outer = [(2, 0), (3, 1), (4, 6), (5, 7)]
        self.ends = [(r, r ^ 1) for r in (0, 1, 6, 7)]
        rank = lax.axis_index("rows")
        core = lax.axis_index("feat") % 2
        self.is_inner = (rank >= 2) & (rank < 6)
        self.order = rank ^ jnp.arange(8)
        self.place = jnp.stack([rank, core, self.is_inner.astype(jnp.int32)])

    def near(self, array, bit):
        return lax.ppermute(array, "feat", [(f, f ^ bit) for f in range(4)])

    def send(self, array, pairs):
        return lax.ppermute(array, "rows", pairs)

    def run(self, features, targets, block_index, turned, per):
        rows, columns = features.shape
        steps, block = block_index.shape
        count = steps * per
        hold = lax.optimization_barrier
        own = pick(block_index, self.place, features, targets, per)
        half = columns // 2

        pair = self.send(own, self.pair)
        mid = self.send(own, self.inner)
        own_b = self.send(own, self.beside)
        pair, mid, own_b = hold((pair, mid, own_b))

        far = self.send(pair, self.inner)
        mid_end = self.send(mid, self.outer)
        pair_b = self.send(pair, self.beside)
        far, mid_end, pair_b = hold((far, mid_end, pair_b))

        third = jnp.where(self.is_inner, far, mid_end)
        third_b = self.send(third, self.beside)
        far_end = self.send(far, self.outer)
        last_in = self.send(own_b, self.inner)
        slots = [own, own_b, pair, pair_b, third]
        gram = pl.pallas_call(
            gram_kernel,
            out_shape=jax.ShapeDtypeStruct((5 * count, rows), jnp.float32),
            in_specs=[VMEM] * len(slots) + [HBM],
            out_specs=VMEM,
            scratch_shapes=held(features),
            compiler_params=GRAM,
            cost_estimate=cost(5 * count * rows, columns),
        )(*slots, features)
        gram = gram + self.near(gram, 1)
        third_b, far_end, last_in, gram = hold((third_b, far_end, last_in, gram))

        left = self.send(far_end[:, :half], self.ends)
        right = self.send(third_b[:, half:], self.outer)
        gram_near = self.near(gram, 2)
        slots = slots + [third_b, mid, far_end]
        second = pl.pallas_call(
            functools.partial(cross_kernel, steps, per, 5),
            out_shape=jax.ShapeDtypeStruct((2 * count + block, rows), jnp.float32),
            in_specs=[SMEM] + [VMEM] * len(slots) + [HBM],
            out_specs=VMEM,
            scratch_shapes=held(features),
            compiler_params=GRAM,
            cost_estimate=cost((2 * count + block) * rows, columns),
        )(self.place, *slots, features)
        second = second + self.near(second, 1)
        left, right, gram_near = hold((left, right, gram_near))

        second_near = self.near(second, 2)
        slots = slots + [last_in, left, right]
        last, first = pl.pallas_call(
            functools.partial(last_kernel, steps, per),
            out_shape=(
                jax.ShapeDtypeStruct((count, rows + steps * block), jnp.float32),
                jax.ShapeDtypeStruct((steps * block, targets.shape[1] // 2), jnp.float32),
            ),
            in_specs=[SMEM] + [VMEM] * len(slots) + [HBM],
            out_specs=(VMEM, VMEM),
            scratch_shapes=held(features),
            compiler_params=GRAM,
            cost_estimate=cost(count * (rows + steps * block), columns),
        )(self.place, *slots, features)
        last, second_near = hold((last, second_near))
        last = last + self.near(last, 1)
        last_near = self.near(last, 2)
        parts = (steps, block - per, rows)
        first, high, low, cross = pl.pallas_call(
            functools.partial(ready_kernel, steps, per),
            out_shape=(
                jax.ShapeDtypeStruct((steps, block, targets.shape[1]), jnp.float32),
                jax.ShapeDtypeStruct(parts, jnp.bfloat16),
                jax.ShapeDtypeStruct(parts, jnp.bfloat16),
                jax.ShapeDtypeStruct((block, rows), jnp.float32),
            ),
            in_specs=[SMEM] + [VMEM] * 7,
            out_specs=(VMEM,) * 4,
            compiler_params=PARAMS,
            cost_estimate=cost(3 * steps * block * block, targets.shape[1]),
        )(self.place, first, self.near(first, 1), turned, gram, gram_near, second, second_near)
        return [high, low, cross, last, last_near], first


class Gathers:
    def __init__(self):
        size = lax.axis_size("rows")
        self.order = (lax.axis_index("rows") + jnp.arange(size)) % size

    def turn(self, own):
        every = lax.all_gather(own, "rows", axis=0, tiled=True)
        start = lax.axis_index("rows") * own.shape[0]
        return lax.dynamic_slice_in_dim(
            jnp.concatenate([every, every], axis=0), start, every.shape[0], 0
        )

    def run(self, features, targets, block_index, turned, per):
        steps = block_index.shape[0]
        rank = lax.axis_index("rows")
        picks = lax.dynamic_slice_in_dim(block_index, rank * per, per, 1).reshape(-1)
        picks = picks - rank * features.shape[0]
        every = self.turn(jnp.take(features, picks, axis=0))
        width = targets.shape[1] // lax.axis_size("feat")
        start = lax.axis_index("feat") * width
        share = jnp.take(lax.dynamic_slice_in_dim(targets, start, width, 1), picks, axis=0)
        share = lax.all_gather(self.turn(share), "feat", axis=1, tiled=True)
        blocks = by_step(every, steps, per)
        cross = jnp.concatenate(
            [dot_rows(blocks[step], blocks[before]) for step, before in pairs_of(steps)], axis=1
        )
        gram, cross = lax.psum((dot_rows(every, features), cross), "feat")
        first = lax.dot_general(
            turned,
            by_step(share, steps, per),
            (((2,), (1,)), ((0,), (0,))),
            precision=lax.Precision.HIGHEST,
            preferred_element_type=jnp.float32,
        )
        return [gram, cross], first


def local(features, targets, block_index, inverse):
    rank = lax.axis_index("rows")
    row_count = lax.axis_size("rows")
    rows = features.shape[0]
    steps, block = block_index.shape
    per = block // row_count
    fits = rows == len(pairs_of(steps)) * block and per % 16 == 0 and features.shape[1] % (128 * PIECES) == 0
    lined = fits and (row_count, lax.axis_size("feat")) == (8, 4)
    mover = Lines() if lined else Gathers()

    place = jnp.arange(block)
    moved = jnp.repeat(mover.order, per) * per + place % per
    swap = moved[:, None] == place[None, :]
    picks = jnp.sum(jnp.where(swap[None], block_index[:, None, :], 0), axis=2)
    swap = swap.astype(jnp.float32)
    turned = jnp.stack([exact_dot(exact_dot(swap, inverse[step]), swap.T) for step in range(steps)])
    same = jnp.concatenate(
        [
            (picks[step][:, None] == picks[before][None, :]).astype(jnp.float32)
            for step, before in pairs_of(steps)
        ],
        axis=1,
    )
    own = picks[:, :per].reshape(-1, 1) - rank * rows

    sums, first = mover.run(features, targets, block_index, turned, per)
    operands = sums + [same, first, turned, own, targets]
    out = jax.ShapeDtypeStruct(targets.shape, jnp.float32)
    return pl.pallas_call(
        functools.partial(finish_kernel, steps, per, len(sums) > 2),
        out_shape=(out, out),
        in_specs=[VMEM] * len(operands),
        out_specs=(VMEM, VMEM),
        compiler_params=PARAMS,
        cost_estimate=cost(3 * rows * steps * block, targets.shape[1]),
    )(*operands)


def solution(mesh):
    return jax.shard_map(
        local,
        mesh=mesh,
        in_specs=(P("rows", "feat"), P("rows", None), P(), P()),
        out_specs=(P("rows", None), P("rows", None)),
        check_vma=False,
    )
```

time: 111 us -> 101 us (0.910)
  waiting for transfers between devices: 31.8 us -> 47.5 us
  local copies, waits for them, and re-layouts: 20.8 us -> 5.69 us
  starting transfers between devices: 33.6 us -> 18.6 us
  Pallas kernels: 17.9 us -> 23.9 us
  other arithmetic: 2.43 us -> 1.2 us
    ppermute x20 -> x11, waiting for transfers between devices: 24.5 us -> 43.6 us  [send(): return lax.ppermute(array, 'rows', pairs)]
    ppermute x20 -> x11, starting transfers between devices: 30.7 us -> 15.2 us  [send(): return lax.ppermute(array, 'rows', pairs)]
    unnamed x64 -> x20, local copies, waits for them, and re-layouts: 20.5 us -> 5.41 us
    ppermute x7, waiting for transfers between devices: 7.33 us -> 3.88 us  [near(): return lax.ppermute(array, 'feat', [(f, f ^ bit) for f in range(4)])]
    pallas_call x4 -> x3, Pallas kernels: 6.82 us -> 9.18 us  [the longest x1 4.41 us: pick(): pl.pallas_call(functools.partial(pick_kernel, per), out_shape=jax.ShapeDt...]
    pallas_call x1, Pallas kernels: 4.75 us -> 6.68 us  [run(): pl.pallas_call(functools.partial(last_kernel, steps, per), out_shape=(jax...]
    pallas_call x1, Pallas kernels: 3.86 us -> 5.24 us  [run(): pl.pallas_call(functools.partial(cross_kernel, steps, per, 5), out_shape=...]
    add x1, other arithmetic: 1.2 us -> 0.05 us  [run(): gram = gram + self.near(gram, 1)]
  transfers between devices with their start and end apart: 27 -> 18, of which waited for: 9 -> 9; matrix products, arithmetic and copies ran while one was open for 5% -> 3% of each run, Pallas kernels for 12% -> 11%
where the time goes in v4:
time: 101 us; the launch traced here: 100 us
  waiting for transfers between devices  47.5 us (47%)
  Pallas kernels  23.9 us (24%)
  starting transfers between devices  18.6 us (18%)
  local copies, waits for them, and re-layouts  5.69 us (6%)
  matrix products  2.36 us (2%)
  other arithmetic  1.2 us (1%)
  between operations  1.01 us (1%)
    ppermute x11, waiting for transfers between devices, send(): return lax.ppermute(array, 'rows', pairs)  43.6 us
    ppermute x11, starting transfers between devices, send(): return lax.ppermute(array, 'rows', pairs)  15.2 us
    pallas_call x1, Pallas kernels, run(): pl.pallas_call(functools.partial(last_kernel, steps, per), out_shape=(jax...  6.68 us
    unnamed x20, local copies, waits for them, and re-layouts  5.41 us
    pallas_call x1, Pallas kernels, run(): pl.pallas_call(functools.partial(cross_kernel, steps, per, 5), out_shape=...  5.24 us
    pallas_call x1, Pallas kernels, pick(): pl.pallas_call(functools.partial(pick_kernel, per), out_shape=jax.ShapeDt...  4.41 us
    ppermute x7, waiting for transfers between devices, near(): return lax.ppermute(array, 'feat', [(f, f ^ bit) for f in range(4)])  3.88 us
    ppermute x7, starting transfers between devices, near(): return lax.ppermute(array, 'feat', [(f, f ^ bit) for f in range(4)])  3.44 us
  transfers between devices with their start and end apart: 18, of which 9 were waited for; matrix products, arithmetic and copies ran while one was open for 3% of the time, Pallas kernels for 11%

profile of v4, /device:TPU:0, one launch (start us, length us, event | category | flops | bytes accessed | tf_op | source)
XLA Modules:
  0.0 100.2 jit_solution(7479079559769062426)
XLA Ops:
  0.7 0.6 pad_add_fusion.place_ref
  1.3 4.4 %shard_map.59.refs_0_ = bf16[48,6656]{1,0:T(8,128)(2,1)} custom-call(s32[3,128]{1,0:T(4,128)} %index_hbm.1, s32[3]{0:T(128)} %pad_add_fusion.place_ref, bf16[384,6144]{1,0:T(8,128)(2,1)} %refs_8_.1, f32[384,512]{1,0:T(8,128)} %refs_9_.1), custom_call_target="tpu_custom_call" | custom-call | flops 245366784 | bytes 73728 | tf_op jit(solution)/shard_map/pallas_call | solution.py:205
  5.7 3.1 %collective-permute-start = (bf16[48,6656]{1,0:T(8,128)(2,1)}, bf16[48,6656]{1,0:T(8,128)(2,1)S(1)}, u32[]{:S(2)}, u32[]{:S(2)}) collective-permute-start(bf16[48,6656]{1,0:T(8,128)(2,1)} %shard_map.59.refs_0_), channel_id=1, source_target_pairs={{0,8},{4,12},{8,0},{12,4},{16,24},{20,28},{24,16},{28,20},{1,9},{5... | collective-permute-start | bytes 1916936 | tf_op jit(solution)/shard_map/ppermute | solution.py:301
  8.8 0.7 collective-permute-start.1
  9.5 1.6 %collective-permute-start.2 = (bf16[48,6656]{1,0:T(8,128)(2,1)}, bf16[48,6656]{1,0:T(8,128)(2,1)S(1)}, u32[]{:S(2)}, u32[]{:S(2)}) collective-permute-start(bf16[48,6656]{1,0:T(8,128)(2,1)} %shard_map.59.refs_0_), channel_id=1, source_target_pairs={{0,4},{4,0},{8,12},{12,8},{16,20},{20,16},{24,28},{28,24},{1,5},{5... | collective-permute-start | bytes 1916936 | tf_op jit(solution)/shard_map/ppermute | solution.py:301
  11.1 0.1 broadcast_in_dim.27
  11.2 0.1 mul.21
  11.2 12.1 %collective-permute-done.refs_2_ = bf16[48,6656]{1,0:T(8,128)(2,1)S(1)} collective-permute-done((bf16[48,6656]{1,0:T(8,128)(2,1)}, bf16[48,6656]{1,0:T(8,128)(2,1)S(1)}, u32[]{:S(2)}, u32[]{:S(2)}) %collective-permute-start) | collective-permute-done | bytes 639008 | tf_op jit(solution)/shard_map/ppermute | solution.py:301
  23.4 2.2 %collective-permute-done.2.refs_1_ = bf16[48,6656]{1,0:T(8,128)(2,1)S(1)} collective-permute-done((bf16[48,6656]{1,0:T(8,128)(2,1)}, bf16[48,6656]{1,0:T(8,128)(2,1)S(1)}, u32[]{:S(2)}, u32[]{:S(2)}) %collective-permute-start.2) | collective-permute-done | bytes 639008 | tf_op jit(solution)/shard_map/ppermute | solution.py:301
  25.6 0.7 collective-permute-start.3
  26.3 1.6 %collective-permute-start.5 = (bf16[48,6656]{1,0:T(8,128)(2,1)S(1)}, bf16[48,6656]{1,0:T(8,128)(2,1)S(1)}, u32[]{:S(2)}, u32[]{:S(2)}) collective-permute-start(bf16[48,6656]{1,0:T(8,128)(2,1)S(1)} %collective-permute-done.refs_2_), channel_id=1, source_target_pairs={{0,4},{4,0},{8,12},{12,8},{16,20},{20,16},{24,28},{28,24},{1,5},{5... | collective-permute-start | bytes 1916936 | tf_op jit(solution)/shard_map/ppermute | solution.py:301
  27.9 1.3 %collective-permute-start.4 = (bf16[48,6656]{1,0:T(8,128)(2,1)S(1)}, bf16[48,6656]{1,0:T(8,128)(2,1)S(1)}, u32[]{:S(2)}, u32[]{:S(2)}) collective-permute-start(bf16[48,6656]{1,0:T(8,128)(2,1)S(1)} %collective-permute-done.1.refs_6_), channel_id=1, source_target_pairs={{8,0},{12,4},{16,24},{20,28},{9,1},{13,5},{17,25},{21,29},{10,2},{... | collective-permute-start | bytes 1916936 | tf_op jit(solution)/shard_map/ppermute | solution.py:301
  29.2 0.1 iota_compare_fusion
  29.3 0.2 fusion
  29.5 0.7 collective-permute-start.8
  30.3 17.1 %collective-permute-done.4 = bf16[48,6656]{1,0:T(8,128)(2,1)S(1)} collective-permute-done((bf16[48,6656]{1,0:T(8,128)(2,1)S(1)}, bf16[48,6656]{1,0:T(8,128)(2,1)S(1)}, u32[]{:S(2)}, u32[]{:S(2)}) %collective-permute-start.4) | collective-permute-done | bytes 639008 | tf_op jit(solution)/shard_map/ppermute | solution.py:301
  47.4 1.3 %collective-permute-start.7 = (bf16[48,6656]{1,0:T(8,128)(2,1)S(1)}, bf16[48,6656]{1,0:T(8,128)(2,1)S(1)}, u32[]{:S(2)}, u32[]{:S(2)}) collective-permute-start(bf16[48,6656]{1,0:T(8,128)(2,1)S(1)} %collective-permute-done.3), channel_id=1, source_target_pairs={{8,0},{12,4},{16,24},{20,28},{9,1},{13,5},{17,25},{21,29},{10,2},{... | collective-permute-start | bytes 1916936 | tf_op jit(solution)/shard_map/ppermute | solution.py:301
  48.7 0.1 broadcast_select_fusion.refs_4_
  48.8 0.6 collective-permute-start.6
  49.3 0.1 select_reduce_fusion
  49.5 2.3 %copy-done = bf16[384,6144]{1,0:T(8,128)(2,1)S(1)} copy-done((bf16[384,6144]{1,0:T(8,128)(2,1)S(1)}, bf16[384,6144]{1,0:T(8,128)(2,1)}, u32[]{:S(2)}) %copy-start) | copy-done | bytes 4718616
  51.8 1.1 %copy-done.1 = bf16[48,6656]{1,0:T(8,128)(2,1)S(1)} copy-done((bf16[48,6656]{1,0:T(8,128)(2,1)S(1)}, bf16[48,6656]{1,0:T(8,128)(2,1)}, u32[]{:S(2)}) %copy-start.1) | copy-done | bytes 639000
  52.9 2.8 %shard_map.60 = f32[240,384]{1,0:T(8,128)S(1)} custom-call(bf16[48,6656]{1,0:T(8,128)(2,1)S(1)} %copy-done.1, bf16[48,6656]{1,0:T(8,128)(2,1)S(1)} %collective-permute-done.2.refs_1_, bf16[48,6656]{1,0:T(8,128)(2,1)S(1)} %collective-permute-done.refs_2_, bf16[48,6656]{1,0:T(8,128)(2,1)S(1)} %collective-permute-done.5.refs_3_, ...), custom_call_target="tpu_custom_call" | custom-call | flops 1132462080 | bytes 368640 | tf_op jit(solution)/shard_map/pallas_call | solution.py:326
  55.8 0.2 fusion.2
  56.0 1.4 %collective-permute-done.9 = f32[240,384]{1,0:T(8,128)S(1)} collective-permute-done((f32[240,384]{1,0:T(8,128)S(1)}, f32[240,384]{1,0:T(8,128)S(1)}, u32[]{:S(2)}, u32[]{:S(2)}) %collective-permute-start.9) | collective-permute-done | bytes 368672 | tf_op jit(solution)/shard_map/ppermute | solution.py:298
  57.5 5.1 %collective-permute-done.6.refs_5_ = bf16[48,6656]{1,0:T(8,128)(2,1)S(1)} collective-permute-done((bf16[48,6656]{1,0:T(8,128)(2,1)S(1)}, bf16[48,6656]{1,0:T(8,128)(2,1)S(1)}, u32[]{:S(2)}, u32[]{:S(2)}) %collective-permute-start.6) | collective-permute-done | bytes 639008 | tf_op jit(solution)/shard_map/ppermute | solution.py:301
  62.5 0.4 collective-permute-done.7.refs_7_
  63.0 5.2 %shard_map.62 = f32[224,384]{1,0:T(8,128)S(1)} custom-call(s32[3]{0:T(128)S(1)} %copy-done.7, bf16[48,6656]{1,0:T(8,128)(2,1)S(1)} %copy-done.1, bf16[48,6656]{1,0:T(8,128)(2,1)S(1)} %collective-permute-done.2.refs_1_, bf16[48,6656]{1,0:T(8,128)(2,1)S(1)} %collective-permute-done.refs_2_, bf16[48,6656]{1,0:T(8,128)(2,1)S(1)} %collective-permute-done.5.refs_3_, ...), custom_call_target="tpu_custom_call" | custom-call | flops 1056964608 | bytes 344064 | tf_op jit(solution)/shard_map/pallas_call | solution.py:342
  68.3 0.1 broadcast_compare_fusion.2
  68.5 1.3 %collective-permute-start.11 = (bf16[48,3584]{1,0:T(8,128)(2,1)S(1)}, bf16[48,3584]{1,0:T(8,128)(2,1)S(1)}, u32[]{:S(2)}, u32[]{:S(2)}) collective-permute-start(bf16[48,3584]{1,0:T(8,128)(2,1)S(1)} %slice.31), channel_id=1, source_target_pairs={{8,0},{12,4},{16,24},{20,28},{9,1},{13,5},{17,25},{21,29},{10,2},{... | collective-permute-start | bytes 1032200 | tf_op jit(solution)/shard_map/ppermute | solution.py:301
  69.8 1.6 %collective-permute-start.12 = (f32[240,384]{1,0:T(8,128)S(1)}, f32[240,384]{1,0:T(8,128)S(1)}, u32[]{:S(2)}, u32[]{:S(2)}) collective-permute-start(f32[240,384]{1,0:T(8,128)S(1)} %add.31.refs_3_), channel_id=1, source_target_pairs={{0,2},{1,3},{2,0},{3,1},{4,6},{5,7},{6,4},{7,5},{8,10},{9,11},{10,... | collective-permute-start | bytes 1105928 | tf_op jit(solution)/shard_map/ppermute | solution.py:298
  71.4 2.4 %collective-permute-start.10 = (bf16[48,3072]{1,0:T(8,128)(2,1)S(1)}, bf16[48,3072]{1,0:T(8,128)(2,1)S(1)}, u32[]{:S(2)}, u32[]{:S(2)}) collective-permute-start(bf16[48,3072]{1,0:T(8,128)(2,1)S(1)} %slice.30), channel_id=1, source_target_pairs={{0,4},{4,0},{24,28},{28,24},{1,5},{5,1},{25,29},{29,25},{2,6},{6,2... | collective-permute-start | bytes 884744 | tf_op jit(solution)/shard_map/ppermute | solution.py:301
  73.8 0.6 collective-permute-start.15
  74.4 0.3 convolution_bitcast_fusion
  74.7 1.1 %fusion.4 = f32[128,128]{1,0:T(8,128)S(1)} fusion(f32[3,128,128]{2,1,0:T(8,128)} %param.7, s32[128]{0:T(128)S(1)} %fusion.15), kind=kOutput, calls=%fused_computation.11 | convolution fusion | flops 25182208 | bytes 131584 | tf_op jit(solution)/shard_map/dot_general | solution.py:32
  75.8 6.6 %collective-permute-done.10.refs_9_ = bf16[48,3072]{1,0:T(8,128)(2,1)S(1)} collective-permute-done((bf16[48,3072]{1,0:T(8,128)(2,1)S(1)}, bf16[48,3072]{1,0:T(8,128)(2,1)S(1)}, u32[]{:S(2)}, u32[]{:S(2)}) %collective-permute-start.10) | collective-permute-done | bytes 294944 | tf_op jit(solution)/shard_map/ppermute | solution.py:301
  82.4 6.7 %shard_map.61 = (f32[48,768]{1,0:T(8,128)S(1)}, f32[384,256]{1,0:T(8,128)}) custom-call(s32[3]{0:T(128)S(1)} %copy-done.7, bf16[48,6656]{1,0:T(8,128)(2,1)S(1)} %copy-done.1, bf16[48,6656]{1,0:T(8,128)(2,1)S(1)} %collective-permute-done.2.refs_1_, bf16[48,6656]{1,0:T(8,128)(2,1)S(1)} %collective-permute-done.refs_2_, ...), custom_call_target="tpu_custom_call" | custom-call | flops 452984832 | bytes 147456 | tf_op jit(solution)/shard_map/pallas_call | solution.py:356
  89.2 0.5 collective-permute-start.16
  89.7 0.3 convolution_bitcast_fusion.1
  90.0 0.3 convolution_bitcast_fusion.2
  90.2 0.8 collective-permute-done.16
  91.1 0.6 collective-permute-start.17
  91.7 0.1 sub.11.refs_8_
  91.9 1.0 copy-done.4
  92.9 1.0 copy-done.6
  93.8 1.6 %shard_map.63 = (f32[3,128,512]{2,1,0:T(8,128)S(1)}, bf16[3,112,384]{2,1,0:T(8,128)(2,1)S(1)}, bf16[3,112,384]{2,1,0:T(8,128)(2,1)S(1)}, f32[128,384]{1,0:T(8,128)S(1)}) custom-call(s32[3]{0:T(128)S(1)} %copy-done.7, f32[384,256]{1,0:T(8,128)} %get-tuple-element.35.refs_0_, f32[384,256]{1,0:T(8,128)S(1)} %collective-permute-done.13.refs_1_, ...), custom_call_target="tpu_custom_call" | custom-call | flops 150994944 | bytes 589824 | tf_op jit(solution)/shard_map/pallas_call | solution.py:372
  95.5 1.6 %collective-permute-done.17.refs_4_ = f32[48,768]{1,0:T(8,128)S(1)} collective-permute-done((f32[48,768]{1,0:T(8,128)S(1)}, f32[48,768]{1,0:T(8,128)S(1)}, u32[]{:S(2)}, u32[]{:S(2)}) %collective-permute-start.17) | collective-permute-done | bytes 147488 | tf_op jit(solution)/shard_map/ppermute | solution.py:298
  97.1 3.1 %shard_map.64 = (f32[384,512]{1,0:T(8,128)}, f32[384,512]{1,0:T(8,128)}) custom-call(bf16[3,112,384]{2,1,0:T(8,128)(2,1)S(1)} %get-tuple-element.39.refs_0_, bf16[3,112,384]{2,1,0:T(8,128)(2,1)S(1)} %get-tuple-element.40.refs_1_, f32[128,384]{1,0:T(8,128)S(1)} %get-tuple-element.41.refs_2_, f32[48,768]{1,0:T(8,128)S(1)} %add.35.refs_3_, ...), custom_call_target="tpu_custom_call" | custom-call | flops 452984832 | bytes 1769472 | tf_op jit(solution)/shard_map/pallas_call | solution.py:453
  (39 shorter events, 0.5 us)
Async XLA Ops:
  0.6 48.7 %copy-start.9 = (s32[3,128]{1,0:T(4,128)S(1)}, s32[3,128]{1,0:T(4,128)}, u32[]{:S(2)}) copy-start(s32[3,128]{1,0:T(4,128)} %index_hbm.1) | copy-start | bytes 4612
  0.6 28.7 %copy-start.8 = (f32[3,128,128]{2,1,0:T(8,128)S(1)}, f32[3,128,128]{2,1,0:T(8,128)}, u32[]{:S(2)}) copy-start(f32[3,128,128]{2,1,0:T(8,128)} %param.7) | copy-start | bytes 589828
  5.7 17.7 %collective-permute-start = (bf16[48,6656]{1,0:T(8,128)(2,1)}, bf16[48,6656]{1,0:T(8,128)(2,1)S(1)}, u32[]{:S(2)}, u32[]{:S(2)}) collective-permute-start(bf16[48,6656]{1,0:T(8,128)(2,1)} %shard_map.59.refs_0_), channel_id=1, source_target_pairs={{0,8},{4,12},{8,0},{12,4},{16,24},{20,28},{24,16},{28,20},{1,9},{5... | collective-permute-start | bytes 1916936 | tf_op jit(solution)/shard_map/ppermute | solution.py:301
  8.8 14.6 %collective-permute-start.1 = (bf16[48,6656]{1,0:T(8,128)(2,1)}, bf16[48,6656]{1,0:T(8,128)(2,1)S(1)}, u32[]{:S(2)}, u32[]{:S(2)}) collective-permute-start(bf16[48,6656]{1,0:T(8,128)(2,1)} %shard_map.59.refs_0_), channel_id=1, source_target_pairs={{8,16},{12,20},{16,8},{20,12},{9,17},{13,21},{17,9},{21,13},{10,18... | collective-permute-start | bytes 1916936 | tf_op jit(solution)/shard_map/ppermute | solution.py:301
  9.5 16.1 %collective-permute-start.2 = (bf16[48,6656]{1,0:T(8,128)(2,1)}, bf16[48,6656]{1,0:T(8,128)(2,1)S(1)}, u32[]{:S(2)}, u32[]{:S(2)}) collective-permute-start(bf16[48,6656]{1,0:T(8,128)(2,1)} %shard_map.59.refs_0_), channel_id=1, source_target_pairs={{0,4},{4,0},{8,12},{12,8},{16,20},{20,16},{24,28},{28,24},{1,5},{5... | collective-permute-start | bytes 1916936 | tf_op jit(solution)/shard_map/ppermute | solution.py:301
  25.6 4.6 %collective-permute-start.3 = (bf16[48,6656]{1,0:T(8,128)(2,1)S(1)}, bf16[48,6656]{1,0:T(8,128)(2,1)S(1)}, u32[]{:S(2)}, u32[]{:S(2)}) collective-permute-start(bf16[48,6656]{1,0:T(8,128)(2,1)S(1)} %collective-permute-done.refs_2_), channel_id=1, source_target_pairs={{8,16},{12,20},{16,8},{20,12},{9,17},{13,21},{17,9},{21,13},{10,18... | collective-permute-start | bytes 1916936 | tf_op jit(solution)/shard_map/ppermute | solution.py:301
  26.3 21.1 %collective-permute-start.5 = (bf16[48,6656]{1,0:T(8,128)(2,1)S(1)}, bf16[48,6656]{1,0:T(8,128)(2,1)S(1)}, u32[]{:S(2)}, u32[]{:S(2)}) collective-permute-start(bf16[48,6656]{1,0:T(8,128)(2,1)S(1)} %collective-permute-done.refs_2_), channel_id=1, source_target_pairs={{0,4},{4,0},{8,12},{12,8},{16,20},{20,16},{24,28},{28,24},{1,5},{5... | collective-permute-start | bytes 1916936 | tf_op jit(solution)/shard_map/ppermute | solution.py:301
  27.9 19.5 %collective-permute-start.4 = (bf16[48,6656]{1,0:T(8,128)(2,1)S(1)}, bf16[48,6656]{1,0:T(8,128)(2,1)S(1)}, u32[]{:S(2)}, u32[]{:S(2)}) collective-permute-start(bf16[48,6656]{1,0:T(8,128)(2,1)S(1)} %collective-permute-done.1.refs_6_), channel_id=1, source_target_pairs={{8,0},{12,4},{16,24},{20,28},{9,1},{13,5},{17,25},{21,29},{10,2},{... | collective-permute-start | bytes 1916936 | tf_op jit(solution)/shard_map/ppermute | solution.py:301
  29.5 27.9 %collective-permute-start.8 = (bf16[48,6656]{1,0:T(8,128)(2,1)S(1)}, bf16[48,6656]{1,0:T(8,128)(2,1)S(1)}, u32[]{:S(2)}, u32[]{:S(2)}) collective-permute-start(bf16[48,6656]{1,0:T(8,128)(2,1)S(1)} %collective-permute-done.2.refs_1_), channel_id=1, source_target_pairs={{8,16},{12,20},{16,8},{20,12},{9,17},{13,21},{17,9},{21,13},{10,18... | collective-permute-start | bytes 1916936 | tf_op jit(solution)/shard_map/ppermute | solution.py:301
  47.4 15.6 %collective-permute-start.7 = (bf16[48,6656]{1,0:T(8,128)(2,1)S(1)}, bf16[48,6656]{1,0:T(8,128)(2,1)S(1)}, u32[]{:S(2)}, u32[]{:S(2)}) collective-permute-start(bf16[48,6656]{1,0:T(8,128)(2,1)S(1)} %collective-permute-done.3), channel_id=1, source_target_pairs={{8,0},{12,4},{16,24},{20,28},{9,1},{13,5},{17,25},{21,29},{10,2},{... | collective-permute-start | bytes 1916936 | tf_op jit(solution)/shard_map/ppermute | solution.py:301
  48.8 13.8 %collective-permute-start.6 = (bf16[48,6656]{1,0:T(8,128)(2,1)S(1)}, bf16[48,6656]{1,0:T(8,128)(2,1)S(1)}, u32[]{:S(2)}, u32[]{:S(2)}) collective-permute-start(bf16[48,6656]{1,0:T(8,128)(2,1)S(1)} %broadcast_select_fusion.refs_4_), channel_id=1, source_target_pairs={{0,4},{4,0},{8,12},{12,8},{16,20},{20,16},{24,28},{28,24},{1,5},{5... | collective-permute-start | bytes 1916936 | tf_op jit(solution)/shard_map/ppermute | solution.py:301
  49.5 2.3 %copy-start = (bf16[384,6144]{1,0:T(8,128)(2,1)S(1)}, bf16[384,6144]{1,0:T(8,128)(2,1)}, u32[]{:S(2)}) copy-start(bf16[384,6144]{1,0:T(8,128)(2,1)} %refs_8_.1) | copy-start | bytes 14155780
  51.8 1.1 %copy-start.1 = (bf16[48,6656]{1,0:T(8,128)(2,1)S(1)}, bf16[48,6656]{1,0:T(8,128)(2,1)}, u32[]{:S(2)}) copy-start(bf16[48,6656]{1,0:T(8,128)(2,1)} %shard_map.59.refs_0_) | copy-start | bytes 1916932
  52.9 10.1 %copy-start.7 = (s32[3]{0:T(128)S(1)}, s32[3]{0:T(128)}, u32[]{:S(2)}) copy-start(s32[3]{0:T(128)} %pad_add_fusion.place_ref) | copy-start | bytes 40
  55.7 1.8 %collective-permute-start.9 = (f32[240,384]{1,0:T(8,128)S(1)}, f32[240,384]{1,0:T(8,128)S(1)}, u32[]{:S(2)}, u32[]{:S(2)}) collective-permute-start(f32[240,384]{1,0:T(8,128)S(1)} %shard_map.60), channel_id=1, source_target_pairs={{0,1},{1,0},{2,3},{3,2},{4,5},{5,4},{6,7},{7,6},{8,9},{9,8},{10,11... | collective-permute-start | bytes 1105928 | tf_op jit(solution)/shard_map/ppermute | solution.py:298
  68.2 5.5 %collective-permute-start.14 = (f32[224,384]{1,0:T(8,128)S(1)}, f32[224,384]{1,0:T(8,128)S(1)}, u32[]{:S(2)}, u32[]{:S(2)}) collective-permute-start(f32[224,384]{1,0:T(8,128)S(1)} %shard_map.62), channel_id=1, source_target_pairs={{0,1},{1,0},{2,3},{3,2},{4,5},{5,4},{6,7},{7,6},{8,9},{9,8},{10,11... | collective-permute-start | bytes 1032200 | tf_op jit(solution)/shard_map/ppermute | solution.py:298
  68.5 13.9 %collective-permute-start.11 = (bf16[48,3584]{1,0:T(8,128)(2,1)S(1)}, bf16[48,3584]{1,0:T(8,128)(2,1)S(1)}, u32[]{:S(2)}, u32[]{:S(2)}) collective-permute-start(bf16[48,3584]{1,0:T(8,128)(2,1)S(1)} %slice.31), channel_id=1, source_target_pairs={{8,0},{12,4},{16,24},{20,28},{9,1},{13,5},{17,25},{21,29},{10,2},{... | collective-permute-start | bytes 1032200 | tf_op jit(solution)/shard_map/ppermute | solution.py:301
  69.8 12.6 %collective-permute-start.12 = (f32[240,384]{1,0:T(8,128)S(1)}, f32[240,384]{1,0:T(8,128)S(1)}, u32[]{:S(2)}, u32[]{:S(2)}) collective-permute-start(f32[240,384]{1,0:T(8,128)S(1)} %add.31.refs_3_), channel_id=1, source_target_pairs={{0,2},{1,3},{2,0},{3,1},{4,6},{5,7},{6,4},{7,5},{8,10},{9,11},{10,... | collective-permute-start | bytes 1105928 | tf_op jit(solution)/shard_map/ppermute | solution.py:298
  71.4 11.0 %collective-permute-start.10 = (bf16[48,3072]{1,0:T(8,128)(2,1)S(1)}, bf16[48,3072]{1,0:T(8,128)(2,1)S(1)}, u32[]{:S(2)}, u32[]{:S(2)}) collective-permute-start(bf16[48,3072]{1,0:T(8,128)(2,1)S(1)} %slice.30), channel_id=1, source_target_pairs={{0,4},{4,0},{24,28},{28,24},{1,5},{5,1},{25,29},{29,25},{2,6},{6,2... | collective-permute-start | bytes 884744 | tf_op jit(solution)/shard_map/ppermute | solution.py:301
  73.8 15.3 %collective-permute-start.15 = (f32[224,384]{1,0:T(8,128)S(1)}, f32[224,384]{1,0:T(8,128)S(1)}, u32[]{:S(2)}, u32[]{:S(2)}) collective-permute-start(f32[224,384]{1,0:T(8,128)S(1)} %add.34.refs_5_), channel_id=1, source_target_pairs={{0,2},{1,3},{2,0},{3,1},{4,6},{5,7},{6,4},{7,5},{8,10},{9,11},{10,... | collective-permute-start | bytes 1032200 | tf_op jit(solution)/shard_map/ppermute | solution.py:298
  75.8 21.3 %copy-start.2 = (f32[384,512]{1,0:T(8,128)S(1)}, f32[384,512]{1,0:T(8,128)}, u32[]{:S(2)}) copy-start(f32[384,512]{1,0:T(8,128)} %refs_9_.1) | copy-start | bytes 2359300
  82.4 6.7 %copy-start.3 = (f32[240,384]{1,0:T(8,128)}, f32[240,384]{1,0:T(8,128)S(1)}, u32[]{:S(2)}) copy-start(f32[240,384]{1,0:T(8,128)S(1)} %collective-permute-done.12.refs_4_) | copy-start | bytes 1105924
  89.1 2.8 %collective-permute-start.13 = (f32[384,256]{1,0:T(8,128)}, f32[384,256]{1,0:T(8,128)S(1)}, u32[]{:S(2)}, u32[]{:S(2)}) collective-permute-start(f32[384,256]{1,0:T(8,128)} %get-tuple-element.35.refs_0_), channel_id=1, source_target_pairs={{0,1},{1,0},{2,3},{3,2},{4,5},{5,4},{6,7},{7,6},{8,9},{9,8},{10,11... | collective-permute-start | bytes 1179656 | tf_op jit(solution)/shard_map/ppermute | solution.py:298
  89.2 1.9 %copy-start.5 = (f32[224,384]{1,0:T(8,128)}, f32[224,384]{1,0:T(8,128)S(1)}, u32[]{:S(2)}) copy-start(f32[224,384]{1,0:T(8,128)S(1)} %collective-permute-done.15.refs_6_) | copy-start | bytes 1032196
  89.2 1.9 %collective-permute-start.16 = (f32[48,768]{1,0:T(8,128)S(1)}, f32[48,768]{1,0:T(8,128)S(1)}, u32[]{:S(2)}, u32[]{:S(2)}) collective-permute-start(f32[48,768]{1,0:T(8,128)S(1)} %get-tuple-element.42), channel_id=1, source_target_pairs={{0,1},{1,0},{2,3},{3,2},{4,5},{5,4},{6,7},{7,6},{8,9},{9,8},{10,11... | collective-permute-start | bytes 442376 | tf_op jit(solution)/shard_map/ppermute | solution.py:298
  91.1 6.0 %collective-permute-start.17 = (f32[48,768]{1,0:T(8,128)S(1)}, f32[48,768]{1,0:T(8,128)S(1)}, u32[]{:S(2)}, u32[]{:S(2)}) collective-permute-start(f32[48,768]{1,0:T(8,128)S(1)} %add.35.refs_3_), channel_id=1, source_target_pairs={{0,2},{1,3},{2,0},{3,1},{4,6},{5,7},{6,4},{7,5},{8,10},{9,11},{10,... | collective-permute-start | bytes 442376 | tf_op jit(solution)/shard_map/ppermute | solution.py:298
  91.9 1.0 copy-start.4
  92.9 1.0 copy-start.6

commit v5 on v4

--- a/solution.py
+++ b/solution.py
@@ -14,7 +14,7 @@
 PIECES = 4
 PARAMS = pltpu.CompilerParams(vmem_limit_bytes=24 * 1024 * 1024)
 PICK = pltpu.CompilerParams(vmem_limit_bytes=58 * 1024 * 1024)
-GRAM = pltpu.CompilerParams(vmem_limit_bytes=46 * 1024 * 1024)
+GRAM = pltpu.CompilerParams(vmem_limit_bytes=48 * 1024 * 1024)
 
 
 def quadratic(gram):
@@ -70,9 +70,8 @@
 def finish_kernel(steps, per, last, *refs):
     refs = list(refs)
     if last:
-        high_ref, low_ref, cross_ref = refs[:3]
-        end = refs[3][...] + refs[4][...]
-        refs = refs[5:]
+        place_ref, high_ref, low_ref, cross_ref, mine_ref, other_ref = refs[:6]
+        refs = refs[6:]
     else:
         gram_ref, cross_ref = refs[:2]
         refs = refs[2:]
@@ -80,13 +79,21 @@
     block = first_ref.shape[1]
     rows = targets_ref.shape[0]
     if last:
-        column = lax.broadcasted_iota(jnp.int32, (block, block), 0) < block - per
-        end_gram = quadratic(end[:, :rows])
-        end = end[:, rows:]
+        core = place_ref[1]
+        mine, other = mine_ref[...], other_ref[...]
+        end_gram = quadratic(jnp.where(core == 0, mine, other))
+        end = jnp.where(core == 0, other, mine)
+        count = steps * per
+        begun = block - end.shape[0] // steps
+        column = lax.broadcasted_iota(jnp.int32, (block, block), 0) < begun
+
+        def end_of(array, step):
+            slots = [array[i : i + count] for i in range(0, array.shape[0], count)]
+            return of_step(slots, step, per)
 
         def of(one, other):
-            part = end[one * per : (one + 1) * per, other * block : (other + 1) * block]
-            return jnp.concatenate([jnp.zeros((block - per, block), jnp.float32), part], axis=0)
+            part = end_of(end, one)[:, other * block : (other + 1) * block]
+            return jnp.concatenate([jnp.zeros((begun, block), jnp.float32), part], axis=0)
 
     between = {}
     for at, (step, before) in enumerate(pairs_of(steps)):
@@ -114,7 +121,7 @@
     coeff_ref[...] = coeffs
     for step in range(steps):
         if last:
-            part = split(end_gram[step * per : (step + 1) * per])
+            part = split(end_of(end_gram, step))
             kernel = tuple(
                 jnp.concatenate([ref[step], one], axis=0) for ref, one in zip((high_ref, low_ref), part)
             )
@@ -136,12 +143,11 @@
         first_ref[step, :, :half] = fine_dot(inverse, jnp.where(core == 0, mine, other))
         first_ref[step, :, half:] = fine_dot(inverse, jnp.where(core == 0, other, mine))
     gram = gram_refs[0][...] + gram_refs[1][...]
-    second = gram_refs[2][...] + gram_refs[3][...]
-    cross_ref[...] = second[-block:]
-    kernel = quadratic(jnp.concatenate([gram, second[:-block]], axis=0))
+    cross_ref[...] = gram[-block:]
+    kernel = quadratic(gram[:-block])
     kernel = kernel.reshape(-1, steps, per, kernel.shape[-1])
     for step in range(steps):
-        high_ref[step], low_ref[step] = split(kernel[:, step].reshape(block - per, -1))
+        high_ref[step], low_ref[step] = split(kernel[:, step].reshape(high_ref.shape[1:]))
 
 
 def pieces_of(features_ref):
@@ -170,9 +176,9 @@
 ):
     index = pltpu.make_async_copy(index_hbm, index_ref, side_sems.at[0])
     index.start()
-    copies = fetch(features_ref, held_ref, sems)
     side = pltpu.make_async_copy(targets_ref, held_targets, side_sems.at[1])
     side.start()
+    copies = fetch(features_ref, held_ref, sems)
     index.wait()
     rank, core = place_ref[0], place_ref[1]
     rows, columns = features_ref.shape
@@ -188,15 +194,15 @@
     def take(array):
         return jnp.dot(chosen, array, preferred_element_type=jnp.float32).astype(jnp.bfloat16)
 
-    for copy, at in zip(copies, pieces_of(features_ref)):
-        copy.wait()
-        out_ref[:, at] = take(held_ref[:, at])
     side.wait()
     width = targets_ref.shape[1] // 2
     values = jnp.where(core == 0, held_targets[:, :width], held_targets[:, width:])
     high, low = split(values)
     out_ref[:, columns : columns + width] = take(high)
     out_ref[:, columns + width :] = take(low)
+    for copy, at in zip(copies, pieces_of(features_ref)):
+        copy.wait()
+        out_ref[:, at] = take(held_ref[:, at])
 
 
 def pick(block_index, place, features, targets, per):
@@ -218,43 +224,35 @@
     )(block_index, place, features, targets)
 
 
-def gram_kernel(*refs):
+def gram_kernel(steps, per, missing, *refs):
     *slot_refs, features_ref, out_ref, held_ref, sems = refs
-    total = None
-    for copy, at in zip(fetch(features_ref, held_ref, sems), pieces_of(features_ref)):
+    copies = fetch(features_ref, held_ref, sems)
+    total = [None] * (1 + len(pairs_of(steps)))
+    for at in pieces_of(features_ref):
+        slots = [ref[:, at] for ref in slot_refs]
+        slots += [jnp.zeros_like(slots[0])] * missing
+        rows = [of_step(slots, step, per) for step in range(steps)]
+        for i, (step, before) in enumerate(pairs_of(steps)):
+            total[1 + i] = add(total[1 + i], dot_rows(rows[step], rows[before]))
+    for copy, at in zip(copies, pieces_of(features_ref)):
         slots = jnp.concatenate([ref[:, at] for ref in slot_refs], axis=0)
         copy.wait()
-        total = add(total, dot_rows(slots, held_ref[:, at]))
-    out_ref[...] = total
-
-
-def cross_kernel(steps, per, count, place_ref, *refs):
-    *slot_refs, features_ref, out_ref, held_ref, sems = refs
-    inner = place_ref[2] == 1
-    total = [None] * (1 + len(pairs_of(steps)))
-    copies = fetch(features_ref, held_ref, sems)
-    for copy, at in zip(copies, pieces_of(features_ref)):
-        slots = [ref[:, at] for ref in slot_refs]
-        other = slots.pop()
-        slots[-1] = jnp.where(inner, slots[-1], other)
-        rows = [of_step(slots + [jnp.zeros_like(other)], step, per) for step in range(steps)]
-        for i, (step, before) in enumerate(pairs_of(steps)):
-            total[1 + i] = add(total[1 + i], dot_rows(rows[step], rows[before]))
-        copy.wait()
-        total[0] = add(total[0], dot_rows(jnp.concatenate(slots[count:], axis=0), held_ref[:, at]))
+        total[0] = add(total[0], dot_rows(slots, held_ref[:, at]))
     new = total[0].shape[0]
     out_ref[:new] = total[0]
     out_ref[new:] = jnp.concatenate(total[1:], axis=1)
 
 
-def last_kernel(steps, per, place_ref, *refs):
-    *slot_refs, inner_ref, left_ref, right_ref, features_ref, out_ref, first_ref, held_ref, sems = refs
+def last_kernel(steps, per, begun, place_ref, *refs):
+    *slot_refs, inner_ref, left_ref, right_ref, features_ref = refs[:-5]
+    keep_ref, send_ref, first_ref, held_ref, sems = refs[-5:]
+    core = place_ref[1]
     inner = place_ref[2] == 1
     columns = features_ref.shape[1]
     half = left_ref.shape[1]
     copies = fetch(features_ref, held_ref, sems)
 
-    def every(at):
+    def slots_at(at):
         slots = [ref[:, at] for ref in slot_refs]
         other = slots.pop()
         slots[-1] = jnp.where(inner, slots[-1], other)
@@ -262,22 +260,25 @@
             last = left_ref[:, at]
         else:
             last = right_ref[:, at.start - half : at.stop - half]
-        last = jnp.where(inner, inner_ref[:, at], last)
-        rows = [of_step(slots + [last], step, per) for step in range(steps)]
-        return last, jnp.concatenate(rows, axis=0)
+        return slots + [jnp.where(inner, inner_ref[:, at], last)]
+
+    def every(slots):
+        return jnp.concatenate([of_step(slots, step, per) for step in range(steps)], axis=0)
 
     total, cross = None, None
+    for at in pieces_of(features_ref):
+        slots = slots_at(at)
+        cross = add(cross, dot_rows(every(slots), jnp.concatenate(slots[begun:], axis=0)))
     for copy, at in zip(copies, pieces_of(features_ref)):
-        last, rows = every(at)
-        cross = add(cross, dot_rows(rows, last))
+        new = jnp.concatenate(slots_at(at)[begun:], axis=0)
         copy.wait()
-        total = add(total, dot_rows(held_ref[:, at], last))
-    wide = features_ref.shape[0]
-    out_ref[:, :wide] = total.T
-    out_ref[:, wide:] = cross.T
+        total = add(total, dot_rows(held_ref[:, at], new))
+    total, cross = total.T, cross.T
+    keep_ref[...] = jnp.where(core == 0, total, cross)
+    send_ref[...] = jnp.where(core == 0, cross, total)
     width = (inner_ref.shape[1] - columns) // 2
-    high = every(slice(columns, columns + width))[1]
-    low = every(slice(columns + width, columns + 2 * width))[1]
+    high = every(slots_at(slice(columns, columns + width)))
+    low = every(slots_at(slice(columns + width, columns + 2 * width)))
     first_ref[...] = high.astype(jnp.float32) + low.astype(jnp.float32)
 
 
@@ -316,21 +317,22 @@
         far = self.send(pair, self.inner)
         mid_end = self.send(mid, self.outer)
         pair_b = self.send(pair, self.beside)
-        far, mid_end, pair_b = hold((far, mid_end, pair_b))
+        far, mid_end, pair_b, own_b = hold((far, mid_end, pair_b, own_b))
 
         third = jnp.where(self.is_inner, far, mid_end)
         third_b = self.send(third, self.beside)
         far_end = self.send(far, self.outer)
         last_in = self.send(own_b, self.inner)
         slots = [own, own_b, pair, pair_b, third]
+        begun = len(slots)
         gram = pl.pallas_call(
-            gram_kernel,
-            out_shape=jax.ShapeDtypeStruct((5 * count, rows), jnp.float32),
-            in_specs=[VMEM] * len(slots) + [HBM],
+            functools.partial(gram_kernel, steps, per, 8 - begun),
+            out_shape=jax.ShapeDtypeStruct((begun * count + block, rows), jnp.float32),
+            in_specs=[VMEM] * begun + [HBM],
             out_specs=VMEM,
             scratch_shapes=held(features),
             compiler_params=GRAM,
-            cost_estimate=cost(5 * count * rows, columns),
+            cost_estimate=cost((begun * count + block) * rows, columns),
         )(*slots, features)
         gram = gram + self.near(gram, 1)
         third_b, far_end, last_in, gram = hold((third_b, far_end, last_in, gram))
@@ -338,37 +340,26 @@
         left = self.send(far_end[:, :half], self.ends)
         right = self.send(third_b[:, half:], self.outer)
         gram_near = self.near(gram, 2)
-        slots = slots + [third_b, mid, far_end]
-        second = pl.pallas_call(
-            functools.partial(cross_kernel, steps, per, 5),
-            out_shape=jax.ShapeDtypeStruct((2 * count + block, rows), jnp.float32),
-            in_specs=[SMEM] + [VMEM] * len(slots) + [HBM],
-            out_specs=VMEM,
-            scratch_shapes=held(features),
-            compiler_params=GRAM,
-            cost_estimate=cost((2 * count + block) * rows, columns),
-        )(self.place, *slots, features)
-        second = second + self.near(second, 1)
         left, right, gram_near = hold((left, right, gram_near))
 
-        second_near = self.near(second, 2)
-        slots = slots + [last_in, left, right]
-        last, first = pl.pallas_call(
-            functools.partial(last_kernel, steps, per),
+        slots = slots + [third_b, mid, far_end, last_in, left, right]
+        end = jax.ShapeDtypeStruct(((8 - begun) * count, rows), jnp.float32)
+        keep, given, first = pl.pallas_call(
+            functools.partial(last_kernel, steps, per, begun),
             out_shape=(
-                jax.ShapeDtypeStruct((count, rows + steps * block), jnp.float32),
+                end,
+                end,
                 jax.ShapeDtypeStruct((steps * block, targets.shape[1] // 2), jnp.float32),
             ),
             in_specs=[SMEM] + [VMEM] * len(slots) + [HBM],
-            out_specs=(VMEM, VMEM),
+            out_specs=(VMEM,) * 3,
             scratch_shapes=held(features),
             compiler_params=GRAM,
-            cost_estimate=cost(count * (rows + steps * block), columns),
+            cost_estimate=cost((8 - begun) * count * (rows + steps * block), columns),
         )(self.place, *slots, features)
-        last, second_near = hold((last, second_near))
-        last = last + self.near(last, 1)
-        last_near = self.near(last, 2)
-        parts = (steps, block - per, rows)
+        keep = keep + self.near(given, 1)
+        keep = keep + self.near(keep, 2)
+        parts = (steps, begun * per, rows)
         first, high, low, cross = pl.pallas_call(
             functools.partial(ready_kernel, steps, per),
             out_shape=(
@@ -377,12 +368,12 @@
                 jax.ShapeDtypeStruct(parts, jnp.bfloat16),
                 jax.ShapeDtypeStruct((block, rows), jnp.float32),
             ),
-            in_specs=[SMEM] + [VMEM] * 7,
+            in_specs=[SMEM] + [VMEM] * 5,
             out_specs=(VMEM,) * 4,
             compiler_params=PARAMS,
             cost_estimate=cost(3 * steps * block * block, targets.shape[1]),
-        )(self.place, first, self.near(first, 1), turned, gram, gram_near, second, second_near)
-        return [high, low, cross, last, last_near], first
+        )(self.place, first, self.near(first, 1), turned, gram, gram_near)
+        return [self.place, high, low, cross, keep, self.near(keep, 1)], first
 
 
 class Gathers:
@@ -451,9 +442,9 @@
     operands = sums + [same, first, turned, own, targets]
     out = jax.ShapeDtypeStruct(targets.shape, jnp.float32)
     return pl.pallas_call(
-        functools.partial(finish_kernel, steps, per, len(sums) > 2),
+        functools.partial(finish_kernel, steps, per, lined),
         out_shape=(out, out),
-        in_specs=[VMEM] * len(operands),
+        in_specs=([SMEM] if lined else []) + [VMEM] * (len(operands) - lined),
         out_specs=(VMEM, VMEM),
         compiler_params=PARAMS,
         cost_estimate=cost(3 * rows * steps * block, targets.shape[1]),

time: 101 us -> 110 us (1.089)
  the two profiles are of different devices: /device:TPU:0 before, /device:TPU:13 now
where the time goes in v5:
time: 110 us; the launch traced here: 109 us
  waiting for transfers between devices  34.8 us (32%)
  starting transfers between devices  30.9 us (28%)
  Pallas kernels  22.9 us (21%)
  local copies, waits for them, and re-layouts  7.52 us (7%)
  matrix products  6.57 us (6%)
  other arithmetic  5.35 us (5%)
    ppermute x11, waiting for transfers between devices, send(): return lax.ppermute(array, 'rows', pairs)  25.7 us
    ppermute x11, starting transfers between devices, send(): return lax.ppermute(array, 'rows', pairs)  18.4 us
    ppermute x6, starting transfers between devices, near(): return lax.ppermute(array, 'feat', [(f, f ^ bit) for f in range(4)])  12.5 us
    ppermute x6, waiting for transfers between devices, near(): return lax.ppermute(array, 'feat', [(f, f ^ bit) for f in range(4)])  9.1 us
    pallas_call x1, Pallas kernels, run(): pl.pallas_call(functools.partial(last_kernel, steps, per, begun), out_sha...  7.54 us
    dot_general x6, matrix products, exact_dot(): jnp.dot(left, right, precision=lax.Precision.HIGHEST, preferred_element_t...  6.57 us
    unnamed x28, local copies, waits for them, and re-layouts  5.51 us
    pallas_call x1, Pallas kernels, pick(): pl.pallas_call(functools.partial(pick_kernel, per), out_shape=jax.ShapeDt...  5.25 us
  transfers between devices with their start and end apart: 17, of which 8 were waited for; matrix products, arithmetic and copies ran while one was open for 12% of the time, Pallas kernels for 6%

profile of v5, /device:TPU:13, one launch (start us, length us, event | category | flops | bytes accessed | tf_op | source)
XLA Modules:
  0.0 109.0 jit_solution(6041898640523831669)
XLA Ops:
  0.7 0.6 pad_add_fusion.place_ref.refs_0_
  1.3 5.3 %shard_map.59.refs_0_ = bf16[48,6656]{1,0:T(8,128)(2,1)} custom-call(s32[3,128]{1,0:T(4,128)} %index_hbm.1, s32[3]{0:T(128)} %pad_add_fusion.place_ref.refs_0_, bf16[384,6144]{1,0:T(8,128)(2,1)} %refs_11_.1, f32[384,512]{1,0:T(8,128)} %refs_10_.1), custom_call_target="tpu_custom_call" | custom-call | flops 245366784 | bytes 73728 | tf_op jit(solution)/shard_map/pallas_call | solution.py:211
  6.8 4.3 %collective-permute-start.1 = (bf16[48,6656]{1,0:T(8,128)(2,1)}, bf16[48,6656]{1,0:T(8,128)(2,1)S(1)}, u32[]{:S(2)}, u32[]{:S(2)}) collective-permute-start(bf16[48,6656]{1,0:T(8,128)(2,1)} %shard_map.59.refs_0_), channel_id=1, source_target_pairs={{8,16},{12,20},{16,8},{20,12},{9,17},{13,21},{17,9},{21,13},{10,18... | collective-permute-start | bytes 1916936 | tf_op jit(solution)/shard_map/ppermute | solution.py:302
  11.1 0.3 collective-permute-start.2
  11.4 10.7 %collective-permute-done.refs_2_ = bf16[48,6656]{1,0:T(8,128)(2,1)S(1)} collective-permute-done((bf16[48,6656]{1,0:T(8,128)(2,1)}, bf16[48,6656]{1,0:T(8,128)(2,1)S(1)}, u32[]{:S(2)}, u32[]{:S(2)}) %collective-permute-start) | collective-permute-done | bytes 639008 | tf_op jit(solution)/shard_map/ppermute | solution.py:302
  22.0 3.0 %collective-permute-done.1.refs_6_ = bf16[48,6656]{1,0:T(8,128)(2,1)S(1)} collective-permute-done((bf16[48,6656]{1,0:T(8,128)(2,1)}, bf16[48,6656]{1,0:T(8,128)(2,1)S(1)}, u32[]{:S(2)}, u32[]{:S(2)}) %collective-permute-start.1) | collective-permute-done | bytes 639008 | tf_op jit(solution)/shard_map/ppermute | solution.py:302
  25.1 0.9 collective-permute-done.2.refs_1_
  26.0 2.2 %collective-permute-start.3 = (bf16[48,6656]{1,0:T(8,128)(2,1)S(1)}, bf16[48,6656]{1,0:T(8,128)(2,1)}, u32[]{:S(2)}, u32[]{:S(2)}) collective-permute-start(bf16[48,6656]{1,0:T(8,128)(2,1)S(1)} %collective-permute-done.refs_2_), channel_id=1, source_target_pairs={{8,16},{12,20},{16,8},{20,12},{9,17},{13,21},{17,9},{21,13},{10,18... | collective-permute-start | bytes 1916936 | tf_op jit(solution)/shard_map/ppermute | solution.py:302
  28.2 0.3 collective-permute-start.5
  28.5 1.3 %collective-permute-start.4 = (bf16[48,6656]{1,0:T(8,128)(2,1)S(1)}, bf16[48,6656]{1,0:T(8,128)(2,1)S(1)}, u32[]{:S(2)}, u32[]{:S(2)}) collective-permute-start(bf16[48,6656]{1,0:T(8,128)(2,1)S(1)} %collective-permute-done.1.refs_6_), channel_id=1, source_target_pairs={{8,0},{12,4},{16,24},{20,28},{9,1},{13,5},{17,25},{21,29},{10,2},{... | collective-permute-start | bytes 1916936 | tf_op jit(solution)/shard_map/ppermute | solution.py:302
  29.8 0.8 copy-done.5
  31.1 10.6 %collective-permute-done.3 = bf16[48,6656]{1,0:T(8,128)(2,1)} collective-permute-done((bf16[48,6656]{1,0:T(8,128)(2,1)S(1)}, bf16[48,6656]{1,0:T(8,128)(2,1)}, u32[]{:S(2)}, u32[]{:S(2)}) %collective-permute-start.3) | collective-permute-done | bytes 639008 | tf_op jit(solution)/shard_map/ppermute | solution.py:302
  41.7 0.4 collective-permute-done.5.refs_3_
  42.1 0.4 copy-done.10
  42.5 3.7 %collective-permute-start.7 = (bf16[48,6656]{1,0:T(8,128)(2,1)}, bf16[48,6656]{1,0:T(8,128)(2,1)S(1)}, u32[]{:S(2)}, u32[]{:S(2)}) collective-permute-start(bf16[48,6656]{1,0:T(8,128)(2,1)} %collective-permute-done.3), channel_id=1, source_target_pairs={{8,0},{12,4},{16,24},{20,28},{9,1},{13,5},{17,25},{21,29},{10,2},{... | collective-permute-start | bytes 1916936 | tf_op jit(solution)/shard_map/ppermute | solution.py:302
  46.3 1.2 %broadcast_select_fusion.refs_4_ = bf16[48,6656]{1,0:T(8,128)(2,1)S(1)} fusion(bf16[48,6656]{1,0:T(8,128)(2,1)} %collective-permute-done.3, bf16[48,6656]{1,0:T(8,128)(2,1)} %copy-done.10, pred[]{:T(512)S(6)} %and.23), kind=kLoop, calls=%fused_computation.3 | loop fusion | flops 319488 | bytes 1916929 | tf_op jit(solution)/shard_map/jit(_where)/select_n | solution.py:322
  47.5 1.3 %collective-permute-start.6 = (bf16[48,6656]{1,0:T(8,128)(2,1)S(1)}, bf16[48,6656]{1,0:T(8,128)(2,1)S(1)}, u32[]{:S(2)}, u32[]{:S(2)}) collective-permute-start(bf16[48,6656]{1,0:T(8,128)(2,1)S(1)} %broadcast_select_fusion.refs_4_), channel_id=1, source_target_pairs={{0,4},{4,0},{8,12},{12,8},{16,20},{20,16},{24,28},{28,24},{1,5},{5... | collective-permute-start | bytes 1916936 | tf_op jit(solution)/shard_map/ppermute | solution.py:302
  48.8 2.8 %collective-permute-start.8 = (bf16[48,6656]{1,0:T(8,128)(2,1)S(1)}, bf16[48,6656]{1,0:T(8,128)(2,1)S(1)}, u32[]{:S(2)}, u32[]{:S(2)}) collective-permute-start(bf16[48,6656]{1,0:T(8,128)(2,1)S(1)} %collective-permute-done.2.refs_1_), channel_id=1, source_target_pairs={{8,16},{12,20},{16,8},{20,12},{9,17},{13,21},{17,9},{21,13},{10,18... | collective-permute-start | bytes 1916936 | tf_op jit(solution)/shard_map/ppermute | solution.py:302
  51.6 1.1 copy-done
  52.7 4.4 %shard_map.60 = f32[368,384]{1,0:T(8,128)S(1)} custom-call(bf16[48,6656]{1,0:T(8,128)(2,1)S(1)} %copy-done, bf16[48,6656]{1,0:T(8,128)(2,1)S(1)} %collective-permute-done.2.refs_1_, bf16[48,6656]{1,0:T(8,128)(2,1)S(1)} %collective-permute-done.refs_2_, bf16[48,6656]{1,0:T(8,128)(2,1)S(1)} %collective-permute-done.5.refs_3_, ...), custom_call_target="tpu_custom_call" | custom-call | flops 1736441856 | bytes 565248 | tf_op jit(solution)/shard_map/pallas_call | solution.py:328
  57.1 4.3 %collective-permute-start.9 = (f32[368,384]{1,0:T(8,128)S(1)}, f32[368,384]{1,0:T(8,128)S(1)}, u32[]{:S(2)}, u32[]{:S(2)}) collective-permute-start(f32[368,384]{1,0:T(8,128)S(1)} %shard_map.60), channel_id=1, source_target_pairs={{0,1},{1,0},{2,3},{3,2},{4,5},{5,4},{6,7},{7,6},{8,9},{9,8},{10,11... | collective-permute-start | bytes 1695752 | tf_op jit(solution)/shard_map/ppermute | solution.py:299
  61.4 0.9 fusion
  62.3 0.8 fusion.2
  63.1 0.9 add.31.refs_3_
  64.0 0.8 slice.31
  65.0 0.8 copy-done.3
  65.8 1.3 %collective-permute-start.11 = (bf16[48,3584]{1,0:T(8,128)(2,1)}, bf16[48,3584]{1,0:T(8,128)(2,1)S(1)}, u32[]{:S(2)}, u32[]{:S(2)}) collective-permute-start(bf16[48,3584]{1,0:T(8,128)(2,1)} %slice.31), channel_id=1, source_target_pairs={{8,0},{12,4},{16,24},{20,28},{9,1},{13,5},{17,25},{21,29},{10,2},{... | collective-permute-start | bytes 1032200 | tf_op jit(solution)/shard_map/ppermute | solution.py:302
  67.1 1.3 %collective-permute-start.12 = (f32[368,384]{1,0:T(8,128)}, f32[368,384]{1,0:T(8,128)}, u32[]{:S(2)}, u32[]{:S(2)}) collective-permute-start(f32[368,384]{1,0:T(8,128)} %add.31.refs_3_), channel_id=1, source_target_pairs={{0,2},{1,3},{2,0},{3,1},{4,6},{5,7},{6,4},{7,5},{8,10},{9,11},{10,... | collective-permute-start | bytes 1695752 | tf_op jit(solution)/shard_map/ppermute | solution.py:299
  68.4 0.7 broadcast_compare_fusion.2
  69.1 1.0 slice.30
  70.1 0.7 collective-permute-start.10
  70.7 1.8 %convolution_bitcast_fusion = f32[1,128,128]{2,1,0:T(8,128)} fusion(f32[128,128]{1,0:T(8,128)} %fusion, s32[128]{0:T(128)S(1)} %fusion.15), kind=kOutput, calls=%fused_computation | convolution fusion | flops 25182208 | bytes 131584 | tf_op jit(solution)/shard_map/dot_general | solution.py:32
  72.5 1.7 %fusion.4 = f32[128,128]{1,0:T(8,128)} fusion(f32[3,128,128]{2,1,0:T(8,128)} %param.7, s32[128]{0:T(128)S(1)} %fusion.15), kind=kOutput, calls=%fused_computation.11 | convolution fusion | flops 25182208 | bytes 131584 | tf_op jit(solution)/shard_map/dot_general | solution.py:32
  74.2 4.2 %collective-permute-done.12.refs_4_ = f32[368,384]{1,0:T(8,128)} collective-permute-done((f32[368,384]{1,0:T(8,128)}, f32[368,384]{1,0:T(8,128)}, u32[]{:S(2)}, u32[]{:S(2)}) %collective-permute-start.12) | collective-permute-done | bytes 565280 | tf_op jit(solution)/shard_map/ppermute | solution.py:299
  78.4 1.1 copy-done.4
  79.5 1.1 copy-done.6
  80.6 7.5 %shard_map.61 = (f32[144,384]{1,0:T(8,128)S(1)}, f32[144,384]{1,0:T(8,128)S(1)}, f32[384,256]{1,0:T(8,128)}) custom-call(s32[3]{0:T(128)S(1)} %copy-done.7, bf16[48,6656]{1,0:T(8,128)(2,1)S(1)} %copy-done.1, bf16[48,6656]{1,0:T(8,128)(2,1)S(1)} %collective-permute-done.2.refs_1_, bf16[48,6656]{1,0:T(8,128)(2,1)S(1)} %collective-permute-done.refs_2_, ...), custom_call_target="tpu_custom_call" | custom-call | flops 1358954496 | bytes 442368 | tf_op jit(solution)/shard_map/pallas_call | solution.py:347
  88.1 4.4 %collective-permute-start.14 = (f32[144,384]{1,0:T(8,128)S(1)}, f32[144,384]{1,0:T(8,128)S(1)}, u32[]{:S(2)}, u32[]{:S(2)}) collective-permute-start(f32[144,384]{1,0:T(8,128)S(1)} %get-tuple-element.42), channel_id=1, source_target_pairs={{0,1},{1,0},{2,3},{3,2},{4,5},{5,4},{6,7},{7,6},{8,9},{9,8},{10,11... | collective-permute-start | bytes 663560 | tf_op jit(solution)/shard_map/ppermute | solution.py:299
  92.6 1.0 collective-permute-done.14
  93.6 1.3 %collective-permute-start.15 = (f32[144,384]{1,0:T(8,128)S(1)}, f32[144,384]{1,0:T(8,128)S(1)}, u32[]{:S(2)}, u32[]{:S(2)}) collective-permute-start(f32[144,384]{1,0:T(8,128)S(1)} %add.34), channel_id=1, source_target_pairs={{0,2},{1,3},{2,0},{3,1},{4,6},{5,7},{6,4},{7,5},{8,10},{9,11},{10,... | collective-permute-start | bytes 663560 | tf_op jit(solution)/shard_map/ppermute | solution.py:299
  94.9 0.3 convolution_bitcast_fusion.1
  95.3 1.1 %convolution_bitcast_fusion.2 = f32[1,128,128]{2,1,0:T(8,128)S(1)} fusion(f32[128,128]{1,0:T(8,128)} %fusion.4, s32[128]{0:T(128)S(1)} %fusion.15), kind=kOutput, calls=%fused_computation.2 | convolution fusion | flops 25182208 | bytes 131584 | tf_op jit(solution)/shard_map/dot_general | solution.py:32
  96.4 3.9 %collective-permute-done.15 = f32[144,384]{1,0:T(8,128)S(1)} collective-permute-done((f32[144,384]{1,0:T(8,128)S(1)}, f32[144,384]{1,0:T(8,128)S(1)}, u32[]{:S(2)}, u32[]{:S(2)}) %collective-permute-start.15) | collective-permute-done | bytes 221216 | tf_op jit(solution)/shard_map/ppermute | solution.py:299
  100.4 1.3 %collective-permute-start.16 = (f32[144,384]{1,0:T(8,128)S(1)}, f32[144,384]{1,0:T(8,128)S(1)}, u32[]{:S(2)}, u32[]{:S(2)}) collective-permute-start(f32[144,384]{1,0:T(8,128)S(1)} %add.35.refs_4_), channel_id=1, source_target_pairs={{0,1},{1,0},{2,3},{3,2},{4,5},{5,4},{6,7},{7,6},{8,9},{9,8},{10,11... | collective-permute-start | bytes 663560 | tf_op jit(solution)/shard_map/ppermute | solution.py:299
  101.6 0.9 pad_maximum_fusion.refs_2_.refs_8_
  102.5 0.8 add_convert_fusion.refs_6_
  103.3 1.9 %shard_map.62 = (f32[3,128,512]{2,1,0:T(8,128)S(1)}, bf16[3,80,384]{2,1,0:T(8,128)(2,1)S(1)}, bf16[3,80,384]{2,1,0:T(8,128)(2,1)S(1)}, f32[128,384]{1,0:T(8,128)S(1)}) custom-call(s32[3]{0:T(128)S(1)} %copy-done.7, f32[384,256]{1,0:T(8,128)} %get-tuple-element.36.refs_0_, f32[384,256]{1,0:T(8,128)S(1)} %collective-permute-done.13.refs_1_, ...), custom_call_target="tpu_custom_call" | custom-call | flops 150994944 | bytes 589824 | tf_op jit(solution)/shard_map/pallas_call | solution.py:363
  105.2 3.7 %shard_map.63 = (f32[384,512]{1,0:T(8,128)}, f32[384,512]{1,0:T(8,128)}) custom-call(s32[3]{0:T(128)S(1)} %copy-done.7, bf16[3,80,384]{2,1,0:T(8,128)(2,1)S(1)} %get-tuple-element.38.refs_1_, bf16[3,80,384]{2,1,0:T(8,128)(2,1)S(1)} %get-tuple-element.39.refs_2_, f32[128,384]{1,0:T(8,128)S(1)} %get-tuple-element.40.refs_3_, f32[144,384]{1,0:T(8,128)S(1)} %add.35.refs_4_, ...), custom_call_target="tpu_custom_call" | custom-call | flops 452984832 | bytes 1769472 | tf_op jit(solution)/shard_map/pallas_call | solution.py:444
  (44 shorter events, 1.1 us)
Async XLA Ops:
  0.6 30.3 %copy-start.13 = (s32[3,128]{1,0:T(4,128)S(1)}, s32[3,128]{1,0:T(4,128)}, u32[]{:S(2)}) copy-start(s32[3,128]{1,0:T(4,128)} %index_hbm.1) | copy-start | bytes 4612
  6.5 15.5 %collective-permute-start = (bf16[48,6656]{1,0:T(8,128)(2,1)}, bf16[48,6656]{1,0:T(8,128)(2,1)S(1)}, u32[]{:S(2)}, u32[]{:S(2)}) collective-permute-start(bf16[48,6656]{1,0:T(8,128)(2,1)} %shard_map.59.refs_0_), channel_id=1, source_target_pairs={{0,8},{4,12},{8,0},{12,4},{16,24},{20,28},{24,16},{28,20},{1,9},{5... | collective-permute-start | bytes 1916936 | tf_op jit(solution)/shard_map/ppermute | solution.py:302
  6.8 18.3 %collective-permute-start.1 = (bf16[48,6656]{1,0:T(8,128)(2,1)}, bf16[48,6656]{1,0:T(8,128)(2,1)S(1)}, u32[]{:S(2)}, u32[]{:S(2)}) collective-permute-start(bf16[48,6656]{1,0:T(8,128)(2,1)} %shard_map.59.refs_0_), channel_id=1, source_target_pairs={{8,16},{12,20},{16,8},{20,12},{9,17},{13,21},{17,9},{21,13},{10,18... | collective-permute-start | bytes 1916936 | tf_op jit(solution)/shard_map/ppermute | solution.py:302
  11.1 14.9 %collective-permute-start.2 = (bf16[48,6656]{1,0:T(8,128)(2,1)}, bf16[48,6656]{1,0:T(8,128)(2,1)S(1)}, u32[]{:S(2)}, u32[]{:S(2)}) collective-permute-start(bf16[48,6656]{1,0:T(8,128)(2,1)} %shard_map.59.refs_0_), channel_id=1, source_target_pairs={{0,4},{4,0},{8,12},{12,8},{16,20},{20,16},{24,28},{28,24},{1,5},{5... | collective-permute-start | bytes 1916936 | tf_op jit(solution)/shard_map/ppermute | solution.py:302
  26.0 15.7 %collective-permute-start.3 = (bf16[48,6656]{1,0:T(8,128)(2,1)S(1)}, bf16[48,6656]{1,0:T(8,128)(2,1)}, u32[]{:S(2)}, u32[]{:S(2)}) collective-permute-start(bf16[48,6656]{1,0:T(8,128)(2,1)S(1)} %collective-permute-done.refs_2_), channel_id=1, source_target_pairs={{8,16},{12,20},{16,8},{20,12},{9,17},{13,21},{17,9},{21,13},{10,18... | collective-permute-start | bytes 1916936 | tf_op jit(solution)/shard_map/ppermute | solution.py:302
  28.2 13.9 %collective-permute-start.5 = (bf16[48,6656]{1,0:T(8,128)(2,1)S(1)}, bf16[48,6656]{1,0:T(8,128)(2,1)S(1)}, u32[]{:S(2)}, u32[]{:S(2)}) collective-permute-start(bf16[48,6656]{1,0:T(8,128)(2,1)S(1)} %collective-permute-done.refs_2_), channel_id=1, source_target_pairs={{0,4},{4,0},{8,12},{12,8},{16,20},{20,16},{24,28},{28,24},{1,5},{5... | collective-permute-start | bytes 1916936 | tf_op jit(solution)/shard_map/ppermute | solution.py:302
  28.5 13.2 %collective-permute-start.4 = (bf16[48,6656]{1,0:T(8,128)(2,1)S(1)}, bf16[48,6656]{1,0:T(8,128)(2,1)S(1)}, u32[]{:S(2)}, u32[]{:S(2)}) collective-permute-start(bf16[48,6656]{1,0:T(8,128)(2,1)S(1)} %collective-permute-done.1.refs_6_), channel_id=1, source_target_pairs={{8,0},{12,4},{16,24},{20,28},{9,1},{13,5},{17,25},{21,29},{10,2},{... | collective-permute-start | bytes 1916936 | tf_op jit(solution)/shard_map/ppermute | solution.py:302
  29.8 0.8 copy-start.5
  41.7 0.8 copy-start.10
  42.5 21.5 %collective-permute-start.7 = (bf16[48,6656]{1,0:T(8,128)(2,1)}, bf16[48,6656]{1,0:T(8,128)(2,1)S(1)}, u32[]{:S(2)}, u32[]{:S(2)}) collective-permute-start(bf16[48,6656]{1,0:T(8,128)(2,1)} %collective-permute-done.3), channel_id=1, source_target_pairs={{8,0},{12,4},{16,24},{20,28},{9,1},{13,5},{17,25},{21,29},{10,2},{... | collective-permute-start | bytes 1916936 | tf_op jit(solution)/shard_map/ppermute | solution.py:302
  46.3 15.1 %copy-start.12 = (f32[3,128,128]{2,1,0:T(8,128)S(1)}, f32[3,128,128]{2,1,0:T(8,128)}, u32[]{:S(2)}) copy-start(f32[3,128,128]{2,1,0:T(8,128)} %param.7) | copy-start | bytes 589828
  46.3 32.1 %copy-start.1 = (bf16[48,6656]{1,0:T(8,128)(2,1)S(1)}, bf16[48,6656]{1,0:T(8,128)(2,1)}, u32[]{:S(2)}) copy-start(bf16[48,6656]{1,0:T(8,128)(2,1)} %shard_map.59.refs_0_) | copy-start | bytes 1916932
  46.3 32.1 %copy-start.7 = (s32[3]{0:T(128)S(1)}, s32[3]{0:T(128)}, u32[]{:S(2)}) copy-start(s32[3]{0:T(128)} %pad_add_fusion.place_ref.refs_0_) | copy-start | bytes 40
  47.5 16.5 %collective-permute-start.6 = (bf16[48,6656]{1,0:T(8,128)(2,1)S(1)}, bf16[48,6656]{1,0:T(8,128)(2,1)S(1)}, u32[]{:S(2)}, u32[]{:S(2)}) collective-permute-start(bf16[48,6656]{1,0:T(8,128)(2,1)S(1)} %broadcast_select_fusion.refs_4_), channel_id=1, source_target_pairs={{0,4},{4,0},{8,12},{12,8},{16,20},{20,16},{24,28},{28,24},{1,5},{5... | collective-permute-start | bytes 1916936 | tf_op jit(solution)/shard_map/ppermute | solution.py:302
  48.8 15.2 %collective-permute-start.8 = (bf16[48,6656]{1,0:T(8,128)(2,1)S(1)}, bf16[48,6656]{1,0:T(8,128)(2,1)S(1)}, u32[]{:S(2)}, u32[]{:S(2)}) collective-permute-start(bf16[48,6656]{1,0:T(8,128)(2,1)S(1)} %collective-permute-done.2.refs_1_), channel_id=1, source_target_pairs={{8,16},{12,20},{16,8},{20,12},{9,17},{13,21},{17,9},{21,13},{10,18... | collective-permute-start | bytes 1916936 | tf_op jit(solution)/shard_map/ppermute | solution.py:302
  51.6 1.1 copy-start
  57.1 6.0 %collective-permute-start.9 = (f32[368,384]{1,0:T(8,128)S(1)}, f32[368,384]{1,0:T(8,128)S(1)}, u32[]{:S(2)}, u32[]{:S(2)}) collective-permute-start(f32[368,384]{1,0:T(8,128)S(1)} %shard_map.60), channel_id=1, source_target_pairs={{0,1},{1,0},{2,3},{3,2},{4,5},{5,4},{6,7},{7,6},{8,9},{9,8},{10,11... | collective-permute-start | bytes 1695752 | tf_op jit(solution)/shard_map/ppermute | solution.py:299
  64.0 1.0 copy-start.8
  64.0 3.1 %copy-start.9 = (bf16[48,6656]{1,0:T(8,128)(2,1)}, bf16[48,6656]{1,0:T(8,128)(2,1)S(1)}, u32[]{:S(2)}) copy-start(bf16[48,6656]{1,0:T(8,128)(2,1)S(1)} %collective-permute-done.8.refs_8_) | copy-start | bytes 1916932
  65.0 0.8 copy-start.3
  65.8 8.5 %collective-permute-start.11 = (bf16[48,3584]{1,0:T(8,128)(2,1)}, bf16[48,3584]{1,0:T(8,128)(2,1)S(1)}, u32[]{:S(2)}, u32[]{:S(2)}) collective-permute-start(bf16[48,3584]{1,0:T(8,128)(2,1)} %slice.31), channel_id=1, source_target_pairs={{8,0},{12,4},{16,24},{20,28},{9,1},{13,5},{17,25},{21,29},{10,2},{... | collective-permute-start | bytes 1032200 | tf_op jit(solution)/shard_map/ppermute | solution.py:302
  67.1 11.3 %collective-permute-start.12 = (f32[368,384]{1,0:T(8,128)}, f32[368,384]{1,0:T(8,128)}, u32[]{:S(2)}, u32[]{:S(2)}) collective-permute-start(f32[368,384]{1,0:T(8,128)} %add.31.refs_3_), channel_id=1, source_target_pairs={{0,2},{1,3},{2,0},{3,1},{4,6},{5,7},{6,4},{7,5},{8,10},{9,11},{10,... | collective-permute-start | bytes 1695752 | tf_op jit(solution)/shard_map/ppermute | solution.py:299
  70.1 4.2 %collective-permute-start.10 = (bf16[48,3072]{1,0:T(8,128)(2,1)S(1)}, bf16[48,3072]{1,0:T(8,128)(2,1)S(1)}, u32[]{:S(2)}, u32[]{:S(2)}) collective-permute-start(bf16[48,3072]{1,0:T(8,128)(2,1)S(1)} %slice.30), channel_id=1, source_target_pairs={{0,4},{4,0},{24,28},{28,24},{1,5},{5,1},{25,29},{29,25},{2,6},{6,2... | collective-permute-start | bytes 884744 | tf_op jit(solution)/shard_map/ppermute | solution.py:302
  72.5 22.4 %copy-start.11 = (f32[128,128]{1,0:T(8,128)S(1)}, f32[128,128]{1,0:T(8,128)}, u32[]{:S(2)}) copy-start(f32[128,128]{1,0:T(8,128)} %fusion.2) | copy-start | bytes 196612
  78.4 1.1 copy-start.4
  79.5 1.1 copy-start.6
  88.1 17.1 %copy-start.2 = (f32[384,512]{1,0:T(8,128)S(1)}, f32[384,512]{1,0:T(8,128)}, u32[]{:S(2)}) copy-start(f32[384,512]{1,0:T(8,128)} %refs_10_.1) | copy-start | bytes 2359300
  88.1 5.5 %collective-permute-start.14 = (f32[144,384]{1,0:T(8,128)S(1)}, f32[144,384]{1,0:T(8,128)S(1)}, u32[]{:S(2)}, u32[]{:S(2)}) collective-permute-start(f32[144,384]{1,0:T(8,128)S(1)} %get-tuple-element.42), channel_id=1, source_target_pairs={{0,1},{1,0},{2,3},{3,2},{4,5},{5,4},{6,7},{7,6},{8,9},{9,8},{10,11... | collective-permute-start | bytes 663560 | tf_op jit(solution)/shard_map/ppermute | solution.py:299
  92.5 10.8 %collective-permute-start.13 = (f32[384,256]{1,0:T(8,128)}, f32[384,256]{1,0:T(8,128)S(1)}, u32[]{:S(2)}, u32[]{:S(2)}) collective-permute-start(f32[384,256]{1,0:T(8,128)} %get-tuple-element.36.refs_0_), channel_id=1, source_target_pairs={{0,1},{1,0},{2,3},{3,2},{4,5},{5,4},{6,7},{7,6},{8,9},{9,8},{10,11... | collective-permute-start | bytes 1179656 | tf_op jit(solution)/shard_map/ppermute | solution.py:299
  93.6 6.7 %collective-permute-start.15 = (f32[144,384]{1,0:T(8,128)S(1)}, f32[144,384]{1,0:T(8,128)S(1)}, u32[]{:S(2)}, u32[]{:S(2)}) collective-permute-start(f32[144,384]{1,0:T(8,128)S(1)} %add.34), channel_id=1, source_target_pairs={{0,2},{1,3},{2,0},{3,1},{4,6},{5,7},{6,4},{7,5},{8,10},{9,11},{10,... | collective-permute-start | bytes 663560 | tf_op jit(solution)/shard_map/ppermute | solution.py:299
  100.4 4.9 %collective-permute-start.16 = (f32[144,384]{1,0:T(8,128)S(1)}, f32[144,384]{1,0:T(8,128)S(1)}, u32[]{:S(2)}, u32[]{:S(2)}) collective-permute-start(f32[144,384]{1,0:T(8,128)S(1)} %add.35.refs_4_), channel_id=1, source_target_pairs={{0,1},{1,0},{2,3},{3,2},{4,5},{5,4},{6,7},{7,6},{8,9},{9,8},{10,11... | collective-permute-start | bytes 663560 | tf_op jit(solution)/shard_map/ppermute | solution.py:299

commit v6 on v5

--- a/solution.py
+++ b/solution.py
@@ -14,7 +14,7 @@
 PIECES = 4
 PARAMS = pltpu.CompilerParams(vmem_limit_bytes=24 * 1024 * 1024)
 PICK = pltpu.CompilerParams(vmem_limit_bytes=58 * 1024 * 1024)
-GRAM = pltpu.CompilerParams(vmem_limit_bytes=48 * 1024 * 1024)
+GRAM = pltpu.CompilerParams(vmem_limit_bytes=46 * 1024 * 1024)
 
 
 def quadratic(gram):
@@ -70,8 +70,8 @@
 def finish_kernel(steps, per, last, *refs):
     refs = list(refs)
     if last:
-        place_ref, high_ref, low_ref, cross_ref, mine_ref, other_ref = refs[:6]
-        refs = refs[6:]
+        place_ref, early_ref, cross_ref, mine_ref, other_ref = refs[:5]
+        refs = refs[5:]
     else:
         gram_ref, cross_ref = refs[:2]
         refs = refs[2:]
@@ -123,7 +123,7 @@
         if last:
             part = split(end_of(end_gram, step))
             kernel = tuple(
-                jnp.concatenate([ref[step], one], axis=0) for ref, one in zip((high_ref, low_ref), part)
+                jnp.concatenate([early_ref[i, step], part[i]], axis=0) for i in range(2)
             )
         else:
             kernel = quadratic(gram_ref[...].reshape(-1, steps, per, rows)[:, step].reshape(block, rows))
@@ -132,7 +132,7 @@
 
 
 def ready_kernel(steps, per, place_ref, *refs):
-    mine_ref, other_ref, inverse_ref, *gram_refs, first_ref, high_ref, low_ref, cross_ref = refs
+    mine_ref, other_ref, inverse_ref, *gram_refs, first_ref, early_ref, cross_ref = refs
     core = place_ref[1]
     block = inverse_ref.shape[1]
     half = mine_ref.shape[1]
@@ -142,12 +142,13 @@
         mine, other = mine_ref[rows], other_ref[rows]
         first_ref[step, :, :half] = fine_dot(inverse, jnp.where(core == 0, mine, other))
         first_ref[step, :, half:] = fine_dot(inverse, jnp.where(core == 0, other, mine))
-    gram = gram_refs[0][...] + gram_refs[1][...]
+    mine, other = gram_refs[0][...], gram_refs[1][...]
+    gram = jnp.concatenate([jnp.where(core == 0, mine, other), jnp.where(core == 0, other, mine)], axis=0)
     cross_ref[...] = gram[-block:]
     kernel = quadratic(gram[:-block])
     kernel = kernel.reshape(-1, steps, per, kernel.shape[-1])
     for step in range(steps):
-        high_ref[step], low_ref[step] = split(kernel[:, step].reshape(high_ref.shape[1:]))
+        early_ref[0, step], early_ref[1, step] = split(kernel[:, step].reshape(early_ref.shape[2:]))
 
 
 def pieces_of(features_ref):
@@ -224,8 +225,8 @@
     )(block_index, place, features, targets)
 
 
-def gram_kernel(steps, per, missing, *refs):
-    *slot_refs, features_ref, out_ref, held_ref, sems = refs
+def gram_kernel(steps, per, missing, place_ref, *refs):
+    *slot_refs, features_ref, keep_ref, send_ref, held_ref, sems = refs
     copies = fetch(features_ref, held_ref, sems)
     total = [None] * (1 + len(pairs_of(steps)))
     for at in pieces_of(features_ref):
@@ -238,9 +239,11 @@
         slots = jnp.concatenate([ref[:, at] for ref in slot_refs], axis=0)
         copy.wait()
         total[0] = add(total[0], dot_rows(slots, held_ref[:, at]))
-    new = total[0].shape[0]
-    out_ref[:new] = total[0]
-    out_ref[new:] = jnp.concatenate(total[1:], axis=1)
+    total = jnp.concatenate([total[0], jnp.concatenate(total[1:], axis=1)], axis=0)
+    half = keep_ref.shape[0]
+    core = place_ref[1]
+    keep_ref[...] = jnp.where(core == 0, total[:half], total[half:])
+    send_ref[...] = jnp.where(core == 0, total[half:], total[:half])
 
 
 def last_kernel(steps, per, begun, place_ref, *refs):
@@ -249,17 +252,13 @@
     core = place_ref[1]
     inner = place_ref[2] == 1
     columns = features_ref.shape[1]
-    half = left_ref.shape[1]
     copies = fetch(features_ref, held_ref, sems)
 
     def slots_at(at):
         slots = [ref[:, at] for ref in slot_refs]
         other = slots.pop()
         slots[-1] = jnp.where(inner, slots[-1], other)
-        if at.start < half:
-            last = left_ref[:, at]
-        else:
-            last = right_ref[:, at.start - half : at.stop - half]
+        last = jnp.where(core == 0, left_ref[:, at], right_ref[:, at])
         return slots + [jnp.where(inner, inner_ref[:, at], last)]
 
     def every(slots):
@@ -288,7 +287,9 @@
         self.pair = [(r, r ^ 2) for r in range(8)]
         self.inner = [(r, r ^ 6) for r in range(2, 6)]
         self.outer = [(2, 0), (3, 1), (4, 6), (5, 7)]
-        self.ends = [(r, r ^ 1) for r in (0, 1, 6, 7)]
+        ends = [(r, r ^ 1) for r in (0, 1, 6, 7)]
+        self.ends = [(4 * r + f, 4 * to + f) for r, to in ends for f in (0, 2)]
+        self.outer_second = [(4 * r + f, 4 * to + f) for r, to in self.outer for f in (1, 3)]
         rank = lax.axis_index("rows")
         core = lax.axis_index("feat") % 2
         self.is_inner = (rank >= 2) & (rank < 6)
@@ -307,7 +308,6 @@
         count = steps * per
         hold = lax.optimization_barrier
         own = pick(block_index, self.place, features, targets, per)
-        half = columns // 2
 
         pair = self.send(own, self.pair)
         mid = self.send(own, self.inner)
@@ -325,22 +325,24 @@
         last_in = self.send(own_b, self.inner)
         slots = [own, own_b, pair, pair_b, third]
         begun = len(slots)
-        gram = pl.pallas_call(
+        part = jax.ShapeDtypeStruct(((begun * count + block) // 2, rows), jnp.float32)
+        gram, given = pl.pallas_call(
             functools.partial(gram_kernel, steps, per, 8 - begun),
-            out_shape=jax.ShapeDtypeStruct((begun * count + block, rows), jnp.float32),
-            in_specs=[VMEM] * begun + [HBM],
-            out_specs=VMEM,
+            out_shape=(part, part),
+            in_specs=[SMEM] + [VMEM] * begun + [HBM],
+            out_specs=(VMEM, VMEM),
             scratch_shapes=held(features),
             compiler_params=GRAM,
             cost_estimate=cost((begun * count + block) * rows, columns),
-        )(*slots, features)
-        gram = gram + self.near(gram, 1)
+        )(self.place, *slots, features)
+        gram = gram + self.near(given, 1)
         third_b, far_end, last_in, gram = hold((third_b, far_end, last_in, gram))
 
-        left = self.send(far_end[:, :half], self.ends)
-        right = self.send(third_b[:, half:], self.outer)
+        left = lax.ppermute(far_end, ("rows", "feat"), self.ends)
+        right = lax.ppermute(third_b, ("rows", "feat"), self.outer_second)
         gram_near = self.near(gram, 2)
         left, right, gram_near = hold((left, right, gram_near))
+        gram = gram + gram_near
 
         slots = slots + [third_b, mid, far_end, last_in, left, right]
         end = jax.ShapeDtypeStruct(((8 - begun) * count, rows), jnp.float32)
@@ -358,22 +360,21 @@
             cost_estimate=cost((8 - begun) * count * (rows + steps * block), columns),
         )(self.place, *slots, features)
         keep = keep + self.near(given, 1)
-        keep = keep + self.near(keep, 2)
-        parts = (steps, begun * per, rows)
-        first, high, low, cross = pl.pallas_call(
+        keep_near = self.near(keep, 2)
+        first, early, cross = pl.pallas_call(
             functools.partial(ready_kernel, steps, per),
             out_shape=(
                 jax.ShapeDtypeStruct((steps, block, targets.shape[1]), jnp.float32),
-                jax.ShapeDtypeStruct(parts, jnp.bfloat16),
-                jax.ShapeDtypeStruct(parts, jnp.bfloat16),
+                jax.ShapeDtypeStruct((2, steps, begun * per, rows), jnp.bfloat16),
                 jax.ShapeDtypeStruct((block, rows), jnp.float32),
             ),
             in_specs=[SMEM] + [VMEM] * 5,
-            out_specs=(VMEM,) * 4,
+            out_specs=(VMEM,) * 3,
             compiler_params=PARAMS,
             cost_estimate=cost(3 * steps * block * block, targets.shape[1]),
-        )(self.place, first, self.near(first, 1), turned, gram, gram_near)
-        return [self.place, high, low, cross, keep, self.near(keep, 1)], first
+        )(self.place, first, self.near(first, 1), turned, gram, self.near(gram, 1))
+        keep, first = hold((keep + keep_near, first))
+        return [self.place, early, cross, keep, self.near(keep, 1)], first
 
 
 class Gathers:

time: 110 us -> 96.8 us (0.88)
  the two profiles are of different devices: /device:TPU:13 before, /device:TPU:0 now
where the time goes in v6:
time: 96.8 us; the launch traced here: 96.5 us
  waiting for transfers between devices  46.9 us (48%)
  Pallas kernels  21.2 us (22%)
  starting transfers between devices  20.6 us (21%)
  local copies, waits for them, and re-layouts  3.01 us (3%)
  other arithmetic  2.3 us (2%)
  matrix products  1.52 us (2%)
    ppermute x9, waiting for transfers between devices, send(): return lax.ppermute(array, 'rows', pairs)  35.1 us
    ppermute x9, starting transfers between devices, send(): return lax.ppermute(array, 'rows', pairs)  12.5 us
    ppermute x7, waiting for transfers between devices, near(): return lax.ppermute(array, 'feat', [(f, f ^ bit) for f in range(4)])  10.8 us
    pallas_call x1, Pallas kernels, run(): pl.pallas_call(functools.partial(last_kernel, steps, per, begun), out_sha...  6.14 us
    pallas_call x1, Pallas kernels, pick(): pl.pallas_call(functools.partial(pick_kernel, per), out_shape=jax.ShapeDt...  5.38 us
    pallas_call x1, Pallas kernels, run(): pl.pallas_call(functools.partial(gram_kernel, steps, per, 8 - begun), out...  4.95 us
    ppermute x7, starting transfers between devices, near(): return lax.ppermute(array, 'feat', [(f, f ^ bit) for f in range(4)])  3.98 us
    pallas_call x1, Pallas kernels, local(): pl.pallas_call(functools.partial(finish_kernel, steps, per, lined), out_s...  3.67 us
  transfers between devices with their start and end apart: 18, of which 10 were waited for; matrix products, arithmetic and copies ran while one was open for 4% of the time, Pallas kernels for 6%

profile of v6, /device:TPU:0, one launch (start us, length us, event | category | flops | bytes accessed | tf_op | source)
XLA Modules:
  0.0 96.5 jit_solution(12901213528450147789)
XLA Ops:
  0.7 0.6 pad_add_fusion.place_ref.refs_0_
  1.2 5.4 %shard_map.59.refs_0_ = bf16[48,6656]{1,0:T(8,128)(2,1)} custom-call(s32[3,128]{1,0:T(4,128)} %index_hbm.1, s32[3]{0:T(128)} %pad_add_fusion.place_ref.refs_0_, bf16[384,6144]{1,0:T(8,128)(2,1)} %refs_11_.1, f32[384,512]{1,0:T(8,128)} %refs_9_.1), custom_call_target="tpu_custom_call" | custom-call | flops 245366784 | bytes 73728 | tf_op jit(solution)/shard_map/pallas_call | solution.py:212
  6.6 3.1 %collective-permute-start = (bf16[48,6656]{1,0:T(8,128)(2,1)}, bf16[48,6656]{1,0:T(8,128)(2,1)S(1)}, u32[]{:S(2)}, u32[]{:S(2)}) collective-permute-start(bf16[48,6656]{1,0:T(8,128)(2,1)} %shard_map.59.refs_0_), channel_id=1, source_target_pairs={{0,8},{4,12},{8,0},{12,4},{16,24},{20,28},{24,16},{28,20},{1,9},{5... | collective-permute-start | bytes 1916936 | tf_op jit(solution)/shard_map/ppermute | solution.py:303
  9.7 0.7 collective-permute-start.1
  10.4 1.6 %collective-permute-start.2 = (bf16[48,6656]{1,0:T(8,128)(2,1)}, bf16[48,6656]{1,0:T(8,128)(2,1)S(1)}, u32[]{:S(2)}, u32[]{:S(2)}) collective-permute-start(bf16[48,6656]{1,0:T(8,128)(2,1)} %shard_map.59.refs_0_), channel_id=1, source_target_pairs={{0,4},{4,0},{8,12},{12,8},{16,20},{20,16},{24,28},{28,24},{1,5},{5... | collective-permute-start | bytes 1916936 | tf_op jit(solution)/shard_map/ppermute | solution.py:303
  12.0 12.3 %collective-permute-done.refs_2_ = bf16[48,6656]{1,0:T(8,128)(2,1)S(1)} collective-permute-done((bf16[48,6656]{1,0:T(8,128)(2,1)}, bf16[48,6656]{1,0:T(8,128)(2,1)S(1)}, u32[]{:S(2)}, u32[]{:S(2)}) %collective-permute-start) | collective-permute-done | bytes 639008 | tf_op jit(solution)/shard_map/ppermute | solution.py:303
  24.3 2.2 %collective-permute-done.2.refs_1_ = bf16[48,6656]{1,0:T(8,128)(2,1)S(1)} collective-permute-done((bf16[48,6656]{1,0:T(8,128)(2,1)}, bf16[48,6656]{1,0:T(8,128)(2,1)S(1)}, u32[]{:S(2)}, u32[]{:S(2)}) %collective-permute-start.2) | collective-permute-done | bytes 639008 | tf_op jit(solution)/shard_map/ppermute | solution.py:303
  26.5 0.7 collective-permute-start.3
  27.2 1.3 %collective-permute-start.4 = (bf16[48,6656]{1,0:T(8,128)(2,1)S(1)}, bf16[48,6656]{1,0:T(8,128)(2,1)}, u32[]{:S(2)}, u32[]{:S(2)}) collective-permute-start(bf16[48,6656]{1,0:T(8,128)(2,1)S(1)} %collective-permute-done.1.refs_6_), channel_id=1, source_target_pairs={{8,0},{12,4},{16,24},{20,28},{9,1},{13,5},{17,25},{21,29},{10,2},{... | collective-permute-start | bytes 1916936 | tf_op jit(solution)/shard_map/ppermute | solution.py:303
  28.5 1.6 %collective-permute-start.5 = (bf16[48,6656]{1,0:T(8,128)(2,1)S(1)}, bf16[48,6656]{1,0:T(8,128)(2,1)S(1)}, u32[]{:S(2)}, u32[]{:S(2)}) collective-permute-start(bf16[48,6656]{1,0:T(8,128)(2,1)S(1)} %collective-permute-done.refs_2_), channel_id=1, source_target_pairs={{0,4},{4,0},{8,12},{12,8},{16,20},{20,16},{24,28},{28,24},{1,5},{5... | collective-permute-start | bytes 1916936 | tf_op jit(solution)/shard_map/ppermute | solution.py:303
  30.1 0.1 broadcast_in_dim.27
  30.2 0.1 mul.21
  30.3 0.1 iota_compare_fusion
  30.4 16.7 %collective-permute-done.4 = bf16[48,6656]{1,0:T(8,128)(2,1)} collective-permute-done((bf16[48,6656]{1,0:T(8,128)(2,1)S(1)}, bf16[48,6656]{1,0:T(8,128)(2,1)}, u32[]{:S(2)}, u32[]{:S(2)}) %collective-permute-start.4) | collective-permute-done | bytes 639008 | tf_op jit(solution)/shard_map/ppermute | solution.py:303
  47.1 1.3 %collective-permute-start.7 = (bf16[48,6656]{1,0:T(8,128)(2,1)S(1)}, bf16[48,6656]{1,0:T(8,128)(2,1)S(1)}, u32[]{:S(2)}, u32[]{:S(2)}) collective-permute-start(bf16[48,6656]{1,0:T(8,128)(2,1)S(1)} %collective-permute-done.3), channel_id=1, source_target_pairs={{8,0},{12,4},{16,24},{20,28},{9,1},{13,5},{17,25},{21,29},{10,2},{... | collective-permute-start | bytes 1916936 | tf_op jit(solution)/shard_map/ppermute | solution.py:303
  48.4 1.2 %broadcast_select_fusion.refs_4_ = bf16[48,6656]{1,0:T(8,128)(2,1)S(1)} fusion(bf16[48,6656]{1,0:T(8,128)(2,1)S(1)} %collective-permute-done.3, bf16[48,6656]{1,0:T(8,128)(2,1)} %collective-permute-done.4, pred[]{:T(512)S(6)} %and.23), kind=kLoop, calls=%fused_computation.3 | loop fusion | flops 319488 | bytes 1916929 | tf_op jit(solution)/shard_map/jit(_where)/select_n | solution.py:322
  49.6 1.6 %collective-permute-start.6 = (bf16[48,6656]{1,0:T(8,128)(2,1)S(1)}, bf16[48,6656]{1,0:T(8,128)(2,1)S(1)}, u32[]{:S(2)}, u32[]{:S(2)}) collective-permute-start(bf16[48,6656]{1,0:T(8,128)(2,1)S(1)} %broadcast_select_fusion.refs_4_), channel_id=1, source_target_pairs={{0,4},{4,0},{8,12},{12,8},{16,20},{20,16},{24,28},{28,24},{1,5},{5... | collective-permute-start | bytes 1916936 | tf_op jit(solution)/shard_map/ppermute | solution.py:303
  51.2 0.7 collective-permute-start.8
  51.9 0.1 select_reduce_fusion
  52.1 1.1 %copy-done = bf16[48,6656]{1,0:T(8,128)(2,1)S(1)} copy-done((bf16[48,6656]{1,0:T(8,128)(2,1)S(1)}, bf16[48,6656]{1,0:T(8,128)(2,1)}, u32[]{:S(2)}) %copy-start) | copy-done | bytes 639000
  53.1 4.9 %shard_map.60 = (f32[184,384]{1,0:T(8,128)S(1)}, f32[184,384]{1,0:T(8,128)S(1)}) custom-call(s32[3]{0:T(128)S(1)} %copy-done.5, bf16[48,6656]{1,0:T(8,128)(2,1)S(1)} %copy-done, bf16[48,6656]{1,0:T(8,128)(2,1)S(1)} %collective-permute-done.2.refs_1_, bf16[48,6656]{1,0:T(8,128)(2,1)S(1)} %collective-permute-done.refs_2_, ...), custom_call_target="tpu_custom_call" | custom-call | flops 1736441856 | bytes 565248 | tf_op jit(solution)/shard_map/pallas_call | solution.py:329
  58.2 0.2 fusion
  58.4 1.3 %collective-permute-done.9 = f32[184,384]{1,0:T(8,128)S(1)} collective-permute-done((f32[184,384]{1,0:T(8,128)S(1)}, f32[184,384]{1,0:T(8,128)S(1)}, u32[]{:S(2)}, u32[]{:S(2)}) %collective-permute-start.9) | collective-permute-done | bytes 282656 | tf_op jit(solution)/shard_map/ppermute | solution.py:300
  59.8 3.9 %collective-permute-done.6.refs_5_ = bf16[48,6656]{1,0:T(8,128)(2,1)S(1)} collective-permute-done((bf16[48,6656]{1,0:T(8,128)(2,1)S(1)}, bf16[48,6656]{1,0:T(8,128)(2,1)S(1)}, u32[]{:S(2)}, u32[]{:S(2)}) %collective-permute-start.6) | collective-permute-done | bytes 639008 | tf_op jit(solution)/shard_map/ppermute | solution.py:303
  63.7 3.4 %collective-permute-start.10 = (bf16[48,6656]{1,0:T(8,128)(2,1)S(1)}, bf16[48,6656]{1,0:T(8,128)(2,1)S(1)}, u32[]{:S(2)}, u32[]{:S(2)}) collective-permute-start(bf16[48,6656]{1,0:T(8,128)(2,1)S(1)} %collective-permute-done.7.refs_7_), channel_id=1, source_target_pairs={{0,4},{2,6},{4,0},{6,2},{24,28},{26,30},{28,24},{30,26}} | collective-permute-start | bytes 1916936 | tf_op jit(solution)/shard_map/ppermute | solution.py:341
  67.1 0.7 collective-permute-start.11
  67.8 0.3 convolution_bitcast_fusion
  68.1 0.2 fusion.2
  68.3 1.6 %collective-permute-start.12 = (f32[184,384]{1,0:T(8,128)S(1)}, f32[184,384]{1,0:T(8,128)S(1)}, u32[]{:S(2)}, u32[]{:S(2)}) collective-permute-start(f32[184,384]{1,0:T(8,128)S(1)} %add.34), channel_id=1, source_target_pairs={{0,2},{1,3},{2,0},{3,1},{4,6},{5,7},{6,4},{7,5},{8,10},{9,11},{10,... | collective-permute-start | bytes 847880 | tf_op jit(solution)/shard_map/ppermute | solution.py:300
  69.9 0.3 convolution_bitcast_fusion.1
  70.2 0.2 fusion.4
  70.4 4.6 %collective-permute-done.12 = f32[184,384]{1,0:T(8,128)S(1)} collective-permute-done((f32[184,384]{1,0:T(8,128)S(1)}, f32[184,384]{1,0:T(8,128)S(1)}, u32[]{:S(2)}, u32[]{:S(2)}) %collective-permute-start.12) | collective-permute-done | bytes 282656 | tf_op jit(solution)/shard_map/ppermute | solution.py:300
  75.0 1.0 %collective-permute-done.10.refs_9_ = bf16[48,6656]{1,0:T(8,128)(2,1)S(1)} collective-permute-done((bf16[48,6656]{1,0:T(8,128)(2,1)S(1)}, bf16[48,6656]{1,0:T(8,128)(2,1)S(1)}, u32[]{:S(2)}, u32[]{:S(2)}) %collective-permute-start.10) | collective-permute-done | bytes 639008 | tf_op jit(solution)/shard_map/ppermute | solution.py:341
  76.0 6.1 %shard_map.61 = (f32[144,384]{1,0:T(8,128)S(1)}, f32[144,384]{1,0:T(8,128)S(1)}, f32[384,256]{1,0:T(8,128)S(1)}) custom-call(s32[3]{0:T(128)S(1)} %copy-done.5, bf16[48,6656]{1,0:T(8,128)(2,1)S(1)} %copy-done.1, bf16[48,6656]{1,0:T(8,128)(2,1)S(1)} %collective-permute-done.2.refs_1_, bf16[48,6656]{1,0:T(8,128)(2,1)S(1)} %collective-permute-done.refs_2_, ...), custom_call_target="tpu_custom_call" | custom-call | flops 1358954496 | bytes 442368 | tf_op jit(solution)/shard_map/pallas_call | solution.py:349
  82.1 0.1 collective-permute-start.15
  82.2 0.5 collective-permute-start.13
  82.7 0.3 convolution_bitcast_fusion.2
  83.0 0.1 collective-permute-start.14
  83.2 0.5 collective-permute-done.15
  83.7 1.6 %collective-permute-start.16 = (f32[144,384]{1,0:T(8,128)S(1)}, f32[144,384]{1,0:T(8,128)S(1)}, u32[]{:S(2)}, u32[]{:S(2)}) collective-permute-start(f32[144,384]{1,0:T(8,128)S(1)} %add.38), channel_id=1, source_target_pairs={{0,2},{1,3},{2,0},{3,1},{4,6},{5,7},{6,4},{7,5},{8,10},{9,11},{10,... | collective-permute-start | bytes 663560 | tf_op jit(solution)/shard_map/ppermute | solution.py:300
  85.3 0.1 broadcast_compare_fusion.2
  85.4 0.7 copy-done.3
  86.1 1.0 copy-done.4
  87.1 1.1 %shard_map.62 = (f32[3,128,512]{2,1,0:T(8,128)S(1)}, bf16[2,3,80,384]{3,2,1,0:T(8,128)(2,1)S(1)}, f32[128,384]{1,0:T(8,128)S(1)}) custom-call(s32[3]{0:T(128)S(1)} %copy-done.5, f32[384,256]{1,0:T(8,128)S(1)} %get-tuple-element.41.refs_0_, f32[384,256]{1,0:T(8,128)S(1)} %collective-permute-done.13.refs_1_, ...), custom_call_target="tpu_custom_call" | custom-call | flops 150994944 | bytes 589824 | tf_op jit(solution)/shard_map/pallas_call | solution.py:364
  88.2 3.1 %collective-permute-done.16 = f32[144,384]{1,0:T(8,128)S(1)} collective-permute-done((f32[144,384]{1,0:T(8,128)S(1)}, f32[144,384]{1,0:T(8,128)S(1)}, u32[]{:S(2)}, u32[]{:S(2)}) %collective-permute-start.16) | collective-permute-done | bytes 221216 | tf_op jit(solution)/shard_map/ppermute | solution.py:300
  91.4 0.1 sub.11.refs_8_
  91.5 1.3 %collective-permute-done.17.refs_4_ = f32[144,384]{1,0:T(8,128)S(1)} collective-permute-done((f32[144,384]{1,0:T(8,128)S(1)}, f32[144,384]{1,0:T(8,128)S(1)}, u32[]{:S(2)}, u32[]{:S(2)}) %collective-permute-start.17) | collective-permute-done | bytes 221216 | tf_op jit(solution)/shard_map/ppermute | solution.py:300
  92.8 3.7 %shard_map.63 = (f32[384,512]{1,0:T(8,128)}, f32[384,512]{1,0:T(8,128)}) custom-call(s32[3]{0:T(128)S(1)} %copy-done.5, bf16[2,3,80,384]{3,2,1,0:T(8,128)(2,1)S(1)} %get-tuple-element.43.refs_1_, f32[128,384]{1,0:T(8,128)S(1)} %get-tuple-element.44.refs_2_, f32[144,384]{1,0:T(8,128)S(1)} %add.39.refs_3_, f32[144,384]{1,0:T(8,128)S(1)} %collective-permute-done.17.refs_4_, ...), custom_call_target="tpu_custom_call" | custom-call | flops 452984832 | bytes 1769472 | tf_op jit(solution)/shard_map/pallas_call | solution.py:445
  (33 shorter events, 0.4 us)
Async XLA Ops:
  0.6 51.3 %copy-start.7 = (s32[3,128]{1,0:T(4,128)S(1)}, s32[3,128]{1,0:T(4,128)}, u32[]{:S(2)}) copy-start(s32[3,128]{1,0:T(4,128)} %index_hbm.1) | copy-start | bytes 4612
  1.2 50.8 %copy-start.5 = (s32[3]{0:T(128)S(1)}, s32[3]{0:T(128)}, u32[]{:S(2)}) copy-start(s32[3]{0:T(128)} %pad_add_fusion.place_ref.refs_0_) | copy-start | bytes 40
  6.6 17.7 %collective-permute-start = (bf16[48,6656]{1,0:T(8,128)(2,1)}, bf16[48,6656]{1,0:T(8,128)(2,1)S(1)}, u32[]{:S(2)}, u32[]{:S(2)}) collective-permute-start(bf16[48,6656]{1,0:T(8,128)(2,1)} %shard_map.59.refs_0_), channel_id=1, source_target_pairs={{0,8},{4,12},{8,0},{12,4},{16,24},{20,28},{24,16},{28,20},{1,9},{5... | collective-permute-start | bytes 1916936 | tf_op jit(solution)/shard_map/ppermute | solution.py:303
  9.7 14.6 %collective-permute-start.1 = (bf16[48,6656]{1,0:T(8,128)(2,1)}, bf16[48,6656]{1,0:T(8,128)(2,1)S(1)}, u32[]{:S(2)}, u32[]{:S(2)}) collective-permute-start(bf16[48,6656]{1,0:T(8,128)(2,1)} %shard_map.59.refs_0_), channel_id=1, source_target_pairs={{8,16},{12,20},{16,8},{20,12},{9,17},{13,21},{17,9},{21,13},{10,18... | collective-permute-start | bytes 1916936 | tf_op jit(solution)/shard_map/ppermute | solution.py:303
  10.4 16.1 %collective-permute-start.2 = (bf16[48,6656]{1,0:T(8,128)(2,1)}, bf16[48,6656]{1,0:T(8,128)(2,1)S(1)}, u32[]{:S(2)}, u32[]{:S(2)}) collective-permute-start(bf16[48,6656]{1,0:T(8,128)(2,1)} %shard_map.59.refs_0_), channel_id=1, source_target_pairs={{0,4},{4,0},{8,12},{12,8},{16,20},{20,16},{24,28},{28,24},{1,5},{5... | collective-permute-start | bytes 1916936 | tf_op jit(solution)/shard_map/ppermute | solution.py:303
  26.5 3.9 %collective-permute-start.3 = (bf16[48,6656]{1,0:T(8,128)(2,1)S(1)}, bf16[48,6656]{1,0:T(8,128)(2,1)S(1)}, u32[]{:S(2)}, u32[]{:S(2)}) collective-permute-start(bf16[48,6656]{1,0:T(8,128)(2,1)S(1)} %collective-permute-done.refs_2_), channel_id=1, source_target_pairs={{8,16},{12,20},{16,8},{20,12},{9,17},{13,21},{17,9},{21,13},{10,18... | collective-permute-start | bytes 1916936 | tf_op jit(solution)/shard_map/ppermute | solution.py:303
  27.2 19.9 %collective-permute-start.4 = (bf16[48,6656]{1,0:T(8,128)(2,1)S(1)}, bf16[48,6656]{1,0:T(8,128)(2,1)}, u32[]{:S(2)}, u32[]{:S(2)}) collective-permute-start(bf16[48,6656]{1,0:T(8,128)(2,1)S(1)} %collective-permute-done.1.refs_6_), channel_id=1, source_target_pairs={{8,0},{12,4},{16,24},{20,28},{9,1},{13,5},{17,25},{21,29},{10,2},{... | collective-permute-start | bytes 1916936 | tf_op jit(solution)/shard_map/ppermute | solution.py:303
  28.5 18.6 %collective-permute-start.5 = (bf16[48,6656]{1,0:T(8,128)(2,1)S(1)}, bf16[48,6656]{1,0:T(8,128)(2,1)S(1)}, u32[]{:S(2)}, u32[]{:S(2)}) collective-permute-start(bf16[48,6656]{1,0:T(8,128)(2,1)S(1)} %collective-permute-done.refs_2_), channel_id=1, source_target_pairs={{0,4},{4,0},{8,12},{12,8},{16,20},{20,16},{24,28},{28,24},{1,5},{5... | collective-permute-start | bytes 1916936 | tf_op jit(solution)/shard_map/ppermute | solution.py:303
  30.4 27.8 %copy-start.6 = (f32[3,128,128]{2,1,0:T(8,128)S(1)}, f32[3,128,128]{2,1,0:T(8,128)}, u32[]{:S(2)}) copy-start(f32[3,128,128]{2,1,0:T(8,128)} %param.7) | copy-start | bytes 589828
  47.1 16.6 %collective-permute-start.7 = (bf16[48,6656]{1,0:T(8,128)(2,1)S(1)}, bf16[48,6656]{1,0:T(8,128)(2,1)S(1)}, u32[]{:S(2)}, u32[]{:S(2)}) collective-permute-start(bf16[48,6656]{1,0:T(8,128)(2,1)S(1)} %collective-permute-done.3), channel_id=1, source_target_pairs={{8,0},{12,4},{16,24},{20,28},{9,1},{13,5},{17,25},{21,29},{10,2},{... | collective-permute-start | bytes 1916936 | tf_op jit(solution)/shard_map/ppermute | solution.py:303
  48.4 27.6 %copy-start.1 = (bf16[48,6656]{1,0:T(8,128)(2,1)S(1)}, bf16[48,6656]{1,0:T(8,128)(2,1)}, u32[]{:S(2)}) copy-start(bf16[48,6656]{1,0:T(8,128)(2,1)} %shard_map.59.refs_0_) | copy-start | bytes 1916932
  49.6 14.1 %collective-permute-start.6 = (bf16[48,6656]{1,0:T(8,128)(2,1)S(1)}, bf16[48,6656]{1,0:T(8,128)(2,1)S(1)}, u32[]{:S(2)}, u32[]{:S(2)}) collective-permute-start(bf16[48,6656]{1,0:T(8,128)(2,1)S(1)} %broadcast_select_fusion.refs_4_), channel_id=1, source_target_pairs={{0,4},{4,0},{8,12},{12,8},{16,20},{20,16},{24,28},{28,24},{1,5},{5... | collective-permute-start | bytes 1916936 | tf_op jit(solution)/shard_map/ppermute | solution.py:303
  51.2 12.5 %collective-permute-start.8 = (bf16[48,6656]{1,0:T(8,128)(2,1)S(1)}, bf16[48,6656]{1,0:T(8,128)(2,1)S(1)}, u32[]{:S(2)}, u32[]{:S(2)}) collective-permute-start(bf16[48,6656]{1,0:T(8,128)(2,1)S(1)} %collective-permute-done.2.refs_1_), channel_id=1, source_target_pairs={{8,16},{12,20},{16,8},{20,12},{9,17},{13,21},{17,9},{21,13},{10,18... | collective-permute-start | bytes 1916936 | tf_op jit(solution)/shard_map/ppermute | solution.py:303
  52.1 1.1 %copy-start = (bf16[48,6656]{1,0:T(8,128)(2,1)S(1)}, bf16[48,6656]{1,0:T(8,128)(2,1)}, u32[]{:S(2)}) copy-start(bf16[48,6656]{1,0:T(8,128)(2,1)} %shard_map.59.refs_0_) | copy-start | bytes 1916932
  58.1 1.6 %collective-permute-start.9 = (f32[184,384]{1,0:T(8,128)S(1)}, f32[184,384]{1,0:T(8,128)S(1)}, u32[]{:S(2)}, u32[]{:S(2)}) collective-permute-start(f32[184,384]{1,0:T(8,128)S(1)} %get-tuple-element.34), channel_id=1, source_target_pairs={{0,1},{1,0},{2,3},{3,2},{4,5},{5,4},{6,7},{7,6},{8,9},{9,8},{10,11... | collective-permute-start | bytes 847880 | tf_op jit(solution)/shard_map/ppermute | solution.py:300
  63.7 12.3 %collective-permute-start.10 = (bf16[48,6656]{1,0:T(8,128)(2,1)S(1)}, bf16[48,6656]{1,0:T(8,128)(2,1)S(1)}, u32[]{:S(2)}, u32[]{:S(2)}) collective-permute-start(bf16[48,6656]{1,0:T(8,128)(2,1)S(1)} %collective-permute-done.7.refs_7_), channel_id=1, source_target_pairs={{0,4},{2,6},{4,0},{6,2},{24,28},{26,30},{28,24},{30,26}} | collective-permute-start | bytes 1916936 | tf_op jit(solution)/shard_map/ppermute | solution.py:341
  67.1 8.9 %collective-permute-start.11 = (bf16[48,6656]{1,0:T(8,128)(2,1)S(1)}, bf16[48,6656]{1,0:T(8,128)(2,1)S(1)}, u32[]{:S(2)}, u32[]{:S(2)}) collective-permute-start(bf16[48,6656]{1,0:T(8,128)(2,1)S(1)} %collective-permute-done.6.refs_5_), channel_id=1, source_target_pairs={{9,1},{11,3},{13,5},{15,7},{17,25},{19,27},{21,29},{23,31}} | collective-permute-start | bytes 1916936 | tf_op jit(solution)/shard_map/ppermute | solution.py:342
  68.3 6.7 %collective-permute-start.12 = (f32[184,384]{1,0:T(8,128)S(1)}, f32[184,384]{1,0:T(8,128)S(1)}, u32[]{:S(2)}, u32[]{:S(2)}) collective-permute-start(f32[184,384]{1,0:T(8,128)S(1)} %add.34), channel_id=1, source_target_pairs={{0,2},{1,3},{2,0},{3,1},{4,6},{5,7},{6,4},{7,5},{8,10},{9,11},{10,... | collective-permute-start | bytes 847880 | tf_op jit(solution)/shard_map/ppermute | solution.py:300
  82.1 10.7 %copy-start.2 = (f32[384,512]{1,0:T(8,128)S(1)}, f32[384,512]{1,0:T(8,128)}, u32[]{:S(2)}) copy-start(f32[384,512]{1,0:T(8,128)} %refs_9_.1) | copy-start | bytes 2359300
  82.1 1.5 %collective-permute-start.15 = (f32[144,384]{1,0:T(8,128)S(1)}, f32[144,384]{1,0:T(8,128)S(1)}, u32[]{:S(2)}, u32[]{:S(2)}) collective-permute-start(f32[144,384]{1,0:T(8,128)S(1)} %get-tuple-element.46), channel_id=1, source_target_pairs={{0,1},{1,0},{2,3},{3,2},{4,5},{5,4},{6,7},{7,6},{8,9},{9,8},{10,11... | collective-permute-start | bytes 663560 | tf_op jit(solution)/shard_map/ppermute | solution.py:300
  82.2 3.9 %collective-permute-start.13 = (f32[384,256]{1,0:T(8,128)S(1)}, f32[384,256]{1,0:T(8,128)S(1)}, u32[]{:S(2)}, u32[]{:S(2)}) collective-permute-start(f32[384,256]{1,0:T(8,128)S(1)} %get-tuple-element.41.refs_0_), channel_id=1, source_target_pairs={{0,1},{1,0},{2,3},{3,2},{4,5},{5,4},{6,7},{7,6},{8,9},{9,8},{10,11... | collective-permute-start | bytes 1179656 | tf_op jit(solution)/shard_map/ppermute | solution.py:300
  83.0 2.3 %collective-permute-start.14 = (f32[184,384]{1,0:T(8,128)S(1)}, f32[184,384]{1,0:T(8,128)S(1)}, u32[]{:S(2)}, u32[]{:S(2)}) collective-permute-start(f32[184,384]{1,0:T(8,128)S(1)} %add.37.refs_3_), channel_id=1, source_target_pairs={{0,1},{1,0},{2,3},{3,2},{4,5},{5,4},{6,7},{7,6},{8,9},{9,8},{10,11... | collective-permute-start | bytes 847880 | tf_op jit(solution)/shard_map/ppermute | solution.py:300
  83.7 7.5 %collective-permute-start.16 = (f32[144,384]{1,0:T(8,128)S(1)}, f32[144,384]{1,0:T(8,128)S(1)}, u32[]{:S(2)}, u32[]{:S(2)}) collective-permute-start(f32[144,384]{1,0:T(8,128)S(1)} %add.38), channel_id=1, source_target_pairs={{0,2},{1,3},{2,0},{3,1},{4,6},{5,7},{6,4},{7,5},{8,10},{9,11},{10,... | collective-permute-start | bytes 663560 | tf_op jit(solution)/shard_map/ppermute | solution.py:300
  85.4 0.7 copy-start.3
  86.1 1.0 copy-start.4
  91.3 1.5 %collective-permute-start.17 = (f32[144,384]{1,0:T(8,128)S(1)}, f32[144,384]{1,0:T(8,128)S(1)}, u32[]{:S(2)}, u32[]{:S(2)}) collective-permute-start(f32[144,384]{1,0:T(8,128)S(1)} %add.39.refs_3_), channel_id=1, source_target_pairs={{0,1},{1,0},{2,3},{3,2},{4,5},{5,4},{6,7},{7,6},{8,9},{9,8},{10,11... | collective-permute-start | bytes 663560 | tf_op jit(solution)/shard_map/ppermute | solution.py:300

commit v7 on v6

--- a/solution.py
+++ b/solution.py
@@ -177,33 +177,33 @@
 ):
     index = pltpu.make_async_copy(index_hbm, index_ref, side_sems.at[0])
     index.start()
+    copies = fetch(features_ref, held_ref, sems)
     side = pltpu.make_async_copy(targets_ref, held_targets, side_sems.at[1])
     side.start()
-    copies = fetch(features_ref, held_ref, sems)
     index.wait()
     rank, core = place_ref[0], place_ref[1]
     rows, columns = features_ref.shape
     steps = index_ref.shape[0]
-    line = lax.broadcasted_iota(jnp.int32, (steps * per, rows), 0)
-    wanted = jnp.zeros((steps * per, rows), jnp.int32)
+    line = lax.broadcasted_iota(jnp.int32, (steps * per, 128), 0)
+    wanted = jnp.zeros((steps * per, 128), jnp.int32)
     for step in range(steps):
         for i in range(per):
             wanted = jnp.where(line == step * per + i, index_ref[step, rank * per + i], wanted)
-    chosen = wanted - rank * rows == lax.broadcasted_iota(jnp.int32, wanted.shape, 1)
+    chosen = wanted[:, :1] - rank * rows == lax.broadcasted_iota(jnp.int32, (steps * per, rows), 1)
     chosen = chosen.astype(jnp.float32).astype(jnp.bfloat16)
 
     def take(array):
         return jnp.dot(chosen, array, preferred_element_type=jnp.float32).astype(jnp.bfloat16)
 
+    for copy, at in zip(copies, pieces_of(features_ref)):
+        copy.wait()
+        out_ref[:, at] = take(held_ref[:, at])
     side.wait()
     width = targets_ref.shape[1] // 2
     values = jnp.where(core == 0, held_targets[:, :width], held_targets[:, width:])
     high, low = split(values)
     out_ref[:, columns : columns + width] = take(high)
     out_ref[:, columns + width :] = take(low)
-    for copy, at in zip(copies, pieces_of(features_ref)):
-        copy.wait()
-        out_ref[:, at] = take(held_ref[:, at])
 
 
 def pick(block_index, place, features, targets, per):
@@ -247,7 +247,7 @@
 
 
 def last_kernel(steps, per, begun, place_ref, *refs):
-    *slot_refs, inner_ref, left_ref, right_ref, features_ref = refs[:-5]
+    *slot_refs, left_in_ref, right_in_ref, left_ref, right_ref, features_ref = refs[:-5]
     keep_ref, send_ref, first_ref, held_ref, sems = refs[-5:]
     core = place_ref[1]
     inner = place_ref[2] == 1
@@ -259,23 +259,29 @@
         other = slots.pop()
         slots[-1] = jnp.where(inner, slots[-1], other)
         last = jnp.where(core == 0, left_ref[:, at], right_ref[:, at])
-        return slots + [jnp.where(inner, inner_ref[:, at], last)]
+        last_in = jnp.where(core == 0, left_in_ref[:, at], right_in_ref[:, at])
+        return slots + [jnp.where(inner, last_in, last)]
 
     def every(slots):
         return jnp.concatenate([of_step(slots, step, per) for step in range(steps)], axis=0)
 
-    total, cross = None, None
-    for at in pieces_of(features_ref):
+    rows = features_ref.shape[0]
+    both = None
+    for copy, at in zip(copies, pieces_of(features_ref)):
         slots = slots_at(at)
-        cross = add(cross, dot_rows(every(slots), jnp.concatenate(slots[begun:], axis=0)))
-    for copy, at in zip(copies, pieces_of(features_ref)):
-        new = jnp.concatenate(slots_at(at)[begun:], axis=0)
-        copy.wait()
-        total = add(total, dot_rows(held_ref[:, at], new))
+        new = jnp.concatenate(slots[begun:], axis=0)
+        if both is None:
+            cross = dot_rows(every(slots), new)
+            copy.wait()
+            both = jnp.concatenate([dot_rows(held_ref[:, at], new), cross], axis=0)
+        else:
+            copy.wait()
+            both = both + dot_rows(jnp.concatenate([held_ref[:, at], every(slots)], axis=0), new)
+    total, cross = both[:rows], both[rows:]
     total, cross = total.T, cross.T
     keep_ref[...] = jnp.where(core == 0, total, cross)
     send_ref[...] = jnp.where(core == 0, cross, total)
-    width = (inner_ref.shape[1] - columns) // 2
+    width = (left_ref.shape[1] - columns) // 2
     high = every(slots_at(slice(columns, columns + width)))
     low = every(slots_at(slice(columns + width, columns + 2 * width)))
     first_ref[...] = high.astype(jnp.float32) + low.astype(jnp.float32)
@@ -289,6 +295,9 @@
         self.outer = [(2, 0), (3, 1), (4, 6), (5, 7)]
         ends = [(r, r ^ 1) for r in (0, 1, 6, 7)]
         self.ends = [(4 * r + f, 4 * to + f) for r, to in ends for f in (0, 2)]
+        inner = [(r, r ^ 1) for r in range(2, 6)]
+        self.inner_beside = [(4 * r + f, 4 * to + f) for r, to in inner for f in (0, 2)]
+        self.inner_second = [(4 * r + f, 4 * to + f) for r, to in self.inner for f in (1, 3)]
         self.outer_second = [(4 * r + f, 4 * to + f) for r, to in self.outer for f in (1, 3)]
         rank = lax.axis_index("rows")
         core = lax.axis_index("feat") % 2
@@ -322,7 +331,6 @@
         third = jnp.where(self.is_inner, far, mid_end)
         third_b = self.send(third, self.beside)
         far_end = self.send(far, self.outer)
-        last_in = self.send(own_b, self.inner)
         slots = [own, own_b, pair, pair_b, third]
         begun = len(slots)
         part = jax.ShapeDtypeStruct(((begun * count + block) // 2, rows), jnp.float32)
@@ -336,15 +344,16 @@
             cost_estimate=cost((begun * count + block) * rows, columns),
         )(self.place, *slots, features)
         gram = gram + self.near(given, 1)
-        third_b, far_end, last_in, gram = hold((third_b, far_end, last_in, gram))
+        third_b, far_end, gram, own_b, mid = hold((third_b, far_end, gram, own_b, mid))
 
         left = lax.ppermute(far_end, ("rows", "feat"), self.ends)
         right = lax.ppermute(third_b, ("rows", "feat"), self.outer_second)
+        left_in = lax.ppermute(mid, ("rows", "feat"), self.inner_beside)
+        right_in = lax.ppermute(own_b, ("rows", "feat"), self.inner_second)
         gram_near = self.near(gram, 2)
-        left, right, gram_near = hold((left, right, gram_near))
-        gram = gram + gram_near
-
-        slots = slots + [third_b, mid, far_end, last_in, left, right]
+        left, right, left_in, right_in = hold((left, right, left_in, right_in))
+
+        slots = [own, own_b, pair, pair_b, third, third_b, mid, far_end, left_in, right_in, left, right]
         end = jax.ShapeDtypeStruct(((8 - begun) * count, rows), jnp.float32)
         keep, given, first = pl.pallas_call(
             functools.partial(last_kernel, steps, per, begun),
@@ -360,6 +369,8 @@
             cost_estimate=cost((8 - begun) * count * (rows + steps * block), columns),
         )(self.place, *slots, features)
         keep = keep + self.near(given, 1)
+        keep, gram_near = hold((keep, gram_near))
+        gram = gram + gram_near
         keep_near = self.near(keep, 2)
         first, early, cross = pl.pallas_call(
             functools.partial(ready_kernel, steps, per),
@@ -373,7 +384,8 @@
             compiler_params=PARAMS,
             cost_estimate=cost(3 * steps * block * block, targets.shape[1]),
         )(self.place, first, self.near(first, 1), turned, gram, self.near(gram, 1))
-        keep, first = hold((keep + keep_near, first))
+        keep, first = hold((keep, first))
+        keep = keep + keep_near
         return [self.place, early, cross, keep, self.near(keep, 1)], first
 
 

time: 96.8 us -> 101 us (1.043)
  other arithmetic: 2.3 us -> 3.97 us
  waiting for transfers between devices: 46.9 us -> 48 us
    ppermute x1, waiting for transfers between devices: 0.98 us -> 6.79 us  [run(): left = lax.ppermute(far_end, ('rows', 'feat'), self.ends)]
    ppermute x7, waiting for transfers between devices: 10.8 us -> 6.22 us  [near(): return lax.ppermute(array, 'feat', [(f, f ^ bit) for f in range(4)])]
    ppermute x0 -> x2, starting transfers between devices: none -> 1.4 us  [the longest x1 0.7 us: run(): left_in = lax.ppermute(mid, ('rows', 'feat'), self.inner_beside)]
    ppermute x9 -> x8, starting transfers between devices: 12.5 us -> 11.8 us  [send(): return lax.ppermute(array, 'rows', pairs)]
    ppermute x9 -> x8, waiting for transfers between devices: 35.1 us -> 35 us  [send(): return lax.ppermute(array, 'rows', pairs)]
    unnamed x16 -> x18, local copies, waits for them, and re-layouts: 2.77 us -> 2.77 us
  transfers between devices with their start and end apart: 18 -> 19, of which waited for: 10 -> 9; matrix products, arithmetic and copies ran while one was open for 4% -> 5% of each run, Pallas kernels for 6% -> 13%
where the time goes in v7:
time: 101 us
  waiting for transfers between devices  48 us (48%)
  starting transfers between devices  21.4 us (21%)
  Pallas kernels  21.1 us (21%)
  other arithmetic  3.97 us (4%)
  local copies, waits for them, and re-layouts  3.01 us (3%)
  matrix products  2.36 us (2%)
    ppermute x8, waiting for transfers between devices, send(): return lax.ppermute(array, 'rows', pairs)  35 us
    ppermute x8, starting transfers between devices, send(): return lax.ppermute(array, 'rows', pairs)  11.8 us
    pallas_call x1, Pallas kernels, run(): pl.pallas_call(functools.partial(last_kernel, steps, per, begun), out_sha...  6.83 us
    ppermute x1, waiting for transfers between devices, run(): left = lax.ppermute(far_end, ('rows', 'feat'), self.ends)  6.79 us
    ppermute x7, waiting for transfers between devices, near(): return lax.ppermute(array, 'feat', [(f, f ^ bit) for f in range(4)])  6.22 us
    pallas_call x1, Pallas kernels, run(): pl.pallas_call(functools.partial(gram_kernel, steps, per, 8 - begun), out...  4.95 us
    pallas_call x1, Pallas kernels, pick(): pl.pallas_call(functools.partial(pick_kernel, per), out_shape=jax.ShapeDt...  4.54 us
    ppermute x7, starting transfers between devices, near(): return lax.ppermute(array, 'feat', [(f, f ^ bit) for f in range(4)])  4.09 us
  transfers between devices with their start and end apart: 19, of which 9 were waited for; matrix products, arithmetic and copies ran while one was open for 5% of the time, Pallas kernels for 13%

profile of v7, /device:TPU:0, one launch (start us, length us, event | category | flops | bytes accessed | tf_op | source)
XLA Modules:
  0.0 100.9 jit_solution(5355737274355778785)
XLA Ops:
  0.6 0.6 pad_add_fusion.place_ref.refs_0_
  1.3 4.5 %shard_map.59.refs_0_ = bf16[48,6656]{1,0:T(8,128)(2,1)} custom-call(s32[3,128]{1,0:T(4,128)} %index_hbm.1, s32[3]{0:T(128)} %pad_add_fusion.place_ref.refs_0_, bf16[384,6144]{1,0:T(8,128)(2,1)} %refs_12_.1, f32[384,512]{1,0:T(8,128)} %refs_9_.1), custom_call_target="tpu_custom_call" | custom-call | flops 245366784 | bytes 73728 | tf_op jit(solution)/shard_map/pallas_call | solution.py:212
  5.8 3.1 %collective-permute-start = (bf16[48,6656]{1,0:T(8,128)(2,1)}, bf16[48,6656]{1,0:T(8,128)(2,1)S(1)}, u32[]{:S(2)}, u32[]{:S(2)}) collective-permute-start(bf16[48,6656]{1,0:T(8,128)(2,1)} %shard_map.59.refs_0_), channel_id=1, source_target_pairs={{0,8},{4,12},{8,0},{12,4},{16,24},{20,28},{24,16},{28,20},{1,9},{5... | collective-permute-start | bytes 1916936 | tf_op jit(solution)/shard_map/ppermute | solution.py:312
  8.9 0.7 collective-permute-start.1
  9.6 1.6 %collective-permute-start.2 = (bf16[48,6656]{1,0:T(8,128)(2,1)}, bf16[48,6656]{1,0:T(8,128)(2,1)S(1)}, u32[]{:S(2)}, u32[]{:S(2)}) collective-permute-start(bf16[48,6656]{1,0:T(8,128)(2,1)} %shard_map.59.refs_0_), channel_id=1, source_target_pairs={{0,4},{4,0},{8,12},{12,8},{16,20},{20,16},{24,28},{28,24},{1,5},{5... | collective-permute-start | bytes 1916936 | tf_op jit(solution)/shard_map/ppermute | solution.py:312
  11.2 12.3 %collective-permute-done.refs_2_ = bf16[48,6656]{1,0:T(8,128)(2,1)S(1)} collective-permute-done((bf16[48,6656]{1,0:T(8,128)(2,1)}, bf16[48,6656]{1,0:T(8,128)(2,1)S(1)}, u32[]{:S(2)}, u32[]{:S(2)}) %collective-permute-start) | collective-permute-done | bytes 639008 | tf_op jit(solution)/shard_map/ppermute | solution.py:312
  23.5 2.2 %collective-permute-done.2.refs_1_ = bf16[48,6656]{1,0:T(8,128)(2,1)S(1)} collective-permute-done((bf16[48,6656]{1,0:T(8,128)(2,1)}, bf16[48,6656]{1,0:T(8,128)(2,1)S(1)}, u32[]{:S(2)}, u32[]{:S(2)}) %collective-permute-start.2) | collective-permute-done | bytes 639008 | tf_op jit(solution)/shard_map/ppermute | solution.py:312
  25.7 0.7 collective-permute-start.3
  26.4 1.3 %collective-permute-start.4 = (bf16[48,6656]{1,0:T(8,128)(2,1)S(1)}, bf16[48,6656]{1,0:T(8,128)(2,1)}, u32[]{:S(2)}, u32[]{:S(2)}) collective-permute-start(bf16[48,6656]{1,0:T(8,128)(2,1)S(1)} %collective-permute-done.1.refs_6_), channel_id=1, source_target_pairs={{8,0},{12,4},{16,24},{20,28},{9,1},{13,5},{17,25},{21,29},{10,2},{... | collective-permute-start | bytes 1916936 | tf_op jit(solution)/shard_map/ppermute | solution.py:312
  27.7 1.6 %collective-permute-start.5 = (bf16[48,6656]{1,0:T(8,128)(2,1)S(1)}, bf16[48,6656]{1,0:T(8,128)(2,1)S(1)}, u32[]{:S(2)}, u32[]{:S(2)}) collective-permute-start(bf16[48,6656]{1,0:T(8,128)(2,1)S(1)} %collective-permute-done.refs_2_), channel_id=1, source_target_pairs={{0,4},{4,0},{8,12},{12,8},{16,20},{20,16},{24,28},{28,24},{1,5},{5... | collective-permute-start | bytes 1916936 | tf_op jit(solution)/shard_map/ppermute | solution.py:312
  29.4 0.1 mul.21
  29.5 16.8 %collective-permute-done.4 = bf16[48,6656]{1,0:T(8,128)(2,1)} collective-permute-done((bf16[48,6656]{1,0:T(8,128)(2,1)S(1)}, bf16[48,6656]{1,0:T(8,128)(2,1)}, u32[]{:S(2)}, u32[]{:S(2)}) %collective-permute-start.4) | collective-permute-done | bytes 639008 | tf_op jit(solution)/shard_map/ppermute | solution.py:312
  46.3 1.3 %collective-permute-start.7 = (bf16[48,6656]{1,0:T(8,128)(2,1)S(1)}, bf16[48,6656]{1,0:T(8,128)(2,1)S(1)}, u32[]{:S(2)}, u32[]{:S(2)}) collective-permute-start(bf16[48,6656]{1,0:T(8,128)(2,1)S(1)} %collective-permute-done.3), channel_id=1, source_target_pairs={{8,0},{12,4},{16,24},{20,28},{9,1},{13,5},{17,25},{21,29},{10,2},{... | collective-permute-start | bytes 1916936 | tf_op jit(solution)/shard_map/ppermute | solution.py:312
  47.6 1.2 %broadcast_select_fusion.refs_4_ = bf16[48,6656]{1,0:T(8,128)(2,1)S(1)} fusion(bf16[48,6656]{1,0:T(8,128)(2,1)S(1)} %collective-permute-done.3, bf16[48,6656]{1,0:T(8,128)(2,1)} %collective-permute-done.4, pred[]{:T(512)S(6)} %and.23), kind=kLoop, calls=%fused_computation.3 | loop fusion | flops 319488 | bytes 1916929 | tf_op jit(solution)/shard_map/jit(_where)/select_n | solution.py:331
  48.8 1.6 %collective-permute-start.6 = (bf16[48,6656]{1,0:T(8,128)(2,1)S(1)}, bf16[48,6656]{1,0:T(8,128)(2,1)S(1)}, u32[]{:S(2)}, u32[]{:S(2)}) collective-permute-start(bf16[48,6656]{1,0:T(8,128)(2,1)S(1)} %broadcast_select_fusion.refs_4_), channel_id=1, source_target_pairs={{0,4},{4,0},{8,12},{12,8},{16,20},{20,16},{24,28},{28,24},{1,5},{5... | collective-permute-start | bytes 1916936 | tf_op jit(solution)/shard_map/ppermute | solution.py:312
  50.4 1.1 %fusion = f32[128,128]{1,0:T(8,128)S(1)} fusion(f32[3,128,128]{2,1,0:T(8,128)} %param.7, s32[128]{0:T(128)S(1)} %fusion.15), kind=kOutput, calls=%fused_computation.7 | convolution fusion | flops 25182208 | bytes 131584 | tf_op jit(solution)/shard_map/dot_general | solution.py:32
  51.5 1.1 %copy-done = bf16[48,6656]{1,0:T(8,128)(2,1)S(1)} copy-done((bf16[48,6656]{1,0:T(8,128)(2,1)S(1)}, bf16[48,6656]{1,0:T(8,128)(2,1)}, u32[]{:S(2)}) %copy-start) | copy-done | bytes 639000
  52.6 4.9 %shard_map.60 = (f32[184,384]{1,0:T(8,128)S(1)}, f32[184,384]{1,0:T(8,128)S(1)}) custom-call(s32[3]{0:T(128)S(1)} %copy-done.5, bf16[48,6656]{1,0:T(8,128)(2,1)S(1)} %copy-done, bf16[48,6656]{1,0:T(8,128)(2,1)S(1)} %collective-permute-done.2.refs_1_, bf16[48,6656]{1,0:T(8,128)(2,1)S(1)} %collective-permute-done.refs_2_, ...), custom_call_target="tpu_custom_call" | custom-call | flops 1736441856 | bytes 565248 | tf_op jit(solution)/shard_map/pallas_call | solution.py:337
  57.6 0.1 iota_compare_fusion
  57.7 0.3 convolution_bitcast_fusion
  58.0 0.1 select_reduce_fusion
  58.2 1.0 %collective-permute-done.8 = f32[184,384]{1,0:T(8,128)S(1)} collective-permute-done((f32[184,384]{1,0:T(8,128)S(1)}, f32[184,384]{1,0:T(8,128)S(1)}, u32[]{:S(2)}, u32[]{:S(2)}) %collective-permute-start.8) | collective-permute-done | bytes 282656 | tf_op jit(solution)/shard_map/ppermute | solution.py:309
  59.2 3.7 %collective-permute-done.6.refs_5_ = bf16[48,6656]{1,0:T(8,128)(2,1)S(1)} collective-permute-done((bf16[48,6656]{1,0:T(8,128)(2,1)S(1)}, bf16[48,6656]{1,0:T(8,128)(2,1)S(1)}, u32[]{:S(2)}, u32[]{:S(2)}) %collective-permute-start.6) | collective-permute-done | bytes 639008 | tf_op jit(solution)/shard_map/ppermute | solution.py:312
  62.9 0.7 collective-permute-start.10
  63.6 0.7 collective-permute-start.11
  64.3 0.7 collective-permute-start.12
  65.0 3.4 %collective-permute-start.9 = (bf16[48,6656]{1,0:T(8,128)(2,1)S(1)}, bf16[48,6656]{1,0:T(8,128)(2,1)S(1)}, u32[]{:S(2)}, u32[]{:S(2)}) collective-permute-start(bf16[48,6656]{1,0:T(8,128)(2,1)S(1)} %collective-permute-done.7.refs_7_), channel_id=1, source_target_pairs={{0,4},{2,6},{4,0},{6,2},{24,28},{26,30},{28,24},{30,26}} | collective-permute-start | bytes 1916936 | tf_op jit(solution)/shard_map/ppermute | solution.py:349
  68.5 0.2 fusion.2
  68.7 0.2 fusion.4
  69.0 1.6 %collective-permute-start.15 = (f32[184,384]{1,0:T(8,128)S(1)}, f32[184,384]{1,0:T(8,128)S(1)}, u32[]{:S(2)}, u32[]{:S(2)}) collective-permute-start(f32[184,384]{1,0:T(8,128)S(1)} %add.34), channel_id=1, source_target_pairs={{0,2},{1,3},{2,0},{3,1},{4,6},{5,7},{6,4},{7,5},{8,10},{9,11},{10,... | collective-permute-start | bytes 847880 | tf_op jit(solution)/shard_map/ppermute | solution.py:309
  70.5 6.8 %collective-permute-done.9.refs_10_ = bf16[48,6656]{1,0:T(8,128)(2,1)S(1)} collective-permute-done((bf16[48,6656]{1,0:T(8,128)(2,1)S(1)}, bf16[48,6656]{1,0:T(8,128)(2,1)S(1)}, u32[]{:S(2)}, u32[]{:S(2)}) %collective-permute-start.9) | collective-permute-done | bytes 639008 | tf_op jit(solution)/shard_map/ppermute | solution.py:349
  77.3 6.8 %shard_map.61 = (f32[144,384]{1,0:T(8,128)S(1)}, f32[144,384]{1,0:T(8,128)S(1)}, f32[384,256]{1,0:T(8,128)S(1)}) custom-call(s32[3]{0:T(128)S(1)} %copy-done.5, bf16[48,6656]{1,0:T(8,128)(2,1)S(1)} %copy-done.1, bf16[48,6656]{1,0:T(8,128)(2,1)S(1)} %collective-permute-done.2.refs_1_, bf16[48,6656]{1,0:T(8,128)(2,1)S(1)} %collective-permute-done.refs_2_, ...), custom_call_target="tpu_custom_call" | custom-call | flops 1358954496 | bytes 442368 | tf_op jit(solution)/shard_map/pallas_call | solution.py:358
  84.3 0.3 convolution_bitcast_fusion.1
  84.6 0.6 collective-permute-start.13
  85.1 0.3 convolution_bitcast_fusion.2
  85.4 0.3 collective-permute-done.14
  85.7 0.7 add.37
  86.5 0.2 collective-permute-start.16
  86.7 1.6 %collective-permute-start.17 = (f32[144,384]{1,0:T(8,128)}, f32[144,384]{1,0:T(8,128)S(1)}, u32[]{:S(2)}, u32[]{:S(2)}) collective-permute-start(f32[144,384]{1,0:T(8,128)} %add.37), channel_id=1, source_target_pairs={{0,2},{1,3},{2,0},{3,1},{4,6},{5,7},{6,4},{7,5},{8,10},{9,11},{10,... | collective-permute-start | bytes 663560 | tf_op jit(solution)/shard_map/ppermute | solution.py:309
  88.3 0.1 broadcast_compare_fusion.2
  88.4 0.7 copy-done.3
  89.1 1.0 copy-done.4
  90.1 1.1 %shard_map.62 = (f32[3,128,512]{2,1,0:T(8,128)S(1)}, bf16[2,3,80,384]{3,2,1,0:T(8,128)(2,1)S(1)}, f32[128,384]{1,0:T(8,128)S(1)}) custom-call(s32[3]{0:T(128)S(1)} %copy-done.5, f32[384,256]{1,0:T(8,128)S(1)} %get-tuple-element.47.refs_0_, f32[384,256]{1,0:T(8,128)S(1)} %collective-permute-done.13.refs_1_, ...), custom_call_target="tpu_custom_call" | custom-call | flops 150994944 | bytes 589824 | tf_op jit(solution)/shard_map/pallas_call | solution.py:375
  91.2 3.5 %collective-permute-done.17 = f32[144,384]{1,0:T(8,128)S(1)} collective-permute-done((f32[144,384]{1,0:T(8,128)}, f32[144,384]{1,0:T(8,128)S(1)}, u32[]{:S(2)}, u32[]{:S(2)}) %collective-permute-start.17) | collective-permute-done | bytes 221216 | tf_op jit(solution)/shard_map/ppermute | solution.py:309
  94.7 1.0 add.39.refs_3_
  95.7 0.1 sub.11.refs_8_
  95.9 1.3 %collective-permute-done.18.refs_4_ = f32[144,384]{1,0:T(8,128)S(1)} collective-permute-done((f32[144,384]{1,0:T(8,128)S(1)}, f32[144,384]{1,0:T(8,128)S(1)}, u32[]{:S(2)}, u32[]{:S(2)}) %collective-permute-start.18) | collective-permute-done | bytes 221216 | tf_op jit(solution)/shard_map/ppermute | solution.py:309
  97.2 3.7 %shard_map.63 = (f32[384,512]{1,0:T(8,128)}, f32[384,512]{1,0:T(8,128)}) custom-call(s32[3]{0:T(128)S(1)} %copy-done.5, bf16[2,3,80,384]{3,2,1,0:T(8,128)(2,1)S(1)} %get-tuple-element.52.refs_1_, f32[128,384]{1,0:T(8,128)S(1)} %get-tuple-element.53.refs_2_, f32[144,384]{1,0:T(8,128)S(1)} %add.39.refs_3_, f32[144,384]{1,0:T(8,128)S(1)} %collective-permute-done.18.refs_4_, ...), custom_call_target="tpu_custom_call" | custom-call | flops 452984832 | bytes 1769472 | tf_op jit(solution)/shard_map/pallas_call | solution.py:457
  (37 shorter events, 0.5 us)
Async XLA Ops:
  1.3 50.2 %copy-start.5 = (s32[3]{0:T(128)S(1)}, s32[3]{0:T(128)}, u32[]{:S(2)}) copy-start(s32[3]{0:T(128)} %pad_add_fusion.place_ref.refs_0_) | copy-start | bytes 40
  5.8 17.7 %collective-permute-start = (bf16[48,6656]{1,0:T(8,128)(2,1)}, bf16[48,6656]{1,0:T(8,128)(2,1)S(1)}, u32[]{:S(2)}, u32[]{:S(2)}) collective-permute-start(bf16[48,6656]{1,0:T(8,128)(2,1)} %shard_map.59.refs_0_), channel_id=1, source_target_pairs={{0,8},{4,12},{8,0},{12,4},{16,24},{20,28},{24,16},{28,20},{1,9},{5... | collective-permute-start | bytes 1916936 | tf_op jit(solution)/shard_map/ppermute | solution.py:312
  8.9 14.6 %collective-permute-start.1 = (bf16[48,6656]{1,0:T(8,128)(2,1)}, bf16[48,6656]{1,0:T(8,128)(2,1)S(1)}, u32[]{:S(2)}, u32[]{:S(2)}) collective-permute-start(bf16[48,6656]{1,0:T(8,128)(2,1)} %shard_map.59.refs_0_), channel_id=1, source_target_pairs={{8,16},{12,20},{16,8},{20,12},{9,17},{13,21},{17,9},{21,13},{10,18... | collective-permute-start | bytes 1916936 | tf_op jit(solution)/shard_map/ppermute | solution.py:312
  9.6 16.1 %collective-permute-start.2 = (bf16[48,6656]{1,0:T(8,128)(2,1)}, bf16[48,6656]{1,0:T(8,128)(2,1)S(1)}, u32[]{:S(2)}, u32[]{:S(2)}) collective-permute-start(bf16[48,6656]{1,0:T(8,128)(2,1)} %shard_map.59.refs_0_), channel_id=1, source_target_pairs={{0,4},{4,0},{8,12},{12,8},{16,20},{20,16},{24,28},{28,24},{1,5},{5... | collective-permute-start | bytes 1916936 | tf_op jit(solution)/shard_map/ppermute | solution.py:312
  25.7 3.8 %collective-permute-start.3 = (bf16[48,6656]{1,0:T(8,128)(2,1)S(1)}, bf16[48,6656]{1,0:T(8,128)(2,1)S(1)}, u32[]{:S(2)}, u32[]{:S(2)}) collective-permute-start(bf16[48,6656]{1,0:T(8,128)(2,1)S(1)} %collective-permute-done.refs_2_), channel_id=1, source_target_pairs={{8,16},{12,20},{16,8},{20,12},{9,17},{13,21},{17,9},{21,13},{10,18... | collective-permute-start | bytes 1916936 | tf_op jit(solution)/shard_map/ppermute | solution.py:312
  26.4 19.9 %collective-permute-start.4 = (bf16[48,6656]{1,0:T(8,128)(2,1)S(1)}, bf16[48,6656]{1,0:T(8,128)(2,1)}, u32[]{:S(2)}, u32[]{:S(2)}) collective-permute-start(bf16[48,6656]{1,0:T(8,128)(2,1)S(1)} %collective-permute-done.1.refs_6_), channel_id=1, source_target_pairs={{8,0},{12,4},{16,24},{20,28},{9,1},{13,5},{17,25},{21,29},{10,2},{... | collective-permute-start | bytes 1916936 | tf_op jit(solution)/shard_map/ppermute | solution.py:312
  27.7 18.6 %collective-permute-start.5 = (bf16[48,6656]{1,0:T(8,128)(2,1)S(1)}, bf16[48,6656]{1,0:T(8,128)(2,1)S(1)}, u32[]{:S(2)}, u32[]{:S(2)}) collective-permute-start(bf16[48,6656]{1,0:T(8,128)(2,1)S(1)} %collective-permute-done.refs_2_), channel_id=1, source_target_pairs={{0,4},{4,0},{8,12},{12,8},{16,20},{20,16},{24,28},{28,24},{1,5},{5... | collective-permute-start | bytes 1916936 | tf_op jit(solution)/shard_map/ppermute | solution.py:312
  29.5 28.5 %copy-start.8 = (s32[3,128]{1,0:T(4,128)S(1)}, s32[3,128]{1,0:T(4,128)}, u32[]{:S(2)}) copy-start(s32[3,128]{1,0:T(4,128)} %index_hbm.1) | copy-start | bytes 4612
  46.3 16.6 %collective-permute-start.7 = (bf16[48,6656]{1,0:T(8,128)(2,1)S(1)}, bf16[48,6656]{1,0:T(8,128)(2,1)S(1)}, u32[]{:S(2)}, u32[]{:S(2)}) collective-permute-start(bf16[48,6656]{1,0:T(8,128)(2,1)S(1)} %collective-permute-done.3), channel_id=1, source_target_pairs={{8,0},{12,4},{16,24},{20,28},{9,1},{13,5},{17,25},{21,29},{10,2},{... | collective-permute-start | bytes 1916936 | tf_op jit(solution)/shard_map/ppermute | solution.py:312
  47.6 20.9 %copy-start.7 = (f32[3,128,128]{2,1,0:T(8,128)S(1)}, f32[3,128,128]{2,1,0:T(8,128)}, u32[]{:S(2)}) copy-start(f32[3,128,128]{2,1,0:T(8,128)} %param.7) | copy-start | bytes 589828
  47.6 29.8 %copy-start.1 = (bf16[48,6656]{1,0:T(8,128)(2,1)S(1)}, bf16[48,6656]{1,0:T(8,128)(2,1)}, u32[]{:S(2)}) copy-start(bf16[48,6656]{1,0:T(8,128)(2,1)} %shard_map.59.refs_0_) | copy-start | bytes 1916932
  48.8 14.1 %collective-permute-start.6 = (bf16[48,6656]{1,0:T(8,128)(2,1)S(1)}, bf16[48,6656]{1,0:T(8,128)(2,1)S(1)}, u32[]{:S(2)}, u32[]{:S(2)}) collective-permute-start(bf16[48,6656]{1,0:T(8,128)(2,1)S(1)} %broadcast_select_fusion.refs_4_), channel_id=1, source_target_pairs={{0,4},{4,0},{8,12},{12,8},{16,20},{20,16},{24,28},{28,24},{1,5},{5... | collective-permute-start | bytes 1916936 | tf_op jit(solution)/shard_map/ppermute | solution.py:312
  51.5 1.1 %copy-start = (bf16[48,6656]{1,0:T(8,128)(2,1)S(1)}, bf16[48,6656]{1,0:T(8,128)(2,1)}, u32[]{:S(2)}) copy-start(bf16[48,6656]{1,0:T(8,128)(2,1)} %shard_map.59.refs_0_) | copy-start | bytes 1916932
  57.5 1.6 %collective-permute-start.8 = (f32[184,384]{1,0:T(8,128)S(1)}, f32[184,384]{1,0:T(8,128)S(1)}, u32[]{:S(2)}, u32[]{:S(2)}) collective-permute-start(f32[184,384]{1,0:T(8,128)S(1)} %get-tuple-element.38), channel_id=1, source_target_pairs={{0,1},{1,0},{2,3},{3,2},{4,5},{5,4},{6,7},{7,6},{8,9},{9,8},{10,11... | collective-permute-start | bytes 847880 | tf_op jit(solution)/shard_map/ppermute | solution.py:309
  62.9 7.6 %collective-permute-start.10 = (bf16[48,6656]{1,0:T(8,128)(2,1)S(1)}, bf16[48,6656]{1,0:T(8,128)(2,1)S(1)}, u32[]{:S(2)}, u32[]{:S(2)}) collective-permute-start(bf16[48,6656]{1,0:T(8,128)(2,1)S(1)} %collective-permute-done.6.refs_5_), channel_id=1, source_target_pairs={{9,1},{11,3},{13,5},{15,7},{17,25},{19,27},{21,29},{23,31}} | collective-permute-start | bytes 1916936 | tf_op jit(solution)/shard_map/ppermute | solution.py:350
  63.6 6.9 %collective-permute-start.11 = (bf16[48,6656]{1,0:T(8,128)(2,1)S(1)}, bf16[48,6656]{1,0:T(8,128)(2,1)S(1)}, u32[]{:S(2)}, u32[]{:S(2)}) collective-permute-start(bf16[48,6656]{1,0:T(8,128)(2,1)S(1)} %collective-permute-done.1.refs_6_), channel_id=1, source_target_pairs={{8,12},{10,14},{12,8},{14,10},{16,20},{18,22},{20,16},{22,18}} | collective-permute-start | bytes 1916936 | tf_op jit(solution)/shard_map/ppermute | solution.py:351
  64.3 6.2 %collective-permute-start.12 = (bf16[48,6656]{1,0:T(8,128)(2,1)S(1)}, bf16[48,6656]{1,0:T(8,128)(2,1)S(1)}, u32[]{:S(2)}, u32[]{:S(2)}) collective-permute-start(bf16[48,6656]{1,0:T(8,128)(2,1)S(1)} %collective-permute-done.2.refs_1_), channel_id=1, source_target_pairs={{9,17},{11,19},{13,21},{15,23},{17,9},{19,11},{21,13},{23,15}} | collective-permute-start | bytes 1916936 | tf_op jit(solution)/shard_map/ppermute | solution.py:352
  65.0 12.3 %collective-permute-start.9 = (bf16[48,6656]{1,0:T(8,128)(2,1)S(1)}, bf16[48,6656]{1,0:T(8,128)(2,1)S(1)}, u32[]{:S(2)}, u32[]{:S(2)}) collective-permute-start(bf16[48,6656]{1,0:T(8,128)(2,1)S(1)} %collective-permute-done.7.refs_7_), channel_id=1, source_target_pairs={{0,4},{2,6},{4,0},{6,2},{24,28},{26,30},{28,24},{30,26}} | collective-permute-start | bytes 1916936 | tf_op jit(solution)/shard_map/ppermute | solution.py:349
  69.0 17.5 %collective-permute-start.15 = (f32[184,384]{1,0:T(8,128)S(1)}, f32[184,384]{1,0:T(8,128)S(1)}, u32[]{:S(2)}, u32[]{:S(2)}) collective-permute-start(f32[184,384]{1,0:T(8,128)S(1)} %add.34), channel_id=1, source_target_pairs={{0,2},{1,3},{2,0},{3,1},{4,6},{5,7},{6,4},{7,5},{8,10},{9,11},{10,... | collective-permute-start | bytes 847880 | tf_op jit(solution)/shard_map/ppermute | solution.py:309
  70.5 6.8 %copy-start.6 = (bf16[48,6656]{1,0:T(8,128)(2,1)}, bf16[48,6656]{1,0:T(8,128)(2,1)S(1)}, u32[]{:S(2)}) copy-start(bf16[48,6656]{1,0:T(8,128)(2,1)S(1)} %collective-permute-done.10.refs_11_) | copy-start | bytes 1916932
  84.2 13.0 %copy-start.2 = (f32[384,512]{1,0:T(8,128)S(1)}, f32[384,512]{1,0:T(8,128)}, u32[]{:S(2)}) copy-start(f32[384,512]{1,0:T(8,128)} %refs_9_.1) | copy-start | bytes 2359300
  84.2 1.5 %collective-permute-start.14 = (f32[144,384]{1,0:T(8,128)S(1)}, f32[144,384]{1,0:T(8,128)S(1)}, u32[]{:S(2)}, u32[]{:S(2)}) collective-permute-start(f32[144,384]{1,0:T(8,128)S(1)} %get-tuple-element.50), channel_id=1, source_target_pairs={{0,1},{1,0},{2,3},{3,2},{4,5},{5,4},{6,7},{7,6},{8,9},{9,8},{10,11... | collective-permute-start | bytes 663560 | tf_op jit(solution)/shard_map/ppermute | solution.py:309
  84.6 3.8 %collective-permute-start.13 = (f32[384,256]{1,0:T(8,128)S(1)}, f32[384,256]{1,0:T(8,128)S(1)}, u32[]{:S(2)}, u32[]{:S(2)}) collective-permute-start(f32[384,256]{1,0:T(8,128)S(1)} %get-tuple-element.47.refs_0_), channel_id=1, source_target_pairs={{0,1},{1,0},{2,3},{3,2},{4,5},{5,4},{6,7},{7,6},{8,9},{9,8},{10,11... | collective-permute-start | bytes 1179656 | tf_op jit(solution)/shard_map/ppermute | solution.py:309
  86.5 1.9 %collective-permute-start.16 = (f32[184,384]{1,0:T(8,128)S(1)}, f32[184,384]{1,0:T(8,128)S(1)}, u32[]{:S(2)}, u32[]{:S(2)}) collective-permute-start(f32[184,384]{1,0:T(8,128)S(1)} %add.38.refs_3_), channel_id=1, source_target_pairs={{0,1},{1,0},{2,3},{3,2},{4,5},{5,4},{6,7},{7,6},{8,9},{9,8},{10,11... | collective-permute-start | bytes 847880 | tf_op jit(solution)/shard_map/ppermute | solution.py:309
  86.7 8.0 %collective-permute-start.17 = (f32[144,384]{1,0:T(8,128)}, f32[144,384]{1,0:T(8,128)S(1)}, u32[]{:S(2)}, u32[]{:S(2)}) collective-permute-start(f32[144,384]{1,0:T(8,128)} %add.37), channel_id=1, source_target_pairs={{0,2},{1,3},{2,0},{3,1},{4,6},{5,7},{6,4},{7,5},{8,10},{9,11},{10,... | collective-permute-start | bytes 663560 | tf_op jit(solution)/shard_map/ppermute | solution.py:309
  88.4 0.7 copy-start.3
  89.1 1.0 copy-start.4
  95.7 1.5 %collective-permute-start.18 = (f32[144,384]{1,0:T(8,128)S(1)}, f32[144,384]{1,0:T(8,128)S(1)}, u32[]{:S(2)}, u32[]{:S(2)}) collective-permute-start(f32[144,384]{1,0:T(8,128)S(1)} %add.39.refs_3_), channel_id=1, source_target_pairs={{0,1},{1,0},{2,3},{3,2},{4,5},{5,4},{6,7},{7,6},{8,9},{9,8},{10,11... | collective-permute-start | bytes 663560 | tf_op jit(solution)/shard_map/ppermute | solution.py:309

commit v8 on v6

--- a/solution.py
+++ b/solution.py
@@ -177,33 +177,33 @@
 ):
     index = pltpu.make_async_copy(index_hbm, index_ref, side_sems.at[0])
     index.start()
+    copies = fetch(features_ref, held_ref, sems)
     side = pltpu.make_async_copy(targets_ref, held_targets, side_sems.at[1])
     side.start()
-    copies = fetch(features_ref, held_ref, sems)
     index.wait()
     rank, core = place_ref[0], place_ref[1]
     rows, columns = features_ref.shape
     steps = index_ref.shape[0]
-    line = lax.broadcasted_iota(jnp.int32, (steps * per, rows), 0)
-    wanted = jnp.zeros((steps * per, rows), jnp.int32)
+    line = lax.broadcasted_iota(jnp.int32, (steps * per, 128), 0)
+    wanted = jnp.zeros((steps * per, 128), jnp.int32)
     for step in range(steps):
         for i in range(per):
             wanted = jnp.where(line == step * per + i, index_ref[step, rank * per + i], wanted)
-    chosen = wanted - rank * rows == lax.broadcasted_iota(jnp.int32, wanted.shape, 1)
+    chosen = wanted[:, :1] - rank * rows == lax.broadcasted_iota(jnp.int32, (steps * per, rows), 1)
     chosen = chosen.astype(jnp.float32).astype(jnp.bfloat16)
 
     def take(array):
         return jnp.dot(chosen, array, preferred_element_type=jnp.float32).astype(jnp.bfloat16)
 
+    for copy, at in zip(copies, pieces_of(features_ref)):
+        copy.wait()
+        out_ref[:, at] = take(held_ref[:, at])
     side.wait()
     width = targets_ref.shape[1] // 2
     values = jnp.where(core == 0, held_targets[:, :width], held_targets[:, width:])
     high, low = split(values)
     out_ref[:, columns : columns + width] = take(high)
     out_ref[:, columns + width :] = take(low)
-    for copy, at in zip(copies, pieces_of(features_ref)):
-        copy.wait()
-        out_ref[:, at] = take(held_ref[:, at])
 
 
 def pick(block_index, place, features, targets, per):
@@ -312,16 +312,16 @@
         pair = self.send(own, self.pair)
         mid = self.send(own, self.inner)
         own_b = self.send(own, self.beside)
-        pair, mid, own_b = hold((pair, mid, own_b))
+        pair, own_b = hold((pair, own_b))
 
         far = self.send(pair, self.inner)
         mid_end = self.send(mid, self.outer)
         pair_b = self.send(pair, self.beside)
-        far, mid_end, pair_b, own_b = hold((far, mid_end, pair_b, own_b))
-
+        far, pair_b, own_b = hold((far, pair_b, own_b))
+
+        far_end = self.send(far, self.outer)
         third = jnp.where(self.is_inner, far, mid_end)
         third_b = self.send(third, self.beside)
-        far_end = self.send(far, self.outer)
         last_in = self.send(own_b, self.inner)
         slots = [own, own_b, pair, pair_b, third]
         begun = len(slots)

time: 96.8 us -> 93.8 us (0.969)
  starting transfers between devices: 20.6 us -> 18 us
    ppermute x9, starting transfers between devices: 12.5 us -> 10.9 us  [send(): return lax.ppermute(array, 'rows', pairs)]
    ppermute x1, waiting for transfers between devices: 0.98 us -> 1.99 us  [run(): left = lax.ppermute(far_end, ('rows', 'feat'), self.ends)]
    ppermute x1, starting transfers between devices: 3.42 us -> 2.41 us  [run(): left = lax.ppermute(far_end, ('rows', 'feat'), self.ends)]
  transfers between devices with their start and end apart: 18 -> 18, of which waited for: 10 -> 11; matrix products, arithmetic and copies ran while one was open for 4% -> 4% of each run, Pallas kernels for 6% -> 6%
where the time goes in v8:
time: 93.8 us; the launch traced here: 93.4 us
  waiting for transfers between devices  47.3 us (50%)
  Pallas kernels  20.4 us (22%)
  starting transfers between devices  18 us (19%)
  local copies, waits for them, and re-layouts  3 us (3%)
  other arithmetic  2.3 us (2%)
  matrix products  1.52 us (2%)
  between operations  0.97 us (1%)
    ppermute x9, waiting for transfers between devices, send(): return lax.ppermute(array, 'rows', pairs)  34.5 us
    ppermute x9, starting transfers between devices, send(): return lax.ppermute(array, 'rows', pairs)  10.9 us
    ppermute x7, waiting for transfers between devices, near(): return lax.ppermute(array, 'feat', [(f, f ^ bit) for f in range(4)])  10.8 us
    pallas_call x1, Pallas kernels, run(): pl.pallas_call(functools.partial(last_kernel, steps, per, begun), out_sha...  6.14 us
    pallas_call x1, Pallas kernels, run(): pl.pallas_call(functools.partial(gram_kernel, steps, per, 8 - begun), out...  4.95 us
    pallas_call x1, Pallas kernels, pick(): pl.pallas_call(functools.partial(pick_kernel, per), out_shape=jax.ShapeDt...  4.54 us
    ppermute x7, starting transfers between devices, near(): return lax.ppermute(array, 'feat', [(f, f ^ bit) for f in range(4)])  3.96 us
    pallas_call x1, Pallas kernels, local(): pl.pallas_call(functools.partial(finish_kernel, steps, per, lined), out_s...  3.7 us
  transfers between devices with their start and end apart: 18, of which 11 were waited for; matrix products, arithmetic and copies ran while one was open for 4% of the time, Pallas kernels for 6%

profile of v8, /device:TPU:0, one launch (start us, length us, event | category | flops | bytes accessed | tf_op | source)
XLA Modules:
  0.0 93.4 jit_solution(1853483631588234512)
XLA Ops:
  0.7 0.6 pad_add_fusion.place_ref.refs_0_
  1.2 4.5 %shard_map.59.refs_0_ = bf16[48,6656]{1,0:T(8,128)(2,1)} custom-call(s32[3,128]{1,0:T(4,128)} %index_hbm.1, s32[3]{0:T(128)} %pad_add_fusion.place_ref.refs_0_, bf16[384,6144]{1,0:T(8,128)(2,1)} %refs_11_.1, f32[384,512]{1,0:T(8,128)} %refs_9_.1), custom_call_target="tpu_custom_call" | custom-call | flops 245366784 | bytes 73728 | tf_op jit(solution)/shard_map/pallas_call | solution.py:212
  5.8 3.1 %collective-permute-start = (bf16[48,6656]{1,0:T(8,128)(2,1)}, bf16[48,6656]{1,0:T(8,128)(2,1)S(1)}, u32[]{:S(2)}, u32[]{:S(2)}) collective-permute-start(bf16[48,6656]{1,0:T(8,128)(2,1)} %shard_map.59.refs_0_), channel_id=1, source_target_pairs={{0,8},{4,12},{8,0},{12,4},{16,24},{20,28},{24,16},{28,20},{1,9},{5... | collective-permute-start | bytes 1916936 | tf_op jit(solution)/shard_map/ppermute | solution.py:303
  8.9 1.5 %collective-permute-start.1 = (bf16[48,6656]{1,0:T(8,128)(2,1)}, bf16[48,6656]{1,0:T(8,128)(2,1)S(1)}, u32[]{:S(2)}, u32[]{:S(2)}) collective-permute-start(bf16[48,6656]{1,0:T(8,128)(2,1)} %shard_map.59.refs_0_), channel_id=1, source_target_pairs={{0,4},{4,0},{8,12},{12,8},{16,20},{20,16},{24,28},{28,24},{1,5},{5... | collective-permute-start | bytes 1916936 | tf_op jit(solution)/shard_map/ppermute | solution.py:303
  10.4 0.7 collective-permute-start.4
  11.1 12.4 %collective-permute-done.refs_2_ = bf16[48,6656]{1,0:T(8,128)(2,1)S(1)} collective-permute-done((bf16[48,6656]{1,0:T(8,128)(2,1)}, bf16[48,6656]{1,0:T(8,128)(2,1)S(1)}, u32[]{:S(2)}, u32[]{:S(2)}) %collective-permute-start) | collective-permute-done | bytes 639008 | tf_op jit(solution)/shard_map/ppermute | solution.py:303
  23.5 1.5 %collective-permute-done.1.refs_1_ = bf16[48,6656]{1,0:T(8,128)(2,1)S(1)} collective-permute-done((bf16[48,6656]{1,0:T(8,128)(2,1)}, bf16[48,6656]{1,0:T(8,128)(2,1)S(1)}, u32[]{:S(2)}, u32[]{:S(2)}) %collective-permute-start.1) | collective-permute-done | bytes 639008 | tf_op jit(solution)/shard_map/ppermute | solution.py:303
  24.9 0.7 collective-permute-start.2
  25.6 1.6 %collective-permute-start.3 = (bf16[48,6656]{1,0:T(8,128)(2,1)S(1)}, bf16[48,6656]{1,0:T(8,128)(2,1)S(1)}, u32[]{:S(2)}, u32[]{:S(2)}) collective-permute-start(bf16[48,6656]{1,0:T(8,128)(2,1)S(1)} %collective-permute-done.refs_2_), channel_id=1, source_target_pairs={{0,4},{4,0},{8,12},{12,8},{16,20},{20,16},{24,28},{28,24},{1,5},{5... | collective-permute-start | bytes 1916936 | tf_op jit(solution)/shard_map/ppermute | solution.py:303
  27.2 1.3 %collective-permute-start.5 = (bf16[48,6656]{1,0:T(8,128)(2,1)S(1)}, bf16[48,6656]{1,0:T(8,128)(2,1)}, u32[]{:S(2)}, u32[]{:S(2)}) collective-permute-start(bf16[48,6656]{1,0:T(8,128)(2,1)S(1)} %collective-permute-done.4.refs_6_), channel_id=1, source_target_pairs={{8,0},{12,4},{16,24},{20,28},{9,1},{13,5},{17,25},{21,29},{10,2},{... | collective-permute-start | bytes 1916936 | tf_op jit(solution)/shard_map/ppermute | solution.py:303
  28.6 0.1 mul.21
  28.7 0.1 iota_compare_fusion
  28.8 11.8 %collective-permute-done.3.refs_3_ = bf16[48,6656]{1,0:T(8,128)(2,1)S(1)} collective-permute-done((bf16[48,6656]{1,0:T(8,128)(2,1)S(1)}, bf16[48,6656]{1,0:T(8,128)(2,1)S(1)}, u32[]{:S(2)}, u32[]{:S(2)}) %collective-permute-start.3) | collective-permute-done | bytes 639008 | tf_op jit(solution)/shard_map/ppermute | solution.py:303
  40.6 1.3 %collective-permute-start.7 = (bf16[48,6656]{1,0:T(8,128)(2,1)S(1)}, bf16[48,6656]{1,0:T(8,128)(2,1)S(1)}, u32[]{:S(2)}, u32[]{:S(2)}) collective-permute-start(bf16[48,6656]{1,0:T(8,128)(2,1)S(1)} %collective-permute-done.2), channel_id=1, source_target_pairs={{8,0},{12,4},{16,24},{20,28},{9,1},{13,5},{17,25},{21,29},{10,2},{... | collective-permute-start | bytes 1916936 | tf_op jit(solution)/shard_map/ppermute | solution.py:303
  41.9 4.8 %collective-permute-done.5 = bf16[48,6656]{1,0:T(8,128)(2,1)} collective-permute-done((bf16[48,6656]{1,0:T(8,128)(2,1)S(1)}, bf16[48,6656]{1,0:T(8,128)(2,1)}, u32[]{:S(2)}, u32[]{:S(2)}) %collective-permute-start.5) | collective-permute-done | bytes 639008 | tf_op jit(solution)/shard_map/ppermute | solution.py:303
  46.7 1.2 %broadcast_select_fusion.refs_4_ = bf16[48,6656]{1,0:T(8,128)(2,1)S(1)} fusion(bf16[48,6656]{1,0:T(8,128)(2,1)S(1)} %collective-permute-done.2, bf16[48,6656]{1,0:T(8,128)(2,1)} %collective-permute-done.5, pred[]{:T(512)S(6)} %and.23), kind=kLoop, calls=%fused_computation.3 | loop fusion | flops 319488 | bytes 1916929 | tf_op jit(solution)/shard_map/jit(_where)/select_n | solution.py:323
  47.9 0.1 collective-permute-start.6
  48.0 0.7 collective-permute-start.8
  48.7 0.1 select_reduce_fusion
  48.9 1.1 %copy-done = bf16[48,6656]{1,0:T(8,128)(2,1)S(1)} copy-done((bf16[48,6656]{1,0:T(8,128)(2,1)S(1)}, bf16[48,6656]{1,0:T(8,128)(2,1)}, u32[]{:S(2)}) %copy-start) | copy-done | bytes 639000
  50.0 4.9 %shard_map.60 = (f32[184,384]{1,0:T(8,128)S(1)}, f32[184,384]{1,0:T(8,128)S(1)}) custom-call(s32[3]{0:T(128)S(1)} %copy-done.5, bf16[48,6656]{1,0:T(8,128)(2,1)S(1)} %copy-done, bf16[48,6656]{1,0:T(8,128)(2,1)S(1)} %collective-permute-done.1.refs_1_, bf16[48,6656]{1,0:T(8,128)(2,1)S(1)} %collective-permute-done.refs_2_, ...), custom_call_target="tpu_custom_call" | custom-call | flops 1736441856 | bytes 565248 | tf_op jit(solution)/shard_map/pallas_call | solution.py:329
  54.9 0.1 collective-permute-start.9
  55.0 0.2 fusion
  55.2 1.3 %collective-permute-done.9 = f32[184,384]{1,0:T(8,128)S(1)} collective-permute-done((f32[184,384]{1,0:T(8,128)S(1)}, f32[184,384]{1,0:T(8,128)S(1)}, u32[]{:S(2)}, u32[]{:S(2)}) %collective-permute-start.9) | collective-permute-done | bytes 282656 | tf_op jit(solution)/shard_map/ppermute | solution.py:300
  56.6 4.0 %collective-permute-done.6.refs_5_ = bf16[48,6656]{1,0:T(8,128)(2,1)S(1)} collective-permute-done((bf16[48,6656]{1,0:T(8,128)(2,1)S(1)}, bf16[48,6656]{1,0:T(8,128)(2,1)S(1)}, u32[]{:S(2)}, u32[]{:S(2)}) %collective-permute-start.6) | collective-permute-done | bytes 639008 | tf_op jit(solution)/shard_map/ppermute | solution.py:303
  60.6 2.4 %collective-permute-start.10 = (bf16[48,6656]{1,0:T(8,128)(2,1)S(1)}, bf16[48,6656]{1,0:T(8,128)(2,1)S(1)}, u32[]{:S(2)}, u32[]{:S(2)}) collective-permute-start(bf16[48,6656]{1,0:T(8,128)(2,1)S(1)} %collective-permute-done.7.refs_7_), channel_id=1, source_target_pairs={{0,4},{2,6},{4,0},{6,2},{24,28},{26,30},{28,24},{30,26}} | collective-permute-start | bytes 1916936 | tf_op jit(solution)/shard_map/ppermute | solution.py:341
  63.0 0.7 collective-permute-start.11
  63.7 0.3 convolution_bitcast_fusion
  64.0 0.2 fusion.2
  64.2 1.6 %collective-permute-start.12 = (f32[184,384]{1,0:T(8,128)S(1)}, f32[184,384]{1,0:T(8,128)S(1)}, u32[]{:S(2)}, u32[]{:S(2)}) collective-permute-start(f32[184,384]{1,0:T(8,128)S(1)} %add.34), channel_id=1, source_target_pairs={{0,2},{1,3},{2,0},{3,1},{4,6},{5,7},{6,4},{7,5},{8,10},{9,11},{10,... | collective-permute-start | bytes 847880 | tf_op jit(solution)/shard_map/ppermute | solution.py:300
  65.8 0.3 convolution_bitcast_fusion.1
  66.1 0.2 fusion.4
  66.3 4.6 %collective-permute-done.12 = f32[184,384]{1,0:T(8,128)S(1)} collective-permute-done((f32[184,384]{1,0:T(8,128)S(1)}, f32[184,384]{1,0:T(8,128)S(1)}, u32[]{:S(2)}, u32[]{:S(2)}) %collective-permute-start.12) | collective-permute-done | bytes 282656 | tf_op jit(solution)/shard_map/ppermute | solution.py:300
  70.9 2.0 %collective-permute-done.10.refs_9_ = bf16[48,6656]{1,0:T(8,128)(2,1)S(1)} collective-permute-done((bf16[48,6656]{1,0:T(8,128)(2,1)S(1)}, bf16[48,6656]{1,0:T(8,128)(2,1)S(1)}, u32[]{:S(2)}, u32[]{:S(2)}) %collective-permute-start.10) | collective-permute-done | bytes 639008 | tf_op jit(solution)/shard_map/ppermute | solution.py:341
  72.9 6.1 %shard_map.61 = (f32[144,384]{1,0:T(8,128)S(1)}, f32[144,384]{1,0:T(8,128)S(1)}, f32[384,256]{1,0:T(8,128)S(1)}) custom-call(s32[3]{0:T(128)S(1)} %copy-done.5, bf16[48,6656]{1,0:T(8,128)(2,1)S(1)} %copy-done.1, bf16[48,6656]{1,0:T(8,128)(2,1)S(1)} %collective-permute-done.1.refs_1_, bf16[48,6656]{1,0:T(8,128)(2,1)S(1)} %collective-permute-done.refs_2_, ...), custom_call_target="tpu_custom_call" | custom-call | flops 1358954496 | bytes 442368 | tf_op jit(solution)/shard_map/pallas_call | solution.py:349
  79.1 0.5 collective-permute-start.13
  79.6 0.3 convolution_bitcast_fusion.2
  79.9 0.1 collective-permute-start.14
  80.1 0.5 collective-permute-done.15
  80.6 1.6 %collective-permute-start.16 = (f32[144,384]{1,0:T(8,128)S(1)}, f32[144,384]{1,0:T(8,128)S(1)}, u32[]{:S(2)}, u32[]{:S(2)}) collective-permute-start(f32[144,384]{1,0:T(8,128)S(1)} %add.38), channel_id=1, source_target_pairs={{0,2},{1,3},{2,0},{3,1},{4,6},{5,7},{6,4},{7,5},{8,10},{9,11},{10,... | collective-permute-start | bytes 663560 | tf_op jit(solution)/shard_map/ppermute | solution.py:300
  82.2 0.1 broadcast_compare_fusion.2
  82.3 0.7 copy-done.3
  83.0 1.0 %copy-done.4 = f32[184,384]{1,0:T(8,128)S(1)} copy-done((f32[184,384]{1,0:T(8,128)S(1)}, f32[184,384]{1,0:T(8,128)}, u32[]{:S(2)}) %copy-start.4) | copy-done | bytes 282648
  84.0 1.1 %shard_map.62 = (f32[3,128,512]{2,1,0:T(8,128)S(1)}, bf16[2,3,80,384]{3,2,1,0:T(8,128)(2,1)S(1)}, f32[128,384]{1,0:T(8,128)S(1)}) custom-call(s32[3]{0:T(128)S(1)} %copy-done.5, f32[384,256]{1,0:T(8,128)S(1)} %get-tuple-element.37.refs_0_, f32[384,256]{1,0:T(8,128)S(1)} %collective-permute-done.13.refs_1_, ...), custom_call_target="tpu_custom_call" | custom-call | flops 150994944 | bytes 589824 | tf_op jit(solution)/shard_map/pallas_call | solution.py:364
  85.1 3.1 %collective-permute-done.16 = f32[144,384]{1,0:T(8,128)S(1)} collective-permute-done((f32[144,384]{1,0:T(8,128)S(1)}, f32[144,384]{1,0:T(8,128)S(1)}, u32[]{:S(2)}, u32[]{:S(2)}) %collective-permute-start.16) | collective-permute-done | bytes 221216 | tf_op jit(solution)/shard_map/ppermute | solution.py:300
  88.3 0.1 sub.11.refs_8_
  88.4 1.3 %collective-permute-done.17.refs_4_ = f32[144,384]{1,0:T(8,128)S(1)} collective-permute-done((f32[144,384]{1,0:T(8,128)S(1)}, f32[144,384]{1,0:T(8,128)S(1)}, u32[]{:S(2)}, u32[]{:S(2)}) %collective-permute-start.17) | collective-permute-done | bytes 221216 | tf_op jit(solution)/shard_map/ppermute | solution.py:300
  89.7 3.7 %shard_map.63 = (f32[384,512]{1,0:T(8,128)}, f32[384,512]{1,0:T(8,128)}) custom-call(s32[3]{0:T(128)S(1)} %copy-done.5, bf16[2,3,80,384]{3,2,1,0:T(8,128)(2,1)S(1)} %get-tuple-element.39.refs_1_, f32[128,384]{1,0:T(8,128)S(1)} %get-tuple-element.40.refs_2_, f32[144,384]{1,0:T(8,128)S(1)} %add.39.refs_3_, f32[144,384]{1,0:T(8,128)S(1)} %collective-permute-done.17.refs_4_, ...), custom_call_target="tpu_custom_call" | custom-call | flops 452984832 | bytes 1769472 | tf_op jit(solution)/shard_map/pallas_call | solution.py:445
  (33 shorter events, 0.5 us)
Async XLA Ops:
  0.6 48.1 %copy-start.7 = (s32[3,128]{1,0:T(4,128)S(1)}, s32[3,128]{1,0:T(4,128)}, u32[]{:S(2)}) copy-start(s32[3,128]{1,0:T(4,128)} %index_hbm.1) | copy-start | bytes 4612
  1.2 47.6 %copy-start.5 = (s32[3]{0:T(128)S(1)}, s32[3]{0:T(128)}, u32[]{:S(2)}) copy-start(s32[3]{0:T(128)} %pad_add_fusion.place_ref.refs_0_) | copy-start | bytes 40
  5.8 17.7 %collective-permute-start = (bf16[48,6656]{1,0:T(8,128)(2,1)}, bf16[48,6656]{1,0:T(8,128)(2,1)S(1)}, u32[]{:S(2)}, u32[]{:S(2)}) collective-permute-start(bf16[48,6656]{1,0:T(8,128)(2,1)} %shard_map.59.refs_0_), channel_id=1, source_target_pairs={{0,8},{4,12},{8,0},{12,4},{16,24},{20,28},{24,16},{28,20},{1,9},{5... | collective-permute-start | bytes 1916936 | tf_op jit(solution)/shard_map/ppermute | solution.py:303
  8.9 16.1 %collective-permute-start.1 = (bf16[48,6656]{1,0:T(8,128)(2,1)}, bf16[48,6656]{1,0:T(8,128)(2,1)S(1)}, u32[]{:S(2)}, u32[]{:S(2)}) collective-permute-start(bf16[48,6656]{1,0:T(8,128)(2,1)} %shard_map.59.refs_0_), channel_id=1, source_target_pairs={{0,4},{4,0},{8,12},{12,8},{16,20},{20,16},{24,28},{28,24},{1,5},{5... | collective-permute-start | bytes 1916936 | tf_op jit(solution)/shard_map/ppermute | solution.py:303
  10.4 16.8 %collective-permute-start.4 = (bf16[48,6656]{1,0:T(8,128)(2,1)}, bf16[48,6656]{1,0:T(8,128)(2,1)S(1)}, u32[]{:S(2)}, u32[]{:S(2)}) collective-permute-start(bf16[48,6656]{1,0:T(8,128)(2,1)} %shard_map.59.refs_0_), channel_id=1, source_target_pairs={{8,16},{12,20},{16,8},{20,12},{9,17},{13,21},{17,9},{21,13},{10,18... | collective-permute-start | bytes 1916936 | tf_op jit(solution)/shard_map/ppermute | solution.py:303
  24.9 3.9 %collective-permute-start.2 = (bf16[48,6656]{1,0:T(8,128)(2,1)S(1)}, bf16[48,6656]{1,0:T(8,128)(2,1)S(1)}, u32[]{:S(2)}, u32[]{:S(2)}) collective-permute-start(bf16[48,6656]{1,0:T(8,128)(2,1)S(1)} %collective-permute-done.refs_2_), channel_id=1, source_target_pairs={{8,16},{12,20},{16,8},{20,12},{9,17},{13,21},{17,9},{21,13},{10,18... | collective-permute-start | bytes 1916936 | tf_op jit(solution)/shard_map/ppermute | solution.py:303
  25.6 15.0 %collective-permute-start.3 = (bf16[48,6656]{1,0:T(8,128)(2,1)S(1)}, bf16[48,6656]{1,0:T(8,128)(2,1)S(1)}, u32[]{:S(2)}, u32[]{:S(2)}) collective-permute-start(bf16[48,6656]{1,0:T(8,128)(2,1)S(1)} %collective-permute-done.refs_2_), channel_id=1, source_target_pairs={{0,4},{4,0},{8,12},{12,8},{16,20},{20,16},{24,28},{28,24},{1,5},{5... | collective-permute-start | bytes 1916936 | tf_op jit(solution)/shard_map/ppermute | solution.py:303
  27.2 19.5 %collective-permute-start.5 = (bf16[48,6656]{1,0:T(8,128)(2,1)S(1)}, bf16[48,6656]{1,0:T(8,128)(2,1)}, u32[]{:S(2)}, u32[]{:S(2)}) collective-permute-start(bf16[48,6656]{1,0:T(8,128)(2,1)S(1)} %collective-permute-done.4.refs_6_), channel_id=1, source_target_pairs={{8,0},{12,4},{16,24},{20,28},{9,1},{13,5},{17,25},{21,29},{10,2},{... | collective-permute-start | bytes 1916936 | tf_op jit(solution)/shard_map/ppermute | solution.py:303
  28.8 26.2 %copy-start.6 = (f32[3,128,128]{2,1,0:T(8,128)S(1)}, f32[3,128,128]{2,1,0:T(8,128)}, u32[]{:S(2)}) copy-start(f32[3,128,128]{2,1,0:T(8,128)} %param.7) | copy-start | bytes 589828
  40.6 20.0 %collective-permute-start.7 = (bf16[48,6656]{1,0:T(8,128)(2,1)S(1)}, bf16[48,6656]{1,0:T(8,128)(2,1)S(1)}, u32[]{:S(2)}, u32[]{:S(2)}) collective-permute-start(bf16[48,6656]{1,0:T(8,128)(2,1)S(1)} %collective-permute-done.2), channel_id=1, source_target_pairs={{8,0},{12,4},{16,24},{20,28},{9,1},{13,5},{17,25},{21,29},{10,2},{... | collective-permute-start | bytes 1916936 | tf_op jit(solution)/shard_map/ppermute | solution.py:303
  46.7 26.2 %copy-start.1 = (bf16[48,6656]{1,0:T(8,128)(2,1)S(1)}, bf16[48,6656]{1,0:T(8,128)(2,1)}, u32[]{:S(2)}) copy-start(bf16[48,6656]{1,0:T(8,128)(2,1)} %shard_map.59.refs_0_) | copy-start | bytes 1916932
  47.9 12.7 %collective-permute-start.6 = (bf16[48,6656]{1,0:T(8,128)(2,1)S(1)}, bf16[48,6656]{1,0:T(8,128)(2,1)S(1)}, u32[]{:S(2)}, u32[]{:S(2)}) collective-permute-start(bf16[48,6656]{1,0:T(8,128)(2,1)S(1)} %broadcast_select_fusion.refs_4_), channel_id=1, source_target_pairs={{0,4},{4,0},{8,12},{12,8},{16,20},{20,16},{24,28},{28,24},{1,5},{5... | collective-permute-start | bytes 1916936 | tf_op jit(solution)/shard_map/ppermute | solution.py:303
  48.0 12.6 %collective-permute-start.8 = (bf16[48,6656]{1,0:T(8,128)(2,1)S(1)}, bf16[48,6656]{1,0:T(8,128)(2,1)S(1)}, u32[]{:S(2)}, u32[]{:S(2)}) collective-permute-start(bf16[48,6656]{1,0:T(8,128)(2,1)S(1)} %collective-permute-done.1.refs_1_), channel_id=1, source_target_pairs={{8,16},{12,20},{16,8},{20,12},{9,17},{13,21},{17,9},{21,13},{10,18... | collective-permute-start | bytes 1916936 | tf_op jit(solution)/shard_map/ppermute | solution.py:303
  48.9 1.1 %copy-start = (bf16[48,6656]{1,0:T(8,128)(2,1)S(1)}, bf16[48,6656]{1,0:T(8,128)(2,1)}, u32[]{:S(2)}) copy-start(bf16[48,6656]{1,0:T(8,128)(2,1)} %shard_map.59.refs_0_) | copy-start | bytes 1916932
  54.9 1.6 %collective-permute-start.9 = (f32[184,384]{1,0:T(8,128)S(1)}, f32[184,384]{1,0:T(8,128)S(1)}, u32[]{:S(2)}, u32[]{:S(2)}) collective-permute-start(f32[184,384]{1,0:T(8,128)S(1)} %get-tuple-element.30), channel_id=1, source_target_pairs={{0,1},{1,0},{2,3},{3,2},{4,5},{5,4},{6,7},{7,6},{8,9},{9,8},{10,11... | collective-permute-start | bytes 847880 | tf_op jit(solution)/shard_map/ppermute | solution.py:300
  60.6 12.3 %collective-permute-start.10 = (bf16[48,6656]{1,0:T(8,128)(2,1)S(1)}, bf16[48,6656]{1,0:T(8,128)(2,1)S(1)}, u32[]{:S(2)}, u32[]{:S(2)}) collective-permute-start(bf16[48,6656]{1,0:T(8,128)(2,1)S(1)} %collective-permute-done.7.refs_7_), channel_id=1, source_target_pairs={{0,4},{2,6},{4,0},{6,2},{24,28},{26,30},{28,24},{30,26}} | collective-permute-start | bytes 1916936 | tf_op jit(solution)/shard_map/ppermute | solution.py:341
  63.0 9.9 %collective-permute-start.11 = (bf16[48,6656]{1,0:T(8,128)(2,1)S(1)}, bf16[48,6656]{1,0:T(8,128)(2,1)S(1)}, u32[]{:S(2)}, u32[]{:S(2)}) collective-permute-start(bf16[48,6656]{1,0:T(8,128)(2,1)S(1)} %collective-permute-done.6.refs_5_), channel_id=1, source_target_pairs={{9,1},{11,3},{13,5},{15,7},{17,25},{19,27},{21,29},{23,31}} | collective-permute-start | bytes 1916936 | tf_op jit(solution)/shard_map/ppermute | solution.py:342
  64.2 6.7 %collective-permute-start.12 = (f32[184,384]{1,0:T(8,128)S(1)}, f32[184,384]{1,0:T(8,128)S(1)}, u32[]{:S(2)}, u32[]{:S(2)}) collective-permute-start(f32[184,384]{1,0:T(8,128)S(1)} %add.34), channel_id=1, source_target_pairs={{0,2},{1,3},{2,0},{3,1},{4,6},{5,7},{6,4},{7,5},{8,10},{9,11},{10,... | collective-permute-start | bytes 847880 | tf_op jit(solution)/shard_map/ppermute | solution.py:300
  79.0 10.7 %copy-start.2 = (f32[384,512]{1,0:T(8,128)S(1)}, f32[384,512]{1,0:T(8,128)}, u32[]{:S(2)}) copy-start(f32[384,512]{1,0:T(8,128)} %refs_9_.1) | copy-start | bytes 2359300
  79.0 1.5 %collective-permute-start.15 = (f32[144,384]{1,0:T(8,128)S(1)}, f32[144,384]{1,0:T(8,128)S(1)}, u32[]{:S(2)}, u32[]{:S(2)}) collective-permute-start(f32[144,384]{1,0:T(8,128)S(1)} %get-tuple-element.42), channel_id=1, source_target_pairs={{0,1},{1,0},{2,3},{3,2},{4,5},{5,4},{6,7},{7,6},{8,9},{9,8},{10,11... | collective-permute-start | bytes 663560 | tf_op jit(solution)/shard_map/ppermute | solution.py:300
  79.1 3.9 %collective-permute-start.13 = (f32[384,256]{1,0:T(8,128)S(1)}, f32[384,256]{1,0:T(8,128)S(1)}, u32[]{:S(2)}, u32[]{:S(2)}) collective-permute-start(f32[384,256]{1,0:T(8,128)S(1)} %get-tuple-element.37.refs_0_), channel_id=1, source_target_pairs={{0,1},{1,0},{2,3},{3,2},{4,5},{5,4},{6,7},{7,6},{8,9},{9,8},{10,11... | collective-permute-start | bytes 1179656 | tf_op jit(solution)/shard_map/ppermute | solution.py:300
  79.9 2.3 %collective-permute-start.14 = (f32[184,384]{1,0:T(8,128)S(1)}, f32[184,384]{1,0:T(8,128)S(1)}, u32[]{:S(2)}, u32[]{:S(2)}) collective-permute-start(f32[184,384]{1,0:T(8,128)S(1)} %add.37.refs_3_), channel_id=1, source_target_pairs={{0,1},{1,0},{2,3},{3,2},{4,5},{5,4},{6,7},{7,6},{8,9},{9,8},{10,11... | collective-permute-start | bytes 847880 | tf_op jit(solution)/shard_map/ppermute | solution.py:300
  80.6 7.5 %collective-permute-start.16 = (f32[144,384]{1,0:T(8,128)S(1)}, f32[144,384]{1,0:T(8,128)S(1)}, u32[]{:S(2)}, u32[]{:S(2)}) collective-permute-start(f32[144,384]{1,0:T(8,128)S(1)} %add.38), channel_id=1, source_target_pairs={{0,2},{1,3},{2,0},{3,1},{4,6},{5,7},{6,4},{7,5},{8,10},{9,11},{10,... | collective-permute-start | bytes 663560 | tf_op jit(solution)/shard_map/ppermute | solution.py:300
  82.3 0.7 copy-start.3
  83.0 1.0 %copy-start.4 = (f32[184,384]{1,0:T(8,128)S(1)}, f32[184,384]{1,0:T(8,128)}, u32[]{:S(2)}) copy-start(f32[184,384]{1,0:T(8,128)} %copy-done.3) | copy-start | bytes 847876
  88.2 1.5 %collective-permute-start.17 = (f32[144,384]{1,0:T(8,128)S(1)}, f32[144,384]{1,0:T(8,128)S(1)}, u32[]{:S(2)}, u32[]{:S(2)}) collective-permute-start(f32[144,384]{1,0:T(8,128)S(1)} %add.39.refs_3_), channel_id=1, source_target_pairs={{0,1},{1,0},{2,3},{3,2},{4,5},{5,4},{6,7},{7,6},{8,9},{9,8},{10,11... | collective-permute-start | bytes 663560 | tf_op jit(solution)/shard_map/ppermute | solution.py:300

commit v9 on v8

--- a/solution.py
+++ b/solution.py
@@ -14,7 +14,7 @@
 PIECES = 4
 PARAMS = pltpu.CompilerParams(vmem_limit_bytes=24 * 1024 * 1024)
 PICK = pltpu.CompilerParams(vmem_limit_bytes=58 * 1024 * 1024)
-GRAM = pltpu.CompilerParams(vmem_limit_bytes=46 * 1024 * 1024)
+GRAM = pltpu.CompilerParams(vmem_limit_bytes=32 * 1024 * 1024)
 
 
 def quadratic(gram):
@@ -226,8 +226,7 @@
 
 
 def gram_kernel(steps, per, missing, place_ref, *refs):
-    *slot_refs, features_ref, keep_ref, send_ref, held_ref, sems = refs
-    copies = fetch(features_ref, held_ref, sems)
+    *slot_refs, features_ref, keep_ref, send_ref = refs
     total = [None] * (1 + len(pairs_of(steps)))
     for at in pieces_of(features_ref):
         slots = [ref[:, at] for ref in slot_refs]
@@ -235,10 +234,9 @@
         rows = [of_step(slots, step, per) for step in range(steps)]
         for i, (step, before) in enumerate(pairs_of(steps)):
             total[1 + i] = add(total[1 + i], dot_rows(rows[step], rows[before]))
-    for copy, at in zip(copies, pieces_of(features_ref)):
+    for at in pieces_of(features_ref):
         slots = jnp.concatenate([ref[:, at] for ref in slot_refs], axis=0)
-        copy.wait()
-        total[0] = add(total[0], dot_rows(slots, held_ref[:, at]))
+        total[0] = add(total[0], dot_rows(slots, features_ref[:, at]))
     total = jnp.concatenate([total[0], jnp.concatenate(total[1:], axis=1)], axis=0)
     half = keep_ref.shape[0]
     core = place_ref[1]
@@ -247,12 +245,11 @@
 
 
 def last_kernel(steps, per, begun, place_ref, *refs):
-    *slot_refs, inner_ref, left_ref, right_ref, features_ref = refs[:-5]
-    keep_ref, send_ref, first_ref, held_ref, sems = refs[-5:]
+    *slot_refs, inner_ref, left_ref, right_ref, features_ref = refs[:-3]
+    keep_ref, send_ref, first_ref = refs[-3:]
     core = place_ref[1]
     inner = place_ref[2] == 1
     columns = features_ref.shape[1]
-    copies = fetch(features_ref, held_ref, sems)
 
     def slots_at(at):
         slots = [ref[:, at] for ref in slot_refs]
@@ -268,10 +265,9 @@
     for at in pieces_of(features_ref):
         slots = slots_at(at)
         cross = add(cross, dot_rows(every(slots), jnp.concatenate(slots[begun:], axis=0)))
-    for copy, at in zip(copies, pieces_of(features_ref)):
+    for at in pieces_of(features_ref):
         new = jnp.concatenate(slots_at(at)[begun:], axis=0)
-        copy.wait()
-        total = add(total, dot_rows(held_ref[:, at], new))
+        total = add(total, dot_rows(features_ref[:, at], new))
     total, cross = total.T, cross.T
     keep_ref[...] = jnp.where(core == 0, total, cross)
     send_ref[...] = jnp.where(core == 0, cross, total)
@@ -329,9 +325,8 @@
         gram, given = pl.pallas_call(
             functools.partial(gram_kernel, steps, per, 8 - begun),
             out_shape=(part, part),
-            in_specs=[SMEM] + [VMEM] * begun + [HBM],
+            in_specs=[SMEM] + [VMEM] * begun + [VMEM],
             out_specs=(VMEM, VMEM),
-            scratch_shapes=held(features),
             compiler_params=GRAM,
             cost_estimate=cost((begun * count + block) * rows, columns),
         )(self.place, *slots, features)
@@ -353,9 +348,8 @@
                 end,
                 jax.ShapeDtypeStruct((steps * block, targets.shape[1] // 2), jnp.float32),
             ),
-            in_specs=[SMEM] + [VMEM] * len(slots) + [HBM],
+            in_specs=[SMEM] + [VMEM] * len(slots) + [VMEM],
             out_specs=(VMEM,) * 3,
-            scratch_shapes=held(features),
             compiler_params=GRAM,
             cost_estimate=cost((8 - begun) * count * (rows + steps * block), columns),
         )(self.place, *slots, features)

time: 93.8 us -> 91.1 us (0.971)
  Pallas kernels: 20.4 us -> 16.1 us
  local copies, waits for them, and re-layouts: 3 us -> 5.34 us
  waiting for transfers between devices: 47.3 us -> 46.3 us
    pallas_call x1, Pallas kernels: 6.14 us -> 3.34 us  [run(): pl.pallas_call(functools.partial(last_kernel, steps, per, begun), out_sha...]
    unnamed x16 -> x18, local copies, waits for them, and re-layouts: 2.77 us -> 5.1 us
    pallas_call x1, Pallas kernels: 4.95 us -> 3.49 us  [run(): pl.pallas_call(functools.partial(gram_kernel, steps, per, 8 - begun), out...]
  transfers between devices with their start and end apart: 18 -> 18, of which waited for: 11 -> 11; matrix products, arithmetic and copies ran while one was open for 4% -> 4% of each run, Pallas kernels for 6% -> 5%
where the time goes in v9:
time: 91.1 us; the launch traced here: 90.7 us
  waiting for transfers between devices  46.3 us (51%)
  starting transfers between devices  18 us (20%)
  Pallas kernels  16.1 us (18%)
  local copies, waits for them, and re-layouts  5.34 us (6%)
  other arithmetic  2.39 us (3%)
  matrix products  1.52 us (2%)
  between operations  0.97 us (1%)
    ppermute x9, waiting for transfers between devices, send(): return lax.ppermute(array, 'rows', pairs)  33.6 us
    ppermute x9, starting transfers between devices, send(): return lax.ppermute(array, 'rows', pairs)  10.9 us
    ppermute x7, waiting for transfers between devices, near(): return lax.ppermute(array, 'feat', [(f, f ^ bit) for f in range(4)])  10.8 us
    unnamed x18, local copies, waits for them, and re-layouts  5.1 us
    pallas_call x1, Pallas kernels, pick(): pl.pallas_call(functools.partial(pick_kernel, per), out_shape=jax.ShapeDt...  4.54 us
    ppermute x7, starting transfers between devices, near(): return lax.ppermute(array, 'feat', [(f, f ^ bit) for f in range(4)])  3.97 us
    pallas_call x1, Pallas kernels, local(): pl.pallas_call(functools.partial(finish_kernel, steps, per, lined), out_s...  3.68 us
    pallas_call x1, Pallas kernels, run(): pl.pallas_call(functools.partial(gram_kernel, steps, per, 8 - begun), out...  3.49 us
  transfers between devices with their start and end apart: 18, of which 11 were waited for; matrix products, arithmetic and copies ran while one was open for 4% of the time, Pallas kernels for 5%

profile of v9, /device:TPU:0, one launch (start us, length us, event | category | flops | bytes accessed | tf_op | source)
XLA Modules:
  0.0 90.7 jit_solution(376772570133906193)
XLA Ops:
  0.7 0.7 pad_add_fusion.place_ref.refs_0_
  1.3 4.5 %shard_map.59.refs_0_ = bf16[48,6656]{1,0:T(8,128)(2,1)} custom-call(s32[3,128]{1,0:T(4,128)} %index_hbm.1, s32[3]{0:T(128)} %pad_add_fusion.place_ref.refs_0_, bf16[384,6144]{1,0:T(8,128)(2,1)} %refs_11_.1, f32[384,512]{1,0:T(8,128)} %refs_9_.1), custom_call_target="tpu_custom_call" | custom-call | flops 245366784 | bytes 73728 | tf_op jit(solution)/shard_map/pallas_call | solution.py:212
  5.9 3.1 %collective-permute-start = (bf16[48,6656]{1,0:T(8,128)(2,1)}, bf16[48,6656]{1,0:T(8,128)(2,1)S(1)}, u32[]{:S(2)}, u32[]{:S(2)}) collective-permute-start(bf16[48,6656]{1,0:T(8,128)(2,1)} %shard_map.59.refs_0_), channel_id=1, source_target_pairs={{0,8},{4,12},{8,0},{12,4},{16,24},{20,28},{24,16},{28,20},{1,9},{5... | collective-permute-start | bytes 1916936 | tf_op jit(solution)/shard_map/ppermute | solution.py:299
  9.0 1.5 %collective-permute-start.1 = (bf16[48,6656]{1,0:T(8,128)(2,1)}, bf16[48,6656]{1,0:T(8,128)(2,1)S(1)}, u32[]{:S(2)}, u32[]{:S(2)}) collective-permute-start(bf16[48,6656]{1,0:T(8,128)(2,1)} %shard_map.59.refs_0_), channel_id=1, source_target_pairs={{0,4},{4,0},{8,12},{12,8},{16,20},{20,16},{24,28},{28,24},{1,5},{5... | collective-permute-start | bytes 1916936 | tf_op jit(solution)/shard_map/ppermute | solution.py:299
  10.5 0.7 collective-permute-start.4
  11.2 12.4 %collective-permute-done.refs_2_ = bf16[48,6656]{1,0:T(8,128)(2,1)S(1)} collective-permute-done((bf16[48,6656]{1,0:T(8,128)(2,1)}, bf16[48,6656]{1,0:T(8,128)(2,1)S(1)}, u32[]{:S(2)}, u32[]{:S(2)}) %collective-permute-start) | collective-permute-done | bytes 639008 | tf_op jit(solution)/shard_map/ppermute | solution.py:299
  23.5 1.5 %collective-permute-done.1.refs_1_ = bf16[48,6656]{1,0:T(8,128)(2,1)S(1)} collective-permute-done((bf16[48,6656]{1,0:T(8,128)(2,1)}, bf16[48,6656]{1,0:T(8,128)(2,1)S(1)}, u32[]{:S(2)}, u32[]{:S(2)}) %collective-permute-start.1) | collective-permute-done | bytes 639008 | tf_op jit(solution)/shard_map/ppermute | solution.py:299
  25.0 0.7 collective-permute-start.2
  25.7 1.6 %collective-permute-start.3 = (bf16[48,6656]{1,0:T(8,128)(2,1)S(1)}, bf16[48,6656]{1,0:T(8,128)(2,1)S(1)}, u32[]{:S(2)}, u32[]{:S(2)}) collective-permute-start(bf16[48,6656]{1,0:T(8,128)(2,1)S(1)} %collective-permute-done.refs_2_), channel_id=1, source_target_pairs={{0,4},{4,0},{8,12},{12,8},{16,20},{20,16},{24,28},{28,24},{1,5},{5... | collective-permute-start | bytes 1916936 | tf_op jit(solution)/shard_map/ppermute | solution.py:299
  27.3 1.3 %collective-permute-start.5 = (bf16[48,6656]{1,0:T(8,128)(2,1)S(1)}, bf16[48,6656]{1,0:T(8,128)(2,1)}, u32[]{:S(2)}, u32[]{:S(2)}) collective-permute-start(bf16[48,6656]{1,0:T(8,128)(2,1)S(1)} %collective-permute-done.4.refs_6_), channel_id=1, source_target_pairs={{8,0},{12,4},{16,24},{20,28},{9,1},{13,5},{17,25},{21,29},{10,2},{... | collective-permute-start | bytes 1916936 | tf_op jit(solution)/shard_map/ppermute | solution.py:299
  28.7 0.1 mul.21
  28.8 0.1 iota_compare_fusion
  28.9 11.8 %collective-permute-done.3.refs_3_ = bf16[48,6656]{1,0:T(8,128)(2,1)S(1)} collective-permute-done((bf16[48,6656]{1,0:T(8,128)(2,1)S(1)}, bf16[48,6656]{1,0:T(8,128)(2,1)S(1)}, u32[]{:S(2)}, u32[]{:S(2)}) %collective-permute-start.3) | collective-permute-done | bytes 639008 | tf_op jit(solution)/shard_map/ppermute | solution.py:299
  40.7 1.3 %collective-permute-start.7 = (bf16[48,6656]{1,0:T(8,128)(2,1)S(1)}, bf16[48,6656]{1,0:T(8,128)(2,1)S(1)}, u32[]{:S(2)}, u32[]{:S(2)}) collective-permute-start(bf16[48,6656]{1,0:T(8,128)(2,1)S(1)} %collective-permute-done.2), channel_id=1, source_target_pairs={{8,0},{12,4},{16,24},{20,28},{9,1},{13,5},{17,25},{21,29},{10,2},{... | collective-permute-start | bytes 1916936 | tf_op jit(solution)/shard_map/ppermute | solution.py:299
  42.0 4.8 %collective-permute-done.5 = bf16[48,6656]{1,0:T(8,128)(2,1)} collective-permute-done((bf16[48,6656]{1,0:T(8,128)(2,1)S(1)}, bf16[48,6656]{1,0:T(8,128)(2,1)}, u32[]{:S(2)}, u32[]{:S(2)}) %collective-permute-start.5) | collective-permute-done | bytes 639008 | tf_op jit(solution)/shard_map/ppermute | solution.py:299
  46.8 1.2 %broadcast_select_fusion.refs_4_ = bf16[48,6656]{1,0:T(8,128)(2,1)S(1)} fusion(bf16[48,6656]{1,0:T(8,128)(2,1)S(1)} %collective-permute-done.2, bf16[48,6656]{1,0:T(8,128)(2,1)} %collective-permute-done.5, pred[]{:T(512)S(6)} %and.23), kind=kLoop, calls=%fused_computation.3 | loop fusion | flops 319488 | bytes 1916929 | tf_op jit(solution)/shard_map/jit(_where)/select_n | solution.py:319
  48.0 0.1 collective-permute-start.6
  48.1 0.7 collective-permute-start.8
  48.8 0.1 select_reduce_fusion
  49.0 2.3 %copy-done = bf16[384,6144]{1,0:T(8,128)(2,1)S(1)} copy-done((bf16[384,6144]{1,0:T(8,128)(2,1)S(1)}, bf16[384,6144]{1,0:T(8,128)(2,1)}, u32[]{:S(2)}) %copy-start) | copy-done | bytes 4718616
  51.3 1.1 %copy-done.1 = bf16[48,6656]{1,0:T(8,128)(2,1)S(1)} copy-done((bf16[48,6656]{1,0:T(8,128)(2,1)S(1)}, bf16[48,6656]{1,0:T(8,128)(2,1)}, u32[]{:S(2)}) %copy-start.1) | copy-done | bytes 639000
  52.4 3.5 %shard_map.60 = (f32[184,384]{1,0:T(8,128)S(1)}, f32[184,384]{1,0:T(8,128)S(1)}) custom-call(s32[3]{0:T(128)S(1)} %copy-done.6, bf16[48,6656]{1,0:T(8,128)(2,1)S(1)} %copy-done.1, bf16[48,6656]{1,0:T(8,128)(2,1)S(1)} %collective-permute-done.1.refs_1_, bf16[48,6656]{1,0:T(8,128)(2,1)S(1)} %collective-permute-done.refs_2_, ...), custom_call_target="tpu_custom_call" | custom-call | flops 1736441856 | bytes 565248 | tf_op jit(solution)/shard_map/pallas_call | solution.py:325
  56.0 0.2 fusion
  56.2 1.3 %collective-permute-done.9 = f32[184,384]{1,0:T(8,128)S(1)} collective-permute-done((f32[184,384]{1,0:T(8,128)S(1)}, f32[184,384]{1,0:T(8,128)S(1)}, u32[]{:S(2)}, u32[]{:S(2)}) %collective-permute-start.9) | collective-permute-done | bytes 282656 | tf_op jit(solution)/shard_map/ppermute | solution.py:296
  57.5 3.1 %collective-permute-done.6.refs_5_ = bf16[48,6656]{1,0:T(8,128)(2,1)S(1)} collective-permute-done((bf16[48,6656]{1,0:T(8,128)(2,1)S(1)}, bf16[48,6656]{1,0:T(8,128)(2,1)S(1)}, u32[]{:S(2)}, u32[]{:S(2)}) %collective-permute-start.6) | collective-permute-done | bytes 639008 | tf_op jit(solution)/shard_map/ppermute | solution.py:299
  60.7 2.4 %collective-permute-start.10 = (bf16[48,6656]{1,0:T(8,128)(2,1)S(1)}, bf16[48,6656]{1,0:T(8,128)(2,1)S(1)}, u32[]{:S(2)}, u32[]{:S(2)}) collective-permute-start(bf16[48,6656]{1,0:T(8,128)(2,1)S(1)} %collective-permute-done.7.refs_7_), channel_id=1, source_target_pairs={{0,4},{2,6},{4,0},{6,2},{24,28},{26,30},{28,24},{30,26}} | collective-permute-start | bytes 1916936 | tf_op jit(solution)/shard_map/ppermute | solution.py:336
  63.1 0.7 collective-permute-start.11
  63.8 0.3 convolution_bitcast_fusion
  64.1 0.2 fusion.2
  64.3 1.5 %collective-permute-start.12 = (f32[184,384]{1,0:T(8,128)S(1)}, f32[184,384]{1,0:T(8,128)S(1)}, u32[]{:S(2)}, u32[]{:S(2)}) collective-permute-start(f32[184,384]{1,0:T(8,128)S(1)} %add.34), channel_id=1, source_target_pairs={{0,2},{1,3},{2,0},{3,1},{4,6},{5,7},{6,4},{7,5},{8,10},{9,11},{10,... | collective-permute-start | bytes 847880 | tf_op jit(solution)/shard_map/ppermute | solution.py:296
  65.9 0.3 convolution_bitcast_fusion.1
  66.2 0.2 fusion.4
  66.4 4.6 %collective-permute-done.12 = f32[184,384]{1,0:T(8,128)S(1)} collective-permute-done((f32[184,384]{1,0:T(8,128)S(1)}, f32[184,384]{1,0:T(8,128)S(1)}, u32[]{:S(2)}, u32[]{:S(2)}) %collective-permute-start.12) | collective-permute-done | bytes 282656 | tf_op jit(solution)/shard_map/ppermute | solution.py:296
  71.0 2.0 %collective-permute-done.10.refs_9_ = bf16[48,6656]{1,0:T(8,128)(2,1)S(1)} collective-permute-done((bf16[48,6656]{1,0:T(8,128)(2,1)S(1)}, bf16[48,6656]{1,0:T(8,128)(2,1)S(1)}, u32[]{:S(2)}, u32[]{:S(2)}) %collective-permute-start.10) | collective-permute-done | bytes 639008 | tf_op jit(solution)/shard_map/ppermute | solution.py:336
  73.0 3.3 %shard_map.61 = (f32[144,384]{1,0:T(8,128)S(1)}, f32[144,384]{1,0:T(8,128)S(1)}, f32[384,256]{1,0:T(8,128)S(1)}) custom-call(s32[3]{0:T(128)S(1)} %copy-done.6, bf16[48,6656]{1,0:T(8,128)(2,1)S(1)} %copy-done.2, bf16[48,6656]{1,0:T(8,128)(2,1)S(1)} %collective-permute-done.1.refs_1_, bf16[48,6656]{1,0:T(8,128)(2,1)S(1)} %collective-permute-done.refs_2_, ...), custom_call_target="tpu_custom_call" | custom-call | flops 1358954496 | bytes 442368 | tf_op jit(solution)/shard_map/pallas_call | solution.py:344
  76.4 0.5 collective-permute-start.13
  76.9 0.3 convolution_bitcast_fusion.2
  77.2 0.1 collective-permute-start.14
  77.4 0.5 collective-permute-done.15
  77.9 1.6 %collective-permute-start.16 = (f32[144,384]{1,0:T(8,128)S(1)}, f32[144,384]{1,0:T(8,128)S(1)}, u32[]{:S(2)}, u32[]{:S(2)}) collective-permute-start(f32[144,384]{1,0:T(8,128)S(1)} %add.38), channel_id=1, source_target_pairs={{0,2},{1,3},{2,0},{3,1},{4,6},{5,7},{6,4},{7,5},{8,10},{9,11},{10,... | collective-permute-start | bytes 663560 | tf_op jit(solution)/shard_map/ppermute | solution.py:296
  79.5 0.1 broadcast_compare_fusion.2
  79.6 0.7 copy-done.4
  80.3 1.0 %copy-done.5 = f32[184,384]{1,0:T(8,128)S(1)} copy-done((f32[184,384]{1,0:T(8,128)S(1)}, f32[184,384]{1,0:T(8,128)}, u32[]{:S(2)}) %copy-start.5) | copy-done | bytes 282648
  81.3 1.1 %shard_map.62 = (f32[3,128,512]{2,1,0:T(8,128)S(1)}, bf16[2,3,80,384]{3,2,1,0:T(8,128)(2,1)S(1)}, f32[128,384]{1,0:T(8,128)S(1)}) custom-call(s32[3]{0:T(128)S(1)} %copy-done.6, f32[384,256]{1,0:T(8,128)S(1)} %get-tuple-element.37.refs_0_, f32[384,256]{1,0:T(8,128)S(1)} %collective-permute-done.13.refs_1_, ...), custom_call_target="tpu_custom_call" | custom-call | flops 150994944 | bytes 589824 | tf_op jit(solution)/shard_map/pallas_call | solution.py:358
  82.4 3.1 %collective-permute-done.16 = f32[144,384]{1,0:T(8,128)S(1)} collective-permute-done((f32[144,384]{1,0:T(8,128)S(1)}, f32[144,384]{1,0:T(8,128)S(1)}, u32[]{:S(2)}, u32[]{:S(2)}) %collective-permute-start.16) | collective-permute-done | bytes 221216 | tf_op jit(solution)/shard_map/ppermute | solution.py:296
  85.6 0.1 sub.11.refs_8_
  85.7 1.3 %collective-permute-done.17.refs_4_ = f32[144,384]{1,0:T(8,128)S(1)} collective-permute-done((f32[144,384]{1,0:T(8,128)S(1)}, f32[144,384]{1,0:T(8,128)S(1)}, u32[]{:S(2)}, u32[]{:S(2)}) %collective-permute-start.17) | collective-permute-done | bytes 221216 | tf_op jit(solution)/shard_map/ppermute | solution.py:296
  87.0 3.7 %shard_map.63 = (f32[384,512]{1,0:T(8,128)}, f32[384,512]{1,0:T(8,128)}) custom-call(s32[3]{0:T(128)S(1)} %copy-done.6, bf16[2,3,80,384]{3,2,1,0:T(8,128)(2,1)S(1)} %get-tuple-element.39.refs_1_, f32[128,384]{1,0:T(8,128)S(1)} %get-tuple-element.40.refs_2_, f32[144,384]{1,0:T(8,128)S(1)} %add.39.refs_3_, f32[144,384]{1,0:T(8,128)S(1)} %collective-permute-done.17.refs_4_, ...), custom_call_target="tpu_custom_call" | custom-call | flops 452984832 | bytes 1769472 | tf_op jit(solution)/shard_map/pallas_call | solution.py:439
  (35 shorter events, 0.5 us)
Async XLA Ops:
  0.6 48.2 %copy-start.8 = (s32[3,128]{1,0:T(4,128)S(1)}, s32[3,128]{1,0:T(4,128)}, u32[]{:S(2)}) copy-start(s32[3,128]{1,0:T(4,128)} %index_hbm.1) | copy-start | bytes 4612
  1.3 47.6 %copy-start.6 = (s32[3]{0:T(128)S(1)}, s32[3]{0:T(128)}, u32[]{:S(2)}) copy-start(s32[3]{0:T(128)} %pad_add_fusion.place_ref.refs_0_) | copy-start | bytes 40
  5.9 17.7 %collective-permute-start = (bf16[48,6656]{1,0:T(8,128)(2,1)}, bf16[48,6656]{1,0:T(8,128)(2,1)S(1)}, u32[]{:S(2)}, u32[]{:S(2)}) collective-permute-start(bf16[48,6656]{1,0:T(8,128)(2,1)} %shard_map.59.refs_0_), channel_id=1, source_target_pairs={{0,8},{4,12},{8,0},{12,4},{16,24},{20,28},{24,16},{28,20},{1,9},{5... | collective-permute-start | bytes 1916936 | tf_op jit(solution)/shard_map/ppermute | solution.py:299
  9.0 16.0 %collective-permute-start.1 = (bf16[48,6656]{1,0:T(8,128)(2,1)}, bf16[48,6656]{1,0:T(8,128)(2,1)S(1)}, u32[]{:S(2)}, u32[]{:S(2)}) collective-permute-start(bf16[48,6656]{1,0:T(8,128)(2,1)} %shard_map.59.refs_0_), channel_id=1, source_target_pairs={{0,4},{4,0},{8,12},{12,8},{16,20},{20,16},{24,28},{28,24},{1,5},{5... | collective-permute-start | bytes 1916936 | tf_op jit(solution)/shard_map/ppermute | solution.py:299
  10.5 16.8 %collective-permute-start.4 = (bf16[48,6656]{1,0:T(8,128)(2,1)}, bf16[48,6656]{1,0:T(8,128)(2,1)S(1)}, u32[]{:S(2)}, u32[]{:S(2)}) collective-permute-start(bf16[48,6656]{1,0:T(8,128)(2,1)} %shard_map.59.refs_0_), channel_id=1, source_target_pairs={{8,16},{12,20},{16,8},{20,12},{9,17},{13,21},{17,9},{21,13},{10,18... | collective-permute-start | bytes 1916936 | tf_op jit(solution)/shard_map/ppermute | solution.py:299
  25.0 3.9 %collective-permute-start.2 = (bf16[48,6656]{1,0:T(8,128)(2,1)S(1)}, bf16[48,6656]{1,0:T(8,128)(2,1)S(1)}, u32[]{:S(2)}, u32[]{:S(2)}) collective-permute-start(bf16[48,6656]{1,0:T(8,128)(2,1)S(1)} %collective-permute-done.refs_2_), channel_id=1, source_target_pairs={{8,16},{12,20},{16,8},{20,12},{9,17},{13,21},{17,9},{21,13},{10,18... | collective-permute-start | bytes 1916936 | tf_op jit(solution)/shard_map/ppermute | solution.py:299
  25.7 15.0 %collective-permute-start.3 = (bf16[48,6656]{1,0:T(8,128)(2,1)S(1)}, bf16[48,6656]{1,0:T(8,128)(2,1)S(1)}, u32[]{:S(2)}, u32[]{:S(2)}) collective-permute-start(bf16[48,6656]{1,0:T(8,128)(2,1)S(1)} %collective-permute-done.refs_2_), channel_id=1, source_target_pairs={{0,4},{4,0},{8,12},{12,8},{16,20},{20,16},{24,28},{28,24},{1,5},{5... | collective-permute-start | bytes 1916936 | tf_op jit(solution)/shard_map/ppermute | solution.py:299
  27.3 19.5 %collective-permute-start.5 = (bf16[48,6656]{1,0:T(8,128)(2,1)S(1)}, bf16[48,6656]{1,0:T(8,128)(2,1)}, u32[]{:S(2)}, u32[]{:S(2)}) collective-permute-start(bf16[48,6656]{1,0:T(8,128)(2,1)S(1)} %collective-permute-done.4.refs_6_), channel_id=1, source_target_pairs={{8,0},{12,4},{16,24},{20,28},{9,1},{13,5},{17,25},{21,29},{10,2},{... | collective-permute-start | bytes 1916936 | tf_op jit(solution)/shard_map/ppermute | solution.py:299
  28.9 27.1 %copy-start.7 = (f32[3,128,128]{2,1,0:T(8,128)S(1)}, f32[3,128,128]{2,1,0:T(8,128)}, u32[]{:S(2)}) copy-start(f32[3,128,128]{2,1,0:T(8,128)} %param.7) | copy-start | bytes 589828
  40.7 20.0 %collective-permute-start.7 = (bf16[48,6656]{1,0:T(8,128)(2,1)S(1)}, bf16[48,6656]{1,0:T(8,128)(2,1)S(1)}, u32[]{:S(2)}, u32[]{:S(2)}) collective-permute-start(bf16[48,6656]{1,0:T(8,128)(2,1)S(1)} %collective-permute-done.2), channel_id=1, source_target_pairs={{8,0},{12,4},{16,24},{20,28},{9,1},{13,5},{17,25},{21,29},{10,2},{... | collective-permute-start | bytes 1916936 | tf_op jit(solution)/shard_map/ppermute | solution.py:299
  46.8 26.2 %copy-start.2 = (bf16[48,6656]{1,0:T(8,128)(2,1)S(1)}, bf16[48,6656]{1,0:T(8,128)(2,1)}, u32[]{:S(2)}) copy-start(bf16[48,6656]{1,0:T(8,128)(2,1)} %shard_map.59.refs_0_) | copy-start | bytes 1916932
  48.0 12.7 %collective-permute-start.6 = (bf16[48,6656]{1,0:T(8,128)(2,1)S(1)}, bf16[48,6656]{1,0:T(8,128)(2,1)S(1)}, u32[]{:S(2)}, u32[]{:S(2)}) collective-permute-start(bf16[48,6656]{1,0:T(8,128)(2,1)S(1)} %broadcast_select_fusion.refs_4_), channel_id=1, source_target_pairs={{0,4},{4,0},{8,12},{12,8},{16,20},{20,16},{24,28},{28,24},{1,5},{5... | collective-permute-start | bytes 1916936 | tf_op jit(solution)/shard_map/ppermute | solution.py:299
  48.1 12.6 %collective-permute-start.8 = (bf16[48,6656]{1,0:T(8,128)(2,1)S(1)}, bf16[48,6656]{1,0:T(8,128)(2,1)S(1)}, u32[]{:S(2)}, u32[]{:S(2)}) collective-permute-start(bf16[48,6656]{1,0:T(8,128)(2,1)S(1)} %collective-permute-done.1.refs_1_), channel_id=1, source_target_pairs={{8,16},{12,20},{16,8},{20,12},{9,17},{13,21},{17,9},{21,13},{10,18... | collective-permute-start | bytes 1916936 | tf_op jit(solution)/shard_map/ppermute | solution.py:299
  49.0 2.3 %copy-start = (bf16[384,6144]{1,0:T(8,128)(2,1)S(1)}, bf16[384,6144]{1,0:T(8,128)(2,1)}, u32[]{:S(2)}) copy-start(bf16[384,6144]{1,0:T(8,128)(2,1)} %refs_11_.1) | copy-start | bytes 14155780
  51.3 1.1 %copy-start.1 = (bf16[48,6656]{1,0:T(8,128)(2,1)S(1)}, bf16[48,6656]{1,0:T(8,128)(2,1)}, u32[]{:S(2)}) copy-start(bf16[48,6656]{1,0:T(8,128)(2,1)} %shard_map.59.refs_0_) | copy-start | bytes 1916932
  55.9 1.6 %collective-permute-start.9 = (f32[184,384]{1,0:T(8,128)S(1)}, f32[184,384]{1,0:T(8,128)S(1)}, u32[]{:S(2)}, u32[]{:S(2)}) collective-permute-start(f32[184,384]{1,0:T(8,128)S(1)} %get-tuple-element.30), channel_id=1, source_target_pairs={{0,1},{1,0},{2,3},{3,2},{4,5},{5,4},{6,7},{7,6},{8,9},{9,8},{10,11... | collective-permute-start | bytes 847880 | tf_op jit(solution)/shard_map/ppermute | solution.py:296
  60.7 12.3 %collective-permute-start.10 = (bf16[48,6656]{1,0:T(8,128)(2,1)S(1)}, bf16[48,6656]{1,0:T(8,128)(2,1)S(1)}, u32[]{:S(2)}, u32[]{:S(2)}) collective-permute-start(bf16[48,6656]{1,0:T(8,128)(2,1)S(1)} %collective-permute-done.7.refs_7_), channel_id=1, source_target_pairs={{0,4},{2,6},{4,0},{6,2},{24,28},{26,30},{28,24},{30,26}} | collective-permute-start | bytes 1916936 | tf_op jit(solution)/shard_map/ppermute | solution.py:336
  63.1 9.9 %collective-permute-start.11 = (bf16[48,6656]{1,0:T(8,128)(2,1)S(1)}, bf16[48,6656]{1,0:T(8,128)(2,1)S(1)}, u32[]{:S(2)}, u32[]{:S(2)}) collective-permute-start(bf16[48,6656]{1,0:T(8,128)(2,1)S(1)} %collective-permute-done.6.refs_5_), channel_id=1, source_target_pairs={{9,1},{11,3},{13,5},{15,7},{17,25},{19,27},{21,29},{23,31}} | collective-permute-start | bytes 1916936 | tf_op jit(solution)/shard_map/ppermute | solution.py:337
  64.3 6.7 %collective-permute-start.12 = (f32[184,384]{1,0:T(8,128)S(1)}, f32[184,384]{1,0:T(8,128)S(1)}, u32[]{:S(2)}, u32[]{:S(2)}) collective-permute-start(f32[184,384]{1,0:T(8,128)S(1)} %add.34), channel_id=1, source_target_pairs={{0,2},{1,3},{2,0},{3,1},{4,6},{5,7},{6,4},{7,5},{8,10},{9,11},{10,... | collective-permute-start | bytes 847880 | tf_op jit(solution)/shard_map/ppermute | solution.py:296
  76.3 10.7 %copy-start.3 = (f32[384,512]{1,0:T(8,128)S(1)}, f32[384,512]{1,0:T(8,128)}, u32[]{:S(2)}) copy-start(f32[384,512]{1,0:T(8,128)} %refs_9_.1) | copy-start | bytes 2359300
  76.3 1.5 %collective-permute-start.15 = (f32[144,384]{1,0:T(8,128)S(1)}, f32[144,384]{1,0:T(8,128)S(1)}, u32[]{:S(2)}, u32[]{:S(2)}) collective-permute-start(f32[144,384]{1,0:T(8,128)S(1)} %get-tuple-element.42), channel_id=1, source_target_pairs={{0,1},{1,0},{2,3},{3,2},{4,5},{5,4},{6,7},{7,6},{8,9},{9,8},{10,11... | collective-permute-start | bytes 663560 | tf_op jit(solution)/shard_map/ppermute | solution.py:296
  76.4 3.9 %collective-permute-start.13 = (f32[384,256]{1,0:T(8,128)S(1)}, f32[384,256]{1,0:T(8,128)S(1)}, u32[]{:S(2)}, u32[]{:S(2)}) collective-permute-start(f32[384,256]{1,0:T(8,128)S(1)} %get-tuple-element.37.refs_0_), channel_id=1, source_target_pairs={{0,1},{1,0},{2,3},{3,2},{4,5},{5,4},{6,7},{7,6},{8,9},{9,8},{10,11... | collective-permute-start | bytes 1179656 | tf_op jit(solution)/shard_map/ppermute | solution.py:296
  77.2 2.4 %collective-permute-start.14 = (f32[184,384]{1,0:T(8,128)S(1)}, f32[184,384]{1,0:T(8,128)S(1)}, u32[]{:S(2)}, u32[]{:S(2)}) collective-permute-start(f32[184,384]{1,0:T(8,128)S(1)} %add.37.refs_3_), channel_id=1, source_target_pairs={{0,1},{1,0},{2,3},{3,2},{4,5},{5,4},{6,7},{7,6},{8,9},{9,8},{10,11... | collective-permute-start | bytes 847880 | tf_op jit(solution)/shard_map/ppermute | solution.py:296
  77.9 7.5 %collective-permute-start.16 = (f32[144,384]{1,0:T(8,128)S(1)}, f32[144,384]{1,0:T(8,128)S(1)}, u32[]{:S(2)}, u32[]{:S(2)}) collective-permute-start(f32[144,384]{1,0:T(8,128)S(1)} %add.38), channel_id=1, source_target_pairs={{0,2},{1,3},{2,0},{3,1},{4,6},{5,7},{6,4},{7,5},{8,10},{9,11},{10,... | collective-permute-start | bytes 663560 | tf_op jit(solution)/shard_map/ppermute | solution.py:296
  79.6 0.7 copy-start.4
  80.3 1.0 %copy-start.5 = (f32[184,384]{1,0:T(8,128)S(1)}, f32[184,384]{1,0:T(8,128)}, u32[]{:S(2)}) copy-start(f32[184,384]{1,0:T(8,128)} %copy-done.4) | copy-start | bytes 847876
  85.5 1.5 %collective-permute-start.17 = (f32[144,384]{1,0:T(8,128)S(1)}, f32[144,384]{1,0:T(8,128)S(1)}, u32[]{:S(2)}, u32[]{:S(2)}) collective-permute-start(f32[144,384]{1,0:T(8,128)S(1)} %add.39.refs_3_), channel_id=1, source_target_pairs={{0,1},{1,0},{2,3},{3,2},{4,5},{5,4},{6,7},{7,6},{8,9},{9,8},{10,11... | collective-permute-start | bytes 663560 | tf_op jit(solution)/shard_map/ppermute | solution.py:296

commit v10 on v9

--- a/solution.py
+++ b/solution.py
@@ -173,7 +173,7 @@
 
 
 def pick_kernel(
-    per, index_hbm, place_ref, features_ref, targets_ref, out_ref, index_ref, held_targets, side_sems, held_ref, sems
+    per, index_hbm, features_ref, targets_ref, out_ref, index_ref, held_targets, side_sems, held_ref, sems
 ):
     index = pltpu.make_async_copy(index_hbm, index_ref, side_sems.at[0])
     index.start()
@@ -181,7 +181,7 @@
     side = pltpu.make_async_copy(targets_ref, held_targets, side_sems.at[1])
     side.start()
     index.wait()
-    rank, core = place_ref[0], place_ref[1]
+    rank, core = lax.axis_index("rows"), lax.rem(lax.axis_index("feat"), 2)
     rows, columns = features_ref.shape
     steps = index_ref.shape[0]
     line = lax.broadcasted_iota(jnp.int32, (steps * per, 128), 0)
@@ -206,13 +206,13 @@
     out_ref[:, columns + width :] = take(low)
 
 
-def pick(block_index, place, features, targets, per):
+def pick(block_index, features, targets, per):
     count = block_index.shape[0] * per
     wide = features.shape[1] + targets.shape[1]
     return pl.pallas_call(
         functools.partial(pick_kernel, per),
         out_shape=jax.ShapeDtypeStruct((count, wide), features.dtype),
-        in_specs=[HBM, SMEM, HBM, HBM],
+        in_specs=[HBM, HBM, HBM],
         out_specs=VMEM,
         scratch_shapes=[
             pltpu.SMEM(block_index.shape, jnp.int32),
@@ -222,7 +222,7 @@
         + held(features),
         compiler_params=PICK,
         cost_estimate=cost(count * features.shape[0], wide),
-    )(block_index, place, features, targets)
+    )(block_index, features, targets)
 
 
 def gram_kernel(steps, per, missing, place_ref, *refs):
@@ -303,7 +303,7 @@
         steps, block = block_index.shape
         count = steps * per
         hold = lax.optimization_barrier
-        own = pick(block_index, self.place, features, targets, per)
+        own = pick(block_index, features, targets, per)
 
         pair = self.send(own, self.pair)
         mid = self.send(own, self.inner)

time: 91.1 us -> 89.6 us (0.984)
    unnamed x18 -> x16, local copies, waits for them, and re-layouts: 5.1 us -> 5.1 us
where the time goes in v10:
time: 89.6 us; the launch traced here: 89.2 us
  waiting for transfers between devices  46.3 us (52%)
  starting transfers between devices  18 us (20%)
  Pallas kernels  15.3 us (17%)
  local copies, waits for them, and re-layouts  5.34 us (6%)
  other arithmetic  1.81 us (2%)
  matrix products  1.52 us (2%)
  between operations  0.95 us (1%)
    ppermute x9, waiting for transfers between devices, send(): return lax.ppermute(array, 'rows', pairs)  33.5 us
    ppermute x9, starting transfers between devices, send(): return lax.ppermute(array, 'rows', pairs)  10.9 us
    ppermute x7, waiting for transfers between devices, near(): return lax.ppermute(array, 'feat', [(f, f ^ bit) for f in range(4)])  10.8 us
    unnamed x16, local copies, waits for them, and re-layouts  5.1 us
    ppermute x7, starting transfers between devices, near(): return lax.ppermute(array, 'feat', [(f, f ^ bit) for f in range(4)])  3.95 us
    pallas_call x1, Pallas kernels, pick(): pl.pallas_call(functools.partial(pick_kernel, per), out_shape=jax.ShapeDt...  3.76 us
    pallas_call x1, Pallas kernels, local(): pl.pallas_call(functools.partial(finish_kernel, steps, per, lined), out_s...  3.67 us
    pallas_call x1, Pallas kernels, run(): pl.pallas_call(functools.partial(gram_kernel, steps, per, 8 - begun), out...  3.49 us
  transfers between devices with their start and end apart: 18, of which 11 were waited for; matrix products, arithmetic and copies ran while one was open for 4% of the time, Pallas kernels for 5%

profile of v10, /device:TPU:0, one launch (start us, length us, event | category | flops | bytes accessed | tf_op | source)
XLA Modules:
  0.0 89.2 jit_solution(12873469972261524781)
XLA Ops:
  0.6 3.8 %shard_map.59.refs_0_ = bf16[48,6656]{1,0:T(8,128)(2,1)} custom-call(s32[3,128]{1,0:T(4,128)} %index_hbm.1, bf16[384,6144]{1,0:T(8,128)(2,1)} %refs_11_.1, f32[384,512]{1,0:T(8,128)} %refs_9_.1), custom_call_target="tpu_custom_call" | custom-call | flops 245366784 | bytes 73728 | tf_op jit(solution)/shard_map/pallas_call | solution.py:212
  4.4 3.1 %collective-permute-start = (bf16[48,6656]{1,0:T(8,128)(2,1)}, bf16[48,6656]{1,0:T(8,128)(2,1)S(1)}, u32[]{:S(2)}, u32[]{:S(2)}) collective-permute-start(bf16[48,6656]{1,0:T(8,128)(2,1)} %shard_map.59.refs_0_), channel_id=1, source_target_pairs={{0,8},{4,12},{8,0},{12,4},{16,24},{20,28},{24,16},{28,20},{1,9},{5... | collective-permute-start | bytes 1916936 | tf_op jit(solution)/shard_map/ppermute | solution.py:299
  7.5 1.5 %collective-permute-start.1 = (bf16[48,6656]{1,0:T(8,128)(2,1)}, bf16[48,6656]{1,0:T(8,128)(2,1)S(1)}, u32[]{:S(2)}, u32[]{:S(2)}) collective-permute-start(bf16[48,6656]{1,0:T(8,128)(2,1)} %shard_map.59.refs_0_), channel_id=1, source_target_pairs={{0,4},{4,0},{8,12},{12,8},{16,20},{20,16},{24,28},{28,24},{1,5},{5... | collective-permute-start | bytes 1916936 | tf_op jit(solution)/shard_map/ppermute | solution.py:299
  9.0 0.7 collective-permute-start.4
  9.7 12.4 %collective-permute-done.refs_2_ = bf16[48,6656]{1,0:T(8,128)(2,1)S(1)} collective-permute-done((bf16[48,6656]{1,0:T(8,128)(2,1)}, bf16[48,6656]{1,0:T(8,128)(2,1)S(1)}, u32[]{:S(2)}, u32[]{:S(2)}) %collective-permute-start) | collective-permute-done | bytes 639008 | tf_op jit(solution)/shard_map/ppermute | solution.py:299
  22.1 1.5 %collective-permute-done.1.refs_1_ = bf16[48,6656]{1,0:T(8,128)(2,1)S(1)} collective-permute-done((bf16[48,6656]{1,0:T(8,128)(2,1)}, bf16[48,6656]{1,0:T(8,128)(2,1)S(1)}, u32[]{:S(2)}, u32[]{:S(2)}) %collective-permute-start.1) | collective-permute-done | bytes 639008 | tf_op jit(solution)/shard_map/ppermute | solution.py:299
  23.5 0.7 collective-permute-start.2
  24.2 1.6 %collective-permute-start.3 = (bf16[48,6656]{1,0:T(8,128)(2,1)S(1)}, bf16[48,6656]{1,0:T(8,128)(2,1)S(1)}, u32[]{:S(2)}, u32[]{:S(2)}) collective-permute-start(bf16[48,6656]{1,0:T(8,128)(2,1)S(1)} %collective-permute-done.refs_2_), channel_id=1, source_target_pairs={{0,4},{4,0},{8,12},{12,8},{16,20},{20,16},{24,28},{28,24},{1,5},{5... | collective-permute-start | bytes 1916936 | tf_op jit(solution)/shard_map/ppermute | solution.py:299
  25.8 1.3 %collective-permute-start.5 = (bf16[48,6656]{1,0:T(8,128)(2,1)S(1)}, bf16[48,6656]{1,0:T(8,128)(2,1)}, u32[]{:S(2)}, u32[]{:S(2)}) collective-permute-start(bf16[48,6656]{1,0:T(8,128)(2,1)S(1)} %collective-permute-done.4.refs_6_), channel_id=1, source_target_pairs={{8,0},{12,4},{16,24},{20,28},{9,1},{13,5},{17,25},{21,29},{10,2},{... | collective-permute-start | bytes 1916936 | tf_op jit(solution)/shard_map/ppermute | solution.py:299
  27.2 0.1 mul.21
  27.3 0.1 iota_compare_fusion
  27.4 0.1 select_reduce_fusion
  27.6 11.7 %collective-permute-done.3.refs_3_ = bf16[48,6656]{1,0:T(8,128)(2,1)S(1)} collective-permute-done((bf16[48,6656]{1,0:T(8,128)(2,1)S(1)}, bf16[48,6656]{1,0:T(8,128)(2,1)S(1)}, u32[]{:S(2)}, u32[]{:S(2)}) %collective-permute-start.3) | collective-permute-done | bytes 639008 | tf_op jit(solution)/shard_map/ppermute | solution.py:299
  39.2 1.3 %collective-permute-start.7 = (bf16[48,6656]{1,0:T(8,128)(2,1)S(1)}, bf16[48,6656]{1,0:T(8,128)(2,1)S(1)}, u32[]{:S(2)}, u32[]{:S(2)}) collective-permute-start(bf16[48,6656]{1,0:T(8,128)(2,1)S(1)} %collective-permute-done.2), channel_id=1, source_target_pairs={{8,0},{12,4},{16,24},{20,28},{9,1},{13,5},{17,25},{21,29},{10,2},{... | collective-permute-start | bytes 1916936 | tf_op jit(solution)/shard_map/ppermute | solution.py:299
  40.5 4.8 %collective-permute-done.5 = bf16[48,6656]{1,0:T(8,128)(2,1)} collective-permute-done((bf16[48,6656]{1,0:T(8,128)(2,1)S(1)}, bf16[48,6656]{1,0:T(8,128)(2,1)}, u32[]{:S(2)}, u32[]{:S(2)}) %collective-permute-start.5) | collective-permute-done | bytes 639008 | tf_op jit(solution)/shard_map/ppermute | solution.py:299
  45.3 1.2 %broadcast_select_fusion.refs_4_ = bf16[48,6656]{1,0:T(8,128)(2,1)S(1)} fusion(bf16[48,6656]{1,0:T(8,128)(2,1)S(1)} %collective-permute-done.2, bf16[48,6656]{1,0:T(8,128)(2,1)} %collective-permute-done.5, pred[]{:T(512)S(6)} %and.23), kind=kLoop, calls=%fused_computation.3 | loop fusion | flops 319488 | bytes 1916929 | tf_op jit(solution)/shard_map/jit(_where)/select_n | solution.py:319
  46.5 0.1 collective-permute-start.6
  46.6 0.7 collective-permute-start.8
  47.3 0.1 pad_add_fusion.place_ref.refs_0_
  47.4 2.3 %copy-done = bf16[384,6144]{1,0:T(8,128)(2,1)S(1)} copy-done((bf16[384,6144]{1,0:T(8,128)(2,1)S(1)}, bf16[384,6144]{1,0:T(8,128)(2,1)}, u32[]{:S(2)}) %copy-start) | copy-done | bytes 4718616
  49.8 1.1 %copy-done.1 = bf16[48,6656]{1,0:T(8,128)(2,1)S(1)} copy-done((bf16[48,6656]{1,0:T(8,128)(2,1)S(1)}, bf16[48,6656]{1,0:T(8,128)(2,1)}, u32[]{:S(2)}) %copy-start.1) | copy-done | bytes 639000
  50.8 3.5 %shard_map.60 = (f32[184,384]{1,0:T(8,128)S(1)}, f32[184,384]{1,0:T(8,128)S(1)}) custom-call(s32[3]{0:T(128)S(1)} %pad_add_fusion.place_ref.refs_0_, bf16[48,6656]{1,0:T(8,128)(2,1)S(1)} %copy-done.1, bf16[48,6656]{1,0:T(8,128)(2,1)S(1)} %collective-permute-done.1.refs_1_, bf16[48,6656]{1,0:T(8,128)(2,1)S(1)} %collective-permute-done.refs_2_, ...), custom_call_target="tpu_custom_call" | custom-call | flops 1736441856 | bytes 565248 | tf_op jit(solution)/shard_map/pallas_call | solution.py:325
  54.4 0.2 fusion
  54.7 1.3 %collective-permute-done.9 = f32[184,384]{1,0:T(8,128)S(1)} collective-permute-done((f32[184,384]{1,0:T(8,128)S(1)}, f32[184,384]{1,0:T(8,128)S(1)}, u32[]{:S(2)}, u32[]{:S(2)}) %collective-permute-start.9) | collective-permute-done | bytes 282656 | tf_op jit(solution)/shard_map/ppermute | solution.py:296
  56.0 3.2 %collective-permute-done.6.refs_5_ = bf16[48,6656]{1,0:T(8,128)(2,1)S(1)} collective-permute-done((bf16[48,6656]{1,0:T(8,128)(2,1)S(1)}, bf16[48,6656]{1,0:T(8,128)(2,1)S(1)}, u32[]{:S(2)}, u32[]{:S(2)}) %collective-permute-start.6) | collective-permute-done | bytes 639008 | tf_op jit(solution)/shard_map/ppermute | solution.py:299
  59.2 2.4 %collective-permute-start.10 = (bf16[48,6656]{1,0:T(8,128)(2,1)S(1)}, bf16[48,6656]{1,0:T(8,128)(2,1)S(1)}, u32[]{:S(2)}, u32[]{:S(2)}) collective-permute-start(bf16[48,6656]{1,0:T(8,128)(2,1)S(1)} %collective-permute-done.7.refs_7_), channel_id=1, source_target_pairs={{0,4},{2,6},{4,0},{6,2},{24,28},{26,30},{28,24},{30,26}} | collective-permute-start | bytes 1916936 | tf_op jit(solution)/shard_map/ppermute | solution.py:336
  61.6 0.7 collective-permute-start.11
  62.3 0.3 convolution_bitcast_fusion
  62.6 0.2 fusion.2
  62.9 1.6 %collective-permute-start.12 = (f32[184,384]{1,0:T(8,128)S(1)}, f32[184,384]{1,0:T(8,128)S(1)}, u32[]{:S(2)}, u32[]{:S(2)}) collective-permute-start(f32[184,384]{1,0:T(8,128)S(1)} %add.34), channel_id=1, source_target_pairs={{0,2},{1,3},{2,0},{3,1},{4,6},{5,7},{6,4},{7,5},{8,10},{9,11},{10,... | collective-permute-start | bytes 847880 | tf_op jit(solution)/shard_map/ppermute | solution.py:296
  64.4 0.3 convolution_bitcast_fusion.1
  64.7 0.2 fusion.4
  64.9 4.6 %collective-permute-done.12 = f32[184,384]{1,0:T(8,128)S(1)} collective-permute-done((f32[184,384]{1,0:T(8,128)S(1)}, f32[184,384]{1,0:T(8,128)S(1)}, u32[]{:S(2)}, u32[]{:S(2)}) %collective-permute-start.12) | collective-permute-done | bytes 282656 | tf_op jit(solution)/shard_map/ppermute | solution.py:296
  69.5 2.0 %collective-permute-done.10.refs_9_ = bf16[48,6656]{1,0:T(8,128)(2,1)S(1)} collective-permute-done((bf16[48,6656]{1,0:T(8,128)(2,1)S(1)}, bf16[48,6656]{1,0:T(8,128)(2,1)S(1)}, u32[]{:S(2)}, u32[]{:S(2)}) %collective-permute-start.10) | collective-permute-done | bytes 639008 | tf_op jit(solution)/shard_map/ppermute | solution.py:336
  71.5 3.3 %shard_map.61 = (f32[144,384]{1,0:T(8,128)S(1)}, f32[144,384]{1,0:T(8,128)S(1)}, f32[384,256]{1,0:T(8,128)S(1)}) custom-call(s32[3]{0:T(128)S(1)} %pad_add_fusion.place_ref.refs_0_, bf16[48,6656]{1,0:T(8,128)(2,1)S(1)} %copy-done.2, bf16[48,6656]{1,0:T(8,128)(2,1)S(1)} %collective-permute-done.1.refs_1_, bf16[48,6656]{1,0:T(8,128)(2,1)S(1)} %collective-permute-done.refs_2_, ...), custom_call_target="tpu_custom_call" | custom-call | flops 1358954496 | bytes 442368 | tf_op jit(solution)/shard_map/pallas_call | solution.py:344
  75.0 0.5 collective-permute-start.13
  75.4 0.3 convolution_bitcast_fusion.2
  75.8 0.1 collective-permute-start.14
  75.9 0.5 collective-permute-done.15
  76.4 1.5 %collective-permute-start.16 = (f32[144,384]{1,0:T(8,128)S(1)}, f32[144,384]{1,0:T(8,128)S(1)}, u32[]{:S(2)}, u32[]{:S(2)}) collective-permute-start(f32[144,384]{1,0:T(8,128)S(1)} %add.38), channel_id=1, source_target_pairs={{0,2},{1,3},{2,0},{3,1},{4,6},{5,7},{6,4},{7,5},{8,10},{9,11},{10,... | collective-permute-start | bytes 663560 | tf_op jit(solution)/shard_map/ppermute | solution.py:296
  78.0 0.1 broadcast_compare_fusion.2
  78.1 0.7 copy-done.4
  78.8 1.0 %copy-done.5 = f32[184,384]{1,0:T(8,128)S(1)} copy-done((f32[184,384]{1,0:T(8,128)S(1)}, f32[184,384]{1,0:T(8,128)}, u32[]{:S(2)}) %copy-start.5) | copy-done | bytes 282648
  79.8 1.1 %shard_map.62 = (f32[3,128,512]{2,1,0:T(8,128)S(1)}, bf16[2,3,80,384]{3,2,1,0:T(8,128)(2,1)S(1)}, f32[128,384]{1,0:T(8,128)S(1)}) custom-call(s32[3]{0:T(128)S(1)} %pad_add_fusion.place_ref.refs_0_, f32[384,256]{1,0:T(8,128)S(1)} %get-tuple-element.37.refs_0_, f32[384,256]{1,0:T(8,128)S(1)} %collective-permute-done.13.refs_1_, ...), custom_call_target="tpu_custom_call" | custom-call | flops 150994944 | bytes 589824 | tf_op jit(solution)/shard_map/pallas_call | solution.py:358
  80.9 3.1 %collective-permute-done.16 = f32[144,384]{1,0:T(8,128)S(1)} collective-permute-done((f32[144,384]{1,0:T(8,128)S(1)}, f32[144,384]{1,0:T(8,128)S(1)}, u32[]{:S(2)}, u32[]{:S(2)}) %collective-permute-start.16) | collective-permute-done | bytes 221216 | tf_op jit(solution)/shard_map/ppermute | solution.py:296
  84.1 0.1 sub.11.refs_8_
  84.2 1.3 %collective-permute-done.17.refs_4_ = f32[144,384]{1,0:T(8,128)S(1)} collective-permute-done((f32[144,384]{1,0:T(8,128)S(1)}, f32[144,384]{1,0:T(8,128)S(1)}, u32[]{:S(2)}, u32[]{:S(2)}) %collective-permute-start.17) | collective-permute-done | bytes 221216 | tf_op jit(solution)/shard_map/ppermute | solution.py:296
  85.6 3.7 %shard_map.63 = (f32[384,512]{1,0:T(8,128)}, f32[384,512]{1,0:T(8,128)}) custom-call(s32[3]{0:T(128)S(1)} %pad_add_fusion.place_ref.refs_0_, bf16[2,3,80,384]{3,2,1,0:T(8,128)(2,1)S(1)} %get-tuple-element.39.refs_1_, f32[128,384]{1,0:T(8,128)S(1)} %get-tuple-element.40.refs_2_, f32[144,384]{1,0:T(8,128)S(1)} %add.39.refs_3_, ...), custom_call_target="tpu_custom_call" | custom-call | flops 452984832 | bytes 1769472 | tf_op jit(solution)/shard_map/pallas_call | solution.py:439
  (33 shorter events, 0.5 us)
Async XLA Ops:
  0.6 26.8 %copy-start.7 = (s32[3,128]{1,0:T(4,128)S(1)}, s32[3,128]{1,0:T(4,128)}, u32[]{:S(2)}) copy-start(s32[3,128]{1,0:T(4,128)} %index_hbm.1) | copy-start | bytes 4612
  4.4 17.7 %collective-permute-start = (bf16[48,6656]{1,0:T(8,128)(2,1)}, bf16[48,6656]{1,0:T(8,128)(2,1)S(1)}, u32[]{:S(2)}, u32[]{:S(2)}) collective-permute-start(bf16[48,6656]{1,0:T(8,128)(2,1)} %shard_map.59.refs_0_), channel_id=1, source_target_pairs={{0,8},{4,12},{8,0},{12,4},{16,24},{20,28},{24,16},{28,20},{1,9},{5... | collective-permute-start | bytes 1916936 | tf_op jit(solution)/shard_map/ppermute | solution.py:299
  7.5 16.1 %collective-permute-start.1 = (bf16[48,6656]{1,0:T(8,128)(2,1)}, bf16[48,6656]{1,0:T(8,128)(2,1)S(1)}, u32[]{:S(2)}, u32[]{:S(2)}) collective-permute-start(bf16[48,6656]{1,0:T(8,128)(2,1)} %shard_map.59.refs_0_), channel_id=1, source_target_pairs={{0,4},{4,0},{8,12},{12,8},{16,20},{20,16},{24,28},{28,24},{1,5},{5... | collective-permute-start | bytes 1916936 | tf_op jit(solution)/shard_map/ppermute | solution.py:299
  9.0 16.8 %collective-permute-start.4 = (bf16[48,6656]{1,0:T(8,128)(2,1)}, bf16[48,6656]{1,0:T(8,128)(2,1)S(1)}, u32[]{:S(2)}, u32[]{:S(2)}) collective-permute-start(bf16[48,6656]{1,0:T(8,128)(2,1)} %shard_map.59.refs_0_), channel_id=1, source_target_pairs={{8,16},{12,20},{16,8},{20,12},{9,17},{13,21},{17,9},{21,13},{10,18... | collective-permute-start | bytes 1916936 | tf_op jit(solution)/shard_map/ppermute | solution.py:299
  23.5 4.0 %collective-permute-start.2 = (bf16[48,6656]{1,0:T(8,128)(2,1)S(1)}, bf16[48,6656]{1,0:T(8,128)(2,1)S(1)}, u32[]{:S(2)}, u32[]{:S(2)}) collective-permute-start(bf16[48,6656]{1,0:T(8,128)(2,1)S(1)} %collective-permute-done.refs_2_), channel_id=1, source_target_pairs={{8,16},{12,20},{16,8},{20,12},{9,17},{13,21},{17,9},{21,13},{10,18... | collective-permute-start | bytes 1916936 | tf_op jit(solution)/shard_map/ppermute | solution.py:299
  24.2 15.0 %collective-permute-start.3 = (bf16[48,6656]{1,0:T(8,128)(2,1)S(1)}, bf16[48,6656]{1,0:T(8,128)(2,1)S(1)}, u32[]{:S(2)}, u32[]{:S(2)}) collective-permute-start(bf16[48,6656]{1,0:T(8,128)(2,1)S(1)} %collective-permute-done.refs_2_), channel_id=1, source_target_pairs={{0,4},{4,0},{8,12},{12,8},{16,20},{20,16},{24,28},{28,24},{1,5},{5... | collective-permute-start | bytes 1916936 | tf_op jit(solution)/shard_map/ppermute | solution.py:299
  25.8 19.5 %collective-permute-start.5 = (bf16[48,6656]{1,0:T(8,128)(2,1)S(1)}, bf16[48,6656]{1,0:T(8,128)(2,1)}, u32[]{:S(2)}, u32[]{:S(2)}) collective-permute-start(bf16[48,6656]{1,0:T(8,128)(2,1)S(1)} %collective-permute-done.4.refs_6_), channel_id=1, source_target_pairs={{8,0},{12,4},{16,24},{20,28},{9,1},{13,5},{17,25},{21,29},{10,2},{... | collective-permute-start | bytes 1916936 | tf_op jit(solution)/shard_map/ppermute | solution.py:299
  27.5 26.9 %copy-start.6 = (f32[3,128,128]{2,1,0:T(8,128)S(1)}, f32[3,128,128]{2,1,0:T(8,128)}, u32[]{:S(2)}) copy-start(f32[3,128,128]{2,1,0:T(8,128)} %param.7) | copy-start | bytes 589828
  39.2 20.0 %collective-permute-start.7 = (bf16[48,6656]{1,0:T(8,128)(2,1)S(1)}, bf16[48,6656]{1,0:T(8,128)(2,1)S(1)}, u32[]{:S(2)}, u32[]{:S(2)}) collective-permute-start(bf16[48,6656]{1,0:T(8,128)(2,1)S(1)} %collective-permute-done.2), channel_id=1, source_target_pairs={{8,0},{12,4},{16,24},{20,28},{9,1},{13,5},{17,25},{21,29},{10,2},{... | collective-permute-start | bytes 1916936 | tf_op jit(solution)/shard_map/ppermute | solution.py:299
  45.3 26.2 %copy-start.2 = (bf16[48,6656]{1,0:T(8,128)(2,1)S(1)}, bf16[48,6656]{1,0:T(8,128)(2,1)}, u32[]{:S(2)}) copy-start(bf16[48,6656]{1,0:T(8,128)(2,1)} %shard_map.59.refs_0_) | copy-start | bytes 1916932
  46.5 12.7 %collective-permute-start.6 = (bf16[48,6656]{1,0:T(8,128)(2,1)S(1)}, bf16[48,6656]{1,0:T(8,128)(2,1)S(1)}, u32[]{:S(2)}, u32[]{:S(2)}) collective-permute-start(bf16[48,6656]{1,0:T(8,128)(2,1)S(1)} %broadcast_select_fusion.refs_4_), channel_id=1, source_target_pairs={{0,4},{4,0},{8,12},{12,8},{16,20},{20,16},{24,28},{28,24},{1,5},{5... | collective-permute-start | bytes 1916936 | tf_op jit(solution)/shard_map/ppermute | solution.py:299
  46.6 12.6 %collective-permute-start.8 = (bf16[48,6656]{1,0:T(8,128)(2,1)S(1)}, bf16[48,6656]{1,0:T(8,128)(2,1)S(1)}, u32[]{:S(2)}, u32[]{:S(2)}) collective-permute-start(bf16[48,6656]{1,0:T(8,128)(2,1)S(1)} %collective-permute-done.1.refs_1_), channel_id=1, source_target_pairs={{8,16},{12,20},{16,8},{20,12},{9,17},{13,21},{17,9},{21,13},{10,18... | collective-permute-start | bytes 1916936 | tf_op jit(solution)/shard_map/ppermute | solution.py:299
  47.4 2.3 %copy-start = (bf16[384,6144]{1,0:T(8,128)(2,1)S(1)}, bf16[384,6144]{1,0:T(8,128)(2,1)}, u32[]{:S(2)}) copy-start(bf16[384,6144]{1,0:T(8,128)(2,1)} %refs_11_.1) | copy-start | bytes 14155780
  49.8 1.1 %copy-start.1 = (bf16[48,6656]{1,0:T(8,128)(2,1)S(1)}, bf16[48,6656]{1,0:T(8,128)(2,1)}, u32[]{:S(2)}) copy-start(bf16[48,6656]{1,0:T(8,128)(2,1)} %shard_map.59.refs_0_) | copy-start | bytes 1916932
  54.3 1.6 %collective-permute-start.9 = (f32[184,384]{1,0:T(8,128)S(1)}, f32[184,384]{1,0:T(8,128)S(1)}, u32[]{:S(2)}, u32[]{:S(2)}) collective-permute-start(f32[184,384]{1,0:T(8,128)S(1)} %get-tuple-element.30), channel_id=1, source_target_pairs={{0,1},{1,0},{2,3},{3,2},{4,5},{5,4},{6,7},{7,6},{8,9},{9,8},{10,11... | collective-permute-start | bytes 847880 | tf_op jit(solution)/shard_map/ppermute | solution.py:296
  59.2 12.3 %collective-permute-start.10 = (bf16[48,6656]{1,0:T(8,128)(2,1)S(1)}, bf16[48,6656]{1,0:T(8,128)(2,1)S(1)}, u32[]{:S(2)}, u32[]{:S(2)}) collective-permute-start(bf16[48,6656]{1,0:T(8,128)(2,1)S(1)} %collective-permute-done.7.refs_7_), channel_id=1, source_target_pairs={{0,4},{2,6},{4,0},{6,2},{24,28},{26,30},{28,24},{30,26}} | collective-permute-start | bytes 1916936 | tf_op jit(solution)/shard_map/ppermute | solution.py:336
  61.6 9.9 %collective-permute-start.11 = (bf16[48,6656]{1,0:T(8,128)(2,1)S(1)}, bf16[48,6656]{1,0:T(8,128)(2,1)S(1)}, u32[]{:S(2)}, u32[]{:S(2)}) collective-permute-start(bf16[48,6656]{1,0:T(8,128)(2,1)S(1)} %collective-permute-done.6.refs_5_), channel_id=1, source_target_pairs={{9,1},{11,3},{13,5},{15,7},{17,25},{19,27},{21,29},{23,31}} | collective-permute-start | bytes 1916936 | tf_op jit(solution)/shard_map/ppermute | solution.py:337
  62.9 6.7 %collective-permute-start.12 = (f32[184,384]{1,0:T(8,128)S(1)}, f32[184,384]{1,0:T(8,128)S(1)}, u32[]{:S(2)}, u32[]{:S(2)}) collective-permute-start(f32[184,384]{1,0:T(8,128)S(1)} %add.34), channel_id=1, source_target_pairs={{0,2},{1,3},{2,0},{3,1},{4,6},{5,7},{6,4},{7,5},{8,10},{9,11},{10,... | collective-permute-start | bytes 847880 | tf_op jit(solution)/shard_map/ppermute | solution.py:296
  74.9 10.7 %copy-start.3 = (f32[384,512]{1,0:T(8,128)S(1)}, f32[384,512]{1,0:T(8,128)}, u32[]{:S(2)}) copy-start(f32[384,512]{1,0:T(8,128)} %refs_9_.1) | copy-start | bytes 2359300
  74.9 1.5 %collective-permute-start.15 = (f32[144,384]{1,0:T(8,128)S(1)}, f32[144,384]{1,0:T(8,128)S(1)}, u32[]{:S(2)}, u32[]{:S(2)}) collective-permute-start(f32[144,384]{1,0:T(8,128)S(1)} %get-tuple-element.42), channel_id=1, source_target_pairs={{0,1},{1,0},{2,3},{3,2},{4,5},{5,4},{6,7},{7,6},{8,9},{9,8},{10,11... | collective-permute-start | bytes 663560 | tf_op jit(solution)/shard_map/ppermute | solution.py:296
  75.0 3.9 %collective-permute-start.13 = (f32[384,256]{1,0:T(8,128)S(1)}, f32[384,256]{1,0:T(8,128)S(1)}, u32[]{:S(2)}, u32[]{:S(2)}) collective-permute-start(f32[384,256]{1,0:T(8,128)S(1)} %get-tuple-element.37.refs_0_), channel_id=1, source_target_pairs={{0,1},{1,0},{2,3},{3,2},{4,5},{5,4},{6,7},{7,6},{8,9},{9,8},{10,11... | collective-permute-start | bytes 1179656 | tf_op jit(solution)/shard_map/ppermute | solution.py:296
  75.8 2.3 %collective-permute-start.14 = (f32[184,384]{1,0:T(8,128)S(1)}, f32[184,384]{1,0:T(8,128)S(1)}, u32[]{:S(2)}, u32[]{:S(2)}) collective-permute-start(f32[184,384]{1,0:T(8,128)S(1)} %add.37.refs_3_), channel_id=1, source_target_pairs={{0,1},{1,0},{2,3},{3,2},{4,5},{5,4},{6,7},{7,6},{8,9},{9,8},{10,11... | collective-permute-start | bytes 847880 | tf_op jit(solution)/shard_map/ppermute | solution.py:296
  76.4 7.5 %collective-permute-start.16 = (f32[144,384]{1,0:T(8,128)S(1)}, f32[144,384]{1,0:T(8,128)S(1)}, u32[]{:S(2)}, u32[]{:S(2)}) collective-permute-start(f32[144,384]{1,0:T(8,128)S(1)} %add.38), channel_id=1, source_target_pairs={{0,2},{1,3},{2,0},{3,1},{4,6},{5,7},{6,4},{7,5},{8,10},{9,11},{10,... | collective-permute-start | bytes 663560 | tf_op jit(solution)/shard_map/ppermute | solution.py:296
  78.1 0.7 copy-start.4
  78.8 1.0 %copy-start.5 = (f32[184,384]{1,0:T(8,128)S(1)}, f32[184,384]{1,0:T(8,128)}, u32[]{:S(2)}) copy-start(f32[184,384]{1,0:T(8,128)} %copy-done.4) | copy-start | bytes 847876
  84.0 1.5 %collective-permute-start.17 = (f32[144,384]{1,0:T(8,128)S(1)}, f32[144,384]{1,0:T(8,128)S(1)}, u32[]{:S(2)}, u32[]{:S(2)}) collective-permute-start(f32[144,384]{1,0:T(8,128)S(1)} %add.39.refs_3_), channel_id=1, source_target_pairs={{0,1},{1,0},{2,3},{3,2},{4,5},{5,4},{6,7},{7,6},{8,9},{9,8},{10,11... | collective-permute-start | bytes 663560 | tf_op jit(solution)/shard_map/ppermute | solution.py:296
